TPU v7x, 512 devices: a whole 4x4x16 slice. The times are simulated.
512 devices in a mesh: grp: 16 (over z_hi, x), dev: 32 (over y, z_lo, core).
Axes of the slice: x: 4, y: 4, z: 16 (z_hi: 4, z_lo: 4; z = z_hi * 4 + z_lo), core: 2. Of those that a mesh axis runs over, the one named last changes fastest.
Arguments:
- embeddings: float32 [114688, 1024], P(('grp', 'dev')), may hold values from -120 to 120
- partner: int32 [114688], P(('grp', 'dev')), may hold values from 0 to 114687, as said below
Outputs:
- loss: float32 [], replicated
- grad: float32 [114688, 1024], P(('grp', 'dev'))
Inputs may be any that keep to these rules, and one draw needn't show every extreme that they name: partner[partner[i]] == i and partner[i] != i for every i, and partner[i] lies in the same aligned block of 448 rows as i.
All inputs are finite; a program needn't handle non-finite values.
Results may differ from a plain program's by a relative error of at most 0.00145.
The roundings to bfloat16 on the way count: a program that leaves them out, or rounds other values in their place, can miss the bound.
Values may be sent and summed in bfloat16 or wider, within the bound.
No kernel may reach another device: no remote copies, remote signals or barrier semaphores. Data moves between devices by JAX's collectives and lax.ppermute only.
A program may use at most 64 MiB of HBM per device.

v0:
```python
import jax
import jax.numpy as jnp
from jax import lax
from jax.sharding import PartitionSpec as P

ROUNDS = 6


SOFTMAX_TEMPER = 0.1


def shifted(value, axis, steps):
    count = lax.axis_size(axis)
    pairs = [(source, (source + steps) % count) for source in range(count)]
    return lax.ppermute(value, axis, pairs)


def tile_terms(own_rows, column_block, row_index, column_index, row_partner):
    similarity_logits = (
        lax.dot_general(
            own_rows, column_block, (((1,), (1,)), ((), ())), preferred_element_type=jnp.float32
        )
        / SOFTMAX_TEMPER
    )
    exponential_scores = jnp.where(
        row_index[:, None] == column_index[None, :],
        jnp.float32(0.0),
        jnp.exp(similarity_logits - 1.0 / SOFTMAX_TEMPER),
    )
    match = row_partner[:, None] == column_index[None, :]
    return (similarity_logits, exponential_scores, match)


def per_device(embeddings, partner):
    norm = jnp.sqrt(jnp.sum(embeddings * embeddings, axis=1, keepdims=True) + 1e-06)
    unit32 = embeddings / norm
    unit = unit32.astype(jnp.bfloat16)
    total_dev = lax.axis_size(("grp", "dev"))
    device_id = lax.axis_index(("grp", "dev"))
    row_block = embeddings.shape[0]
    width = embeddings.shape[1]
    local = jnp.arange(row_block, dtype=jnp.int32)
    row_index = device_id * row_block + local
    offsets = list(range(0, ROUNDS + 1))
    gathered = []
    sources = []
    row_total_sum = jnp.zeros((row_block,), jnp.float32)
    row_positive = jnp.zeros((row_block,), jnp.float32)
    for step in offsets:
        if step == 0:
            column_block = unit
        else:
            column_block = shifted(unit, ("grp", "dev"), step)
        source = (device_id - step) % total_dev
        column_index = source * row_block + local
        gathered.append(column_block)
        sources.append(source)
        similarity_logits, exponential_scores, match = tile_terms(
            unit, column_block, row_index, column_index, partner
        )
        picked = jnp.where(match, similarity_logits, jnp.float32(0.0))
        row_total_sum = row_total_sum + jnp.sum(exponential_scores, axis=1)
        row_positive = row_positive + jnp.sum(picked, axis=1)
        if step > 0:
            got_sum, got_pos = shifted(
                (jnp.sum(exponential_scores, axis=0), jnp.sum(picked, axis=0)),
                ("grp", "dev"),
                -step,
            )
            row_total_sum = row_total_sum + got_sum
            row_positive = row_positive + got_pos
    total_rows = row_block * total_dev
    local_loss = jnp.sum(jnp.log(row_total_sum) + 1.0 / SOFTMAX_TEMPER - row_positive)
    loss = lax.psum(local_loss, ("grp", "dev")) / total_rows
    unit_gradient = jnp.zeros((row_block, width), jnp.float32)
    for index, step in enumerate(offsets):
        column_block = gathered[index]
        source = sources[index]
        column_index = source * row_block + local
        similarity_logits, exponential_scores, match = tile_terms(
            unit, column_block, row_index, column_index, partner
        )
        if step == 0:
            denom_cols = row_total_sum
        else:
            denom_cols = shifted(row_total_sum, ("grp", "dev"), step)
        weight = (
            exponential_scores / row_total_sum[:, None]
            + exponential_scores / denom_cols[None, :]
            - 2.0 * match.astype(jnp.float32)
        ).astype(jnp.bfloat16)
        unit_gradient = unit_gradient + jnp.dot(
            weight, column_block, preferred_element_type=jnp.float32
        )
        if step > 0:
            term = lax.dot_general(
                weight, unit, (((0,), (0,)), ((), ())), preferred_element_type=jnp.float32
            )
            unit_gradient = unit_gradient + shifted(term, ("grp", "dev"), -step)
    unit_gradient = unit_gradient / SOFTMAX_TEMPER
    radial = jnp.sum(unit32 * unit_gradient, axis=1, keepdims=True)
    grad = (unit_gradient - unit32 * radial) / norm
    return (loss, grad)


def solution(mesh):
    in_specs = (P(("grp", "dev"), None), P(("grp", "dev")))
    out_specs = (P(), P(("grp", "dev"), None))
    return jax.shard_map(
        per_device, mesh=mesh, in_specs=in_specs, out_specs=out_specs, check_vma=False
    )
```

profile of v0, /device:TPU:1, one launch (start us, length us, event | category | flops | bytes accessed | tf_op | source)
XLA Modules:
  0.0 510.9 jit_solution(3709933465335567623)
XLA Ops:
  0.6 1.4 multiply_reduce_fusion.1
  2.2 4.9 collective-permute-start
  7.2 3.5 collective-permute-start.2
  10.7 3.6 collective-permute-start.4
  14.3 2.3 collective-permute-start.6
  16.6 5.2 %collective-permute-start.8 = (bf16[224,1024]{1,0:T(8,128)(2,1)S(1)}, bf16[224,1024]{1,0:T(8,128)(2,1)}, u32[]{:S(2)}, u32[]{:S(2)}) collective-permute-start(bf16[224,1024]{1,0:T(8,128)(2,1)S(1)} %fusion.88), channel_id=1, source_target_pairs={{0,5},{1,6},{2,7},{3,8},{4,9},{5,10},{6,11},{7,12},{8,13},{9,14},{... | collective-permute-start | bytes 1376264 | tf_op jit(solution)/shard_map/ppermute | solution.py:15
  22.3 4.4 collective-permute-start.10
  27.0 9.6 %collective-permute-done.2 = bf16[224,1024]{1,0:T(8,128)(2,1)S(1)} collective-permute-done((bf16[224,1024]{1,0:T(8,128)(2,1)S(1)}, bf16[224,1024]{1,0:T(8,128)(2,1)S(1)}, u32[]{:S(2)}, u32[]{:S(2)}) %collective-permute-start.2) | collective-permute-done | bytes 458784 | tf_op jit(solution)/shard_map/ppermute | solution.py:15
  36.9 7.6 %collective-permute-done.4 = bf16[224,1024]{1,0:T(8,128)(2,1)S(1)} collective-permute-done((bf16[224,1024]{1,0:T(8,128)(2,1)S(1)}, bf16[224,1024]{1,0:T(8,128)(2,1)S(1)}, u32[]{:S(2)}, u32[]{:S(2)}) %collective-permute-start.4) | collective-permute-done | bytes 458784 | tf_op jit(solution)/shard_map/ppermute | solution.py:15
  45.3 17.0 %collective-permute-done.6 = bf16[224,1024]{1,0:T(8,128)(2,1)S(1)} collective-permute-done((bf16[224,1024]{1,0:T(8,128)(2,1)S(1)}, bf16[224,1024]{1,0:T(8,128)(2,1)S(1)}, u32[]{:S(2)}, u32[]{:S(2)}) %collective-permute-start.6) | collective-permute-done | bytes 458784 | tf_op jit(solution)/shard_map/ppermute | solution.py:15
  63.1 24.8 %collective-permute-done.8 = bf16[224,1024]{1,0:T(8,128)(2,1)} collective-permute-done((bf16[224,1024]{1,0:T(8,128)(2,1)S(1)}, bf16[224,1024]{1,0:T(8,128)(2,1)}, u32[]{:S(2)}, u32[]{:S(2)}) %collective-permute-start.8) | collective-permute-done | bytes 458784 | tf_op jit(solution)/shard_map/ppermute | solution.py:15
  87.9 1.3 convolution_multiply_fusion.1
  89.3 35.9 %collective-permute-done.10 = bf16[224,1024]{1,0:T(8,128)(2,1)S(1)} collective-permute-done((bf16[224,1024]{1,0:T(8,128)(2,1)S(1)}, bf16[224,1024]{1,0:T(8,128)(2,1)S(1)}, u32[]{:S(2)}, u32[]{:S(2)}) %collective-permute-start.10) | collective-permute-done | bytes 458784 | tf_op jit(solution)/shard_map/ppermute | solution.py:15
  125.9 1.5 fusion.51
  127.4 1.9 collective-permute-start.17
  129.3 1.9 collective-permute-start.16
  131.3 1.9 collective-permute-start.15
  133.2 1.9 collective-permute-start.14
  135.1 1.9 collective-permute-start.13
  137.1 2.4 collective-permute-start.12
  139.5 3.4 collective-permute-start.11
  142.9 2.4 collective-permute-start.9
  145.3 1.9 collective-permute-start.7
  147.3 1.9 collective-permute-start.5
  149.2 2.2 collective-permute-start.3
  151.4 2.1 collective-permute-start.1
  153.8 2.5 collective-permute-done.1
  156.9 8.1 %collective-permute-start.28 = (f32[224]{0:T(256)S(1)}, f32[224]{0:T(256)S(1)}, u32[]{:S(2)}, u32[]{:S(2)}) collective-permute-start(f32[224]{0:T(256)S(1)} %get-tuple-element.63), channel_id=1, source_target_pairs={{0,6},{1,7},{2,8},{3,9},{4,10},{5,11},{6,12},{7,13},{8,14},{9,15},... | collective-permute-start | bytes 2696 | tf_op jit(solution)/shard_map/ppermute | solution.py:15
  165.1 2.8 collective-permute-start.26
  167.8 4.0 collective-permute-start.24
  171.8 5.1 collective-permute-start.22
  176.9 2.4 collective-permute-start.20
  179.7 110.0 %psum.7 = f32[]{:T(128)} all-reduce(f32[]{:T(128)} %get-tuple-element.62), channel_id=1, replica_groups=mesh['grp'=16,'dev'=32] {'grp','dev'}, use_global_device_ids=true, to_apply=%region_28.29 | all-reduce | flops 1 | bytes 8 | tf_op jit(solution)/shard_map/psum | solution.py:74
  290.4 3.4 collective-permute-start.18
  293.8 1.4 fusion.65
  295.7 3.6 collective-permute-start.29
  299.6 2.1 collective-permute-start.27
  302.2 5.2 %collective-permute-start.25 = (f32[224,1024]{1,0:T(8,128)S(1)}, f32[224,1024]{1,0:T(8,128)S(1)}, u32[]{:S(2)}, u32[]{:S(2)}) collective-permute-start(f32[224,1024]{1,0:T(8,128)S(1)} %fusion.73), channel_id=1, source_target_pairs={{0,508},{1,509},{2,510},{3,511},{4,0},{5,1},{6,2},{7,3},{8,4},{9,5... | collective-permute-start | bytes 2752520 | tf_op jit(solution)/shard_map/ppermute | solution.py:15
  307.8 3.3 collective-permute-start.23
  311.5 2.4 collective-permute-start.21
  314.3 44.7 %collective-permute-done.29 = f32[224,1024]{1,0:T(8,128)S(1)} collective-permute-done((f32[224,1024]{1,0:T(8,128)S(1)}, f32[224,1024]{1,0:T(8,128)S(1)}, u32[]{:S(2)}, u32[]{:S(2)}) %collective-permute-start.29) | collective-permute-done | bytes 917536 | tf_op jit(solution)/shard_map/ppermute | solution.py:15
  359.0 3.0 collective-permute-start.19
  362.0 1.4 fusion.71
  365.3 42.7 %collective-permute-done.27 = f32[224,1024]{1,0:T(8,128)S(1)} collective-permute-done((f32[224,1024]{1,0:T(8,128)S(1)}, f32[224,1024]{1,0:T(8,128)S(1)}, u32[]{:S(2)}, u32[]{:S(2)}) %collective-permute-start.27) | collective-permute-done | bytes 917536 | tf_op jit(solution)/shard_map/ppermute | solution.py:15
  408.0 45.3 %collective-permute-done.25 = f32[224,1024]{1,0:T(8,128)S(1)} collective-permute-done((f32[224,1024]{1,0:T(8,128)S(1)}, f32[224,1024]{1,0:T(8,128)S(1)}, u32[]{:S(2)}, u32[]{:S(2)}) %collective-permute-start.25) | collective-permute-done | bytes 917536 | tf_op jit(solution)/shard_map/ppermute | solution.py:15
  453.4 22.4 %collective-permute-done.23 = f32[224,1024]{1,0:T(8,128)S(1)} collective-permute-done((f32[224,1024]{1,0:T(8,128)S(1)}, f32[224,1024]{1,0:T(8,128)S(1)}, u32[]{:S(2)}, u32[]{:S(2)}) %collective-permute-start.23) | collective-permute-done | bytes 917536 | tf_op jit(solution)/shard_map/ppermute | solution.py:15
  475.8 22.3 %collective-permute-done.21 = f32[224,1024]{1,0:T(8,128)S(1)} collective-permute-done((f32[224,1024]{1,0:T(8,128)S(1)}, f32[224,1024]{1,0:T(8,128)S(1)}, u32[]{:S(2)}, u32[]{:S(2)}) %collective-permute-start.21) | collective-permute-done | bytes 917536 | tf_op jit(solution)/shard_map/ppermute | solution.py:15
  498.2 9.3 %collective-permute-done.19 = f32[224,1024]{1,0:T(8,128)S(1)} collective-permute-done((f32[224,1024]{1,0:T(8,128)S(1)}, f32[224,1024]{1,0:T(8,128)S(1)}, u32[]{:S(2)}, u32[]{:S(2)}) %collective-permute-start.19) | collective-permute-done | bytes 917536 | tf_op jit(solution)/shard_map/ppermute | solution.py:15
  (76 shorter events, 11.1 us)
Async XLA Ops:
  0.6 1.5 copy-start
  2.2 20.0 %collective-permute-start = (bf16[224,1024]{1,0:T(8,128)(2,1)S(1)}, bf16[224,1024]{1,0:T(8,128)(2,1)S(1)}, u32[]{:S(2)}, u32[]{:S(2)}) collective-permute-start(bf16[224,1024]{1,0:T(8,128)(2,1)S(1)} %fusion.88), channel_id=1, source_target_pairs={{0,1},{1,2},{2,3},{3,4},{4,5},{5,6},{6,7},{7,8},{8,9},{9,10},{10,1... | collective-permute-start | bytes 1376264 | tf_op jit(solution)/shard_map/ppermute | solution.py:15
  7.2 29.4 %collective-permute-start.2 = (bf16[224,1024]{1,0:T(8,128)(2,1)S(1)}, bf16[224,1024]{1,0:T(8,128)(2,1)S(1)}, u32[]{:S(2)}, u32[]{:S(2)}) collective-permute-start(bf16[224,1024]{1,0:T(8,128)(2,1)S(1)} %fusion.88), channel_id=1, source_target_pairs={{0,2},{1,3},{2,4},{3,5},{4,6},{5,7},{6,8},{7,9},{8,10},{9,11},{10,... | collective-permute-start | bytes 1376264 | tf_op jit(solution)/shard_map/ppermute | solution.py:15
  10.7 33.8 %collective-permute-start.4 = (bf16[224,1024]{1,0:T(8,128)(2,1)S(1)}, bf16[224,1024]{1,0:T(8,128)(2,1)S(1)}, u32[]{:S(2)}, u32[]{:S(2)}) collective-permute-start(bf16[224,1024]{1,0:T(8,128)(2,1)S(1)} %fusion.88), channel_id=1, source_target_pairs={{0,3},{1,4},{2,5},{3,6},{4,7},{5,8},{6,9},{7,10},{8,11},{9,12},{10... | collective-permute-start | bytes 1376264 | tf_op jit(solution)/shard_map/ppermute | solution.py:15
  14.3 48.0 %collective-permute-start.6 = (bf16[224,1024]{1,0:T(8,128)(2,1)S(1)}, bf16[224,1024]{1,0:T(8,128)(2,1)S(1)}, u32[]{:S(2)}, u32[]{:S(2)}) collective-permute-start(bf16[224,1024]{1,0:T(8,128)(2,1)S(1)} %fusion.88), channel_id=1, source_target_pairs={{0,4},{1,5},{2,6},{3,7},{4,8},{5,9},{6,10},{7,11},{8,12},{9,13},{1... | collective-permute-start | bytes 1376264 | tf_op jit(solution)/shard_map/ppermute | solution.py:15
  16.6 71.3 %collective-permute-start.8 = (bf16[224,1024]{1,0:T(8,128)(2,1)S(1)}, bf16[224,1024]{1,0:T(8,128)(2,1)}, u32[]{:S(2)}, u32[]{:S(2)}) collective-permute-start(bf16[224,1024]{1,0:T(8,128)(2,1)S(1)} %fusion.88), channel_id=1, source_target_pairs={{0,5},{1,6},{2,7},{3,8},{4,9},{5,10},{6,11},{7,12},{8,13},{9,14},{... | collective-permute-start | bytes 1376264 | tf_op jit(solution)/shard_map/ppermute | solution.py:15
  22.3 102.9 %collective-permute-start.10 = (bf16[224,1024]{1,0:T(8,128)(2,1)S(1)}, bf16[224,1024]{1,0:T(8,128)(2,1)S(1)}, u32[]{:S(2)}, u32[]{:S(2)}) collective-permute-start(bf16[224,1024]{1,0:T(8,128)(2,1)S(1)} %fusion.88), channel_id=1, source_target_pairs={{0,6},{1,7},{2,8},{3,9},{4,10},{5,11},{6,12},{7,13},{8,14},{9,15},... | collective-permute-start | bytes 1376264 | tf_op jit(solution)/shard_map/ppermute | solution.py:15
  36.9 88.3 %copy-start.5 = (f32[224,224]{0,1:T(8,128)}, f32[224,224]{0,1:T(8,128)S(1)}, u32[]{:S(2)}) copy-start(f32[224,224]{0,1:T(8,128)S(1)} %convolution_multiply_fusion.4) | copy-start | bytes 602116
  44.5 0.8 copy-start.1
  45.3 79.9 %copy-start.7 = (f32[224,224]{0,1:T(8,128)}, f32[224,224]{0,1:T(8,128)S(1)}, u32[]{:S(2)}) copy-start(f32[224,224]{0,1:T(8,128)S(1)} %convolution_multiply_fusion.3) | copy-start | bytes 602116
  62.3 0.8 copy-start.3
  63.1 62.1 %copy-start.9 = (f32[224,224]{0,1:T(8,128)}, f32[224,224]{0,1:T(8,128)S(1)}, u32[]{:S(2)}) copy-start(f32[224,224]{0,1:T(8,128)S(1)} %convolution_multiply_fusion.2) | copy-start | bytes 602116
  89.2 38.2 %copy-start.11 = (f32[224,224]{0,1:T(8,128)}, f32[224,224]{0,1:T(8,128)S(1)}, u32[]{:S(2)}) copy-start(f32[224,224]{0,1:T(8,128)S(1)} %convolution_multiply_fusion.1) | copy-start | bytes 602116
  125.2 2.2 copy-start.14
  125.2 0.7 copy-start.13
  127.4 9.6 %collective-permute-start.17 = (f32[224]{0:T(256)S(1)}, f32[224]{0:T(256)S(1)}, u32[]{:S(2)}, u32[]{:S(2)}) collective-permute-start(f32[224]{0:T(256)S(1)} %get-tuple-element.38), channel_id=1, source_target_pairs={{0,506},{1,507},{2,508},{3,509},{4,510},{5,511},{6,0},{7,1},{8,2},... | collective-permute-start | bytes 2696 | tf_op jit(solution)/shard_map/ppermute | solution.py:15
  129.3 10.1 %collective-permute-start.16 = (f32[224]{0:T(256)S(1)}, f32[224]{0:T(256)S(1)}, u32[]{:S(2)}, u32[]{:S(2)}) collective-permute-start(f32[224]{0:T(256)S(1)} %get-tuple-element.59), channel_id=1, source_target_pairs={{0,507},{1,508},{2,509},{3,510},{4,511},{5,0},{6,1},{7,2},{8,3},{9... | collective-permute-start | bytes 2696 | tf_op jit(solution)/shard_map/ppermute | solution.py:15
  131.3 11.7 %collective-permute-start.15 = (f32[224]{0:T(256)S(1)}, f32[224]{0:T(256)S(1)}, u32[]{:S(2)}, u32[]{:S(2)}) collective-permute-start(f32[224]{0:T(256)S(1)} %get-tuple-element.55), channel_id=1, source_target_pairs={{0,508},{1,509},{2,510},{3,511},{4,0},{5,1},{6,2},{7,3},{8,4},{9,5... | collective-permute-start | bytes 2696 | tf_op jit(solution)/shard_map/ppermute | solution.py:15
  133.2 12.1 %collective-permute-start.14 = (f32[224]{0:T(256)S(1)}, f32[224]{0:T(256)S(1)}, u32[]{:S(2)}, u32[]{:S(2)}) collective-permute-start(f32[224]{0:T(256)S(1)} %get-tuple-element.51), channel_id=1, source_target_pairs={{0,509},{1,510},{2,511},{3,0},{4,1},{5,2},{6,3},{7,4},{8,5},{9,6},... | collective-permute-start | bytes 2696 | tf_op jit(solution)/shard_map/ppermute | solution.py:15
  135.1 12.1 %collective-permute-start.13 = (f32[224]{0:T(256)S(1)}, f32[224]{0:T(256)S(1)}, u32[]{:S(2)}, u32[]{:S(2)}) collective-permute-start(f32[224]{0:T(256)S(1)} %get-tuple-element.47), channel_id=1, source_target_pairs={{0,510},{1,511},{2,0},{3,1},{4,2},{5,3},{6,4},{7,5},{8,6},{9,7},{1... | collective-permute-start | bytes 2696 | tf_op jit(solution)/shard_map/ppermute | solution.py:15
  137.1 12.1 %collective-permute-start.12 = (f32[224]{0:T(256)S(1)}, f32[224]{0:T(256)S(1)}, u32[]{:S(2)}, u32[]{:S(2)}) collective-permute-start(f32[224]{0:T(256)S(1)} %get-tuple-element.41), channel_id=1, source_target_pairs={{0,511},{1,0},{2,1},{3,2},{4,3},{5,4},{6,5},{7,6},{8,7},{9,8},{10,... | collective-permute-start | bytes 2696 | tf_op jit(solution)/shard_map/ppermute | solution.py:15
  139.5 11.9 %collective-permute-start.11 = (f32[224]{0:T(256)S(1)}, f32[224]{0:T(256)S(1)}, u32[]{:S(2)}, u32[]{:S(2)}) collective-permute-start(f32[224]{0:T(256)S(1)} %get-tuple-element.13), channel_id=1, source_target_pairs={{0,506},{1,507},{2,508},{3,509},{4,510},{5,511},{6,0},{7,1},{8,2},... | collective-permute-start | bytes 2696 | tf_op jit(solution)/shard_map/ppermute | solution.py:15
  142.9 10.6 %collective-permute-start.9 = (f32[224]{0:T(256)S(1)}, f32[224]{0:T(256)S(1)}, u32[]{:S(2)}, u32[]{:S(2)}) collective-permute-start(f32[224]{0:T(256)S(1)} %get-tuple-element.60), channel_id=1, source_target_pairs={{0,507},{1,508},{2,509},{3,510},{4,511},{5,0},{6,1},{7,2},{8,3},{9... | collective-permute-start | bytes 2696 | tf_op jit(solution)/shard_map/ppermute | solution.py:15
  145.3 8.3 %collective-permute-start.7 = (f32[224]{0:T(256)S(1)}, f32[224]{0:T(256)S(1)}, u32[]{:S(2)}, u32[]{:S(2)}) collective-permute-start(f32[224]{0:T(256)S(1)} %get-tuple-element.56), channel_id=1, source_target_pairs={{0,508},{1,509},{2,510},{3,511},{4,0},{5,1},{6,2},{7,3},{8,4},{9,5... | collective-permute-start | bytes 2696 | tf_op jit(solution)/shard_map/ppermute | solution.py:15
  147.3 6.3 %collective-permute-start.5 = (f32[224]{0:T(256)S(1)}, f32[224]{0:T(256)S(1)}, u32[]{:S(2)}, u32[]{:S(2)}) collective-permute-start(f32[224]{0:T(256)S(1)} %get-tuple-element.52), channel_id=1, source_target_pairs={{0,509},{1,510},{2,511},{3,0},{4,1},{5,2},{6,3},{7,4},{8,5},{9,6},... | collective-permute-start | bytes 2696 | tf_op jit(solution)/shard_map/ppermute | solution.py:15
  149.2 4.6 collective-permute-start.3
  151.4 4.9 collective-permute-start.1
  156.9 133.5 %collective-permute-start.28 = (f32[224]{0:T(256)S(1)}, f32[224]{0:T(256)S(1)}, u32[]{:S(2)}, u32[]{:S(2)}) collective-permute-start(f32[224]{0:T(256)S(1)} %get-tuple-element.63), channel_id=1, source_target_pairs={{0,6},{1,7},{2,8},{3,9},{4,10},{5,11},{6,12},{7,13},{8,14},{9,15},... | collective-permute-start | bytes 2696 | tf_op jit(solution)/shard_map/ppermute | solution.py:15
  165.1 130.6 %collective-permute-start.26 = (f32[224]{0:T(256)S(1)}, f32[224]{0:T(256)S(1)}, u32[]{:S(2)}, u32[]{:S(2)}) collective-permute-start(f32[224]{0:T(256)S(1)} %get-tuple-element.63), channel_id=1, source_target_pairs={{0,5},{1,6},{2,7},{3,8},{4,9},{5,10},{6,11},{7,12},{8,13},{9,14},{... | collective-permute-start | bytes 2696 | tf_op jit(solution)/shard_map/ppermute | solution.py:15
  167.8 131.8 %collective-permute-start.24 = (f32[224]{0:T(256)S(1)}, f32[224]{0:T(256)S(1)}, u32[]{:S(2)}, u32[]{:S(2)}) collective-permute-start(f32[224]{0:T(256)S(1)} %get-tuple-element.63), channel_id=1, source_target_pairs={{0,4},{1,5},{2,6},{3,7},{4,8},{5,9},{6,10},{7,11},{8,12},{9,13},{1... | collective-permute-start | bytes 2696 | tf_op jit(solution)/shard_map/ppermute | solution.py:15
  171.8 130.3 %collective-permute-start.22 = (f32[224]{0:T(256)S(1)}, f32[224]{0:T(256)S(1)}, u32[]{:S(2)}, u32[]{:S(2)}) collective-permute-start(f32[224]{0:T(256)S(1)} %get-tuple-element.63), channel_id=1, source_target_pairs={{0,3},{1,4},{2,5},{3,6},{4,7},{5,8},{6,9},{7,10},{8,11},{9,12},{10... | collective-permute-start | bytes 2696 | tf_op jit(solution)/shard_map/ppermute | solution.py:15
  176.9 130.9 %collective-permute-start.20 = (f32[224]{0:T(256)S(1)}, f32[224]{0:T(256)S(1)}, u32[]{:S(2)}, u32[]{:S(2)}) collective-permute-start(f32[224]{0:T(256)S(1)} %get-tuple-element.63), channel_id=1, source_target_pairs={{0,2},{1,3},{2,4},{3,5},{4,6},{5,7},{6,8},{7,9},{8,10},{9,11},{10,... | collective-permute-start | bytes 2696 | tf_op jit(solution)/shard_map/ppermute | solution.py:15
  290.4 21.1 %collective-permute-start.18 = (f32[224]{0:T(256)S(1)}, f32[224]{0:T(256)S(1)}, u32[]{:S(2)}, u32[]{:S(2)}) collective-permute-start(f32[224]{0:T(256)S(1)} %get-tuple-element.63), channel_id=1, source_target_pairs={{0,1},{1,2},{2,3},{3,4},{4,5},{5,6},{6,7},{7,8},{8,9},{9,10},{10,1... | collective-permute-start | bytes 2696 | tf_op jit(solution)/shard_map/ppermute | solution.py:15
  293.8 1.4 copy-start.15
  293.8 1.4 copy-start.16
  295.2 4.1 copy-start.12
  295.6 6.1 %copy-start.10 = (f32[224,224]{0,1:T(8,128)S(1)}, f32[224,224]{0,1:T(8,128)}, u32[]{:S(2)}) copy-start(f32[224,224]{0,1:T(8,128)} %copy-done.9) | copy-start | bytes 602116
  295.7 63.3 %collective-permute-start.29 = (f32[224,1024]{1,0:T(8,128)S(1)}, f32[224,1024]{1,0:T(8,128)S(1)}, u32[]{:S(2)}, u32[]{:S(2)}) collective-permute-start(f32[224,1024]{1,0:T(8,128)S(1)} %fusion.65), channel_id=1, source_target_pairs={{0,506},{1,507},{2,508},{3,509},{4,510},{5,511},{6,0},{7,1},{8,2},... | collective-permute-start | bytes 2752520 | tf_op jit(solution)/shard_map/ppermute | solution.py:15
  299.6 7.8 %copy-start.8 = (f32[224,224]{0,1:T(8,128)S(1)}, f32[224,224]{0,1:T(8,128)}, u32[]{:S(2)}) copy-start(f32[224,224]{0,1:T(8,128)} %copy-done.7) | copy-start | bytes 602116
  299.6 108.4 %collective-permute-start.27 = (f32[224,1024]{1,0:T(8,128)S(1)}, f32[224,1024]{1,0:T(8,128)S(1)}, u32[]{:S(2)}, u32[]{:S(2)}) collective-permute-start(f32[224,1024]{1,0:T(8,128)S(1)} %fusion.69), channel_id=1, source_target_pairs={{0,507},{1,508},{2,509},{3,510},{4,511},{5,0},{6,1},{7,2},{8,3},{9... | collective-permute-start | bytes 2752520 | tf_op jit(solution)/shard_map/ppermute | solution.py:15
  302.2 9.0 %copy-start.6 = (f32[224,224]{0,1:T(8,128)S(1)}, f32[224,224]{0,1:T(8,128)}, u32[]{:S(2)}) copy-start(f32[224,224]{0,1:T(8,128)} %copy-done.5) | copy-start | bytes 602116
  302.2 151.2 %collective-permute-start.25 = (f32[224,1024]{1,0:T(8,128)S(1)}, f32[224,1024]{1,0:T(8,128)S(1)}, u32[]{:S(2)}, u32[]{:S(2)}) collective-permute-start(f32[224,1024]{1,0:T(8,128)S(1)} %fusion.73), channel_id=1, source_target_pairs={{0,508},{1,509},{2,510},{3,511},{4,0},{5,1},{6,2},{7,3},{8,4},{9,5... | collective-permute-start | bytes 2752520 | tf_op jit(solution)/shard_map/ppermute | solution.py:15
  307.8 168.0 %collective-permute-start.23 = (f32[224,1024]{1,0:T(8,128)S(1)}, f32[224,1024]{1,0:T(8,128)S(1)}, u32[]{:S(2)}, u32[]{:S(2)}) collective-permute-start(f32[224,1024]{1,0:T(8,128)S(1)} %fusion.77), channel_id=1, source_target_pairs={{0,509},{1,510},{2,511},{3,0},{4,1},{5,2},{6,3},{7,4},{8,5},{9,6},... | collective-permute-start | bytes 2752520 | tf_op jit(solution)/shard_map/ppermute | solution.py:15
  311.5 186.7 %collective-permute-start.21 = (f32[224,1024]{1,0:T(8,128)S(1)}, f32[224,1024]{1,0:T(8,128)S(1)}, u32[]{:S(2)}, u32[]{:S(2)}) collective-permute-start(f32[224,1024]{1,0:T(8,128)S(1)} %fusion.81), channel_id=1, source_target_pairs={{0,510},{1,511},{2,0},{3,1},{4,2},{5,3},{6,4},{7,5},{8,6},{9,7},{1... | collective-permute-start | bytes 2752520 | tf_op jit(solution)/shard_map/ppermute | solution.py:15
  314.3 49.2 %copy-start.4 = (bf16[224,1024]{1,0:T(8,128)(2,1)S(1)}, bf16[224,1024]{1,0:T(8,128)(2,1)}, u32[]{:S(2)}) copy-start(bf16[224,1024]{1,0:T(8,128)(2,1)} %copy-done.3) | copy-start | bytes 1376260
  359.0 148.4 %collective-permute-start.19 = (f32[224,1024]{1,0:T(8,128)S(1)}, f32[224,1024]{1,0:T(8,128)S(1)}, u32[]{:S(2)}, u32[]{:S(2)}) collective-permute-start(f32[224,1024]{1,0:T(8,128)S(1)} %fusion.85), channel_id=1, source_target_pairs={{0,511},{1,0},{2,1},{3,2},{4,3},{5,4},{6,5},{7,6},{8,7},{9,8},{10,... | collective-permute-start | bytes 2752520 | tf_op jit(solution)/shard_map/ppermute | solution.py:15
  363.4 1.0 copy-start.2
where the time goes:
time: 512 us; the launch traced here: 511 us
  waiting for transfers between devices  285 us (56%)
  blocking collectives  110 us (21%)
  starting transfers between devices  95.2 us (19%)
  matrix products  12.3 us (2%)
    ppermute x30, waiting for transfers between devices, shifted(): return lax.ppermute(value, axis, pairs)  285 us
    psum x1, blocking collectives, per_device(): loss = lax.psum(local_loss, ('grp', 'dev')) / total_rows  110 us
    ppermute x30, starting transfers between devices, shifted(): return lax.ppermute(value, axis, pairs)  95.2 us
  transfers between devices with their start and end apart: 30, of which 13 were waited for; matrix products, arithmetic and copies ran while one was open for 2% of the time, Pallas kernels for 0%

commit v1 on v0

v1 whole, which is shorter than its diff:
```python
import jax
import jax.numpy as jnp
import numpy as np
from jax import lax
from jax.experimental import pallas as pl
from jax.experimental.pallas import tpu as pltpu
from jax.sharding import Mesh
from jax.sharding import PartitionSpec as P

ROUNDS = 6
SOFTMAX_TEMPER = 0.1
AXES = ("zh", "x", "y", "zl", "core")
SHAPE = (4, 4, 4, 4, 2)
RUNS = 64
DEV_AXES = ("y", "zl", "core")
ROWS = 224
WIDTH = 1024

RECEIVED = np.array([[1, 2, 3], [3, 0, 2], [0, 3, 1], [2, 1, 0]], np.int32)


def crosses(run):
    return run % 16 == 15


def routes():
    names = ("P1", "P2", "P3a", "P3b", "Y1", "Y2", "Y3a", "Y3b", "X1", "X2", "X3", "X4", "X5", "X6")
    table = {name: [] for name in names}

    def chip(run, k):
        return (run % RUNS) * 4 + k

    def add(name, *pairs):
        for source, target in pairs:
            for core in (0, 1):
                table[name].append((2 * source + core, 2 * target + core))

    for run in range(RUNS):
        for name, moves in (
            ("P1", ((0, 2), (1, 0), (2, 3), (3, 1))),
            ("P2", ((1, 3), (2, 0), (0, 1), (3, 2))),
            ("P3a", ((2, 3), (1, 0))),
            ("P3b", ((1, 2), (2, 1))),
        ):
            add(name, *((chip(run, a), chip(run, b)) for a, b in moves))
        for name, ups, downs in (
            ("Y1", (0, 1), (2, 3)),
            ("Y2", (0, 2), (1, 3)),
            ("Y3a", (0,), (3,)),
            ("Y3b", (1,), (2,)),
        ):
            if not crosses(run):
                add(name, *((chip(run, k), chip(run + 1, k)) for k in ups))
            if not crosses(run - 1):
                add(name, *((chip(run, k), chip(run - 1, k)) for k in downs))
        if crosses(run):
            low = [chip(run, k) for k in range(4)]
            high = [chip(run + 1, k) for k in range(4)]
            for name in ("X1", "X3", "X4"):
                add(name, (low[3], high[0]), (high[0], low[3]))
            for name in ("X2", "X5"):
                add(name, (high[0], high[1]), (low[3], low[2]))
            add("X6", (high[1], high[2]), (low[2], low[1]))
    return table


ROUTES = routes()


def edge_routes():
    pairs = []
    for group in range(16):
        for inner in range(8):
            pairs.append((group * 32 + 24 + inner, ((group + 1) % 16) * 32 + inner))
            pairs.append((group * 32 + inner, ((group - 1) % 16) * 32 + 24 + inner))
    return pairs


EDGE = edge_routes()


def after(value, *others):
    return lax.optimization_barrier((value,) + others)[0]


def vmem(count):
    return [pl.BlockSpec(memory_space=pltpu.VMEM)] * count


def smem(count):
    return [pl.BlockSpec(memory_space=pltpu.SMEM)] * count


PARAMS = pltpu.CompilerParams(vmem_limit_bytes=48 * 1024 * 1024)


def scores(rows, columns):
    return lax.dot_general(rows, columns, (((1,), (1,)), ((), ())), preferred_element_type=jnp.float32)


def fold(values):
    tail = jnp.concatenate([values[:, 128:], jnp.zeros((ROWS, 256 - ROWS), jnp.float32)], axis=1)
    return values[:, :128] + tail


def own_kernel(unit_ref, other_ref, partner_ref, e_own_ref, e_other_ref, sum_own_ref, sum_other_ref, pos_ref):
    unit = unit_ref[...]
    row = lax.broadcasted_iota(jnp.int32, (ROWS, ROWS), 0)
    column = lax.broadcasted_iota(jnp.int32, (ROWS, ROWS), 1)
    partner = partner_ref[...]
    logits = scores(unit, unit) / SOFTMAX_TEMPER
    expo = jnp.where(row == column, 0.0, jnp.exp(logits - 1.0 / SOFTMAX_TEMPER))
    e_own_ref[...] = expo
    sum_own_ref[...] = fold(expo)
    picked = jnp.where(partner == row, logits, 0.0)
    logits = scores(other_ref[...], unit) / SOFTMAX_TEMPER
    expo = jnp.exp(logits - 1.0 / SOFTMAX_TEMPER)
    e_other_ref[...] = expo
    sum_other_ref[...] = fold(expo)
    picked = picked + jnp.where(partner == row + ROWS, logits, 0.0)
    pos_ref[...] = jnp.sum(fold(picked), axis=0, keepdims=True)


def own_call(unit, other, partner):
    f32 = jnp.float32
    return pl.pallas_call(
        own_kernel,
        out_shape=(
            jax.ShapeDtypeStruct((ROWS, ROWS), f32),
            jax.ShapeDtypeStruct((ROWS, ROWS), f32),
            jax.ShapeDtypeStruct((ROWS, 128), f32),
            jax.ShapeDtypeStruct((ROWS, 128), f32),
            jax.ShapeDtypeStruct((1, 128), f32),
        ),
        in_specs=vmem(3),
        out_specs=tuple(vmem(5)),
        compiler_params=PARAMS,
        cost_estimate=pl.CostEstimate(flops=2 * 448 * ROWS * WIDTH, bytes_accessed=2 << 20, transcendentals=448 * ROWS),
        name="own_scores",
    )(unit, other, partner)


def block_kernel(n_cand, last, *refs):
    flags_ref, unit_ref, other_ref, sum_own_ref, sum_other_ref = refs[:5]
    cands = refs[5 : 5 + n_cand]
    rest = refs[5 + n_cand :]
    if last:
        pos_ref, rest = rest[0], rest[1:]
    e_own_ref, e_other_ref = rest[:2]
    rest = rest[2:]
    if last:
        pay_ref, rest = rest[0], rest[1:]
    else:
        sum_own_out, sum_other_out = rest[:2]
        rest = rest[2:]
    if n_cand > 1:
        block_ref, rest = rest[0], rest[1:]
        block_ref[...] = cands[0][...]
        for number in range(1, n_cand):

            @pl.when(flags_ref[0] == number)
            def _(number=number):
                block_ref[...] = cands[number][...]
    else:
        block_ref = cands[0]
    block = block_ref[...]
    expo = jnp.exp(scores(unit_ref[...], block) / SOFTMAX_TEMPER - 1.0 / SOFTMAX_TEMPER)
    e_own_ref[...] = expo
    sum_own = sum_own_ref[...] + fold(expo)
    expo = jnp.exp(scores(other_ref[...], block) / SOFTMAX_TEMPER - 1.0 / SOFTMAX_TEMPER)
    expo = jnp.where(flags_ref[1] == 1, 0.0, expo)
    e_other_ref[...] = expo
    sum_other = sum_other_ref[...] + fold(expo)
    if last:
        pay_ref[...] = jnp.zeros((8, 128), jnp.float32)
        for half, total in enumerate((sum_own, sum_other)):
            across = jnp.sum(jnp.transpose(total), axis=0, keepdims=True)
            pay_ref[2 * half : 2 * half + 1, :] = across[:, :128]
            pay_ref[2 * half + 1 : 2 * half + 2, : ROWS - 128] = across[:, 128:]
        pay_ref[4:5, :] = pos_ref[...]
    else:
        sum_own_out[...] = sum_own
        sum_other_out[...] = sum_other


def block_call(flags, unit, other, sums, cands, pos=None):
    f32 = jnp.float32
    last = pos is not None
    n = len(cands)
    shapes = [jax.ShapeDtypeStruct((ROWS, ROWS), f32)] * 2
    if last:
        shapes.append(jax.ShapeDtypeStruct((8, 128), f32))
    else:
        shapes += [jax.ShapeDtypeStruct((ROWS, 128), f32)] * 2
    if n > 1:
        shapes.append(jax.ShapeDtypeStruct((ROWS, WIDTH), jnp.bfloat16))
    operands = [unit, other, *sums, *cands] + ([pos] if last else [])

    def kernel(*refs):
        block_kernel(n, last, *refs)

    out = pl.pallas_call(
        kernel,
        out_shape=tuple(shapes),
        in_specs=smem(1) + vmem(len(operands)),
        out_specs=tuple(vmem(len(shapes))),
        compiler_params=PARAMS,
        cost_estimate=pl.CostEstimate(flops=2 * 448 * ROWS * WIDTH, bytes_accessed=2 << 20, transcendentals=448 * ROWS),
        name="block_scores",
    )(flags, *operands)
    block = out[-1] if n > 1 else cands[0]
    if last:
        return out[:2], out[2], block
    return out[:2], out[2:4], block


def denom_kernel(place_ref, pay_ref, inv_ref, other_ref, edge_ref, loss_ref):
    y, k, core = place_ref[0], place_ref[1], place_ref[2]
    pay = pay_ref[...].reshape(16, 2, 8, 128)
    lane = lax.broadcasted_iota(jnp.int32, (16, 2, 128), 2)
    part = lax.broadcasted_iota(jnp.int32, (16, 2, 128), 1)
    real = part * 128 + lane < ROWS
    first = jnp.where(real, pay[:, 0, 0:2] + pay[:, 1, 2:4], 1.0)
    second = jnp.where(real, pay[:, 1, 0:2] + pay[:, 0, 2:4], 1.0)
    total = jnp.log(first) + jnp.log(second)
    total = jnp.sum(total.reshape(32, 128), axis=0, keepdims=True)
    total = total - jnp.sum(pay[:, :, 4].reshape(32, 128), axis=0, keepdims=True)
    loss_ref[...] = jnp.broadcast_to(jnp.sum(total, axis=1, keepdims=True), (8, 128))
    first, second = 1.0 / first, 1.0 / second
    inv_ref[...] = jnp.where(core == 0, first, second)
    other_all = jnp.where(core == 0, second, first)
    chip = lax.broadcasted_iota(jnp.int32, (16, 2, 128), 0)
    other_ref[...] = jnp.sum(jnp.where(chip == y * 4 + k, other_all, 0.0), axis=0)
    edge_ref[...] = inv_ref[pl.ds(jnp.where(y == 3, 12, 0), 4)]


def denom_call(place, pay):
    f32 = jnp.float32
    return pl.pallas_call(
        denom_kernel,
        out_shape=(
            jax.ShapeDtypeStruct((16, 2, 128), f32),
            jax.ShapeDtypeStruct((2, 128), f32),
            jax.ShapeDtypeStruct((4, 2, 128), f32),
            jax.ShapeDtypeStruct((8, 128), f32),
        ),
        in_specs=smem(1) + vmem(1),
        out_specs=tuple(vmem(4)),
        compiler_params=PARAMS,
        name="denoms",
    )(place, pay)


def lanes(pair):
    return jnp.concatenate([pair[0:1, :], pair[1:2, : ROWS - 128]], axis=1)


def grad_kernel(shift, *refs):
    where_ref, inv_ref, edge_ref, row_ref, partner_ref = refs[:5]
    expos, blocks = refs[5:12], refs[12:19]
    out_ref = refs[19]
    mine = lanes(row_ref[...])
    mine = jnp.transpose(jnp.broadcast_to(mine, (128, ROWS)))[:, 0:1]
    total = None
    for number in range(7):
        place = where_ref[number]
        inside = inv_ref[pl.ds(jnp.minimum(place, 15), 1)]
        outside = edge_ref[pl.ds(jnp.maximum(place - 16, 0), 1)]
        column = lanes(jnp.where(place < 16, inside, outside)[0])
        weight = expos[number][...] * (mine + column)
        if number == 0:
            row = lax.broadcasted_iota(jnp.int32, (ROWS, ROWS), 0) + shift
            weight = weight - jnp.where(partner_ref[...] == row, 2.0, 0.0)
        term = jnp.dot(weight.astype(jnp.bfloat16), blocks[number][...], preferred_element_type=jnp.float32)
        total = term if total is None else total + term
    out_ref[...] = total


def grad_call(shift, where, inv, edge, row, partner, expos, blocks):
    def kernel(*refs):
        grad_kernel(shift, *refs)

    return pl.pallas_call(
        kernel,
        out_shape=jax.ShapeDtypeStruct((ROWS, WIDTH), jnp.float32),
        in_specs=smem(1) + vmem(18),
        out_specs=pl.BlockSpec(memory_space=pltpu.VMEM),
        compiler_params=PARAMS,
        cost_estimate=pl.CostEstimate(flops=2 * 7 * ROWS * ROWS * WIDTH, bytes_accessed=6 << 20, transcendentals=0),
        name="unit_gradient",
    )(where, inv, edge, row, partner, *expos, *blocks)


def final_kernel(emb_ref, mine_ref, got_ref, out_ref):
    emb = emb_ref[...]
    norm = jnp.sqrt(jnp.sum(emb * emb, axis=1, keepdims=True) + 1e-06)
    unit32 = emb / norm
    unit_gradient = (mine_ref[...] + got_ref[...]) / SOFTMAX_TEMPER
    radial = jnp.sum(unit32 * unit_gradient, axis=1, keepdims=True)
    out_ref[...] = (unit_gradient - unit32 * radial) / norm


def final_call(emb, mine, got):
    spec = pl.BlockSpec((56, WIDTH), lambda i: (i, 0))
    return pl.pallas_call(
        final_kernel,
        out_shape=jax.ShapeDtypeStruct((ROWS, WIDTH), jnp.float32),
        grid=(4,),
        in_specs=[spec] * 3,
        out_specs=spec,
        compiler_params=PARAMS,
        cost_estimate=pl.CostEstimate(flops=10 * ROWS * WIDTH, bytes_accessed=16 * ROWS * WIDTH, transcendentals=0),
        name="final",
    )(emb, mine, got)


def send(value, name):
    return lax.ppermute(value, AXES, ROUTES[name])


def per_device(embeddings, partner):
    norm = jnp.sqrt(jnp.sum(embeddings * embeddings, axis=1, keepdims=True) + 1e-06)
    unit = (embeddings / norm).astype(jnp.bfloat16)

    core = lax.axis_index("core")
    k = lax.axis_index("zl")
    y = lax.axis_index("y")
    run = lax.axis_index(("zh", "x", "y"))
    below, above = run % 16 == 15, run % 16 == 0
    end = (below & (k == 3)) | (above & (k == 0))
    mid = (below & (k == 2)) | (above & (k == 1))
    inner = (k == 1) | (k == 2)

    local = (partner % (2 * ROWS) - core * ROWS) % (2 * ROWS)
    local = local.reshape(1, ROWS).astype(jnp.int32)

    sources = jnp.asarray(RECEIVED)[k]
    steps_in = sources - k
    steps_out = jnp.where(steps_in < 0, steps_in + 4, steps_in - 4)
    excluded = jnp.where(core == 0, -3, 3)
    out_in = (steps_in == excluded).astype(jnp.int32)
    out_out = (steps_out == excluded).astype(jnp.int32)
    line = y + jnp.where(steps_in < 0, 1, -1)
    place_in = y * 4 + sources
    place_out = jnp.where((line < 0) | (line > 3), 16 + sources, line * 4 + sources)
    where = jnp.concatenate([(y * 4 + k)[None], place_in, place_out]).astype(jnp.int32)
    pick3 = inner.astype(jnp.int32)
    pick_y1 = jnp.where(end, 2, jnp.where(mid, 1, 0)).astype(jnp.int32)
    pick_y2 = jnp.where(end, 1, jnp.where(mid_receiver(below, above, k), 2, 0)).astype(jnp.int32)
    pick_y3 = jnp.where(end, 2, jnp.where(mid, 3, inner.astype(jnp.int32))).astype(jnp.int32)
    zero = jnp.int32(0)

    other = lax.ppermute(unit, ("core",), [(0, 1), (1, 0)])
    r1 = send(unit, "P1")
    x1 = send(unit, "X1")
    expo0, pos = None, None
    e_own, e_other, sum_own, sum_other, pos = own_call(unit, other, local)
    expos, blocks, sums = [(e_own, e_other)], [unit], (sum_own, sum_other)

    def add(flags, cands, last=False):
        nonlocal sums
        pair, rest, block = block_call(jnp.stack(flags), unit, other, sums, cands, pos if last else None)
        expos.append(pair)
        blocks.append(block)
        if last:
            return rest
        sums = rest

    r2 = send(after(unit, sum_own), "P2")
    y1 = send(r1, "Y1")
    x2 = send(x1, "X2")
    x3 = send(r1, "X3")
    add([zero, out_in[0]], [r1])
    p3b = send(unit, "P3b")
    p3a = send(r1, "P3a")
    x5 = send(x3, "X5")
    y2 = send(r2, "Y2")
    x4 = send(r2, "X4")
    x6 = send(x2, "X6")
    add([zero, out_in[1]], [r2])
    y3a = send(p3a, "Y3a")
    y3b = send(p3b, "Y3b")
    add([pick3, out_in[2]], [p3a, p3b])
    add([pick_y1, out_out[0]], [y1, x2, x4])
    add([pick_y2, out_out[1]], [y2, x3, x6])
    pay = add([pick_y3, out_out[2]], [y3a, y3b, x1, x5], last=True)

    pays = lax.all_to_all(jnp.broadcast_to(pay[None], (32, 8, 128)), DEV_AXES, 0, 0)
    place = jnp.stack([y, k, core]).astype(jnp.int32)
    inv, other_inv, edge, loss = denom_call(place, pays)
    edge = lax.ppermute(edge, AXES, EDGE)
    mine_inv = lax.dynamic_index_in_dim(inv, y * 4 + k, 0, keepdims=False)

    for_other = grad_call(ROWS, where, inv, edge, other_inv, local, [e[1] for e in expos], blocks)
    got = lax.ppermute(for_other, ("core",), [(0, 1), (1, 0)])
    mine = grad_call(0, where, inv, edge, mine_inv, local, [e[0] for e in expos], blocks)
    grad = final_call(embeddings, mine, got)

    for axis, bit in (("x", 1), ("x", 2), ("zh", 1), ("zh", 2)):
        loss = loss + lax.ppermute(loss, (axis,), [(i, i ^ bit) for i in range(4)])
    total_rows = ROWS * 512
    loss = loss[0, 0] / total_rows + 1.0 / SOFTMAX_TEMPER
    return (loss, grad)


def mid_receiver(below, above, k):
    return (below & (k == 1)) | (above & (k == 2))


def solution(mesh):
    split = Mesh(mesh.devices.reshape(SHAPE), AXES)
    in_specs = (P(AXES, None), P(AXES))
    out_specs = (P(), P(AXES, None))
    return jax.shard_map(per_device, mesh=split, in_specs=in_specs, out_specs=out_specs, check_vma=False)
```

time: 512 us -> 179 us (0.35)
  the two profiles are of different devices: /device:TPU:1 before, /device:TPU:30 now
where the time goes in v1:
time: 179 us; the launch traced here: 178 us
  starting transfers between devices  79.1 us (44%)
  waiting for transfers between devices  41.6 us (23%)
  local copies, waits for them, and re-layouts  29.3 us (16%)
  Pallas kernels  18.8 us (11%)
  other arithmetic  6.03 us (3%)
  between operations  2.86 us (2%)
    unnamed x82, local copies, waits for them, and re-layouts  27.4 us
    ppermute x14, starting transfers between devices, send(): return lax.ppermute(value, AXES, ROUTES[name])  26 us
    ppermute x4, starting transfers between devices, per_device(): loss = loss + lax.ppermute(loss, (axis,), [(i, i ^ bit) for i in range(4)])  25.5 us
    ppermute x14, waiting for transfers between devices, send(): return lax.ppermute(value, AXES, ROUTES[name])  19.3 us
    all_to_all x1, starting transfers between devices, per_device(): lax.all_to_all(jnp.broadcast_to(pay[None], (32, 8, 128)), DEV_AXES, 0, 0)  15.4 us
    ppermute x4, waiting for transfers between devices, per_device(): loss = loss + lax.ppermute(loss, (axis,), [(i, i ^ bit) for i in range(4)])  10.2 us
    pallas_call x6, Pallas kernels, block_call(): pl.pallas_call(kernel, out_shape=tuple(shapes), in_specs=smem(1) + vmem(l...  9.47 us
    ppermute x1, starting transfers between devices, per_device(): edge = lax.ppermute(edge, AXES, EDGE)  8.31 us
  transfers between devices with their start and end apart: 22, of which 9 were waited for; matrix products, arithmetic and copies ran while one was open for 3% of the time, Pallas kernels for 6%

profile of v1, /device:TPU:30, one launch (start us, length us, event | category | flops | bytes accessed | tf_op | source)
XLA Modules:
  0.0 177.6 jit_solution(3939178184975949648)
XLA Ops:
  0.6 1.4 multiply_reduce_fusion
  2.2 1.9 %collective-permute-start = (bf16[224,1024]{1,0:T(8,128)(2,1)S(1)}, bf16[224,1024]{1,0:T(8,128)(2,1)S(1)}, u32[]{:S(2)}, u32[]{:S(2)}) collective-permute-start(bf16[224,1024]{1,0:T(8,128)(2,1)S(1)} %divide_convert_fusion.unit_ref.refs_1_.refs_12_), channel_id=1, source_target_pairs={{0,1},{1,0},{2,3},{3,2},{4,5},{5,4},{6,7},{7,6},{8,9},{9,8},{10,11... | collective-permute-start | bytes 1376264 | tf_op jit(solution)/shard_map/ppermute | solution.py:353
  4.2 5.2 %collective-permute-start.1 = (bf16[224,1024]{1,0:T(8,128)(2,1)S(1)}, bf16[224,1024]{1,0:T(8,128)(2,1)S(1)}, u32[]{:S(2)}, u32[]{:S(2)}) collective-permute-start(bf16[224,1024]{1,0:T(8,128)(2,1)S(1)} %divide_convert_fusion.unit_ref.refs_1_.refs_12_), channel_id=1, source_target_pairs={{0,4},{1,5},{2,0},{3,1},{4,6},{5,7},{6,2},{7,3},{8,12},{9,13},{10,... | collective-permute-start | bytes 1376264 | tf_op jit(solution)/shard_map/ppermute | solution.py:318
  9.3 1.5 collective-permute-start.4
  14.1 4.9 %collective-permute-start.2 = (bf16[224,1024]{1,0:T(8,128)(2,1)S(1)}, bf16[224,1024]{1,0:T(8,128)(2,1)S(1)}, u32[]{:S(2)}, u32[]{:S(2)}) collective-permute-start(bf16[224,1024]{1,0:T(8,128)(2,1)S(1)} %divide_convert_fusion.unit_ref.refs_1_.refs_12_), channel_id=1, source_target_pairs={{2,6},{3,7},{4,0},{5,1},{0,2},{1,3},{6,4},{7,5},{10,14},{11,15},{1... | collective-permute-start | bytes 1376264 | tf_op jit(solution)/shard_map/ppermute | solution.py:318
  19.0 1.2 collective-permute-done.1.refs_5_.refs_13_
  20.2 1.3 collective-permute-start.3
  21.5 1.3 collective-permute-start.5
  22.8 1.4 collective-permute-start.7
  24.3 1.4 collective-permute-start.10
  25.7 15.9 %collective-permute-done.2.refs_5_.refs_14_ = bf16[224,1024]{1,0:T(8,128)(2,1)S(1)} collective-permute-done((bf16[224,1024]{1,0:T(8,128)(2,1)S(1)}, bf16[224,1024]{1,0:T(8,128)(2,1)S(1)}, u32[]{:S(2)}, u32[]{:S(2)}) %collective-permute-start.2) | collective-permute-done | bytes 458784 | tf_op jit(solution)/shard_map/ppermute | solution.py:318
  41.6 1.4 collective-permute-start.8
  46.7 1.4 collective-permute-start.13
  48.1 1.3 collective-permute-start.9
  49.4 1.5 collective-permute-start.11
  50.9 1.3 collective-permute-start.12
  52.2 1.5 collective-permute-start.14
  56.5 1.0 block_scores.6
  58.2 1.0 block_scores.7
  60.6 1.7 block_scores.8
  63.7 1.8 %block_scores.9 = (f32[224,224]{1,0:T(8,128)S(1)}, f32[224,224]{1,0:T(8,128)S(1)}, f32[224,128]{1,0:T(8,128)S(1)}, f32[224,128]{1,0:T(8,128)S(1)}, bf16[224,1024]{1,0:T(8,128)(2,1)S(1)}) custom-call(s32[2]{0:T(128)S(1)} %pad_add_fusion.5.refs_0_, bf16[224,1024]{1,0:T(8,128)(2,1)S(1)} %divide_convert_fusion.unit_ref.refs_1_.refs_12_, ...), custom_call_target="tpu_custom_call" | custom-call | flops 205520896 | bytes 2097152 | tf_op jit(solution)/shard_map/block_scores/pallas_call | solution.py:202
  66.9 2.0 %block_scores.10 = (f32[224,224]{1,0:T(8,128)S(1)}, f32[224,224]{1,0:T(8,128)S(1)}, f32[224,128]{1,0:T(8,128)S(1)}, f32[224,128]{1,0:T(8,128)S(1)}, bf16[224,1024]{1,0:T(8,128)(2,1)S(1)}) custom-call(s32[2]{0:T(128)S(1)} %pad_add_fusion.4.refs_0_, bf16[224,1024]{1,0:T(8,128)(2,1)S(1)} %divide_convert_fusion.unit_ref.refs_1_.refs_12_, ...), custom_call_target="tpu_custom_call" | custom-call | flops 205520896 | bytes 2097152 | tf_op jit(solution)/shard_map/block_scores/pallas_call | solution.py:202
  70.3 1.3 collective-permute-done.12.refs_5_
  71.6 1.9 %block_scores.11 = (f32[224,224]{1,0:T(8,128)S(1)}, f32[224,224]{1,0:T(8,128)S(1)}, f32[8,128]{1,0:T(8,128)S(1)}, bf16[224,1024]{1,0:T(8,128)(2,1)S(1)}) custom-call(s32[2]{0:T(128)S(1)} %pad_add_fusion.3.refs_0_, bf16[224,1024]{1,0:T(8,128)(2,1)S(1)} %divide_convert_fusion.unit_ref.refs_1_.refs_12_, ...), custom_call_target="tpu_custom_call" | custom-call | flops 205520896 | bytes 2097152 | tf_op jit(solution)/shard_map/block_scores/pallas_call | solution.py:202
  76.4 15.4 %all-to-all-start = ((f32[32,8,128]{2,1,0:T(8,128)}), f32[32,8,128]{2,1,0:T(8,128)S(1)}, u32[]{:S(2)}, u32[]{:S(2)}) async-start(f32[32,8,128]{2,1,0:T(8,128)} %broadcast_in_dim.18), calls=%async_computation | async-start | bytes 262144 | tf_op jit(solution)/shard_map/all_to_all | solution.py:388
  91.9 6.9 %all-to-all-done.pay_ref = f32[32,8,128]{2,1,0:T(8,128)S(1)} async-done(((f32[32,8,128]{2,1,0:T(8,128)}), f32[32,8,128]{2,1,0:T(8,128)S(1)}, u32[]{:S(2)}, u32[]{:S(2)}) %all-to-all-start) | async-done | bytes 131104 | tf_op jit(solution)/shard_map/all_to_all | solution.py:388
  99.4 8.3 %collective-permute-start.19 = (f32[4,2,128]{2,1,0:T(2,128)S(1)}, f32[4,2,128]{2,1,0:T(2,128)S(1)}, u32[]{:S(2)}, u32[]{:S(2)}) collective-permute-start(f32[4,2,128]{2,1,0:T(2,128)S(1)} %get-tuple-element.56), channel_id=1, source_target_pairs={{24,32},{0,504},{25,33},{1,505},{26,34},{2,506},{27,35},{3,507},{2... | collective-permute-start | bytes 12296 | tf_op jit(solution)/shard_map/ppermute | solution.py:391
  107.8 5.2 %collective-permute-done.19.refs_2_ = f32[4,2,128]{2,1,0:T(2,128)S(1)} collective-permute-done((f32[4,2,128]{2,1,0:T(2,128)S(1)}, f32[4,2,128]{2,1,0:T(2,128)S(1)}, u32[]{:S(2)}, u32[]{:S(2)}) %collective-permute-start.19) | collective-permute-done | bytes 4128 | tf_op jit(solution)/shard_map/ppermute | solution.py:391
  113.1 1.0 copy-done.4
  114.1 1.0 copy-done.7
  115.1 0.9 copy-done.14
  116.1 0.9 copy-done.28
  117.0 0.9 copy-done.30
  118.9 0.9 copy-done.34
  119.8 0.9 copy-done.36
  121.7 2.7 %unit_gradient.3 = f32[224,1024]{1,0:T(8,128)} custom-call(s32[7]{0:T(128)S(1)} %pad_add_fusion.7.refs_0_, f32[16,2,128]{2,1,0:T(2,128)S(1)} %get-tuple-element.55.refs_1_, f32[4,2,128]{2,1,0:T(2,128)S(1)} %collective-permute-done.19.refs_2_, f32[2,128]{1,0:T(2,128)S(1)} %get-tuple-element.68.refs_3_, s32[1,224]{1,0:T(1,128)S(1)} %bitcast.28, ...), custom_call_target="tpu_custom_call" | custom-call | flops 719323136 | bytes 6291456 | tf_op jit(solution)/shard_map/unit_gradient/pallas_call | solution.py:283
  124.4 1.9 %collective-permute-start.20 = (f32[224,1024]{1,0:T(8,128)}, f32[224,1024]{1,0:T(8,128)}, u32[]{:S(2)}, u32[]{:S(2)}) collective-permute-start(f32[224,1024]{1,0:T(8,128)} %unit_gradient.3), channel_id=1, source_target_pairs={{0,1},{1,0},{2,3},{3,2},{4,5},{5,4},{6,7},{7,6},{8,9},{9,8},{10,11... | collective-permute-start | bytes 2752520 | tf_op jit(solution)/shard_map/ppermute | solution.py:395
  126.3 1.9 %collective-permute-start.15 = (f32[8,128]{1,0:T(8,128)S(1)}, f32[8,128]{1,0:T(8,128)S(1)}, u32[]{:S(2)}, u32[]{:S(2)}) collective-permute-start(f32[8,128]{1,0:T(8,128)S(1)} %get-tuple-element.54), channel_id=1, source_target_pairs={{0,32},{32,0},{64,96},{96,64},{1,33},{33,1},{65,97},{97,65},{2,34}... | collective-permute-start | bytes 12296 | tf_op jit(solution)/shard_map/ppermute | solution.py:400
  128.2 3.6 %collective-permute-done.15 = f32[8,128]{1,0:T(8,128)S(1)} collective-permute-done((f32[8,128]{1,0:T(8,128)S(1)}, f32[8,128]{1,0:T(8,128)S(1)}, u32[]{:S(2)}, u32[]{:S(2)}) %collective-permute-start.15) | collective-permute-done | bytes 4128 | tf_op jit(solution)/shard_map/ppermute | solution.py:400
  131.8 1.9 %collective-permute-start.16 = (f32[8,128]{1,0:T(8,128)S(1)}, f32[8,128]{1,0:T(8,128)S(1)}, u32[]{:S(2)}, u32[]{:S(2)}) collective-permute-start(f32[8,128]{1,0:T(8,128)S(1)} %add.92), channel_id=1, source_target_pairs={{0,64},{32,96},{64,0},{96,32},{1,65},{33,97},{65,1},{97,33},{2,66}... | collective-permute-start | bytes 12296 | tf_op jit(solution)/shard_map/ppermute | solution.py:400
  133.7 5.1 %collective-permute-done.16 = f32[8,128]{1,0:T(8,128)S(1)} collective-permute-done((f32[8,128]{1,0:T(8,128)S(1)}, f32[8,128]{1,0:T(8,128)S(1)}, u32[]{:S(2)}, u32[]{:S(2)}) %collective-permute-start.16) | collective-permute-done | bytes 4128 | tf_op jit(solution)/shard_map/ppermute | solution.py:400
  138.8 9.1 %collective-permute-start.17 = (f32[8,128]{1,0:T(8,128)S(1)}, f32[8,128]{1,0:T(8,128)S(1)}, u32[]{:S(2)}, u32[]{:S(2)}) collective-permute-start(f32[8,128]{1,0:T(8,128)S(1)} %add.93), channel_id=1, source_target_pairs={{0,128},{128,0},{256,384},{384,256},{1,129},{129,1},{257,385},{385... | collective-permute-start | bytes 12296 | tf_op jit(solution)/shard_map/ppermute | solution.py:400
  147.9 1.6 collective-permute-done.17
  149.5 12.6 %collective-permute-start.18 = (f32[8,128]{1,0:T(8,128)S(1)}, f32[8,128]{1,0:T(8,128)S(1)}, u32[]{:S(2)}, u32[]{:S(2)}) collective-permute-start(f32[8,128]{1,0:T(8,128)S(1)} %add.94), channel_id=1, source_target_pairs={{0,256},{128,384},{256,0},{384,128},{1,257},{129,385},{257,1},{385... | collective-permute-start | bytes 12296 | tf_op jit(solution)/shard_map/ppermute | solution.py:400
  162.1 1.0 copy-done.5
  163.1 1.0 copy-done.8
  169.8 1.7 unit_gradient.2.mine_ref
  172.7 3.7 %final.1 = f32[224,1024]{1,0:T(8,128)} custom-call(f32[224,1024]{1,0:T(8,128)S(1)} %copy-done, f32[224,1024]{1,0:T(8,128)S(1)} %unit_gradient.2.mine_ref, f32[224,1024]{1,0:T(8,128)} %collective-permute-done.20.got_ref), custom_call_target="tpu_custom_call" | custom-call | flops 2293760 | bytes 3670016 | tf_op jit(solution)/shard_map/final/pallas_call | solution.py:305
  (111 shorter events, 27.8 us)
Async XLA Ops:
  0.6 1.5 copy-start
  2.2 10.0 %collective-permute-start = (bf16[224,1024]{1,0:T(8,128)(2,1)S(1)}, bf16[224,1024]{1,0:T(8,128)(2,1)S(1)}, u32[]{:S(2)}, u32[]{:S(2)}) collective-permute-start(bf16[224,1024]{1,0:T(8,128)(2,1)S(1)} %divide_convert_fusion.unit_ref.refs_1_.refs_12_), channel_id=1, source_target_pairs={{0,1},{1,0},{2,3},{3,2},{4,5},{5,4},{6,7},{7,6},{8,9},{9,8},{10,11... | collective-permute-start | bytes 1376264 | tf_op jit(solution)/shard_map/ppermute | solution.py:353
  4.2 16.0 %collective-permute-start.1 = (bf16[224,1024]{1,0:T(8,128)(2,1)S(1)}, bf16[224,1024]{1,0:T(8,128)(2,1)S(1)}, u32[]{:S(2)}, u32[]{:S(2)}) collective-permute-start(bf16[224,1024]{1,0:T(8,128)(2,1)S(1)} %divide_convert_fusion.unit_ref.refs_1_.refs_12_), channel_id=1, source_target_pairs={{0,4},{1,5},{2,0},{3,1},{4,6},{5,7},{6,2},{7,3},{8,12},{9,13},{10,... | collective-permute-start | bytes 1376264 | tf_op jit(solution)/shard_map/ppermute | solution.py:318
  9.3 14.9 %collective-permute-start.4 = (bf16[224,1024]{1,0:T(8,128)(2,1)S(1)}, bf16[224,1024]{1,0:T(8,128)(2,1)}, u32[]{:S(2)}, u32[]{:S(2)}) collective-permute-start(bf16[224,1024]{1,0:T(8,128)(2,1)S(1)} %divide_convert_fusion.unit_ref.refs_1_.refs_12_), channel_id=1, source_target_pairs={{2,4},{3,5},{4,2},{5,3},{10,12},{11,13},{12,10},{13,11},{18,20},{1... | collective-permute-start | bytes 1376264 | tf_op jit(solution)/shard_map/ppermute | solution.py:318
  10.8 12.0 %collective-permute-start.6 = (bf16[224,1024]{1,0:T(8,128)(2,1)S(1)}, bf16[224,1024]{1,0:T(8,128)(2,1)S(1)}, u32[]{:S(2)}, u32[]{:S(2)}) collective-permute-start(bf16[224,1024]{1,0:T(8,128)(2,1)S(1)} %divide_convert_fusion.unit_ref.refs_1_.refs_12_), channel_id=1, source_target_pairs={{126,128},{127,129},{128,126},{129,127},{254,256},{255,257},{256,2... | collective-permute-start | bytes 1376264 | tf_op jit(solution)/shard_map/ppermute | solution.py:318
  14.1 27.5 %collective-permute-start.2 = (bf16[224,1024]{1,0:T(8,128)(2,1)S(1)}, bf16[224,1024]{1,0:T(8,128)(2,1)S(1)}, u32[]{:S(2)}, u32[]{:S(2)}) collective-permute-start(bf16[224,1024]{1,0:T(8,128)(2,1)S(1)} %divide_convert_fusion.unit_ref.refs_1_.refs_12_), channel_id=1, source_target_pairs={{2,6},{3,7},{4,0},{5,1},{0,2},{1,3},{6,4},{7,5},{10,14},{11,15},{1... | collective-permute-start | bytes 1376264 | tf_op jit(solution)/shard_map/ppermute | solution.py:318
  20.2 26.5 %collective-permute-start.3 = (bf16[224,1024]{1,0:T(8,128)(2,1)S(1)}, bf16[224,1024]{1,0:T(8,128)(2,1)}, u32[]{:S(2)}, u32[]{:S(2)}) collective-permute-start(bf16[224,1024]{1,0:T(8,128)(2,1)S(1)} %collective-permute-done.1.refs_5_.refs_13_), channel_id=1, source_target_pairs={{4,6},{5,7},{2,0},{3,1},{12,14},{13,15},{10,8},{11,9},{20,22},{21,... | collective-permute-start | bytes 1376264 | tf_op jit(solution)/shard_map/ppermute | solution.py:318
  21.5 26.6 %collective-permute-start.5 = (bf16[224,1024]{1,0:T(8,128)(2,1)S(1)}, bf16[224,1024]{1,0:T(8,128)(2,1)}, u32[]{:S(2)}, u32[]{:S(2)}) collective-permute-start(bf16[224,1024]{1,0:T(8,128)(2,1)S(1)} %collective-permute-done.1.refs_5_.refs_13_), channel_id=1, source_target_pairs={{0,8},{1,9},{2,10},{3,11},{8,16},{9,17},{10,18},{11,19},{12,4},{13... | collective-permute-start | bytes 1376264 | tf_op jit(solution)/shard_map/ppermute | solution.py:318
  22.8 34.7 %copy-start.9 = (bf16[224,1024]{1,0:T(8,128)(2,1)}, bf16[224,1024]{1,0:T(8,128)(2,1)S(1)}, u32[]{:S(2)}) copy-start(bf16[224,1024]{1,0:T(8,128)(2,1)S(1)} %collective-permute-done.6.refs_7_) | copy-start | bytes 1376260
  22.8 26.6 %collective-permute-start.7 = (bf16[224,1024]{1,0:T(8,128)(2,1)S(1)}, bf16[224,1024]{1,0:T(8,128)(2,1)}, u32[]{:S(2)}, u32[]{:S(2)}) collective-permute-start(bf16[224,1024]{1,0:T(8,128)(2,1)S(1)} %collective-permute-done.6.refs_7_), channel_id=1, source_target_pairs={{128,130},{129,131},{126,124},{127,125},{256,258},{257,259},{254,2... | collective-permute-start | bytes 1376264 | tf_op jit(solution)/shard_map/ppermute | solution.py:318
  24.3 26.6 %collective-permute-start.10 = (bf16[224,1024]{1,0:T(8,128)(2,1)S(1)}, bf16[224,1024]{1,0:T(8,128)(2,1)}, u32[]{:S(2)}, u32[]{:S(2)}) collective-permute-start(bf16[224,1024]{1,0:T(8,128)(2,1)S(1)} %collective-permute-done.1.refs_5_.refs_13_), channel_id=1, source_target_pairs={{126,128},{127,129},{128,126},{129,127},{254,256},{255,257},{256,2... | collective-permute-start | bytes 1376264 | tf_op jit(solution)/shard_map/ppermute | solution.py:318
  41.6 10.5 %collective-permute-start.8 = (bf16[224,1024]{1,0:T(8,128)(2,1)S(1)}, bf16[224,1024]{1,0:T(8,128)(2,1)}, u32[]{:S(2)}, u32[]{:S(2)}) collective-permute-start(bf16[224,1024]{1,0:T(8,128)(2,1)S(1)} %collective-permute-done.2.refs_5_.refs_14_), channel_id=1, source_target_pairs={{126,128},{127,129},{128,126},{129,127},{254,256},{255,257},{256,2... | collective-permute-start | bytes 1376264 | tf_op jit(solution)/shard_map/ppermute | solution.py:318
  46.7 23.6 %collective-permute-start.13 = (bf16[224,1024]{1,0:T(8,128)(2,1)}, bf16[224,1024]{1,0:T(8,128)(2,1)}, u32[]{:S(2)}, u32[]{:S(2)}) collective-permute-start(bf16[224,1024]{1,0:T(8,128)(2,1)} %collective-permute-done.4.refs_6_), channel_id=1, source_target_pairs={{2,10},{3,11},{10,18},{11,19},{12,4},{13,5},{18,26},{19,27},{20,12... | collective-permute-start | bytes 1376264 | tf_op jit(solution)/shard_map/ppermute | solution.py:318
  48.1 18.8 %collective-permute-start.9 = (bf16[224,1024]{1,0:T(8,128)(2,1)S(1)}, bf16[224,1024]{1,0:T(8,128)(2,1)}, u32[]{:S(2)}, u32[]{:S(2)}) collective-permute-start(bf16[224,1024]{1,0:T(8,128)(2,1)S(1)} %collective-permute-done.2.refs_5_.refs_14_), channel_id=1, source_target_pairs={{0,8},{1,9},{4,12},{5,13},{8,16},{9,17},{12,20},{13,21},{10,2},{11... | collective-permute-start | bytes 1376264 | tf_op jit(solution)/shard_map/ppermute | solution.py:318
  49.4 17.5 %collective-permute-start.11 = (bf16[224,1024]{1,0:T(8,128)(2,1)}, bf16[224,1024]{1,0:T(8,128)(2,1)}, u32[]{:S(2)}, u32[]{:S(2)}) collective-permute-start(bf16[224,1024]{1,0:T(8,128)(2,1)} %collective-permute-done.7.refs_6_), channel_id=1, source_target_pairs={{130,132},{131,133},{124,122},{125,123},{258,260},{259,261},{252,2... | collective-permute-start | bytes 1376264 | tf_op jit(solution)/shard_map/ppermute | solution.py:318
  50.9 20.7 %collective-permute-start.12 = (bf16[224,1024]{1,0:T(8,128)(2,1)}, bf16[224,1024]{1,0:T(8,128)(2,1)}, u32[]{:S(2)}, u32[]{:S(2)}) collective-permute-start(bf16[224,1024]{1,0:T(8,128)(2,1)} %collective-permute-done.3.refs_5_), channel_id=1, source_target_pairs={{0,8},{1,9},{8,16},{9,17},{14,6},{15,7},{16,24},{17,25},{22,14},{2... | collective-permute-start | bytes 1376264 | tf_op jit(solution)/shard_map/ppermute | solution.py:318
  52.2 19.4 %collective-permute-start.14 = (bf16[224,1024]{1,0:T(8,128)(2,1)}, bf16[224,1024]{1,0:T(8,128)(2,1)}, u32[]{:S(2)}, u32[]{:S(2)}) collective-permute-start(bf16[224,1024]{1,0:T(8,128)(2,1)} %collective-permute-done.10.refs_6_), channel_id=1, source_target_pairs={{128,130},{129,131},{126,124},{127,125},{256,258},{257,259},{254,2... | collective-permute-start | bytes 1376264 | tf_op jit(solution)/shard_map/ppermute | solution.py:318
  58.2 1.0 copy-start.15
  66.9 2.0 %copy-start.1 = (bf16[224,1024]{1,0:T(8,128)(2,1)}, bf16[224,1024]{1,0:T(8,128)(2,1)S(1)}, u32[]{:S(2)}) copy-start(bf16[224,1024]{1,0:T(8,128)(2,1)S(1)} %get-tuple-element.65.refs_16_) | copy-start | bytes 1376260
  66.9 4.7 %copy-start.10 = (bf16[224,1024]{1,0:T(8,128)(2,1)S(1)}, bf16[224,1024]{1,0:T(8,128)(2,1)}, u32[]{:S(2)}) copy-start(bf16[224,1024]{1,0:T(8,128)(2,1)} %copy-done.9) | copy-start | bytes 1376260
  70.3 3.2 %copy-start.3 = (bf16[224,1024]{1,0:T(8,128)(2,1)}, bf16[224,1024]{1,0:T(8,128)(2,1)S(1)}, u32[]{:S(2)}) copy-start(bf16[224,1024]{1,0:T(8,128)(2,1)S(1)} %get-tuple-element.66.refs_17_) | copy-start | bytes 1376260
  73.5 0.8 copy-start.6
  75.7 37.4 %copy-start.2 = (bf16[224,1024]{1,0:T(8,128)(2,1)S(1)}, bf16[224,1024]{1,0:T(8,128)(2,1)}, u32[]{:S(2)}) copy-start(bf16[224,1024]{1,0:T(8,128)(2,1)} %copy-done.1) | copy-start | bytes 1376260
  76.4 22.4 %all-to-all-start = ((f32[32,8,128]{2,1,0:T(8,128)}), f32[32,8,128]{2,1,0:T(8,128)S(1)}, u32[]{:S(2)}, u32[]{:S(2)}) async-start(f32[32,8,128]{2,1,0:T(8,128)} %broadcast_in_dim.18), calls=%async_computation | async-start | bytes 262144 | tf_op jit(solution)/shard_map/all_to_all | solution.py:388
  99.4 13.6 %collective-permute-start.19 = (f32[4,2,128]{2,1,0:T(2,128)S(1)}, f32[4,2,128]{2,1,0:T(2,128)S(1)}, u32[]{:S(2)}, u32[]{:S(2)}) collective-permute-start(f32[4,2,128]{2,1,0:T(2,128)S(1)} %get-tuple-element.56), channel_id=1, source_target_pairs={{24,32},{0,504},{25,33},{1,505},{26,34},{2,506},{27,35},{3,507},{2... | collective-permute-start | bytes 12296 | tf_op jit(solution)/shard_map/ppermute | solution.py:391
  113.1 1.0 copy-start.4
  114.1 1.0 copy-start.7
  115.1 0.9 copy-start.14
  116.1 0.9 copy-start.28
  117.0 0.9 copy-start.30
  117.9 0.9 copy-start.32
  118.9 0.9 copy-start.34
  119.8 0.9 copy-start.36
  120.8 0.9 copy-start.38
  121.7 40.4 %copy-start.12 = (f32[224,224]{1,0:T(8,128)S(1)}, f32[224,224]{1,0:T(8,128)}, u32[]{:S(2)}) copy-start(f32[224,224]{1,0:T(8,128)} %copy-done.11) | copy-start | bytes 602116
  124.4 48.3 %collective-permute-start.20 = (f32[224,1024]{1,0:T(8,128)}, f32[224,1024]{1,0:T(8,128)}, u32[]{:S(2)}, u32[]{:S(2)}) collective-permute-start(f32[224,1024]{1,0:T(8,128)} %unit_gradient.3), channel_id=1, source_target_pairs={{0,1},{1,0},{2,3},{3,2},{4,5},{5,4},{6,7},{7,6},{8,9},{9,8},{10,11... | collective-permute-start | bytes 2752520 | tf_op jit(solution)/shard_map/ppermute | solution.py:395
  126.3 5.5 %collective-permute-start.15 = (f32[8,128]{1,0:T(8,128)S(1)}, f32[8,128]{1,0:T(8,128)S(1)}, u32[]{:S(2)}, u32[]{:S(2)}) collective-permute-start(f32[8,128]{1,0:T(8,128)S(1)} %get-tuple-element.54), channel_id=1, source_target_pairs={{0,32},{32,0},{64,96},{96,64},{1,33},{33,1},{65,97},{97,65},{2,34}... | collective-permute-start | bytes 12296 | tf_op jit(solution)/shard_map/ppermute | solution.py:400
  131.8 7.0 %collective-permute-start.16 = (f32[8,128]{1,0:T(8,128)S(1)}, f32[8,128]{1,0:T(8,128)S(1)}, u32[]{:S(2)}, u32[]{:S(2)}) collective-permute-start(f32[8,128]{1,0:T(8,128)S(1)} %add.92), channel_id=1, source_target_pairs={{0,64},{32,96},{64,0},{96,32},{1,65},{33,97},{65,1},{97,33},{2,66}... | collective-permute-start | bytes 12296 | tf_op jit(solution)/shard_map/ppermute | solution.py:400
  138.8 10.7 %collective-permute-start.17 = (f32[8,128]{1,0:T(8,128)S(1)}, f32[8,128]{1,0:T(8,128)S(1)}, u32[]{:S(2)}, u32[]{:S(2)}) collective-permute-start(f32[8,128]{1,0:T(8,128)S(1)} %add.93), channel_id=1, source_target_pairs={{0,128},{128,0},{256,384},{384,256},{1,129},{129,1},{257,385},{385... | collective-permute-start | bytes 12296 | tf_op jit(solution)/shard_map/ppermute | solution.py:400
  149.5 22.1 %collective-permute-start.18 = (f32[8,128]{1,0:T(8,128)S(1)}, f32[8,128]{1,0:T(8,128)S(1)}, u32[]{:S(2)}, u32[]{:S(2)}) collective-permute-start(f32[8,128]{1,0:T(8,128)S(1)} %add.94), channel_id=1, source_target_pairs={{0,256},{128,384},{256,0},{384,128},{1,257},{129,385},{257,1},{385... | collective-permute-start | bytes 12296 | tf_op jit(solution)/shard_map/ppermute | solution.py:400
  162.1 1.0 copy-start.5
  163.1 1.0 copy-start.8
  164.1 0.9 copy-start.16
  165.1 0.9 copy-start.18
  166.0 0.9 copy-start.20
  166.9 0.9 copy-start.22
  167.9 0.9 copy-start.24
  168.8 0.9 copy-start.26
  (15 other events, 10.4 us)

commit v2 on v1

--- a/solution.py
+++ b/solution.py
@@ -1,6 +1,5 @@
 import jax
 import jax.numpy as jnp
-import numpy as np
 from jax import lax
 from jax.experimental import pallas as pl
 from jax.experimental.pallas import tpu as pltpu
@@ -15,9 +14,6 @@
 DEV_AXES = ("y", "zl", "core")
 ROWS = 224
 WIDTH = 1024
-
-RECEIVED = np.array([[1, 2, 3], [3, 0, 2], [0, 3, 1], [2, 1, 0]], np.int32)
-
 
 def crosses(run):
     return run % 16 == 15
@@ -91,7 +87,7 @@
     return [pl.BlockSpec(memory_space=pltpu.SMEM)] * count
 
 
-PARAMS = pltpu.CompilerParams(vmem_limit_bytes=48 * 1024 * 1024)
+PARAMS = pltpu.CompilerParams(vmem_limit_bytes=12 * 1024 * 1024)
 
 
 def scores(rows, columns):
@@ -103,11 +99,14 @@
     return values[:, :128] + tail
 
 
-def own_kernel(unit_ref, other_ref, partner_ref, e_own_ref, e_other_ref, sum_own_ref, sum_other_ref, pos_ref):
+def own_kernel(ids_ref, unit_ref, other_ref, partner_ref, local_ref, e_own_ref, e_other_ref, sum_own_ref, sum_other_ref, pos_ref):
     unit = unit_ref[...]
     row = lax.broadcasted_iota(jnp.int32, (ROWS, ROWS), 0)
     column = lax.broadcasted_iota(jnp.int32, (ROWS, ROWS), 1)
-    partner = partner_ref[...]
+    shift = ids_ref[2] * ROWS
+    partner = partner_ref[...] - (ids_ref[3] * (8 * ROWS) + ids_ref[1] * (2 * ROWS) + shift)
+    partner = jnp.where(partner < 0, partner + 2 * ROWS, partner)
+    local_ref[...] = partner
     logits = scores(unit, unit) / SOFTMAX_TEMPER
     expo = jnp.where(row == column, 0.0, jnp.exp(logits - 1.0 / SOFTMAX_TEMPER))
     e_own_ref[...] = expo
@@ -121,27 +120,49 @@
     pos_ref[...] = jnp.sum(fold(picked), axis=0, keepdims=True)
 
 
-def own_call(unit, other, partner):
+def own_call(ids, unit, other, partner):
     f32 = jnp.float32
     return pl.pallas_call(
         own_kernel,
         out_shape=(
+            jax.ShapeDtypeStruct((1, ROWS), jnp.int32),
             jax.ShapeDtypeStruct((ROWS, ROWS), f32),
             jax.ShapeDtypeStruct((ROWS, ROWS), f32),
             jax.ShapeDtypeStruct((ROWS, 128), f32),
             jax.ShapeDtypeStruct((ROWS, 128), f32),
             jax.ShapeDtypeStruct((1, 128), f32),
         ),
-        in_specs=vmem(3),
-        out_specs=tuple(vmem(5)),
+        in_specs=smem(1) + vmem(3),
+        out_specs=tuple(vmem(6)),
         compiler_params=PARAMS,
         cost_estimate=pl.CostEstimate(flops=2 * 448 * ROWS * WIDTH, bytes_accessed=2 << 20, transcendentals=448 * ROWS),
         name="own_scores",
-    )(unit, other, partner)
-
-
-def block_kernel(n_cand, last, *refs):
-    flags_ref, unit_ref, other_ref, sum_own_ref, sum_other_ref = refs[:5]
+    )(ids, unit, other, partner)
+
+
+def received(number, k):
+    first = jnp.where(k == 0, 1, jnp.where(k == 1, 3, jnp.where(k == 2, 0, 2)))
+    return (first, 3 - first, 3 - k)[number]
+
+
+def pick(number, ids_ref):
+    k, run = ids_ref[1], ids_ref[3]
+    below, above = run % 16 == 15, run % 16 == 0
+    end = (below & (k == 3)) | (above & (k == 0))
+    mid = (below & (k == 2)) | (above & (k == 1))
+    far = (below & (k == 1)) | (above & (k == 2))
+    inner = jnp.where((k == 1) | (k == 2), 1, 0)
+    if number == 2:
+        return inner
+    if number == 3:
+        return jnp.where(end, 2, jnp.where(mid, 1, 0))
+    if number == 4:
+        return jnp.where(end, 1, jnp.where(far, 2, 0))
+    return jnp.where(end, 2, jnp.where(mid, 3, inner))
+
+
+def block_kernel(number_in, n_cand, last, *refs):
+    ids_ref, unit_ref, other_ref, sum_own_ref, sum_other_ref = refs[:5]
     cands = refs[5 : 5 + n_cand]
     rest = refs[5 + n_cand :]
     if last:
@@ -153,12 +174,18 @@
     else:
         sum_own_out, sum_other_out = rest[:2]
         rest = rest[2:]
+    k, core = ids_ref[1], ids_ref[2]
+    steps = received(number_in % 3, k) - k
+    if number_in > 2:
+        steps = jnp.where(steps < 0, steps + 4, steps - 4)
+    outside = steps == jnp.where(core == 0, -3, 3)
     if n_cand > 1:
+        choice = pick(number_in, ids_ref)
         block_ref, rest = rest[0], rest[1:]
         block_ref[...] = cands[0][...]
         for number in range(1, n_cand):
 
-            @pl.when(flags_ref[0] == number)
+            @pl.when(choice == number)
             def _(number=number):
                 block_ref[...] = cands[number][...]
     else:
@@ -168,7 +195,7 @@
     e_own_ref[...] = expo
     sum_own = sum_own_ref[...] + fold(expo)
     expo = jnp.exp(scores(other_ref[...], block) / SOFTMAX_TEMPER - 1.0 / SOFTMAX_TEMPER)
-    expo = jnp.where(flags_ref[1] == 1, 0.0, expo)
+    expo = jnp.where(outside, 0.0, expo)
     e_other_ref[...] = expo
     sum_other = sum_other_ref[...] + fold(expo)
     if last:
@@ -183,7 +210,7 @@
         sum_other_out[...] = sum_other
 
 
-def block_call(flags, unit, other, sums, cands, pos=None):
+def block_call(number_in, ids, unit, other, sums, cands, pos=None):
     f32 = jnp.float32
     last = pos is not None
     n = len(cands)
@@ -197,7 +224,7 @@
     operands = [unit, other, *sums, *cands] + ([pos] if last else [])
 
     def kernel(*refs):
-        block_kernel(n, last, *refs)
+        block_kernel(number_in, n, last, *refs)
 
     out = pl.pallas_call(
         kernel,
@@ -207,15 +234,15 @@
         compiler_params=PARAMS,
         cost_estimate=pl.CostEstimate(flops=2 * 448 * ROWS * WIDTH, bytes_accessed=2 << 20, transcendentals=448 * ROWS),
         name="block_scores",
-    )(flags, *operands)
+    )(ids, *operands)
     block = out[-1] if n > 1 else cands[0]
     if last:
         return out[:2], out[2], block
     return out[:2], out[2:4], block
 
 
-def denom_kernel(place_ref, pay_ref, inv_ref, other_ref, edge_ref, loss_ref):
-    y, k, core = place_ref[0], place_ref[1], place_ref[2]
+def denom_kernel(ids_ref, pay_ref, inv_ref, mine_ref, other_ref, edge_ref, loss_ref):
+    y, k, core = ids_ref[0], ids_ref[1], ids_ref[2]
     pay = pay_ref[...].reshape(16, 2, 8, 128)
     lane = lax.broadcasted_iota(jnp.int32, (16, 2, 128), 2)
     part = lax.broadcasted_iota(jnp.int32, (16, 2, 128), 1)
@@ -230,25 +257,28 @@
     inv_ref[...] = jnp.where(core == 0, first, second)
     other_all = jnp.where(core == 0, second, first)
     chip = lax.broadcasted_iota(jnp.int32, (16, 2, 128), 0)
-    other_ref[...] = jnp.sum(jnp.where(chip == y * 4 + k, other_all, 0.0), axis=0)
+    here = chip == y * 4 + k
+    mine_ref[...] = jnp.sum(jnp.where(here, inv_ref[...], 0.0), axis=0)
+    other_ref[...] = jnp.sum(jnp.where(here, other_all, 0.0), axis=0)
     edge_ref[...] = inv_ref[pl.ds(jnp.where(y == 3, 12, 0), 4)]
 
 
-def denom_call(place, pay):
+def denom_call(ids, pay):
     f32 = jnp.float32
     return pl.pallas_call(
         denom_kernel,
         out_shape=(
             jax.ShapeDtypeStruct((16, 2, 128), f32),
             jax.ShapeDtypeStruct((2, 128), f32),
+            jax.ShapeDtypeStruct((2, 128), f32),
             jax.ShapeDtypeStruct((4, 2, 128), f32),
             jax.ShapeDtypeStruct((8, 128), f32),
         ),
         in_specs=smem(1) + vmem(1),
-        out_specs=tuple(vmem(4)),
+        out_specs=tuple(vmem(5)),
         compiler_params=PARAMS,
         name="denoms",
-    )(place, pay)
+    )(ids, pay)
 
 
 def lanes(pair):
@@ -256,17 +286,23 @@
 
 
 def grad_kernel(shift, *refs):
-    where_ref, inv_ref, edge_ref, row_ref, partner_ref = refs[:5]
+    ids_ref, inv_ref, edge_ref, row_ref, partner_ref = refs[:5]
     expos, blocks = refs[5:12], refs[12:19]
     out_ref = refs[19]
     mine = lanes(row_ref[...])
     mine = jnp.transpose(jnp.broadcast_to(mine, (128, ROWS)))[:, 0:1]
     total = None
+    y, k = ids_ref[0], ids_ref[1]
     for number in range(7):
-        place = where_ref[number]
-        inside = inv_ref[pl.ds(jnp.minimum(place, 15), 1)]
-        outside = edge_ref[pl.ds(jnp.maximum(place - 16, 0), 1)]
-        column = lanes(jnp.where(place < 16, inside, outside)[0])
+        chip, line = k, y
+        if number:
+            chip = received((number - 1) % 3, k)
+        if number > 3:
+            line = y + jnp.where(chip < k, 1, -1)
+        inside = inv_ref[pl.ds(jnp.clip(line, 0, 3) * 4 + chip, 1)]
+        if number > 3:
+            inside = jnp.where((line < 0) | (line > 3), edge_ref[pl.ds(chip, 1)], inside)
+        column = lanes(inside[0])
         weight = expos[number][...] * (mine + column)
         if number == 0:
             row = lax.broadcasted_iota(jnp.int32, (ROWS, ROWS), 0) + shift
@@ -276,7 +312,7 @@
     out_ref[...] = total
 
 
-def grad_call(shift, where, inv, edge, row, partner, expos, blocks):
+def grad_call(shift, ids, inv, edge, row, partner, expos, blocks):
     def kernel(*refs):
         grad_kernel(shift, *refs)
 
@@ -288,7 +324,7 @@
         compiler_params=PARAMS,
         cost_estimate=pl.CostEstimate(flops=2 * 7 * ROWS * ROWS * WIDTH, bytes_accessed=6 << 20, transcendentals=0),
         name="unit_gradient",
-    )(where, inv, edge, row, partner, *expos, *blocks)
+    )(ids, inv, edge, row, partner, *expos, *blocks)
 
 
 def final_kernel(emb_ref, mine_ref, got_ref, out_ref):
@@ -322,89 +358,67 @@
     norm = jnp.sqrt(jnp.sum(embeddings * embeddings, axis=1, keepdims=True) + 1e-06)
     unit = (embeddings / norm).astype(jnp.bfloat16)
 
-    core = lax.axis_index("core")
-    k = lax.axis_index("zl")
-    y = lax.axis_index("y")
     run = lax.axis_index(("zh", "x", "y"))
-    below, above = run % 16 == 15, run % 16 == 0
-    end = (below & (k == 3)) | (above & (k == 0))
-    mid = (below & (k == 2)) | (above & (k == 1))
-    inner = (k == 1) | (k == 2)
-
-    local = (partner % (2 * ROWS) - core * ROWS) % (2 * ROWS)
-    local = local.reshape(1, ROWS).astype(jnp.int32)
-
-    sources = jnp.asarray(RECEIVED)[k]
-    steps_in = sources - k
-    steps_out = jnp.where(steps_in < 0, steps_in + 4, steps_in - 4)
-    excluded = jnp.where(core == 0, -3, 3)
-    out_in = (steps_in == excluded).astype(jnp.int32)
-    out_out = (steps_out == excluded).astype(jnp.int32)
-    line = y + jnp.where(steps_in < 0, 1, -1)
-    place_in = y * 4 + sources
-    place_out = jnp.where((line < 0) | (line > 3), 16 + sources, line * 4 + sources)
-    where = jnp.concatenate([(y * 4 + k)[None], place_in, place_out]).astype(jnp.int32)
-    pick3 = inner.astype(jnp.int32)
-    pick_y1 = jnp.where(end, 2, jnp.where(mid, 1, 0)).astype(jnp.int32)
-    pick_y2 = jnp.where(end, 1, jnp.where(mid_receiver(below, above, k), 2, 0)).astype(jnp.int32)
-    pick_y3 = jnp.where(end, 2, jnp.where(mid, 3, inner.astype(jnp.int32))).astype(jnp.int32)
-    zero = jnp.int32(0)
+    ids = jnp.stack([lax.axis_index(name) for name in DEV_AXES] + [run]).astype(jnp.int32)
+    partner = partner.reshape(1, ROWS)
 
     other = lax.ppermute(unit, ("core",), [(0, 1), (1, 0)])
     r1 = send(unit, "P1")
-    x1 = send(unit, "X1")
-    expo0, pos = None, None
-    e_own, e_other, sum_own, sum_other, pos = own_call(unit, other, local)
-    expos, blocks, sums = [(e_own, e_other)], [unit], (sum_own, sum_other)
-
-    def add(flags, cands, last=False):
+    local, e_own, e_other, sum_own, sum_other, pos = own_call(ids, unit, other, partner)
+    expos, blocks, sums = [(e_own, e_other)] + [None] * 6, [unit] + [None] * 6, (sum_own, sum_other)
+
+    def add(number, cands):
         nonlocal sums
-        pair, rest, block = block_call(jnp.stack(flags), unit, other, sums, cands, pos if last else None)
-        expos.append(pair)
-        blocks.append(block)
+        last = number == 5
+        pair, rest, block = block_call(number, ids, unit, other, sums, cands, pos if last else None)
+        expos[number + 1] = pair
+        blocks[number + 1] = block
         if last:
             return rest
         sums = rest
 
-    r2 = send(after(unit, sum_own), "P2")
+    x1 = send(after(unit, sums[0]), "X1")
+    r1 = after(r1, sums[0])
+    r2 = send(after(unit, r1), "P2")
     y1 = send(r1, "Y1")
-    x2 = send(x1, "X2")
+    x2 = send(after(x1, r1), "X2")
     x3 = send(r1, "X3")
-    add([zero, out_in[0]], [r1])
-    p3b = send(unit, "P3b")
-    p3a = send(r1, "P3a")
-    x5 = send(x3, "X5")
-    y2 = send(r2, "Y2")
-    x4 = send(r2, "X4")
-    x6 = send(x2, "X6")
-    add([zero, out_in[1]], [r2])
-    y3a = send(p3a, "Y3a")
-    y3b = send(p3b, "Y3b")
-    add([pick3, out_in[2]], [p3a, p3b])
-    add([pick_y1, out_out[0]], [y1, x2, x4])
-    add([pick_y2, out_out[1]], [y2, x3, x6])
-    pay = add([pick_y3, out_out[2]], [y3a, y3b, x1, x5], last=True)
+    add(0, [r1])
+    r2 = after(r2, sums[0])
+    p3b = send(after(unit, r2), "P3b")
+    p3a = send(after(r1, r2), "P3a")
+    y2 = send(after(r2, y1), "Y2")
+    x4 = send(after(r2, x3), "X4")
+    x6 = send(after(x2, r2), "X6")
+    add(1, [r2])
+    p3a = after(p3a, sums[0])
+    p3b = after(p3b, sums[0])
+    y3a = send(after(p3a, y2), "Y3a")
+    y3b = send(after(p3b, y2), "Y3b")
+    x5 = send(after(x3, p3a, p3b), "X5")
+    add(2, [p3a, p3b])
+    add(3, [y1, x2, x4])
+    add(4, [y2, x3, x6])
+    pay = add(5, [y3a, y3b, x1, x5])
 
     pays = lax.all_to_all(jnp.broadcast_to(pay[None], (32, 8, 128)), DEV_AXES, 0, 0)
-    place = jnp.stack([y, k, core]).astype(jnp.int32)
-    inv, other_inv, edge, loss = denom_call(place, pays)
+    inv, mine_inv, other_inv, edge, loss = denom_call(ids, pays)
+    def exchange(value, axis, bit, *meanwhile):
+        got = lax.ppermute(value, (axis,), [(i, i ^ bit) for i in range(4)])
+        return value + after(got, *meanwhile)
+
     edge = lax.ppermute(edge, AXES, EDGE)
-    mine_inv = lax.dynamic_index_in_dim(inv, y * 4 + k, 0, keepdims=False)
-
-    for_other = grad_call(ROWS, where, inv, edge, other_inv, local, [e[1] for e in expos], blocks)
-    got = lax.ppermute(for_other, ("core",), [(0, 1), (1, 0)])
-    mine = grad_call(0, where, inv, edge, mine_inv, local, [e[0] for e in expos], blocks)
-    grad = final_call(embeddings, mine, got)
-
-    for axis, bit in (("x", 1), ("x", 2), ("zh", 1), ("zh", 2)):
-        loss = loss + lax.ppermute(loss, (axis,), [(i, i ^ bit) for i in range(4)])
+    loss = exchange(loss, "x", 1)
+    for_other = grad_call(ROWS, ids, after(inv, loss), edge, other_inv, local, [e[1] for e in expos], blocks)
+    loss = exchange(loss, "x", 2, for_other)
+    got = lax.ppermute(after(for_other, loss), ("core",), [(0, 1), (1, 0)])
+    mine = grad_call(0, ids, after(inv, loss), edge, mine_inv, local, [e[0] for e in expos], blocks)
+    loss = exchange(loss, "zh", 1, mine)
+    grad = final_call(embeddings, mine, after(got, loss))
+    loss = exchange(loss, "zh", 2, grad)
     total_rows = ROWS * 512
     loss = loss[0, 0] / total_rows + 1.0 / SOFTMAX_TEMPER
     return (loss, grad)
-
-
-def mid_receiver(below, above, k):
-    return (below & (k == 1)) | (above & (k == 2))
 
 
 def solution(mesh):

time: 179 us -> 137 us (0.77)
  the two profiles are of different devices: /device:TPU:30 before, /device:TPU:1 now
where the time goes in v2:
time: 137 us; the launch traced here: 136 us
  starting transfers between devices  86.9 us (63%)
  blocking collectives  16.3 us (12%)
  waiting for transfers between devices  13.8 us (10%)
  Pallas kernels  13.7 us (10%)
  between operations  2.79 us (2%)
  other arithmetic  1.63 us (1%)
    ppermute x14, starting transfers between devices, send(): return lax.ppermute(value, AXES, ROUTES[name])  46.2 us
    ppermute x4, starting transfers between devices, exchange(): got = lax.ppermute(value, (axis,), [(i, i ^ bit) for i in range(4)])  16.9 us
    all_to_all x1, blocking collectives, per_device(): lax.all_to_all(jnp.broadcast_to(pay[None], (32, 8, 128)), DEV_AXES, 0, 0)  16.3 us
    ppermute x1, starting transfers between devices, per_device(): edge = lax.ppermute(edge, AXES, EDGE)  10.8 us
    ppermute x1, starting transfers between devices, per_device(): other = lax.ppermute(unit, ('core',), [(0, 1), (1, 0)])  8.79 us
    ppermute x14, waiting for transfers between devices, send(): return lax.ppermute(value, AXES, ROUTES[name])  7.27 us
    ppermute x4, waiting for transfers between devices, exchange(): got = lax.ppermute(value, (axis,), [(i, i ^ bit) for i in range(4)])  6.56 us
    pallas_call x6, Pallas kernels, block_call(): pl.pallas_call(kernel, out_shape=tuple(shapes), in_specs=smem(1) + vmem(l...  6.45 us
  transfers between devices with their start and end apart: 21, of which 6 were waited for; matrix products, arithmetic and copies ran while one was open for 0% of the time, Pallas kernels for 9%

profile of v2, /device:TPU:1, one launch (start us, length us, event | category | flops | bytes accessed | tf_op | source)
XLA Modules:
  0.0 136.5 jit_solution(6265865294911485587)
XLA Ops:
  0.6 1.4 %multiply_reduce_fusion = f32[224]{0:T(256)S(1)} fusion(f32[224,1024]{1,0:T(8,128)} %emb_ref.1), kind=kLoop, calls=%fused_computation.1 | loop fusion | flops 458528 | bytes 918400 | tf_op jit(solution)/shard_map/reduce_sum | solution.py:358
  2.0 0.0 copy-done
  2.1 0.1 divide_convert_fusion.unit_ref.refs_1_.refs_12_
  2.2 8.8 %collective-permute-start = (bf16[224,1024]{1,0:T(8,128)(2,1)S(1)}, bf16[224,1024]{1,0:T(8,128)(2,1)S(1)}, u32[]{:S(2)}, u32[]{:S(2)}) collective-permute-start(bf16[224,1024]{1,0:T(8,128)(2,1)S(1)} %divide_convert_fusion.unit_ref.refs_1_.refs_12_), channel_id=1, source_target_pairs={{0,1},{1,0},{2,3},{3,2},{4,5},{5,4},{6,7},{7,6},{8,9},{9,8},{10,11... | collective-permute-start | bytes 1376264 | tf_op jit(solution)/shard_map/ppermute | solution.py:365
  11.0 1.9 %collective-permute-start.1 = (bf16[224,1024]{1,0:T(8,128)(2,1)S(1)}, bf16[224,1024]{1,0:T(8,128)(2,1)S(1)}, u32[]{:S(2)}, u32[]{:S(2)}) collective-permute-start(bf16[224,1024]{1,0:T(8,128)(2,1)S(1)} %divide_convert_fusion.unit_ref.refs_1_.refs_12_), channel_id=1, source_target_pairs={{0,4},{1,5},{2,0},{3,1},{4,6},{5,7},{6,2},{7,3},{8,12},{9,13},{10,... | collective-permute-start | bytes 1376264 | tf_op jit(solution)/shard_map/ppermute | solution.py:354
  13.0 0.1 pad_add_fusion.ids_ref.refs_0_
  13.0 0.0 collective-permute-done.other_ref.refs_2_
  13.0 0.7 copy-done.1
  13.7 1.0 own_scores.1
  14.8 11.5 %collective-permute-start.6 = (bf16[224,1024]{1,0:T(8,128)(2,1)S(1)}, bf16[224,1024]{1,0:T(8,128)(2,1)S(1)}, u32[]{:S(2)}, u32[]{:S(2)}) collective-permute-start(bf16[224,1024]{1,0:T(8,128)(2,1)S(1)} %divide_convert_fusion.unit_ref.refs_1_.refs_12_), channel_id=1, source_target_pairs={{126,128},{127,129},{128,126},{129,127},{254,256},{255,257},{256,2... | collective-permute-start | bytes 1376264 | tf_op jit(solution)/shard_map/ppermute | solution.py:354
  26.3 1.9 %collective-permute-start.2 = (bf16[224,1024]{1,0:T(8,128)(2,1)S(1)}, bf16[224,1024]{1,0:T(8,128)(2,1)S(1)}, u32[]{:S(2)}, u32[]{:S(2)}) collective-permute-start(bf16[224,1024]{1,0:T(8,128)(2,1)S(1)} %divide_convert_fusion.unit_ref.refs_1_.refs_12_), channel_id=1, source_target_pairs={{2,6},{3,7},{4,0},{5,1},{0,2},{1,3},{6,4},{7,5},{10,14},{11,15},{1... | collective-permute-start | bytes 1376264 | tf_op jit(solution)/shard_map/ppermute | solution.py:354
  28.3 1.3 collective-permute-start.5
  29.6 11.8 %collective-permute-start.8 = (bf16[224,1024]{1,0:T(8,128)(2,1)S(1)}, bf16[224,1024]{1,0:T(8,128)(2,1)S(1)}, u32[]{:S(2)}, u32[]{:S(2)}) collective-permute-start(bf16[224,1024]{1,0:T(8,128)(2,1)S(1)} %collective-permute-done.1.refs_5_.refs_13_), channel_id=1, source_target_pairs={{126,128},{127,129},{128,126},{129,127},{254,256},{255,257},{256,2... | collective-permute-start | bytes 1376264 | tf_op jit(solution)/shard_map/ppermute | solution.py:354
  41.4 0.0 collective-permute-done.6.refs_7_
  41.4 1.3 collective-permute-start.7
  42.7 1.0 block_scores.6
  43.8 1.3 collective-permute-start.3
  45.1 0.7 collective-permute-start.4
  45.8 1.3 collective-permute-start.10
  47.1 3.8 %collective-permute-done.8.refs_6_ = bf16[224,1024]{1,0:T(8,128)(2,1)S(1)} collective-permute-done((bf16[224,1024]{1,0:T(8,128)(2,1)S(1)}, bf16[224,1024]{1,0:T(8,128)(2,1)S(1)}, u32[]{:S(2)}, u32[]{:S(2)}) %collective-permute-start.8) | collective-permute-done | bytes 458784 | tf_op jit(solution)/shard_map/ppermute | solution.py:354
  50.9 8.5 %collective-permute-start.9 = (bf16[224,1024]{1,0:T(8,128)(2,1)S(1)}, bf16[224,1024]{1,0:T(8,128)(2,1)S(1)}, u32[]{:S(2)}, u32[]{:S(2)}) collective-permute-start(bf16[224,1024]{1,0:T(8,128)(2,1)S(1)} %collective-permute-done.2.refs_5_.refs_14_), channel_id=1, source_target_pairs={{126,128},{127,129},{128,126},{129,127},{254,256},{255,257},{256,2... | collective-permute-start | bytes 1376264 | tf_op jit(solution)/shard_map/ppermute | solution.py:354
  59.4 0.0 collective-permute-done.7.refs_6_
  59.4 0.7 collective-permute-start.11
  60.1 1.0 block_scores.7
  61.1 1.3 collective-permute-start.12
  62.5 0.7 collective-permute-start.13
  63.2 1.9 %collective-permute-start.14 = (bf16[224,1024]{1,0:T(8,128)(2,1)S(1)}, bf16[224,1024]{1,0:T(8,128)(2,1)S(1)}, u32[]{:S(2)}, u32[]{:S(2)}) collective-permute-start(bf16[224,1024]{1,0:T(8,128)(2,1)S(1)} %collective-permute-done.8.refs_6_), channel_id=1, source_target_pairs={{128,130},{129,131},{126,124},{127,125},{256,258},{257,259},{254,2... | collective-permute-start | bytes 1376264 | tf_op jit(solution)/shard_map/ppermute | solution.py:354
  65.0 1.1 block_scores.8
  66.1 2.1 %collective-permute-done.9.refs_7_ = bf16[224,1024]{1,0:T(8,128)(2,1)S(1)} collective-permute-done((bf16[224,1024]{1,0:T(8,128)(2,1)S(1)}, bf16[224,1024]{1,0:T(8,128)(2,1)S(1)}, u32[]{:S(2)}, u32[]{:S(2)}) %collective-permute-start.9) | collective-permute-done | bytes 458784 | tf_op jit(solution)/shard_map/ppermute | solution.py:354
  68.2 1.1 block_scores.9
  69.3 1.1 block_scores.10
  70.4 1.4 %collective-permute-done.14.refs_8_ = bf16[224,1024]{1,0:T(8,128)(2,1)S(1)} collective-permute-done((bf16[224,1024]{1,0:T(8,128)(2,1)S(1)}, bf16[224,1024]{1,0:T(8,128)(2,1)S(1)}, u32[]{:S(2)}, u32[]{:S(2)}) %collective-permute-start.14) | collective-permute-done | bytes 458784 | tf_op jit(solution)/shard_map/ppermute | solution.py:354
  71.8 1.2 block_scores.11
  73.0 16.3 %all_to_all.5.pay_ref = f32[32,8,128]{2,1,0:T(8,128)S(1)} all-to-all(f32[32,8,128]{2,1,0:T(8,128)S(1)} %broadcast_in_dim.2), channel_id=1, replica_groups=mesh['zh'=4,'x'=4,'y'=4,'zl'=4,'core'=2] {'y','zl','core'}, dimensions={0} | all-to-all | bytes 262144 | tf_op jit(solution)/shard_map/all_to_all | solution.py:404
  89.4 0.7 denoms.1
  90.0 1.9 %collective-permute-start.15 = (f32[8,128]{1,0:T(8,128)S(1)}, f32[8,128]{1,0:T(8,128)S(1)}, u32[]{:S(2)}, u32[]{:S(2)}) collective-permute-start(f32[8,128]{1,0:T(8,128)S(1)} %get-tuple-element.91), channel_id=1, source_target_pairs={{0,32},{32,0},{64,96},{96,64},{1,33},{33,1},{65,97},{97,65},{2,34}... | collective-permute-start | bytes 12296 | tf_op jit(solution)/shard_map/ppermute | solution.py:407
  91.9 10.8 %collective-permute-start.17 = (f32[4,2,128]{2,1,0:T(2,128)S(1)}, f32[4,2,128]{2,1,0:T(2,128)S(1)}, u32[]{:S(2)}, u32[]{:S(2)}) collective-permute-start(f32[4,2,128]{2,1,0:T(2,128)S(1)} %get-tuple-element.94), channel_id=1, source_target_pairs={{24,32},{0,504},{25,33},{1,505},{26,34},{2,506},{27,35},{3,507},{2... | collective-permute-start | bytes 12296 | tf_op jit(solution)/shard_map/ppermute | solution.py:410
  102.7 1.9 %collective-permute-start.16 = (f32[8,128]{1,0:T(8,128)S(1)}, f32[8,128]{1,0:T(8,128)S(1)}, u32[]{:S(2)}, u32[]{:S(2)}) collective-permute-start(f32[8,128]{1,0:T(8,128)S(1)} %add.39), channel_id=1, source_target_pairs={{0,64},{32,96},{64,0},{96,32},{1,65},{33,97},{65,1},{97,33},{2,66}... | collective-permute-start | bytes 12296 | tf_op jit(solution)/shard_map/ppermute | solution.py:407
  104.7 1.8 %unit_gradient.2 = f32[224,1024]{1,0:T(8,128)S(1)} custom-call(s32[4]{0:T(128)S(1)} %pad_add_fusion.ids_ref.refs_0_, f32[16,2,128]{2,1,0:T(2,128)S(1)} %get-tuple-element.109.refs_1_, f32[4,2,128]{2,1,0:T(2,128)S(1)} %collective-permute-done.17.refs_2_, f32[2,128]{1,0:T(2,128)S(1)} %get-tuple-element.95.refs_3_, s32[1,224]{1,0:T(1,128)S(1)} %get-tuple-element.96.refs_4_, ...), custom_call_target="tpu_custom_call" | custom-call | flops 719323136 | bytes 6291456 | tf_op jit(solution)/shard_map/unit_gradient/pallas_call | solution.py:319
  106.4 2.2 %collective-permute-done.16 = f32[8,128]{1,0:T(8,128)S(1)} collective-permute-done((f32[8,128]{1,0:T(8,128)S(1)}, f32[8,128]{1,0:T(8,128)S(1)}, u32[]{:S(2)}, u32[]{:S(2)}) %collective-permute-start.16) | collective-permute-done | bytes 4128 | tf_op jit(solution)/shard_map/ppermute | solution.py:407
  108.6 4.2 %collective-permute-start.20 = (f32[224,1024]{1,0:T(8,128)S(1)}, f32[224,1024]{1,0:T(8,128)S(1)}, u32[]{:S(2)}, u32[]{:S(2)}) collective-permute-start(f32[224,1024]{1,0:T(8,128)S(1)} %unit_gradient.2), channel_id=1, source_target_pairs={{0,1},{1,0},{2,3},{3,2},{4,5},{5,4},{6,7},{7,6},{8,9},{9,8},{10,11... | collective-permute-start | bytes 2752520 | tf_op jit(solution)/shard_map/ppermute | solution.py:414
  112.8 4.1 %collective-permute-start.18 = (f32[8,128]{1,0:T(8,128)S(1)}, f32[8,128]{1,0:T(8,128)S(1)}, u32[]{:S(2)}, u32[]{:S(2)}) collective-permute-start(f32[8,128]{1,0:T(8,128)S(1)} %add.40), channel_id=1, source_target_pairs={{0,128},{128,0},{256,384},{384,256},{1,129},{129,1},{257,385},{385... | collective-permute-start | bytes 12296 | tf_op jit(solution)/shard_map/ppermute | solution.py:407
  117.0 1.7 %unit_gradient.3.mine_ref = f32[224,1024]{1,0:T(8,128)S(1)} custom-call(s32[4]{0:T(128)S(1)} %pad_add_fusion.ids_ref.refs_0_, f32[16,2,128]{2,1,0:T(2,128)S(1)} %get-tuple-element.109.refs_1_, f32[4,2,128]{2,1,0:T(2,128)S(1)} %collective-permute-done.17.refs_2_, f32[2,128]{1,0:T(2,128)S(1)} %get-tuple-element.110.refs_3_, ...), custom_call_target="tpu_custom_call" | custom-call | flops 719323136 | bytes 6291456 | tf_op jit(solution)/shard_map/unit_gradient/pallas_call | solution.py:319
  118.7 2.4 %collective-permute-done.18 = f32[8,128]{1,0:T(8,128)S(1)} collective-permute-done((f32[8,128]{1,0:T(8,128)S(1)}, f32[8,128]{1,0:T(8,128)S(1)}, u32[]{:S(2)}, u32[]{:S(2)}) %collective-permute-start.18) | collective-permute-done | bytes 4128 | tf_op jit(solution)/shard_map/ppermute | solution.py:407
  121.1 8.9 %collective-permute-start.19 = (f32[8,128]{1,0:T(8,128)S(1)}, f32[8,128]{1,0:T(8,128)S(1)}, u32[]{:S(2)}, u32[]{:S(2)}) collective-permute-start(f32[8,128]{1,0:T(8,128)S(1)} %add.41), channel_id=1, source_target_pairs={{0,256},{128,384},{256,0},{384,128},{1,257},{129,385},{257,1},{385... | collective-permute-start | bytes 12296 | tf_op jit(solution)/shard_map/ppermute | solution.py:407
  130.1 2.1 %final.1 = f32[224,1024]{1,0:T(8,128)} custom-call(f32[224,1024]{1,0:T(8,128)S(1)} %copy-done, f32[224,1024]{1,0:T(8,128)S(1)} %unit_gradient.3.mine_ref, f32[224,1024]{1,0:T(8,128)S(1)} %collective-permute-done.20.got_ref), custom_call_target="tpu_custom_call" | custom-call | flops 2293760 | bytes 3670016 | tf_op jit(solution)/shard_map/final/pallas_call | solution.py:341
  132.2 2.0 %collective-permute-done.19 = f32[8,128]{1,0:T(8,128)S(1)} collective-permute-done((f32[8,128]{1,0:T(8,128)S(1)}, f32[8,128]{1,0:T(8,128)S(1)}, u32[]{:S(2)}, u32[]{:S(2)}) %collective-permute-start.19) | collective-permute-done | bytes 4128 | tf_op jit(solution)/shard_map/ppermute | solution.py:407
  134.2 0.5 slice.3
  (20 shorter events, 0.1 us)
Async XLA Ops:
  0.6 1.5 %copy-start = (f32[224,1024]{1,0:T(8,128)S(1)}, f32[224,1024]{1,0:T(8,128)}, u32[]{:S(2)}) copy-start(f32[224,1024]{1,0:T(8,128)} %emb_ref.1) | copy-start | bytes 2752516
  2.2 10.8 %collective-permute-start = (bf16[224,1024]{1,0:T(8,128)(2,1)S(1)}, bf16[224,1024]{1,0:T(8,128)(2,1)S(1)}, u32[]{:S(2)}, u32[]{:S(2)}) collective-permute-start(bf16[224,1024]{1,0:T(8,128)(2,1)S(1)} %divide_convert_fusion.unit_ref.refs_1_.refs_12_), channel_id=1, source_target_pairs={{0,1},{1,0},{2,3},{3,2},{4,5},{5,4},{6,7},{7,6},{8,9},{9,8},{10,11... | collective-permute-start | bytes 1376264 | tf_op jit(solution)/shard_map/ppermute | solution.py:365
  11.0 15.3 %collective-permute-start.1 = (bf16[224,1024]{1,0:T(8,128)(2,1)S(1)}, bf16[224,1024]{1,0:T(8,128)(2,1)S(1)}, u32[]{:S(2)}, u32[]{:S(2)}) collective-permute-start(bf16[224,1024]{1,0:T(8,128)(2,1)S(1)} %divide_convert_fusion.unit_ref.refs_1_.refs_12_), channel_id=1, source_target_pairs={{0,4},{1,5},{2,0},{3,1},{4,6},{5,7},{6,2},{7,3},{8,12},{9,13},{10,... | collective-permute-start | bytes 1376264 | tf_op jit(solution)/shard_map/ppermute | solution.py:354
  13.0 0.7 copy-start.1
  14.8 26.6 %collective-permute-start.6 = (bf16[224,1024]{1,0:T(8,128)(2,1)S(1)}, bf16[224,1024]{1,0:T(8,128)(2,1)S(1)}, u32[]{:S(2)}, u32[]{:S(2)}) collective-permute-start(bf16[224,1024]{1,0:T(8,128)(2,1)S(1)} %divide_convert_fusion.unit_ref.refs_1_.refs_12_), channel_id=1, source_target_pairs={{126,128},{127,129},{128,126},{129,127},{254,256},{255,257},{256,2... | collective-permute-start | bytes 1376264 | tf_op jit(solution)/shard_map/ppermute | solution.py:354
  26.3 17.4 %collective-permute-start.2 = (bf16[224,1024]{1,0:T(8,128)(2,1)S(1)}, bf16[224,1024]{1,0:T(8,128)(2,1)S(1)}, u32[]{:S(2)}, u32[]{:S(2)}) collective-permute-start(bf16[224,1024]{1,0:T(8,128)(2,1)S(1)} %divide_convert_fusion.unit_ref.refs_1_.refs_12_), channel_id=1, source_target_pairs={{2,6},{3,7},{4,0},{5,1},{0,2},{1,3},{6,4},{7,5},{10,14},{11,15},{1... | collective-permute-start | bytes 1376264 | tf_op jit(solution)/shard_map/ppermute | solution.py:354
  28.3 17.5 %collective-permute-start.5 = (bf16[224,1024]{1,0:T(8,128)(2,1)S(1)}, bf16[224,1024]{1,0:T(8,128)(2,1)S(1)}, u32[]{:S(2)}, u32[]{:S(2)}) collective-permute-start(bf16[224,1024]{1,0:T(8,128)(2,1)S(1)} %collective-permute-done.1.refs_5_.refs_13_), channel_id=1, source_target_pairs={{0,8},{1,9},{2,10},{3,11},{8,16},{9,17},{10,18},{11,19},{12,4},{13... | collective-permute-start | bytes 1376264 | tf_op jit(solution)/shard_map/ppermute | solution.py:354
  29.6 21.3 %collective-permute-start.8 = (bf16[224,1024]{1,0:T(8,128)(2,1)S(1)}, bf16[224,1024]{1,0:T(8,128)(2,1)S(1)}, u32[]{:S(2)}, u32[]{:S(2)}) collective-permute-start(bf16[224,1024]{1,0:T(8,128)(2,1)S(1)} %collective-permute-done.1.refs_5_.refs_13_), channel_id=1, source_target_pairs={{126,128},{127,129},{128,126},{129,127},{254,256},{255,257},{256,2... | collective-permute-start | bytes 1376264 | tf_op jit(solution)/shard_map/ppermute | solution.py:354
  41.4 18.0 %collective-permute-start.7 = (bf16[224,1024]{1,0:T(8,128)(2,1)S(1)}, bf16[224,1024]{1,0:T(8,128)(2,1)S(1)}, u32[]{:S(2)}, u32[]{:S(2)}) collective-permute-start(bf16[224,1024]{1,0:T(8,128)(2,1)S(1)} %collective-permute-done.6.refs_7_), channel_id=1, source_target_pairs={{128,130},{129,131},{126,124},{127,125},{256,258},{257,259},{254,2... | collective-permute-start | bytes 1376264 | tf_op jit(solution)/shard_map/ppermute | solution.py:354
  43.8 17.3 %collective-permute-start.3 = (bf16[224,1024]{1,0:T(8,128)(2,1)S(1)}, bf16[224,1024]{1,0:T(8,128)(2,1)S(1)}, u32[]{:S(2)}, u32[]{:S(2)}) collective-permute-start(bf16[224,1024]{1,0:T(8,128)(2,1)S(1)} %collective-permute-done.1.refs_5_.refs_13_), channel_id=1, source_target_pairs={{4,6},{5,7},{2,0},{3,1},{12,14},{13,15},{10,8},{11,9},{20,22},{21,... | collective-permute-start | bytes 1376264 | tf_op jit(solution)/shard_map/ppermute | solution.py:354
  45.1 16.0 %collective-permute-start.4 = (bf16[224,1024]{1,0:T(8,128)(2,1)S(1)}, bf16[224,1024]{1,0:T(8,128)(2,1)S(1)}, u32[]{:S(2)}, u32[]{:S(2)}) collective-permute-start(bf16[224,1024]{1,0:T(8,128)(2,1)S(1)} %divide_convert_fusion.unit_ref.refs_1_.refs_12_), channel_id=1, source_target_pairs={{2,4},{3,5},{4,2},{5,3},{10,12},{11,13},{12,10},{13,11},{18,20},{1... | collective-permute-start | bytes 1376264 | tf_op jit(solution)/shard_map/ppermute | solution.py:354
  45.8 15.3 %collective-permute-start.10 = (bf16[224,1024]{1,0:T(8,128)(2,1)S(1)}, bf16[224,1024]{1,0:T(8,128)(2,1)S(1)}, u32[]{:S(2)}, u32[]{:S(2)}) collective-permute-start(bf16[224,1024]{1,0:T(8,128)(2,1)S(1)} %collective-permute-done.2.refs_5_.refs_14_), channel_id=1, source_target_pairs={{0,8},{1,9},{4,12},{5,13},{8,16},{9,17},{12,20},{13,21},{10,2},{11... | collective-permute-start | bytes 1376264 | tf_op jit(solution)/shard_map/ppermute | solution.py:354
  50.9 17.3 %collective-permute-start.9 = (bf16[224,1024]{1,0:T(8,128)(2,1)S(1)}, bf16[224,1024]{1,0:T(8,128)(2,1)S(1)}, u32[]{:S(2)}, u32[]{:S(2)}) collective-permute-start(bf16[224,1024]{1,0:T(8,128)(2,1)S(1)} %collective-permute-done.2.refs_5_.refs_14_), channel_id=1, source_target_pairs={{126,128},{127,129},{128,126},{129,127},{254,256},{255,257},{256,2... | collective-permute-start | bytes 1376264 | tf_op jit(solution)/shard_map/ppermute | solution.py:354
  59.4 9.9 %collective-permute-start.11 = (bf16[224,1024]{1,0:T(8,128)(2,1)S(1)}, bf16[224,1024]{1,0:T(8,128)(2,1)S(1)}, u32[]{:S(2)}, u32[]{:S(2)}) collective-permute-start(bf16[224,1024]{1,0:T(8,128)(2,1)S(1)} %collective-permute-done.7.refs_6_), channel_id=1, source_target_pairs={{130,132},{131,133},{124,122},{125,123},{258,260},{259,261},{252,2... | collective-permute-start | bytes 1376264 | tf_op jit(solution)/shard_map/ppermute | solution.py:354
  61.1 9.3 %collective-permute-start.12 = (bf16[224,1024]{1,0:T(8,128)(2,1)S(1)}, bf16[224,1024]{1,0:T(8,128)(2,1)S(1)}, u32[]{:S(2)}, u32[]{:S(2)}) collective-permute-start(bf16[224,1024]{1,0:T(8,128)(2,1)S(1)} %collective-permute-done.3.refs_5_), channel_id=1, source_target_pairs={{0,8},{1,9},{8,16},{9,17},{14,6},{15,7},{16,24},{17,25},{22,14},{2... | collective-permute-start | bytes 1376264 | tf_op jit(solution)/shard_map/ppermute | solution.py:354
  62.5 7.9 %collective-permute-start.13 = (bf16[224,1024]{1,0:T(8,128)(2,1)S(1)}, bf16[224,1024]{1,0:T(8,128)(2,1)S(1)}, u32[]{:S(2)}, u32[]{:S(2)}) collective-permute-start(bf16[224,1024]{1,0:T(8,128)(2,1)S(1)} %collective-permute-done.4.refs_6_), channel_id=1, source_target_pairs={{2,10},{3,11},{10,18},{11,19},{12,4},{13,5},{18,26},{19,27},{20,12... | collective-permute-start | bytes 1376264 | tf_op jit(solution)/shard_map/ppermute | solution.py:354
  63.2 8.7 %collective-permute-start.14 = (bf16[224,1024]{1,0:T(8,128)(2,1)S(1)}, bf16[224,1024]{1,0:T(8,128)(2,1)S(1)}, u32[]{:S(2)}, u32[]{:S(2)}) collective-permute-start(bf16[224,1024]{1,0:T(8,128)(2,1)S(1)} %collective-permute-done.8.refs_6_), channel_id=1, source_target_pairs={{128,130},{129,131},{126,124},{127,125},{256,258},{257,259},{254,2... | collective-permute-start | bytes 1376264 | tf_op jit(solution)/shard_map/ppermute | solution.py:354
  90.0 12.7 %collective-permute-start.15 = (f32[8,128]{1,0:T(8,128)S(1)}, f32[8,128]{1,0:T(8,128)S(1)}, u32[]{:S(2)}, u32[]{:S(2)}) collective-permute-start(f32[8,128]{1,0:T(8,128)S(1)} %get-tuple-element.91), channel_id=1, source_target_pairs={{0,32},{32,0},{64,96},{96,64},{1,33},{33,1},{65,97},{97,65},{2,34}... | collective-permute-start | bytes 12296 | tf_op jit(solution)/shard_map/ppermute | solution.py:407
  91.9 12.7 %collective-permute-start.17 = (f32[4,2,128]{2,1,0:T(2,128)S(1)}, f32[4,2,128]{2,1,0:T(2,128)S(1)}, u32[]{:S(2)}, u32[]{:S(2)}) collective-permute-start(f32[4,2,128]{2,1,0:T(2,128)S(1)} %get-tuple-element.94), channel_id=1, source_target_pairs={{24,32},{0,504},{25,33},{1,505},{26,34},{2,506},{27,35},{3,507},{2... | collective-permute-start | bytes 12296 | tf_op jit(solution)/shard_map/ppermute | solution.py:410
  102.7 5.9 %collective-permute-start.16 = (f32[8,128]{1,0:T(8,128)S(1)}, f32[8,128]{1,0:T(8,128)S(1)}, u32[]{:S(2)}, u32[]{:S(2)}) collective-permute-start(f32[8,128]{1,0:T(8,128)S(1)} %add.39), channel_id=1, source_target_pairs={{0,64},{32,96},{64,0},{96,32},{1,65},{33,97},{65,1},{97,33},{2,66}... | collective-permute-start | bytes 12296 | tf_op jit(solution)/shard_map/ppermute | solution.py:407
  108.6 21.5 %collective-permute-start.20 = (f32[224,1024]{1,0:T(8,128)S(1)}, f32[224,1024]{1,0:T(8,128)S(1)}, u32[]{:S(2)}, u32[]{:S(2)}) collective-permute-start(f32[224,1024]{1,0:T(8,128)S(1)} %unit_gradient.2), channel_id=1, source_target_pairs={{0,1},{1,0},{2,3},{3,2},{4,5},{5,4},{6,7},{7,6},{8,9},{9,8},{10,11... | collective-permute-start | bytes 2752520 | tf_op jit(solution)/shard_map/ppermute | solution.py:414
  112.8 8.3 %collective-permute-start.18 = (f32[8,128]{1,0:T(8,128)S(1)}, f32[8,128]{1,0:T(8,128)S(1)}, u32[]{:S(2)}, u32[]{:S(2)}) collective-permute-start(f32[8,128]{1,0:T(8,128)S(1)} %add.40), channel_id=1, source_target_pairs={{0,128},{128,0},{256,384},{384,256},{1,129},{129,1},{257,385},{385... | collective-permute-start | bytes 12296 | tf_op jit(solution)/shard_map/ppermute | solution.py:407
  121.1 13.1 %collective-permute-start.19 = (f32[8,128]{1,0:T(8,128)S(1)}, f32[8,128]{1,0:T(8,128)S(1)}, u32[]{:S(2)}, u32[]{:S(2)}) collective-permute-start(f32[8,128]{1,0:T(8,128)S(1)} %add.41), channel_id=1, source_target_pairs={{0,256},{128,384},{256,0},{384,128},{1,257},{129,385},{257,1},{385... | collective-permute-start | bytes 12296 | tf_op jit(solution)/shard_map/ppermute | solution.py:407

commit v3 on v2

--- a/solution.py
+++ b/solution.py
@@ -252,7 +252,7 @@
     total = jnp.log(first) + jnp.log(second)
     total = jnp.sum(total.reshape(32, 128), axis=0, keepdims=True)
     total = total - jnp.sum(pay[:, :, 4].reshape(32, 128), axis=0, keepdims=True)
-    loss_ref[...] = jnp.broadcast_to(jnp.sum(total, axis=1, keepdims=True), (8, 128))
+    loss_ref[...] = jnp.broadcast_to(jnp.sum(total, axis=1, keepdims=True), (16, 128))
     first, second = 1.0 / first, 1.0 / second
     inv_ref[...] = jnp.where(core == 0, first, second)
     other_all = jnp.where(core == 0, second, first)
@@ -272,7 +272,7 @@
             jax.ShapeDtypeStruct((2, 128), f32),
             jax.ShapeDtypeStruct((2, 128), f32),
             jax.ShapeDtypeStruct((4, 2, 128), f32),
-            jax.ShapeDtypeStruct((8, 128), f32),
+            jax.ShapeDtypeStruct((16, 128), f32),
         ),
         in_specs=smem(1) + vmem(1),
         out_specs=tuple(vmem(5)),
@@ -362,8 +362,9 @@
     ids = jnp.stack([lax.axis_index(name) for name in DEV_AXES] + [run]).astype(jnp.int32)
     partner = partner.reshape(1, ROWS)
 
-    other = lax.ppermute(unit, ("core",), [(0, 1), (1, 0)])
     r1 = send(unit, "P1")
+    x1 = send(unit, "X1")
+    other = lax.ppermute(after(unit, ids), ("core",), [(0, 1), (1, 0)])
     local, e_own, e_other, sum_own, sum_other, pos = own_call(ids, unit, other, partner)
     expos, blocks, sums = [(e_own, e_other)] + [None] * 6, [unit] + [None] * 6, (sum_own, sum_other)
 
@@ -377,17 +378,16 @@
             return rest
         sums = rest
 
-    x1 = send(after(unit, sums[0]), "X1")
-    r1 = after(r1, sums[0])
+    r1 = after(r1, x1, sums[0])
     r2 = send(after(unit, r1), "P2")
     y1 = send(r1, "Y1")
     x2 = send(after(x1, r1), "X2")
     x3 = send(r1, "X3")
     add(0, [r1])
     r2 = after(r2, sums[0])
+    y2 = send(after(r2, y1), "Y2")
     p3b = send(after(unit, r2), "P3b")
     p3a = send(after(r1, r2), "P3a")
-    y2 = send(after(r2, y1), "Y2")
     x4 = send(after(r2, x3), "X4")
     x6 = send(after(x2, r2), "X6")
     add(1, [r2])
@@ -403,21 +403,15 @@
 
     pays = lax.all_to_all(jnp.broadcast_to(pay[None], (32, 8, 128)), DEV_AXES, 0, 0)
     inv, mine_inv, other_inv, edge, loss = denom_call(ids, pays)
-    def exchange(value, axis, bit, *meanwhile):
-        got = lax.ppermute(value, (axis,), [(i, i ^ bit) for i in range(4)])
-        return value + after(got, *meanwhile)
-
+    losses = lax.all_to_all(loss, ("zh", "x"), 0, 0)
     edge = lax.ppermute(edge, AXES, EDGE)
-    loss = exchange(loss, "x", 1)
-    for_other = grad_call(ROWS, ids, after(inv, loss), edge, other_inv, local, [e[1] for e in expos], blocks)
-    loss = exchange(loss, "x", 2, for_other)
-    got = lax.ppermute(after(for_other, loss), ("core",), [(0, 1), (1, 0)])
-    mine = grad_call(0, ids, after(inv, loss), edge, mine_inv, local, [e[0] for e in expos], blocks)
-    loss = exchange(loss, "zh", 1, mine)
-    grad = final_call(embeddings, mine, after(got, loss))
-    loss = exchange(loss, "zh", 2, grad)
-    total_rows = ROWS * 512
-    loss = loss[0, 0] / total_rows + 1.0 / SOFTMAX_TEMPER
+    inv = after(inv, losses)
+    for_other = grad_call(ROWS, ids, inv, edge, other_inv, local, [e[1] for e in expos], blocks)
+    got = lax.ppermute(for_other, ("core",), [(0, 1), (1, 0)])
+    mine = grad_call(0, ids, after(inv, for_other), edge, mine_inv, local, [e[0] for e in expos], blocks)
+    grad = final_call(embeddings, mine, got)
+    losses = after(losses, mine)
+    loss = jnp.sum(losses[:, 0]) / (ROWS * 512) + 1.0 / SOFTMAX_TEMPER
     return (loss, grad)
 
 

time: 137 us -> 149 us (1.088)
  local copies, waits for them, and re-layouts: 1.24 us -> 15.6 us
  starting transfers between devices: 86.9 us -> 75 us
  waiting for transfers between devices: 13.8 us -> 18.9 us
  Pallas kernels: 13.7 us -> 16.9 us
    ppermute x6 -> x2, starting transfers between devices: 29.9 us -> 12.6 us  [the longest x1 8.91 us: per_device(): other = lax.ppermute(after(unit, ids), ('core',), [(0, 1), (1, 0)])]
    unnamed x4 -> x76, local copies, waits for them, and re-layouts: 0.72 us -> 15.6 us
    all_to_all x0 -> x1, starting transfers between devices: none -> 10.3 us  [per_device(): losses = lax.all_to_all(loss, ('zh', 'x'), 0, 0)]
    ppermute x14, waiting for transfers between devices: 7.27 us -> 14.9 us  [send(): return lax.ppermute(value, AXES, ROUTES[name])]
    ppermute x6 -> x2, waiting for transfers between devices: 6.56 us -> 0.01 us  [the longest x1 0.01 us: per_device(): other = lax.ppermute(after(unit, ids), ('core',), [(0, 1), (1, 0)])]
    all_to_all x0 -> x1, waiting for transfers between devices: none -> 3.97 us  [per_device(): losses = lax.all_to_all(loss, ('zh', 'x'), 0, 0)]
    ppermute x14, starting transfers between devices: 46.2 us -> 42.5 us  [send(): return lax.ppermute(value, AXES, ROUTES[name])]
    pallas_call x1, Pallas kernels: 2.08 us -> 3.73 us  [final_call(): pl.pallas_call(final_kernel, out_shape=jax.ShapeDtypeStruct((ROWS, WIDTH)...]
  transfers between devices with their start and end apart: 21 -> 18, of which waited for: 6 -> 6; matrix products, arithmetic and copies ran while one was open for 0% -> 0% of each run, Pallas kernels for 9% -> 5%
where the time goes in v3:
time: 149 us; the launch traced here: 148 us
  starting transfers between devices  75 us (50%)
  waiting for transfers between devices  18.9 us (13%)
  Pallas kernels  16.9 us (11%)
  blocking collectives  16.1 us (11%)
  local copies, waits for them, and re-layouts  15.6 us (10%)
  between operations  2.98 us (2%)
  other arithmetic  2.22 us (1%)
    ppermute x14, starting transfers between devices, send(): return lax.ppermute(value, AXES, ROUTES[name])  42.5 us
    all_to_all x1, blocking collectives, per_device(): lax.all_to_all(jnp.broadcast_to(pay[None], (32, 8, 128)), DEV_AXES, 0, 0)  16.1 us
    unnamed x76, local copies, waits for them, and re-layouts  15.6 us
    ppermute x14, waiting for transfers between devices, send(): return lax.ppermute(value, AXES, ROUTES[name])  14.9 us
    all_to_all x1, starting transfers between devices, per_device(): losses = lax.all_to_all(loss, ('zh', 'x'), 0, 0)  10.3 us
    ppermute x1, starting transfers between devices, per_device(): edge = lax.ppermute(edge, AXES, EDGE)  9.64 us
    ppermute x1, starting transfers between devices, per_device(): other = lax.ppermute(after(unit, ids), ('core',), [(0, 1), (1, 0)])  8.91 us
    pallas_call x6, Pallas kernels, block_call(): pl.pallas_call(kernel, out_shape=tuple(shapes), in_specs=smem(1) + vmem(l...  6.46 us
  transfers between devices with their start and end apart: 18, of which 6 were waited for; matrix products, arithmetic and copies ran while one was open for 0% of the time, Pallas kernels for 5%

profile of v3, /device:TPU:1, one launch (start us, length us, event | category | flops | bytes accessed | tf_op | source)
XLA Modules:
  0.0 147.8 jit_solution(2944431647845600105)
XLA Ops:
  0.6 1.4 multiply_reduce_fusion
  2.3 8.9 %collective-permute-start = (bf16[224,1024]{1,0:T(8,128)(2,1)S(1)}, bf16[224,1024]{1,0:T(8,128)(2,1)S(1)}, u32[]{:S(2)}, u32[]{:S(2)}) collective-permute-start(bf16[224,1024]{1,0:T(8,128)(2,1)S(1)} %divide_convert_fusion.unit_ref.refs_1_.refs_12_), channel_id=1, source_target_pairs={{0,1},{1,0},{2,3},{3,2},{4,5},{5,4},{6,7},{7,6},{8,9},{9,8},{10,11... | collective-permute-start | bytes 1376264 | tf_op jit(solution)/shard_map/ppermute | solution.py:367
  11.2 1.9 %collective-permute-start.1 = (bf16[224,1024]{1,0:T(8,128)(2,1)S(1)}, bf16[224,1024]{1,0:T(8,128)(2,1)S(1)}, u32[]{:S(2)}, u32[]{:S(2)}) collective-permute-start(bf16[224,1024]{1,0:T(8,128)(2,1)S(1)} %divide_convert_fusion.unit_ref.refs_1_.refs_12_), channel_id=1, source_target_pairs={{0,4},{1,5},{2,0},{3,1},{4,6},{5,7},{6,2},{7,3},{8,12},{9,13},{10,... | collective-permute-start | bytes 1376264 | tf_op jit(solution)/shard_map/ppermute | solution.py:354
  13.2 11.6 %collective-permute-start.2 = (bf16[224,1024]{1,0:T(8,128)(2,1)S(1)}, bf16[224,1024]{1,0:T(8,128)(2,1)S(1)}, u32[]{:S(2)}, u32[]{:S(2)}) collective-permute-start(bf16[224,1024]{1,0:T(8,128)(2,1)S(1)} %divide_convert_fusion.unit_ref.refs_1_.refs_12_), channel_id=1, source_target_pairs={{126,128},{127,129},{128,126},{129,127},{254,256},{255,257},{256,2... | collective-permute-start | bytes 1376264 | tf_op jit(solution)/shard_map/ppermute | solution.py:354
  24.7 1.0 own_scores.1
  26.5 8.9 %collective-permute-done.2.refs_7_ = bf16[224,1024]{1,0:T(8,128)(2,1)S(1)} collective-permute-done((bf16[224,1024]{1,0:T(8,128)(2,1)S(1)}, bf16[224,1024]{1,0:T(8,128)(2,1)S(1)}, u32[]{:S(2)}, u32[]{:S(2)}) %collective-permute-start.2) | collective-permute-done | bytes 458784 | tf_op jit(solution)/shard_map/ppermute | solution.py:354
  35.4 1.9 %collective-permute-start.3 = (bf16[224,1024]{1,0:T(8,128)(2,1)S(1)}, bf16[224,1024]{1,0:T(8,128)(2,1)S(1)}, u32[]{:S(2)}, u32[]{:S(2)}) collective-permute-start(bf16[224,1024]{1,0:T(8,128)(2,1)S(1)} %divide_convert_fusion.unit_ref.refs_1_.refs_12_), channel_id=1, source_target_pairs={{2,6},{3,7},{4,0},{5,1},{0,2},{1,3},{6,4},{7,5},{10,14},{11,15},{1... | collective-permute-start | bytes 1376264 | tf_op jit(solution)/shard_map/ppermute | solution.py:354
  37.3 1.3 collective-permute-start.6
  38.6 8.5 %collective-permute-start.8 = (bf16[224,1024]{1,0:T(8,128)(2,1)S(1)}, bf16[224,1024]{1,0:T(8,128)(2,1)S(1)}, u32[]{:S(2)}, u32[]{:S(2)}) collective-permute-start(bf16[224,1024]{1,0:T(8,128)(2,1)S(1)} %collective-permute-done.1.refs_5_.refs_13_), channel_id=1, source_target_pairs={{126,128},{127,129},{128,126},{129,127},{254,256},{255,257},{256,2... | collective-permute-start | bytes 1376264 | tf_op jit(solution)/shard_map/ppermute | solution.py:354
  47.1 1.3 collective-permute-start.7
  48.4 1.0 block_scores.6
  50.8 1.3 collective-permute-start.4
  52.1 0.7 collective-permute-start.5
  52.8 1.3 collective-permute-start.10
  54.2 3.0 %collective-permute-done.8.refs_6_ = bf16[224,1024]{1,0:T(8,128)(2,1)S(1)} collective-permute-done((bf16[224,1024]{1,0:T(8,128)(2,1)S(1)}, bf16[224,1024]{1,0:T(8,128)(2,1)S(1)}, u32[]{:S(2)}, u32[]{:S(2)}) %collective-permute-start.8) | collective-permute-done | bytes 458784 | tf_op jit(solution)/shard_map/ppermute | solution.py:354
  57.2 8.1 %collective-permute-start.9 = (bf16[224,1024]{1,0:T(8,128)(2,1)S(1)}, bf16[224,1024]{1,0:T(8,128)(2,1)S(1)}, u32[]{:S(2)}, u32[]{:S(2)}) collective-permute-start(bf16[224,1024]{1,0:T(8,128)(2,1)S(1)} %collective-permute-done.3.refs_5_.refs_14_), channel_id=1, source_target_pairs={{126,128},{127,129},{128,126},{129,127},{254,256},{255,257},{256,2... | collective-permute-start | bytes 1376264 | tf_op jit(solution)/shard_map/ppermute | solution.py:354
  65.3 0.7 collective-permute-start.11
  66.0 1.0 block_scores.7
  67.1 0.7 copy-done.17
  68.5 1.3 collective-permute-start.12
  70.5 1.9 %collective-permute-start.14 = (bf16[224,1024]{1,0:T(8,128)(2,1)S(1)}, bf16[224,1024]{1,0:T(8,128)(2,1)S(1)}, u32[]{:S(2)}, u32[]{:S(2)}) collective-permute-start(bf16[224,1024]{1,0:T(8,128)(2,1)S(1)} %collective-permute-done.8.refs_6_), channel_id=1, source_target_pairs={{128,130},{129,131},{126,124},{127,125},{256,258},{257,259},{254,2... | collective-permute-start | bytes 1376264 | tf_op jit(solution)/shard_map/ppermute | solution.py:354
  72.4 1.1 block_scores.8
  74.1 0.7 collective-permute-done.9.refs_7_
  74.9 1.1 block_scores.9
  76.0 1.1 block_scores.10
  77.5 1.9 %collective-permute-done.14.refs_8_ = bf16[224,1024]{1,0:T(8,128)(2,1)S(1)} collective-permute-done((bf16[224,1024]{1,0:T(8,128)(2,1)S(1)}, bf16[224,1024]{1,0:T(8,128)(2,1)S(1)}, u32[]{:S(2)}, u32[]{:S(2)}) %collective-permute-start.14) | collective-permute-done | bytes 458784 | tf_op jit(solution)/shard_map/ppermute | solution.py:354
  79.4 1.2 block_scores.11
  80.6 0.8 copy-done.8
  81.4 16.1 %all_to_all.17.pay_ref = f32[32,8,128]{2,1,0:T(8,128)S(1)} all-to-all(f32[32,8,128]{2,1,0:T(8,128)S(1)} %broadcast_in_dim.2), channel_id=1, replica_groups=mesh['zh'=4,'x'=4,'y'=4,'zl'=4,'core'=2] {'y','zl','core'}, dimensions={0} | all-to-all | bytes 262144 | tf_op jit(solution)/shard_map/all_to_all | solution.py:404
  97.5 1.3 denoms.1
  98.8 10.3 %all-to-all-start.1 = ((f32[16,1,128]{2,1,0:T(1,128)}), f32[16,1,128]{2,1,0:T(1,128)S(1)}, u32[]{:S(2)}, u32[]{:S(2)}) async-start(f32[16,1,128]{2,1,0:T(1,128)} %bitcast.6), calls=%async_computation.1 | async-start | bytes 16384 | tf_op jit(solution)/shard_map/all_to_all | solution.py:406
  109.1 9.6 %collective-permute-start.15 = (f32[4,2,128]{2,1,0:T(2,128)S(1)}, f32[4,2,128]{2,1,0:T(2,128)S(1)}, u32[]{:S(2)}, u32[]{:S(2)}) collective-permute-start(f32[4,2,128]{2,1,0:T(2,128)S(1)} %get-tuple-element.90), channel_id=1, source_target_pairs={{24,32},{0,504},{25,33},{1,505},{26,34},{2,506},{27,35},{3,507},{2... | collective-permute-start | bytes 12296 | tf_op jit(solution)/shard_map/ppermute | solution.py:407
  118.7 4.0 %all-to-all-done.1 = f32[16,1,128]{2,1,0:T(1,128)S(1)} async-done(((f32[16,1,128]{2,1,0:T(1,128)}), f32[16,1,128]{2,1,0:T(1,128)S(1)}, u32[]{:S(2)}, u32[]{:S(2)}) %all-to-all-start.1) | async-done | bytes 8224 | tf_op jit(solution)/shard_map/all_to_all | solution.py:406
  122.7 1.0 copy-done.6
  123.7 1.0 copy-done.9
  124.7 0.9 copy-done.12
  125.7 0.9 copy-done.16
  126.6 0.9 copy-done.20
  127.6 0.9 copy-done.28
  128.5 0.9 copy-done.30
  129.4 0.9 copy-done.34
  130.4 0.9 copy-done.36
  131.4 2.7 %unit_gradient.2 = f32[224,1024]{1,0:T(8,128)} custom-call(s32[4]{0:T(128)S(1)} %pad_add_fusion.ids_ref.refs_0_, f32[16,2,128]{2,1,0:T(2,128)S(1)} %get-tuple-element.104.refs_1_, f32[4,2,128]{2,1,0:T(2,128)S(1)} %collective-permute-done.15.refs_2_, f32[2,128]{1,0:T(2,128)S(1)} %get-tuple-element.91.refs_3_, s32[1,224]{1,0:T(1,128)S(1)} %get-tuple-element.92.refs_4_, ...), custom_call_target="tpu_custom_call" | custom-call | flops 719323136 | bytes 6291456 | tf_op jit(solution)/shard_map/unit_gradient/pallas_call | solution.py:319
  134.1 3.7 %collective-permute-start.16 = (f32[224,1024]{1,0:T(8,128)}, f32[224,1024]{1,0:T(8,128)}, u32[]{:S(2)}, u32[]{:S(2)}) collective-permute-start(f32[224,1024]{1,0:T(8,128)} %unit_gradient.2), channel_id=1, source_target_pairs={{0,1},{1,0},{2,3},{3,2},{4,5},{5,4},{6,7},{7,6},{8,9},{9,8},{10,11... | collective-permute-start | bytes 2752520 | tf_op jit(solution)/shard_map/ppermute | solution.py:410
  137.9 1.0 copy-done.2
  138.9 1.0 copy-done.4
  139.9 1.7 %unit_gradient.3.mine_ref = f32[224,1024]{1,0:T(8,128)S(1)} custom-call(s32[4]{0:T(128)S(1)} %pad_add_fusion.ids_ref.refs_0_, f32[16,2,128]{2,1,0:T(2,128)S(1)} %get-tuple-element.104.refs_1_, f32[4,2,128]{2,1,0:T(2,128)S(1)} %collective-permute-done.15.refs_2_, f32[2,128]{1,0:T(2,128)S(1)} %get-tuple-element.105.refs_3_, ...), custom_call_target="tpu_custom_call" | custom-call | flops 719323136 | bytes 6291456 | tf_op jit(solution)/shard_map/unit_gradient/pallas_call | solution.py:319
  142.9 3.7 %final.1 = f32[224,1024]{1,0:T(8,128)} custom-call(f32[224,1024]{1,0:T(8,128)S(1)} %copy-done, f32[224,1024]{1,0:T(8,128)S(1)} %unit_gradient.3.mine_ref, f32[224,1024]{1,0:T(8,128)} %collective-permute-done.16.got_ref), custom_call_target="tpu_custom_call" | custom-call | flops 2293760 | bytes 3670016 | tf_op jit(solution)/shard_map/final/pallas_call | solution.py:341
  (82 shorter events, 5.5 us)
Async XLA Ops:
  0.6 1.5 copy-start
  2.3 22.4 %copy-start.37 = (s32[224]{0:T(256)S(1)}, s32[224]{0:T(256)}, u32[]{:S(2)}) copy-start(s32[224]{0:T(256)} %param.3) | copy-start | bytes 2692
  2.3 22.4 %collective-permute-start = (bf16[224,1024]{1,0:T(8,128)(2,1)S(1)}, bf16[224,1024]{1,0:T(8,128)(2,1)S(1)}, u32[]{:S(2)}, u32[]{:S(2)}) collective-permute-start(bf16[224,1024]{1,0:T(8,128)(2,1)S(1)} %divide_convert_fusion.unit_ref.refs_1_.refs_12_), channel_id=1, source_target_pairs={{0,1},{1,0},{2,3},{3,2},{4,5},{5,4},{6,7},{7,6},{8,9},{9,8},{10,11... | collective-permute-start | bytes 1376264 | tf_op jit(solution)/shard_map/ppermute | solution.py:367
  11.2 15.3 %collective-permute-start.1 = (bf16[224,1024]{1,0:T(8,128)(2,1)S(1)}, bf16[224,1024]{1,0:T(8,128)(2,1)S(1)}, u32[]{:S(2)}, u32[]{:S(2)}) collective-permute-start(bf16[224,1024]{1,0:T(8,128)(2,1)S(1)} %divide_convert_fusion.unit_ref.refs_1_.refs_12_), channel_id=1, source_target_pairs={{0,4},{1,5},{2,0},{3,1},{4,6},{5,7},{6,2},{7,3},{8,12},{9,13},{10,... | collective-permute-start | bytes 1376264 | tf_op jit(solution)/shard_map/ppermute | solution.py:354
  13.2 22.2 %collective-permute-start.2 = (bf16[224,1024]{1,0:T(8,128)(2,1)S(1)}, bf16[224,1024]{1,0:T(8,128)(2,1)S(1)}, u32[]{:S(2)}, u32[]{:S(2)}) collective-permute-start(bf16[224,1024]{1,0:T(8,128)(2,1)S(1)} %divide_convert_fusion.unit_ref.refs_1_.refs_12_), channel_id=1, source_target_pairs={{126,128},{127,129},{128,126},{129,127},{254,256},{255,257},{256,2... | collective-permute-start | bytes 1376264 | tf_op jit(solution)/shard_map/ppermute | solution.py:354
  35.4 15.4 %collective-permute-start.3 = (bf16[224,1024]{1,0:T(8,128)(2,1)S(1)}, bf16[224,1024]{1,0:T(8,128)(2,1)S(1)}, u32[]{:S(2)}, u32[]{:S(2)}) collective-permute-start(bf16[224,1024]{1,0:T(8,128)(2,1)S(1)} %divide_convert_fusion.unit_ref.refs_1_.refs_12_), channel_id=1, source_target_pairs={{2,6},{3,7},{4,0},{5,1},{0,2},{1,3},{6,4},{7,5},{10,14},{11,15},{1... | collective-permute-start | bytes 1376264 | tf_op jit(solution)/shard_map/ppermute | solution.py:354
  37.3 15.5 %collective-permute-start.6 = (bf16[224,1024]{1,0:T(8,128)(2,1)S(1)}, bf16[224,1024]{1,0:T(8,128)(2,1)S(1)}, u32[]{:S(2)}, u32[]{:S(2)}) collective-permute-start(bf16[224,1024]{1,0:T(8,128)(2,1)S(1)} %collective-permute-done.1.refs_5_.refs_13_), channel_id=1, source_target_pairs={{0,8},{1,9},{2,10},{3,11},{8,16},{9,17},{10,18},{11,19},{12,4},{13... | collective-permute-start | bytes 1376264 | tf_op jit(solution)/shard_map/ppermute | solution.py:354
  38.6 18.6 %collective-permute-start.8 = (bf16[224,1024]{1,0:T(8,128)(2,1)S(1)}, bf16[224,1024]{1,0:T(8,128)(2,1)S(1)}, u32[]{:S(2)}, u32[]{:S(2)}) collective-permute-start(bf16[224,1024]{1,0:T(8,128)(2,1)S(1)} %collective-permute-done.1.refs_5_.refs_13_), channel_id=1, source_target_pairs={{126,128},{127,129},{128,126},{129,127},{254,256},{255,257},{256,2... | collective-permute-start | bytes 1376264 | tf_op jit(solution)/shard_map/ppermute | solution.py:354
  47.1 18.2 %collective-permute-start.7 = (bf16[224,1024]{1,0:T(8,128)(2,1)S(1)}, bf16[224,1024]{1,0:T(8,128)(2,1)S(1)}, u32[]{:S(2)}, u32[]{:S(2)}) collective-permute-start(bf16[224,1024]{1,0:T(8,128)(2,1)S(1)} %collective-permute-done.2.refs_7_), channel_id=1, source_target_pairs={{128,130},{129,131},{126,124},{127,125},{256,258},{257,259},{254,2... | collective-permute-start | bytes 1376264 | tf_op jit(solution)/shard_map/ppermute | solution.py:354
  50.8 17.6 %collective-permute-start.4 = (bf16[224,1024]{1,0:T(8,128)(2,1)S(1)}, bf16[224,1024]{1,0:T(8,128)(2,1)S(1)}, u32[]{:S(2)}, u32[]{:S(2)}) collective-permute-start(bf16[224,1024]{1,0:T(8,128)(2,1)S(1)} %collective-permute-done.1.refs_5_.refs_13_), channel_id=1, source_target_pairs={{4,6},{5,7},{2,0},{3,1},{12,14},{13,15},{10,8},{11,9},{20,22},{21,... | collective-permute-start | bytes 1376264 | tf_op jit(solution)/shard_map/ppermute | solution.py:354
  52.1 16.3 %collective-permute-start.5 = (bf16[224,1024]{1,0:T(8,128)(2,1)S(1)}, bf16[224,1024]{1,0:T(8,128)(2,1)S(1)}, u32[]{:S(2)}, u32[]{:S(2)}) collective-permute-start(bf16[224,1024]{1,0:T(8,128)(2,1)S(1)} %divide_convert_fusion.unit_ref.refs_1_.refs_12_), channel_id=1, source_target_pairs={{2,4},{3,5},{4,2},{5,3},{10,12},{11,13},{12,10},{13,11},{18,20},{1... | collective-permute-start | bytes 1376264 | tf_op jit(solution)/shard_map/ppermute | solution.py:354
  52.8 15.6 %collective-permute-start.10 = (bf16[224,1024]{1,0:T(8,128)(2,1)S(1)}, bf16[224,1024]{1,0:T(8,128)(2,1)S(1)}, u32[]{:S(2)}, u32[]{:S(2)}) collective-permute-start(bf16[224,1024]{1,0:T(8,128)(2,1)S(1)} %collective-permute-done.3.refs_5_.refs_14_), channel_id=1, source_target_pairs={{0,8},{1,9},{4,12},{5,13},{8,16},{9,17},{12,20},{13,21},{10,2},{11... | collective-permute-start | bytes 1376264 | tf_op jit(solution)/shard_map/ppermute | solution.py:354
  57.2 17.6 %collective-permute-start.9 = (bf16[224,1024]{1,0:T(8,128)(2,1)S(1)}, bf16[224,1024]{1,0:T(8,128)(2,1)S(1)}, u32[]{:S(2)}, u32[]{:S(2)}) collective-permute-start(bf16[224,1024]{1,0:T(8,128)(2,1)S(1)} %collective-permute-done.3.refs_5_.refs_14_), channel_id=1, source_target_pairs={{126,128},{127,129},{128,126},{129,127},{254,256},{255,257},{256,2... | collective-permute-start | bytes 1376264 | tf_op jit(solution)/shard_map/ppermute | solution.py:354
  65.3 10.6 %collective-permute-start.11 = (bf16[224,1024]{1,0:T(8,128)(2,1)S(1)}, bf16[224,1024]{1,0:T(8,128)(2,1)S(1)}, u32[]{:S(2)}, u32[]{:S(2)}) collective-permute-start(bf16[224,1024]{1,0:T(8,128)(2,1)S(1)} %collective-permute-done.7.refs_6_), channel_id=1, source_target_pairs={{130,132},{131,133},{124,122},{125,123},{258,260},{259,261},{252,2... | collective-permute-start | bytes 1376264 | tf_op jit(solution)/shard_map/ppermute | solution.py:354
  68.5 9.1 %collective-permute-start.12 = (bf16[224,1024]{1,0:T(8,128)(2,1)S(1)}, bf16[224,1024]{1,0:T(8,128)(2,1)S(1)}, u32[]{:S(2)}, u32[]{:S(2)}) collective-permute-start(bf16[224,1024]{1,0:T(8,128)(2,1)S(1)} %collective-permute-done.4.refs_5_), channel_id=1, source_target_pairs={{0,8},{1,9},{8,16},{9,17},{14,6},{15,7},{16,24},{17,25},{22,14},{2... | collective-permute-start | bytes 1376264 | tf_op jit(solution)/shard_map/ppermute | solution.py:354
  69.8 7.7 %collective-permute-start.13 = (bf16[224,1024]{1,0:T(8,128)(2,1)S(1)}, bf16[224,1024]{1,0:T(8,128)(2,1)S(1)}, u32[]{:S(2)}, u32[]{:S(2)}) collective-permute-start(bf16[224,1024]{1,0:T(8,128)(2,1)S(1)} %collective-permute-done.5.refs_6_), channel_id=1, source_target_pairs={{2,10},{3,11},{10,18},{11,19},{12,4},{13,5},{18,26},{19,27},{20,12... | collective-permute-start | bytes 1376264 | tf_op jit(solution)/shard_map/ppermute | solution.py:354
  70.5 8.9 %collective-permute-start.14 = (bf16[224,1024]{1,0:T(8,128)(2,1)S(1)}, bf16[224,1024]{1,0:T(8,128)(2,1)S(1)}, u32[]{:S(2)}, u32[]{:S(2)}) collective-permute-start(bf16[224,1024]{1,0:T(8,128)(2,1)S(1)} %collective-permute-done.8.refs_6_), channel_id=1, source_target_pairs={{128,130},{129,131},{126,124},{127,125},{256,258},{257,259},{254,2... | collective-permute-start | bytes 1376264 | tf_op jit(solution)/shard_map/ppermute | solution.py:354
  74.1 1.8 %copy-start.21 = (f32[224,224]{1,0:T(8,128)}, f32[224,224]{1,0:T(8,128)S(1)}, u32[]{:S(2)}) copy-start(f32[224,224]{1,0:T(8,128)S(1)} %get-tuple-element.109.refs_8_) | copy-start | bytes 602116
  74.1 48.6 %copy-start.1 = (bf16[224,1024]{1,0:T(8,128)(2,1)}, bf16[224,1024]{1,0:T(8,128)(2,1)S(1)}, u32[]{:S(2)}) copy-start(bf16[224,1024]{1,0:T(8,128)(2,1)S(1)} %get-tuple-element.100.refs_15_) | copy-start | bytes 1376260
  75.9 1.1 copy-start.23
  76.0 1.1 copy-start.29
  76.0 46.7 %copy-start.3 = (bf16[224,1024]{1,0:T(8,128)(2,1)}, bf16[224,1024]{1,0:T(8,128)(2,1)S(1)}, u32[]{:S(2)}) copy-start(bf16[224,1024]{1,0:T(8,128)(2,1)S(1)} %get-tuple-element.101.refs_16_) | copy-start | bytes 1376260
  77.1 3.5 %copy-start.5 = (bf16[224,1024]{1,0:T(8,128)(2,1)}, bf16[224,1024]{1,0:T(8,128)(2,1)S(1)}, u32[]{:S(2)}) copy-start(bf16[224,1024]{1,0:T(8,128)(2,1)S(1)} %get-tuple-element.102.refs_17_) | copy-start | bytes 1376260
  77.1 3.5 %copy-start.25 = (f32[224,224]{1,0:T(8,128)}, f32[224,224]{1,0:T(8,128)S(1)}, u32[]{:S(2)}) copy-start(f32[224,224]{1,0:T(8,128)S(1)} %get-tuple-element.111.refs_10_) | copy-start | bytes 602116
  77.1 3.5 %copy-start.33 = (f32[224,224]{1,0:T(8,128)}, f32[224,224]{1,0:T(8,128)S(1)}, u32[]{:S(2)}) copy-start(f32[224,224]{1,0:T(8,128)S(1)} %get-tuple-element.98.refs_10_) | copy-start | bytes 602116
  81.4 17.4 %copy-start.31 = (f32[224,224]{1,0:T(8,128)}, f32[224,224]{1,0:T(8,128)S(1)}, u32[]{:S(2)}) copy-start(f32[224,224]{1,0:T(8,128)S(1)} %get-tuple-element.112.refs_11_) | copy-start | bytes 602116
  81.4 17.4 %copy-start.35 = (f32[224,224]{1,0:T(8,128)}, f32[224,224]{1,0:T(8,128)S(1)}, u32[]{:S(2)}) copy-start(f32[224,224]{1,0:T(8,128)S(1)} %get-tuple-element.99.refs_11_) | copy-start | bytes 602116
  98.8 23.9 %all-to-all-start.1 = ((f32[16,1,128]{2,1,0:T(1,128)}), f32[16,1,128]{2,1,0:T(1,128)S(1)}, u32[]{:S(2)}, u32[]{:S(2)}) async-start(f32[16,1,128]{2,1,0:T(1,128)} %bitcast.6), calls=%async_computation.1 | async-start | bytes 16384 | tf_op jit(solution)/shard_map/all_to_all | solution.py:406
  109.1 13.6 %collective-permute-start.15 = (f32[4,2,128]{2,1,0:T(2,128)S(1)}, f32[4,2,128]{2,1,0:T(2,128)S(1)}, u32[]{:S(2)}, u32[]{:S(2)}) collective-permute-start(f32[4,2,128]{2,1,0:T(2,128)S(1)} %get-tuple-element.90), channel_id=1, source_target_pairs={{24,32},{0,504},{25,33},{1,505},{26,34},{2,506},{27,35},{3,507},{2... | collective-permute-start | bytes 12296 | tf_op jit(solution)/shard_map/ppermute | solution.py:407
  122.7 1.0 copy-start.6
  123.7 1.0 copy-start.9
  124.7 0.9 copy-start.12
  125.7 0.9 copy-start.16
  126.6 0.9 copy-start.20
  127.6 0.9 copy-start.28
  128.5 0.9 copy-start.30
  129.4 0.9 copy-start.34
  131.3 6.5 %copy-start.7 = (bf16[224,1024]{1,0:T(8,128)(2,1)S(1)}, bf16[224,1024]{1,0:T(8,128)(2,1)}, u32[]{:S(2)}) copy-start(bf16[224,1024]{1,0:T(8,128)(2,1)} %copy-done.5) | copy-start | bytes 1376260
  131.3 6.5 %copy-start.10 = (bf16[224,1024]{1,0:T(8,128)(2,1)S(1)}, bf16[224,1024]{1,0:T(8,128)(2,1)}, u32[]{:S(2)}) copy-start(bf16[224,1024]{1,0:T(8,128)(2,1)} %copy-done.8) | copy-start | bytes 1376260
  131.3 6.5 %copy-start.14 = (f32[224,224]{1,0:T(8,128)S(1)}, f32[224,224]{1,0:T(8,128)}, u32[]{:S(2)}) copy-start(f32[224,224]{1,0:T(8,128)} %copy-done.13) | copy-start | bytes 602116
  131.3 6.5 %copy-start.18 = (f32[224,224]{1,0:T(8,128)S(1)}, f32[224,224]{1,0:T(8,128)}, u32[]{:S(2)}) copy-start(f32[224,224]{1,0:T(8,128)} %copy-done.17) | copy-start | bytes 602116
  131.3 6.5 %copy-start.22 = (f32[224,224]{1,0:T(8,128)S(1)}, f32[224,224]{1,0:T(8,128)}, u32[]{:S(2)}) copy-start(f32[224,224]{1,0:T(8,128)} %copy-done.21) | copy-start | bytes 602116
  131.3 6.5 %copy-start.24 = (f32[224,224]{1,0:T(8,128)S(1)}, f32[224,224]{1,0:T(8,128)}, u32[]{:S(2)}) copy-start(f32[224,224]{1,0:T(8,128)} %copy-done.23) | copy-start | bytes 602116
  131.3 6.5 %copy-start.26 = (f32[224,224]{1,0:T(8,128)S(1)}, f32[224,224]{1,0:T(8,128)}, u32[]{:S(2)}) copy-start(f32[224,224]{1,0:T(8,128)} %copy-done.25) | copy-start | bytes 602116
  131.4 6.5 %copy-start.32 = (f32[224,224]{1,0:T(8,128)S(1)}, f32[224,224]{1,0:T(8,128)}, u32[]{:S(2)}) copy-start(f32[224,224]{1,0:T(8,128)} %copy-done.31) | copy-start | bytes 602116
  134.1 8.9 %collective-permute-start.16 = (f32[224,1024]{1,0:T(8,128)}, f32[224,1024]{1,0:T(8,128)}, u32[]{:S(2)}, u32[]{:S(2)}) collective-permute-start(f32[224,1024]{1,0:T(8,128)} %unit_gradient.2), channel_id=1, source_target_pairs={{0,1},{1,0},{2,3},{3,2},{4,5},{5,4},{6,7},{7,6},{8,9},{9,8},{10,11... | collective-permute-start | bytes 2752520 | tf_op jit(solution)/shard_map/ppermute | solution.py:410
  137.9 1.0 copy-start.2
  138.9 1.0 copy-start.4
  (8 other events, 5.8 us)

commit v4 on v3

--- a/solution.py
+++ b/solution.py
@@ -63,18 +63,6 @@
 ROUTES = routes()
 
 
-def edge_routes():
-    pairs = []
-    for group in range(16):
-        for inner in range(8):
-            pairs.append((group * 32 + 24 + inner, ((group + 1) % 16) * 32 + inner))
-            pairs.append((group * 32 + inner, ((group - 1) % 16) * 32 + 24 + inner))
-    return pairs
-
-
-EDGE = edge_routes()
-
-
 def after(value, *others):
     return lax.optimization_barrier((value,) + others)[0]
 
@@ -241,8 +229,8 @@
     return out[:2], out[2:4], block
 
 
-def denom_kernel(ids_ref, pay_ref, inv_ref, mine_ref, other_ref, edge_ref, loss_ref):
-    y, k, core = ids_ref[0], ids_ref[1], ids_ref[2]
+def denom_kernel(ids_ref, pay_ref, inv_ref, mine_ref, other_ref, post_ref):
+    y, k, core, group = ids_ref[0], ids_ref[1], ids_ref[2], ids_ref[3] // 4
     pay = pay_ref[...].reshape(16, 2, 8, 128)
     lane = lax.broadcasted_iota(jnp.int32, (16, 2, 128), 2)
     part = lax.broadcasted_iota(jnp.int32, (16, 2, 128), 1)
@@ -252,15 +240,18 @@
     total = jnp.log(first) + jnp.log(second)
     total = jnp.sum(total.reshape(32, 128), axis=0, keepdims=True)
     total = total - jnp.sum(pay[:, :, 4].reshape(32, 128), axis=0, keepdims=True)
-    loss_ref[...] = jnp.broadcast_to(jnp.sum(total, axis=1, keepdims=True), (16, 128))
+    total = jnp.sum(total, axis=1, keepdims=True)
     first, second = 1.0 / first, 1.0 / second
-    inv_ref[...] = jnp.where(core == 0, first, second)
+    inv = jnp.where(core == 0, first, second)
     other_all = jnp.where(core == 0, second, first)
-    chip = lax.broadcasted_iota(jnp.int32, (16, 2, 128), 0)
-    here = chip == y * 4 + k
-    mine_ref[...] = jnp.sum(jnp.where(here, inv_ref[...], 0.0), axis=0)
+    inv_ref[...] = inv
+    here = lax.broadcasted_iota(jnp.int32, (16, 2, 128), 0) == y * 4 + k
+    mine_ref[...] = jnp.sum(jnp.where(here, inv, 0.0), axis=0)
     other_ref[...] = jnp.sum(jnp.where(here, other_all, 0.0), axis=0)
-    edge_ref[...] = inv_ref[pl.ds(jnp.where(y == 3, 12, 0), 4)]
+    low = jnp.where(real[:4], inv[:4], total)
+    high = jnp.where(real[:4], inv[12:], total)
+    post_ref[...] = jnp.broadcast_to(low[None], (16, 4, 2, 128))
+    post_ref[pl.ds((group + 1) % 16, 1)] = high[None]
 
 
 def denom_call(ids, pay):
@@ -271,11 +262,10 @@
             jax.ShapeDtypeStruct((16, 2, 128), f32),
             jax.ShapeDtypeStruct((2, 128), f32),
             jax.ShapeDtypeStruct((2, 128), f32),
-            jax.ShapeDtypeStruct((4, 2, 128), f32),
-            jax.ShapeDtypeStruct((16, 128), f32),
+            jax.ShapeDtypeStruct((16, 4, 2, 128), f32),
         ),
         in_specs=smem(1) + vmem(1),
-        out_specs=tuple(vmem(5)),
+        out_specs=tuple(vmem(4)),
         compiler_params=PARAMS,
         name="denoms",
     )(ids, pay)
@@ -292,7 +282,8 @@
     mine = lanes(row_ref[...])
     mine = jnp.transpose(jnp.broadcast_to(mine, (128, ROWS)))[:, 0:1]
     total = None
-    y, k = ids_ref[0], ids_ref[1]
+    y, k, group = ids_ref[0], ids_ref[1], ids_ref[3] // 4
+    beside = jnp.where(y == 0, group + 15, group + 1) % 16
     for number in range(7):
         chip, line = k, y
         if number:
@@ -301,7 +292,7 @@
             line = y + jnp.where(chip < k, 1, -1)
         inside = inv_ref[pl.ds(jnp.clip(line, 0, 3) * 4 + chip, 1)]
         if number > 3:
-            inside = jnp.where((line < 0) | (line > 3), edge_ref[pl.ds(chip, 1)], inside)
+            inside = jnp.where((line < 0) | (line > 3), edge_ref[pl.ds(beside, 1), pl.ds(chip, 1)][0], inside)
         column = lanes(inside[0])
         weight = expos[number][...] * (mine + column)
         if number == 0:
@@ -378,7 +369,7 @@
             return rest
         sums = rest
 
-    r1 = after(r1, x1, sums[0])
+    r1 = after(r1, x1)
     r2 = send(after(unit, r1), "P2")
     y1 = send(r1, "Y1")
     x2 = send(after(x1, r1), "X2")
@@ -402,16 +393,14 @@
     pay = add(5, [y3a, y3b, x1, x5])
 
     pays = lax.all_to_all(jnp.broadcast_to(pay[None], (32, 8, 128)), DEV_AXES, 0, 0)
-    inv, mine_inv, other_inv, edge, loss = denom_call(ids, pays)
-    losses = lax.all_to_all(loss, ("zh", "x"), 0, 0)
-    edge = lax.ppermute(edge, AXES, EDGE)
-    inv = after(inv, losses)
-    for_other = grad_call(ROWS, ids, inv, edge, other_inv, local, [e[1] for e in expos], blocks)
+    inv, mine_inv, other_inv, post = denom_call(ids, pays)
+    posts = lax.all_to_all(post, ("zh", "x"), 0, 0)
+    for_other = grad_call(ROWS, ids, inv, posts, other_inv, local, [e[1] for e in expos], blocks)
     got = lax.ppermute(for_other, ("core",), [(0, 1), (1, 0)])
-    mine = grad_call(0, ids, after(inv, for_other), edge, mine_inv, local, [e[0] for e in expos], blocks)
+    mine = grad_call(0, ids, after(inv, for_other), posts, mine_inv, local, [e[0] for e in expos], blocks)
     grad = final_call(embeddings, mine, got)
-    losses = after(losses, mine)
-    loss = jnp.sum(losses[:, 0]) / (ROWS * 512) + 1.0 / SOFTMAX_TEMPER
+    total = jnp.sum(after(posts, mine)[:, 0, 1, 127])
+    loss = total / (ROWS * 512) + 1.0 / SOFTMAX_TEMPER
     return (loss, grad)
 
 

time: 149 us -> 131 us (0.88)
  blocking collectives: 16.1 us -> 40.3 us
  starting transfers between devices: 75 us -> 56.8 us
  local copies, waits for them, and re-layouts: 15.6 us -> 0.05 us
  waiting for transfers between devices: 18.9 us -> 12.1 us
    all_to_all x0 -> x1, blocking collectives: none -> 23.4 us  [per_device(): posts = lax.all_to_all(post, ('zh', 'x'), 0, 0)]
    unnamed x76 -> x4, local copies, waits for them, and re-layouts: 15.6 us -> 0.04 us
    all_to_all x1 -> x0, starting transfers between devices: 10.3 us -> none  [per_device(): losses = lax.all_to_all(loss, ('zh', 'x'), 0, 0)]
    ppermute x1 -> x0, starting transfers between devices: 9.64 us -> none  [per_device(): edge = lax.ppermute(edge, AXES, EDGE)]
    ppermute x14, starting transfers between devices: 42.5 us -> 49.8 us  [send(): return lax.ppermute(value, AXES, ROUTES[name])]
    ppermute x1, starting transfers between devices: 8.91 us -> 3.27 us  [per_device(): other = lax.ppermute(after(unit, ids), ('core',), [(0, 1), (1, 0)])]
    all_to_all x1 -> x0, waiting for transfers between devices: 3.97 us -> none  [per_device(): losses = lax.all_to_all(loss, ('zh', 'x'), 0, 0)]
    ppermute x14, waiting for transfers between devices: 14.9 us -> 12.1 us  [send(): return lax.ppermute(value, AXES, ROUTES[name])]
  transfers between devices with their start and end apart: 18 -> 16, of which waited for: 6 -> 4; matrix products, arithmetic and copies ran while one was open for 0% -> 1% of each run, Pallas kernels for 5% -> 6%
where the time goes in v4:
time: 131 us
  starting transfers between devices  56.8 us (43%)
  blocking collectives  40.3 us (31%)
  Pallas kernels  16.3 us (12%)
  waiting for transfers between devices  12.1 us (9%)
  between operations  2.74 us (2%)
  other arithmetic  2.31 us (2%)
    ppermute x14, starting transfers between devices, send(): return lax.ppermute(value, AXES, ROUTES[name])  49.8 us
    all_to_all x1, blocking collectives, per_device(): posts = lax.all_to_all(post, ('zh', 'x'), 0, 0)  23.4 us
    all_to_all x1, blocking collectives, per_device(): lax.all_to_all(jnp.broadcast_to(pay[None], (32, 8, 128)), DEV_AXES, 0, 0)  16.9 us
    ppermute x14, waiting for transfers between devices, send(): return lax.ppermute(value, AXES, ROUTES[name])  12.1 us
    pallas_call x6, Pallas kernels, block_call(): pl.pallas_call(kernel, out_shape=tuple(shapes), in_specs=smem(1) + vmem(l...  6.45 us
    pallas_call x2, Pallas kernels, grad_call(): pl.pallas_call(kernel, out_shape=jax.ShapeDtypeStruct((ROWS, WIDTH), jnp....  4.42 us
    pallas_call x1, Pallas kernels, final_call(): pl.pallas_call(final_kernel, out_shape=jax.ShapeDtypeStruct((ROWS, WIDTH)...  3.73 us
    ppermute x1, starting transfers between devices, per_device(): got = lax.ppermute(for_other, ('core',), [(0, 1), (1, 0)])  3.7 us
  transfers between devices with their start and end apart: 16, of which 4 were waited for; matrix products, arithmetic and copies ran while one was open for 1% of the time, Pallas kernels for 6%

profile of v4, /device:TPU:1, one launch (start us, length us, event | category | flops | bytes accessed | tf_op | source)
XLA Modules:
  0.0 130.6 jit_solution(829419435971776278)
XLA Ops:
  0.6 1.4 %multiply_reduce_fusion = f32[224]{0:T(256)S(1)} fusion(f32[224,1024]{1,0:T(8,128)} %emb_ref.1), kind=kLoop, calls=%fused_computation.1 | loop fusion | flops 458528 | bytes 918400 | tf_op jit(solution)/shard_map/reduce_sum | solution.py:349
  2.0 0.0 copy-done
  2.1 0.1 divide_convert_fusion.unit_ref.refs_1_.refs_12_
  2.2 5.7 %collective-permute-start.1 = (bf16[224,1024]{1,0:T(8,128)(2,1)S(1)}, bf16[224,1024]{1,0:T(8,128)(2,1)S(1)}, u32[]{:S(2)}, u32[]{:S(2)}) collective-permute-start(bf16[224,1024]{1,0:T(8,128)(2,1)S(1)} %divide_convert_fusion.unit_ref.refs_1_.refs_12_), channel_id=1, source_target_pairs={{0,4},{1,5},{2,0},{3,1},{4,6},{5,7},{6,2},{7,3},{8,12},{9,13},{10,... | collective-permute-start | bytes 1376264 | tf_op jit(solution)/shard_map/ppermute | solution.py:345
  8.0 13.9 %collective-permute-start.2 = (bf16[224,1024]{1,0:T(8,128)(2,1)S(1)}, bf16[224,1024]{1,0:T(8,128)(2,1)S(1)}, u32[]{:S(2)}, u32[]{:S(2)}) collective-permute-start(bf16[224,1024]{1,0:T(8,128)(2,1)S(1)} %divide_convert_fusion.unit_ref.refs_1_.refs_12_), channel_id=1, source_target_pairs={{126,128},{127,129},{128,126},{129,127},{254,256},{255,257},{256,2... | collective-permute-start | bytes 1376264 | tf_op jit(solution)/shard_map/ppermute | solution.py:345
  21.9 0.1 pad_add_fusion.ids_ref.refs_0_
  22.0 3.3 %collective-permute-start = (bf16[224,1024]{1,0:T(8,128)(2,1)S(1)}, bf16[224,1024]{1,0:T(8,128)(2,1)S(1)}, u32[]{:S(2)}, u32[]{:S(2)}) collective-permute-start(bf16[224,1024]{1,0:T(8,128)(2,1)S(1)} %divide_convert_fusion.unit_ref.refs_1_.refs_12_), channel_id=1, source_target_pairs={{0,1},{1,0},{2,3},{3,2},{4,5},{5,4},{6,7},{7,6},{8,9},{9,8},{10,11... | collective-permute-start | bytes 1376264 | tf_op jit(solution)/shard_map/ppermute | solution.py:358
  25.3 0.0 collective-permute-done.1.refs_5_.refs_13_
  25.3 6.5 %collective-permute-done.2.refs_7_ = bf16[224,1024]{1,0:T(8,128)(2,1)S(1)} collective-permute-done((bf16[224,1024]{1,0:T(8,128)(2,1)S(1)}, bf16[224,1024]{1,0:T(8,128)(2,1)S(1)}, u32[]{:S(2)}, u32[]{:S(2)}) %collective-permute-start.2) | collective-permute-done | bytes 458784 | tf_op jit(solution)/shard_map/ppermute | solution.py:345
  31.8 1.9 %collective-permute-start.3 = (bf16[224,1024]{1,0:T(8,128)(2,1)S(1)}, bf16[224,1024]{1,0:T(8,128)(2,1)S(1)}, u32[]{:S(2)}, u32[]{:S(2)}) collective-permute-start(bf16[224,1024]{1,0:T(8,128)(2,1)S(1)} %divide_convert_fusion.unit_ref.refs_1_.refs_12_), channel_id=1, source_target_pairs={{2,6},{3,7},{4,0},{5,1},{0,2},{1,3},{6,4},{7,5},{10,14},{11,15},{1... | collective-permute-start | bytes 1376264 | tf_op jit(solution)/shard_map/ppermute | solution.py:345
  33.7 1.3 %collective-permute-start.6 = (bf16[224,1024]{1,0:T(8,128)(2,1)S(1)}, bf16[224,1024]{1,0:T(8,128)(2,1)S(1)}, u32[]{:S(2)}, u32[]{:S(2)}) collective-permute-start(bf16[224,1024]{1,0:T(8,128)(2,1)S(1)} %collective-permute-done.1.refs_5_.refs_13_), channel_id=1, source_target_pairs={{0,8},{1,9},{2,10},{3,11},{8,16},{9,17},{10,18},{11,19},{12,4},{13... | collective-permute-start | bytes 1376264 | tf_op jit(solution)/shard_map/ppermute | solution.py:345
  35.1 8.5 %collective-permute-start.8 = (bf16[224,1024]{1,0:T(8,128)(2,1)S(1)}, bf16[224,1024]{1,0:T(8,128)(2,1)S(1)}, u32[]{:S(2)}, u32[]{:S(2)}) collective-permute-start(bf16[224,1024]{1,0:T(8,128)(2,1)S(1)} %collective-permute-done.1.refs_5_.refs_13_), channel_id=1, source_target_pairs={{126,128},{127,129},{128,126},{129,127},{254,256},{255,257},{256,2... | collective-permute-start | bytes 1376264 | tf_op jit(solution)/shard_map/ppermute | solution.py:345
  43.6 1.3 %collective-permute-start.7 = (bf16[224,1024]{1,0:T(8,128)(2,1)S(1)}, bf16[224,1024]{1,0:T(8,128)(2,1)S(1)}, u32[]{:S(2)}, u32[]{:S(2)}) collective-permute-start(bf16[224,1024]{1,0:T(8,128)(2,1)S(1)} %collective-permute-done.2.refs_7_), channel_id=1, source_target_pairs={{128,130},{129,131},{126,124},{127,125},{256,258},{257,259},{254,2... | collective-permute-start | bytes 1376264 | tf_op jit(solution)/shard_map/ppermute | solution.py:345
  44.9 0.0 collective-permute-done.other_ref.refs_2_
  44.9 1.1 own_scores.1
  46.0 1.0 block_scores.6
  47.0 0.0 collective-permute-done.3.refs_5_.refs_14_
  47.0 1.3 collective-permute-start.4
  48.3 0.7 collective-permute-start.5
  49.0 1.3 %collective-permute-start.10 = (bf16[224,1024]{1,0:T(8,128)(2,1)S(1)}, bf16[224,1024]{1,0:T(8,128)(2,1)S(1)}, u32[]{:S(2)}, u32[]{:S(2)}) collective-permute-start(bf16[224,1024]{1,0:T(8,128)(2,1)S(1)} %collective-permute-done.3.refs_5_.refs_14_), channel_id=1, source_target_pairs={{0,8},{1,9},{4,12},{5,13},{8,16},{9,17},{12,20},{13,21},{10,2},{11... | collective-permute-start | bytes 1376264 | tf_op jit(solution)/shard_map/ppermute | solution.py:345
  50.3 2.5 %collective-permute-done.8.refs_6_ = bf16[224,1024]{1,0:T(8,128)(2,1)S(1)} collective-permute-done((bf16[224,1024]{1,0:T(8,128)(2,1)S(1)}, bf16[224,1024]{1,0:T(8,128)(2,1)S(1)}, u32[]{:S(2)}, u32[]{:S(2)}) %collective-permute-start.8) | collective-permute-done | bytes 458784 | tf_op jit(solution)/shard_map/ppermute | solution.py:345
  52.9 8.1 %collective-permute-start.9 = (bf16[224,1024]{1,0:T(8,128)(2,1)S(1)}, bf16[224,1024]{1,0:T(8,128)(2,1)S(1)}, u32[]{:S(2)}, u32[]{:S(2)}) collective-permute-start(bf16[224,1024]{1,0:T(8,128)(2,1)S(1)} %collective-permute-done.3.refs_5_.refs_14_), channel_id=1, source_target_pairs={{126,128},{127,129},{128,126},{129,127},{254,256},{255,257},{256,2... | collective-permute-start | bytes 1376264 | tf_op jit(solution)/shard_map/ppermute | solution.py:345
  61.0 0.0 collective-permute-done.7.refs_6_
  61.0 0.7 collective-permute-start.11
  61.7 1.0 block_scores.7
  62.7 0.0 collective-permute-done.4.refs_5_
  62.8 0.0 collective-permute-done.10.refs_5_
  62.8 1.3 %collective-permute-start.12 = (bf16[224,1024]{1,0:T(8,128)(2,1)S(1)}, bf16[224,1024]{1,0:T(8,128)(2,1)S(1)}, u32[]{:S(2)}, u32[]{:S(2)}) collective-permute-start(bf16[224,1024]{1,0:T(8,128)(2,1)S(1)} %collective-permute-done.4.refs_5_), channel_id=1, source_target_pairs={{0,8},{1,9},{8,16},{9,17},{14,6},{15,7},{16,24},{17,25},{22,14},{2... | collective-permute-start | bytes 1376264 | tf_op jit(solution)/shard_map/ppermute | solution.py:345
  64.1 0.7 collective-permute-start.13
  64.8 3.0 %collective-permute-start.14 = (bf16[224,1024]{1,0:T(8,128)(2,1)S(1)}, bf16[224,1024]{1,0:T(8,128)(2,1)S(1)}, u32[]{:S(2)}, u32[]{:S(2)}) collective-permute-start(bf16[224,1024]{1,0:T(8,128)(2,1)S(1)} %collective-permute-done.8.refs_6_), channel_id=1, source_target_pairs={{128,130},{129,131},{126,124},{127,125},{256,258},{257,259},{254,2... | collective-permute-start | bytes 1376264 | tf_op jit(solution)/shard_map/ppermute | solution.py:345
  67.8 1.1 block_scores.8
  68.8 0.9 collective-permute-done.9.refs_7_
  69.7 1.1 block_scores.9
  70.8 0.0 collective-permute-done.11.refs_7_
  70.8 1.1 block_scores.10
  71.9 0.0 collective-permute-done.12.refs_5_
  71.9 0.0 collective-permute-done.13.refs_6_
  71.9 2.1 %collective-permute-done.14.refs_8_ = bf16[224,1024]{1,0:T(8,128)(2,1)S(1)} collective-permute-done((bf16[224,1024]{1,0:T(8,128)(2,1)S(1)}, bf16[224,1024]{1,0:T(8,128)(2,1)S(1)}, u32[]{:S(2)}, u32[]{:S(2)}) %collective-permute-start.14) | collective-permute-done | bytes 458784 | tf_op jit(solution)/shard_map/ppermute | solution.py:345
  74.0 1.2 block_scores.11
  75.2 16.9 %all_to_all.10.pay_ref = f32[32,8,128]{2,1,0:T(8,128)S(1)} all-to-all(f32[32,8,128]{2,1,0:T(8,128)S(1)} %broadcast_in_dim.2), channel_id=1, replica_groups=mesh['zh'=4,'x'=4,'y'=4,'zl'=4,'core'=2] {'y','zl','core'}, dimensions={0} | all-to-all | bytes 262144 | tf_op jit(solution)/shard_map/all_to_all | solution.py:395
  92.1 0.7 denoms.1
  92.8 23.4 %all_to_all.11.refs_2_ = f32[16,4,2,128]{3,2,1,0:T(2,128)S(1)} all-to-all(f32[16,4,2,128]{3,2,1,0:T(2,128)S(1)} %get-tuple-element.85), channel_id=1, replica_groups=mesh['zh'=4,'x'=4,'y'=4,'zl'=4,'core'=2] {'zh','x'}, dimensions={0} | all-to-all | bytes 131072 | tf_op jit(solution)/shard_map/all_to_all | solution.py:397
  116.2 2.7 %unit_gradient.2 = f32[224,1024]{1,0:T(8,128)} custom-call(s32[4]{0:T(128)S(1)} %pad_add_fusion.ids_ref.refs_0_, f32[16,2,128]{2,1,0:T(2,128)S(1)} %get-tuple-element.100.refs_1_, f32[16,4,2,128]{3,2,1,0:T(2,128)S(1)} %all_to_all.11.refs_2_, f32[2,128]{1,0:T(2,128)S(1)} %get-tuple-element.87.refs_3_, s32[1,224]{1,0:T(1,128)S(1)} %get-tuple-element.88.refs_4_, ...), custom_call_target="tpu_custom_call" | custom-call | flops 719323136 | bytes 6291456 | tf_op jit(solution)/shard_map/unit_gradient/pallas_call | solution.py:310
  118.9 3.7 %collective-permute-start.15 = (f32[224,1024]{1,0:T(8,128)}, f32[224,1024]{1,0:T(8,128)}, u32[]{:S(2)}, u32[]{:S(2)}) collective-permute-start(f32[224,1024]{1,0:T(8,128)} %unit_gradient.2), channel_id=1, source_target_pairs={{0,1},{1,0},{2,3},{3,2},{4,5},{5,4},{6,7},{7,6},{8,9},{9,8},{10,11... | collective-permute-start | bytes 2752520 | tf_op jit(solution)/shard_map/ppermute | solution.py:399
  122.6 1.8 %unit_gradient.3.mine_ref = f32[224,1024]{1,0:T(8,128)S(1)} custom-call(s32[4]{0:T(128)S(1)} %pad_add_fusion.ids_ref.refs_0_, f32[16,2,128]{2,1,0:T(2,128)S(1)} %get-tuple-element.100.refs_1_, f32[16,4,2,128]{3,2,1,0:T(2,128)S(1)} %all_to_all.11.refs_2_, f32[2,128]{1,0:T(2,128)S(1)} %get-tuple-element.101.refs_3_, s32[1,224]{1,0:T(1,128)S(1)} %get-tuple-element.88.refs_4_, ...), custom_call_target="tpu_custom_call" | custom-call | flops 719323136 | bytes 6291456 | tf_op jit(solution)/shard_map/unit_gradient/pallas_call | solution.py:310
  124.4 0.7 slice_reduce_fusion
  125.7 0.0 collective-permute-done.15.got_ref
  125.7 3.7 %final.1 = f32[224,1024]{1,0:T(8,128)} custom-call(f32[224,1024]{1,0:T(8,128)S(1)} %copy-done, f32[224,1024]{1,0:T(8,128)S(1)} %unit_gradient.3.mine_ref, f32[224,1024]{1,0:T(8,128)} %collective-permute-done.15.got_ref), custom_call_target="tpu_custom_call" | custom-call | flops 2293760 | bytes 3670016 | tf_op jit(solution)/shard_map/final/pallas_call | solution.py:332
  (7 shorter events, 0.0 us)
Async XLA Ops:
  0.6 1.5 %copy-start = (f32[224,1024]{1,0:T(8,128)S(1)}, f32[224,1024]{1,0:T(8,128)}, u32[]{:S(2)}) copy-start(f32[224,1024]{1,0:T(8,128)} %emb_ref.1) | copy-start | bytes 2752516
  2.2 23.1 %collective-permute-start.1 = (bf16[224,1024]{1,0:T(8,128)(2,1)S(1)}, bf16[224,1024]{1,0:T(8,128)(2,1)S(1)}, u32[]{:S(2)}, u32[]{:S(2)}) collective-permute-start(bf16[224,1024]{1,0:T(8,128)(2,1)S(1)} %divide_convert_fusion.unit_ref.refs_1_.refs_12_), channel_id=1, source_target_pairs={{0,4},{1,5},{2,0},{3,1},{4,6},{5,7},{6,2},{7,3},{8,12},{9,13},{10,... | collective-permute-start | bytes 1376264 | tf_op jit(solution)/shard_map/ppermute | solution.py:345
  8.0 23.9 %collective-permute-start.2 = (bf16[224,1024]{1,0:T(8,128)(2,1)S(1)}, bf16[224,1024]{1,0:T(8,128)(2,1)S(1)}, u32[]{:S(2)}, u32[]{:S(2)}) collective-permute-start(bf16[224,1024]{1,0:T(8,128)(2,1)S(1)} %divide_convert_fusion.unit_ref.refs_1_.refs_12_), channel_id=1, source_target_pairs={{126,128},{127,129},{128,126},{129,127},{254,256},{255,257},{256,2... | collective-permute-start | bytes 1376264 | tf_op jit(solution)/shard_map/ppermute | solution.py:345
  22.0 22.9 %copy-start.1 = (s32[224]{0:T(256)S(1)}, s32[224]{0:T(256)}, u32[]{:S(2)}) copy-start(s32[224]{0:T(256)} %param.3) | copy-start | bytes 2692
  22.0 22.9 %collective-permute-start = (bf16[224,1024]{1,0:T(8,128)(2,1)S(1)}, bf16[224,1024]{1,0:T(8,128)(2,1)S(1)}, u32[]{:S(2)}, u32[]{:S(2)}) collective-permute-start(bf16[224,1024]{1,0:T(8,128)(2,1)S(1)} %divide_convert_fusion.unit_ref.refs_1_.refs_12_), channel_id=1, source_target_pairs={{0,1},{1,0},{2,3},{3,2},{4,5},{5,4},{6,7},{7,6},{8,9},{9,8},{10,11... | collective-permute-start | bytes 1376264 | tf_op jit(solution)/shard_map/ppermute | solution.py:358
  31.8 15.2 %collective-permute-start.3 = (bf16[224,1024]{1,0:T(8,128)(2,1)S(1)}, bf16[224,1024]{1,0:T(8,128)(2,1)S(1)}, u32[]{:S(2)}, u32[]{:S(2)}) collective-permute-start(bf16[224,1024]{1,0:T(8,128)(2,1)S(1)} %divide_convert_fusion.unit_ref.refs_1_.refs_12_), channel_id=1, source_target_pairs={{2,6},{3,7},{4,0},{5,1},{0,2},{1,3},{6,4},{7,5},{10,14},{11,15},{1... | collective-permute-start | bytes 1376264 | tf_op jit(solution)/shard_map/ppermute | solution.py:345
  33.7 15.2 %collective-permute-start.6 = (bf16[224,1024]{1,0:T(8,128)(2,1)S(1)}, bf16[224,1024]{1,0:T(8,128)(2,1)S(1)}, u32[]{:S(2)}, u32[]{:S(2)}) collective-permute-start(bf16[224,1024]{1,0:T(8,128)(2,1)S(1)} %collective-permute-done.1.refs_5_.refs_13_), channel_id=1, source_target_pairs={{0,8},{1,9},{2,10},{3,11},{8,16},{9,17},{10,18},{11,19},{12,4},{13... | collective-permute-start | bytes 1376264 | tf_op jit(solution)/shard_map/ppermute | solution.py:345
  35.1 17.8 %collective-permute-start.8 = (bf16[224,1024]{1,0:T(8,128)(2,1)S(1)}, bf16[224,1024]{1,0:T(8,128)(2,1)S(1)}, u32[]{:S(2)}, u32[]{:S(2)}) collective-permute-start(bf16[224,1024]{1,0:T(8,128)(2,1)S(1)} %collective-permute-done.1.refs_5_.refs_13_), channel_id=1, source_target_pairs={{126,128},{127,129},{128,126},{129,127},{254,256},{255,257},{256,2... | collective-permute-start | bytes 1376264 | tf_op jit(solution)/shard_map/ppermute | solution.py:345
  43.6 17.5 %collective-permute-start.7 = (bf16[224,1024]{1,0:T(8,128)(2,1)S(1)}, bf16[224,1024]{1,0:T(8,128)(2,1)S(1)}, u32[]{:S(2)}, u32[]{:S(2)}) collective-permute-start(bf16[224,1024]{1,0:T(8,128)(2,1)S(1)} %collective-permute-done.2.refs_7_), channel_id=1, source_target_pairs={{128,130},{129,131},{126,124},{127,125},{256,258},{257,259},{254,2... | collective-permute-start | bytes 1376264 | tf_op jit(solution)/shard_map/ppermute | solution.py:345
  47.0 15.8 %collective-permute-start.4 = (bf16[224,1024]{1,0:T(8,128)(2,1)S(1)}, bf16[224,1024]{1,0:T(8,128)(2,1)S(1)}, u32[]{:S(2)}, u32[]{:S(2)}) collective-permute-start(bf16[224,1024]{1,0:T(8,128)(2,1)S(1)} %collective-permute-done.1.refs_5_.refs_13_), channel_id=1, source_target_pairs={{4,6},{5,7},{2,0},{3,1},{12,14},{13,15},{10,8},{11,9},{20,22},{21,... | collective-permute-start | bytes 1376264 | tf_op jit(solution)/shard_map/ppermute | solution.py:345
  48.3 14.5 %collective-permute-start.5 = (bf16[224,1024]{1,0:T(8,128)(2,1)S(1)}, bf16[224,1024]{1,0:T(8,128)(2,1)S(1)}, u32[]{:S(2)}, u32[]{:S(2)}) collective-permute-start(bf16[224,1024]{1,0:T(8,128)(2,1)S(1)} %divide_convert_fusion.unit_ref.refs_1_.refs_12_), channel_id=1, source_target_pairs={{2,4},{3,5},{4,2},{5,3},{10,12},{11,13},{12,10},{13,11},{18,20},{1... | collective-permute-start | bytes 1376264 | tf_op jit(solution)/shard_map/ppermute | solution.py:345
  49.0 13.8 %collective-permute-start.10 = (bf16[224,1024]{1,0:T(8,128)(2,1)S(1)}, bf16[224,1024]{1,0:T(8,128)(2,1)S(1)}, u32[]{:S(2)}, u32[]{:S(2)}) collective-permute-start(bf16[224,1024]{1,0:T(8,128)(2,1)S(1)} %collective-permute-done.3.refs_5_.refs_14_), channel_id=1, source_target_pairs={{0,8},{1,9},{4,12},{5,13},{8,16},{9,17},{12,20},{13,21},{10,2},{11... | collective-permute-start | bytes 1376264 | tf_op jit(solution)/shard_map/ppermute | solution.py:345
  52.9 16.9 %collective-permute-start.9 = (bf16[224,1024]{1,0:T(8,128)(2,1)S(1)}, bf16[224,1024]{1,0:T(8,128)(2,1)S(1)}, u32[]{:S(2)}, u32[]{:S(2)}) collective-permute-start(bf16[224,1024]{1,0:T(8,128)(2,1)S(1)} %collective-permute-done.3.refs_5_.refs_14_), channel_id=1, source_target_pairs={{126,128},{127,129},{128,126},{129,127},{254,256},{255,257},{256,2... | collective-permute-start | bytes 1376264 | tf_op jit(solution)/shard_map/ppermute | solution.py:345
  61.0 9.8 %collective-permute-start.11 = (bf16[224,1024]{1,0:T(8,128)(2,1)S(1)}, bf16[224,1024]{1,0:T(8,128)(2,1)S(1)}, u32[]{:S(2)}, u32[]{:S(2)}) collective-permute-start(bf16[224,1024]{1,0:T(8,128)(2,1)S(1)} %collective-permute-done.7.refs_6_), channel_id=1, source_target_pairs={{130,132},{131,133},{124,122},{125,123},{258,260},{259,261},{252,2... | collective-permute-start | bytes 1376264 | tf_op jit(solution)/shard_map/ppermute | solution.py:345
  62.8 9.1 %collective-permute-start.12 = (bf16[224,1024]{1,0:T(8,128)(2,1)S(1)}, bf16[224,1024]{1,0:T(8,128)(2,1)S(1)}, u32[]{:S(2)}, u32[]{:S(2)}) collective-permute-start(bf16[224,1024]{1,0:T(8,128)(2,1)S(1)} %collective-permute-done.4.refs_5_), channel_id=1, source_target_pairs={{0,8},{1,9},{8,16},{9,17},{14,6},{15,7},{16,24},{17,25},{22,14},{2... | collective-permute-start | bytes 1376264 | tf_op jit(solution)/shard_map/ppermute | solution.py:345
  64.1 7.8 %collective-permute-start.13 = (bf16[224,1024]{1,0:T(8,128)(2,1)S(1)}, bf16[224,1024]{1,0:T(8,128)(2,1)S(1)}, u32[]{:S(2)}, u32[]{:S(2)}) collective-permute-start(bf16[224,1024]{1,0:T(8,128)(2,1)S(1)} %collective-permute-done.5.refs_6_), channel_id=1, source_target_pairs={{2,10},{3,11},{10,18},{11,19},{12,4},{13,5},{18,26},{19,27},{20,12... | collective-permute-start | bytes 1376264 | tf_op jit(solution)/shard_map/ppermute | solution.py:345
  64.8 9.2 %collective-permute-start.14 = (bf16[224,1024]{1,0:T(8,128)(2,1)S(1)}, bf16[224,1024]{1,0:T(8,128)(2,1)S(1)}, u32[]{:S(2)}, u32[]{:S(2)}) collective-permute-start(bf16[224,1024]{1,0:T(8,128)(2,1)S(1)} %collective-permute-done.8.refs_6_), channel_id=1, source_target_pairs={{128,130},{129,131},{126,124},{127,125},{256,258},{257,259},{254,2... | collective-permute-start | bytes 1376264 | tf_op jit(solution)/shard_map/ppermute | solution.py:345
  118.9 6.8 %collective-permute-start.15 = (f32[224,1024]{1,0:T(8,128)}, f32[224,1024]{1,0:T(8,128)}, u32[]{:S(2)}, u32[]{:S(2)}) collective-permute-start(f32[224,1024]{1,0:T(8,128)} %unit_gradient.2), channel_id=1, source_target_pairs={{0,1},{1,0},{2,3},{3,2},{4,5},{5,4},{6,7},{7,6},{8,9},{9,8},{10,11... | collective-permute-start | bytes 2752520 | tf_op jit(solution)/shard_map/ppermute | solution.py:399

commit v5 on v4

--- a/solution.py
+++ b/solution.py
@@ -20,7 +20,7 @@
 
 
 def routes():
-    names = ("P1", "P2", "P3a", "P3b", "Y1", "Y2", "Y3a", "Y3b", "X1", "X2", "X3", "X4", "X5", "X6")
+    names = ("P1", "P2", "P3a", "P3b", "Y1", "Y2", "Y3a", "Y3b", "X1", "X2", "X3")
     table = {name: [] for name in names}
 
     def chip(run, k):
@@ -52,11 +52,11 @@
         if crosses(run):
             low = [chip(run, k) for k in range(4)]
             high = [chip(run + 1, k) for k in range(4)]
-            for name in ("X1", "X3", "X4"):
+            for name in ("X1", "X2", "P3b"):
                 add(name, (low[3], high[0]), (high[0], low[3]))
-            for name in ("X2", "X5"):
+            for name in ("P3a", "X3"):
                 add(name, (high[0], high[1]), (low[3], low[2]))
-            add("X6", (high[1], high[2]), (low[2], low[1]))
+            add("X3", (high[1], high[2]), (low[2], low[1]))
     return table
 
 
@@ -75,7 +75,7 @@
     return [pl.BlockSpec(memory_space=pltpu.SMEM)] * count
 
 
-PARAMS = pltpu.CompilerParams(vmem_limit_bytes=12 * 1024 * 1024)
+PARAMS = pltpu.CompilerParams(vmem_limit_bytes=8 * 1024 * 1024)
 
 
 def scores(rows, columns):
@@ -279,6 +279,12 @@
     ids_ref, inv_ref, edge_ref, row_ref, partner_ref = refs[:5]
     expos, blocks = refs[5:12], refs[12:19]
     out_ref = refs[19]
+    if shift:
+        posted = edge_ref[:, 0, 1, :]
+        lane = lax.broadcasted_iota(jnp.int32, (16, 128), 1)
+        total = jnp.sum(jnp.where(lane == 127, posted, 0.0), axis=0, keepdims=True)
+        total = jnp.sum(total, axis=1, keepdims=True)
+        refs[20][...] = total / (ROWS * 512) + 1.0 / SOFTMAX_TEMPER
     mine = lanes(row_ref[...])
     mine = jnp.transpose(jnp.broadcast_to(mine, (128, ROWS)))[:, 0:1]
     total = None
@@ -304,14 +310,18 @@
 
 
 def grad_call(shift, ids, inv, edge, row, partner, expos, blocks):
+    shapes = [jax.ShapeDtypeStruct((ROWS, WIDTH), jnp.float32)]
+    if shift:
+        shapes.append(jax.ShapeDtypeStruct((1, 1), jnp.float32))
+
     def kernel(*refs):
         grad_kernel(shift, *refs)
 
     return pl.pallas_call(
         kernel,
-        out_shape=jax.ShapeDtypeStruct((ROWS, WIDTH), jnp.float32),
+        out_shape=tuple(shapes),
         in_specs=smem(1) + vmem(18),
-        out_specs=pl.BlockSpec(memory_space=pltpu.VMEM),
+        out_specs=tuple(vmem(len(shapes))),
         compiler_params=PARAMS,
         cost_estimate=pl.CostEstimate(flops=2 * 7 * ROWS * ROWS * WIDTH, bytes_accessed=6 << 20, transcendentals=0),
         name="unit_gradient",
@@ -328,13 +338,11 @@
 
 
 def final_call(emb, mine, got):
-    spec = pl.BlockSpec((56, WIDTH), lambda i: (i, 0))
     return pl.pallas_call(
         final_kernel,
         out_shape=jax.ShapeDtypeStruct((ROWS, WIDTH), jnp.float32),
-        grid=(4,),
-        in_specs=[spec] * 3,
-        out_specs=spec,
+        in_specs=vmem(3),
+        out_specs=pl.BlockSpec(memory_space=pltpu.VMEM),
         compiler_params=PARAMS,
         cost_estimate=pl.CostEstimate(flops=10 * ROWS * WIDTH, bytes_accessed=16 * ROWS * WIDTH, transcendentals=0),
         name="final",
@@ -354,7 +362,7 @@
     partner = partner.reshape(1, ROWS)
 
     r1 = send(unit, "P1")
-    x1 = send(unit, "X1")
+    x1 = send(after(unit, ids), "X1")
     other = lax.ppermute(after(unit, ids), ("core",), [(0, 1), (1, 0)])
     local, e_own, e_other, sum_own, sum_other, pos = own_call(ids, unit, other, partner)
     expos, blocks, sums = [(e_own, e_other)] + [None] * 6, [unit] + [None] * 6, (sum_own, sum_other)
@@ -369,38 +377,36 @@
             return rest
         sums = rest
 
+    outer = (ids[1] == 0) | (ids[1] == 3)
+    end = ((ids[3] % 16 == 15) & (ids[1] == 3)) | ((ids[3] % 16 == 0) & (ids[1] == 0))
     r1 = after(r1, x1)
     r2 = send(after(unit, r1), "P2")
     y1 = send(r1, "Y1")
-    x2 = send(after(x1, r1), "X2")
-    x3 = send(r1, "X3")
+    x2 = send(r1, "X2")
     add(0, [r1])
     r2 = after(r2, sums[0])
-    y2 = send(after(r2, y1), "Y2")
-    p3b = send(after(unit, r2), "P3b")
-    p3a = send(after(r1, r2), "P3a")
-    x4 = send(after(r2, x3), "X4")
-    x6 = send(after(x2, r2), "X6")
-    add(1, [r2])
+    y2 = send(r2, "Y2")
+    p3b = send(jnp.where(outer, r2, unit), "P3b")
+    p3a = send(jnp.where(end, x1, after(r1, r2)), "P3a")
+    add(1, [after(r2, y1, x2)])
     p3a = after(p3a, sums[0])
     p3b = after(p3b, sums[0])
     y3a = send(after(p3a, y2), "Y3a")
     y3b = send(after(p3b, y2), "Y3b")
-    x5 = send(after(x3, p3a, p3b), "X5")
+    x3 = send(jnp.where(outer, x2, p3a), "X3")
     add(2, [p3a, p3b])
-    add(3, [y1, x2, x4])
-    add(4, [y2, x3, x6])
-    pay = add(5, [y3a, y3b, x1, x5])
+    add(3, [y1, p3a, p3b])
+    add(4, [y2, x2, x3])
+    pay = add(5, [y3a, y3b, x1, x3])
 
     pays = lax.all_to_all(jnp.broadcast_to(pay[None], (32, 8, 128)), DEV_AXES, 0, 0)
     inv, mine_inv, other_inv, post = denom_call(ids, pays)
     posts = lax.all_to_all(post, ("zh", "x"), 0, 0)
-    for_other = grad_call(ROWS, ids, inv, posts, other_inv, local, [e[1] for e in expos], blocks)
+    for_other, loss = grad_call(ROWS, ids, inv, posts, other_inv, local, [e[1] for e in expos], blocks)
     got = lax.ppermute(for_other, ("core",), [(0, 1), (1, 0)])
-    mine = grad_call(0, ids, after(inv, for_other), posts, mine_inv, local, [e[0] for e in expos], blocks)
+    (mine,) = grad_call(0, ids, after(inv, for_other), posts, mine_inv, local, [e[0] for e in expos], blocks)
     grad = final_call(embeddings, mine, got)
-    total = jnp.sum(after(posts, mine)[:, 0, 1, 127])
-    loss = total / (ROWS * 512) + 1.0 / SOFTMAX_TEMPER
+    loss = loss.reshape(())
     return (loss, grad)
 
 

time: 131 us -> 132 us (level)
  starting transfers between devices: 56.8 us -> 46.3 us
  waiting for transfers between devices: 12.1 us -> 19.2 us
  local copies, waits for them, and re-layouts: 0.05 us -> 5.58 us
  other arithmetic: 2.31 us -> 4.42 us
  Pallas kernels: 16.3 us -> 14.5 us
  between operations: 2.74 us -> 1 us
    ppermute x14 -> x11, starting transfers between devices: 49.8 us -> 39.7 us  [send(): return lax.ppermute(value, AXES, ROUTES[name])]
    ppermute x14 -> x11, waiting for transfers between devices: 12.1 us -> 18.9 us  [send(): return lax.ppermute(value, AXES, ROUTES[name])]
    unnamed x4 -> x40, local copies, waits for them, and re-layouts: 0.04 us -> 5.57 us
    select_n x0 -> x3, other arithmetic: none -> 2.8 us  [the longest x1 1.07 us: per_device(): x3 = send(jnp.where(outer, x2, p3a), 'X3')]
    pallas_call x1, Pallas kernels: 3.73 us -> 1.34 us  [final_call(): pl.pallas_call(final_kernel, out_shape=jax.ShapeDtypeStruct((ROWS, WIDTH)...]
  transfers between devices with their start and end apart: 16 -> 13, of which waited for: 4 -> 6; matrix products, arithmetic and copies ran while one was open for 1% -> 2% of each run, Pallas kernels for 6% -> 7%
where the time goes in v5:
time: 132 us; the launch traced here: 131 us
  starting transfers between devices  46.3 us (35%)
  blocking collectives  40 us (30%)
  waiting for transfers between devices  19.2 us (15%)
  Pallas kernels  14.5 us (11%)
  local copies, waits for them, and re-layouts  5.58 us (4%)
  other arithmetic  4.42 us (3%)
    ppermute x11, starting transfers between devices, send(): return lax.ppermute(value, AXES, ROUTES[name])  39.7 us
    all_to_all x1, blocking collectives, per_device(): posts = lax.all_to_all(post, ('zh', 'x'), 0, 0)  24 us
    ppermute x11, waiting for transfers between devices, send(): return lax.ppermute(value, AXES, ROUTES[name])  18.9 us
    all_to_all x1, blocking collectives, per_device(): lax.all_to_all(jnp.broadcast_to(pay[None], (32, 8, 128)), DEV_AXES, 0, 0)  15.9 us
    pallas_call x6, Pallas kernels, block_call(): pl.pallas_call(kernel, out_shape=tuple(shapes), in_specs=smem(1) + vmem(l...  7.5 us
    unnamed x40, local copies, waits for them, and re-layouts  5.57 us
    pallas_call x2, Pallas kernels, grad_call(): pl.pallas_call(kernel, out_shape=tuple(shapes), in_specs=smem(1) + vmem(1...  3.97 us
    ppermute x1, starting transfers between devices, per_device(): got = lax.ppermute(for_other, ('core',), [(0, 1), (1, 0)])  3.67 us
  transfers between devices with their start and end apart: 13, of which 6 were waited for; matrix products, arithmetic and copies ran while one was open for 2% of the time, Pallas kernels for 7%

profile of v5, /device:TPU:1, one launch (start us, length us, event | category | flops | bytes accessed | tf_op | source)
XLA Modules:
  0.0 131.0 jit_solution(10034602976172067016)
XLA Ops:
  0.6 1.4 %multiply_reduce_fusion = f32[224]{0:T(256)S(1)} fusion(f32[224,1024]{1,0:T(8,128)} %emb_ref.1), kind=kLoop, calls=%fused_computation.1 | loop fusion | flops 458528 | bytes 918400 | tf_op jit(solution)/shard_map/reduce_sum | solution.py:357
  2.1 0.0 copy-done
  2.1 0.1 divide_convert_fusion.unit_ref.refs_1_.refs_12_
  2.2 0.4 copy-done.19
  2.6 0.1 pad_add_fusion.ids_ref.refs_0_
  2.7 16.6 %collective-permute-start.2 = (bf16[224,1024]{1,0:T(8,128)(2,1)S(1)}, bf16[224,1024]{1,0:T(8,128)(2,1)S(1)}, u32[]{:S(2)}, u32[]{:S(2)}) collective-permute-start(bf16[224,1024]{1,0:T(8,128)(2,1)S(1)} %divide_convert_fusion.unit_ref.refs_1_.refs_12_), channel_id=1, source_target_pairs={{126,128},{127,129},{128,126},{129,127},{254,256},{255,257},{256,2... | collective-permute-start | bytes 1376264 | tf_op jit(solution)/shard_map/ppermute | solution.py:353
  19.3 1.9 %collective-permute-start.1 = (bf16[224,1024]{1,0:T(8,128)(2,1)S(1)}, bf16[224,1024]{1,0:T(8,128)(2,1)S(1)}, u32[]{:S(2)}, u32[]{:S(2)}) collective-permute-start(bf16[224,1024]{1,0:T(8,128)(2,1)S(1)} %divide_convert_fusion.unit_ref.refs_1_.refs_12_), channel_id=1, source_target_pairs={{0,4},{1,5},{2,0},{3,1},{4,6},{5,7},{6,2},{7,3},{8,12},{9,13},{10,... | collective-permute-start | bytes 1376264 | tf_op jit(solution)/shard_map/ppermute | solution.py:353
  21.2 2.9 %collective-permute-start = (bf16[224,1024]{1,0:T(8,128)(2,1)S(1)}, bf16[224,1024]{1,0:T(8,128)(2,1)S(1)}, u32[]{:S(2)}, u32[]{:S(2)}) collective-permute-start(bf16[224,1024]{1,0:T(8,128)(2,1)S(1)} %divide_convert_fusion.unit_ref.refs_1_.refs_12_), channel_id=1, source_target_pairs={{0,1},{1,0},{2,3},{3,2},{4,5},{5,4},{6,7},{7,6},{8,9},{9,8},{10,11... | collective-permute-start | bytes 1376264 | tf_op jit(solution)/shard_map/ppermute | solution.py:366
  24.1 5.4 %collective-permute-done.2.refs_7_ = bf16[224,1024]{1,0:T(8,128)(2,1)S(1)} collective-permute-done((bf16[224,1024]{1,0:T(8,128)(2,1)S(1)}, bf16[224,1024]{1,0:T(8,128)(2,1)S(1)}, u32[]{:S(2)}, u32[]{:S(2)}) %collective-permute-start.2) | collective-permute-done | bytes 458784 | tf_op jit(solution)/shard_map/ppermute | solution.py:353
  29.5 2.7 %collective-permute-done.1.refs_5_.refs_13_ = bf16[224,1024]{1,0:T(8,128)(2,1)S(1)} collective-permute-done((bf16[224,1024]{1,0:T(8,128)(2,1)S(1)}, bf16[224,1024]{1,0:T(8,128)(2,1)S(1)}, u32[]{:S(2)}, u32[]{:S(2)}) %collective-permute-start.1) | collective-permute-done | bytes 458784 | tf_op jit(solution)/shard_map/ppermute | solution.py:353
  32.3 1.9 %collective-permute-start.3 = (bf16[224,1024]{1,0:T(8,128)(2,1)S(1)}, bf16[224,1024]{1,0:T(8,128)(2,1)S(1)}, u32[]{:S(2)}, u32[]{:S(2)}) collective-permute-start(bf16[224,1024]{1,0:T(8,128)(2,1)S(1)} %divide_convert_fusion.unit_ref.refs_1_.refs_12_), channel_id=1, source_target_pairs={{2,6},{3,7},{4,0},{5,1},{0,2},{1,3},{6,4},{7,5},{10,14},{11,15},{1... | collective-permute-start | bytes 1376264 | tf_op jit(solution)/shard_map/ppermute | solution.py:353
  34.2 5.7 %collective-permute-start.5 = (bf16[224,1024]{1,0:T(8,128)(2,1)S(1)}, bf16[224,1024]{1,0:T(8,128)(2,1)}, u32[]{:S(2)}, u32[]{:S(2)}) collective-permute-start(bf16[224,1024]{1,0:T(8,128)(2,1)S(1)} %collective-permute-done.1.refs_5_.refs_13_), channel_id=1, source_target_pairs={{126,128},{127,129},{128,126},{129,127},{254,256},{255,257},{256,2... | collective-permute-start | bytes 1376264 | tf_op jit(solution)/shard_map/ppermute | solution.py:353
  40.0 2.1 %collective-permute-start.4 = (bf16[224,1024]{1,0:T(8,128)(2,1)S(1)}, bf16[224,1024]{1,0:T(8,128)(2,1)}, u32[]{:S(2)}, u32[]{:S(2)}) collective-permute-start(bf16[224,1024]{1,0:T(8,128)(2,1)S(1)} %collective-permute-done.1.refs_5_.refs_13_), channel_id=1, source_target_pairs={{0,8},{1,9},{2,10},{3,11},{8,16},{9,17},{10,18},{11,19},{12,4},{13... | collective-permute-start | bytes 1376264 | tf_op jit(solution)/shard_map/ppermute | solution.py:353
  42.1 1.1 own_scores.1
  43.1 0.7 copy-done.5
  43.8 0.5 copy-done.17
  44.4 0.6 copy-done.12
  45.0 1.0 block_scores.6
  46.0 0.7 copy-done.3
  46.7 0.7 copy-done.7
  47.4 0.6 copy-done.9
  48.1 0.8 broadcast_select_fusion.2
  48.9 1.9 %collective-permute-start.6 = (bf16[224,1024]{1,0:T(8,128)(2,1)}, bf16[224,1024]{1,0:T(8,128)(2,1)S(1)}, u32[]{:S(2)}, u32[]{:S(2)}) collective-permute-start(bf16[224,1024]{1,0:T(8,128)(2,1)} %broadcast_select_fusion.2), channel_id=1, source_target_pairs={{4,6},{5,7},{2,0},{3,1},{12,14},{13,15},{10,8},{11,9},{20,22},{21,... | collective-permute-start | bytes 1376264 | tf_op jit(solution)/shard_map/ppermute | solution.py:353
  50.8 0.9 broadcast_select_fusion.1
  51.7 5.0 %collective-permute-start.7 = (bf16[224,1024]{1,0:T(8,128)(2,1)S(1)}, bf16[224,1024]{1,0:T(8,128)(2,1)S(1)}, u32[]{:S(2)}, u32[]{:S(2)}) collective-permute-start(bf16[224,1024]{1,0:T(8,128)(2,1)S(1)} %broadcast_select_fusion.1), channel_id=1, source_target_pairs={{2,4},{3,5},{4,2},{5,3},{10,12},{11,13},{12,10},{13,11},{18,20},{1... | collective-permute-start | bytes 1376264 | tf_op jit(solution)/shard_map/ppermute | solution.py:353
  56.7 1.3 %collective-permute-start.8 = (bf16[224,1024]{1,0:T(8,128)(2,1)S(1)}, bf16[224,1024]{1,0:T(8,128)(2,1)S(1)}, u32[]{:S(2)}, u32[]{:S(2)}) collective-permute-start(bf16[224,1024]{1,0:T(8,128)(2,1)S(1)} %collective-permute-done.3.refs_5_.refs_14_), channel_id=1, source_target_pairs={{0,8},{1,9},{4,12},{5,13},{8,16},{9,17},{12,20},{13,21},{10,2},{11... | collective-permute-start | bytes 1376264 | tf_op jit(solution)/shard_map/ppermute | solution.py:353
  58.1 1.0 block_scores.7
  59.1 2.0 %collective-permute-done.6.refs_5_.refs_6_ = bf16[224,1024]{1,0:T(8,128)(2,1)S(1)} collective-permute-done((bf16[224,1024]{1,0:T(8,128)(2,1)}, bf16[224,1024]{1,0:T(8,128)(2,1)S(1)}, u32[]{:S(2)}, u32[]{:S(2)}) %collective-permute-start.6) | collective-permute-done | bytes 458784 | tf_op jit(solution)/shard_map/ppermute | solution.py:353
  61.2 1.1 broadcast_select_fusion
  62.2 1.3 %collective-permute-start.9 = (bf16[224,1024]{1,0:T(8,128)(2,1)S(1)}, bf16[224,1024]{1,0:T(8,128)(2,1)S(1)}, u32[]{:S(2)}, u32[]{:S(2)}) collective-permute-start(bf16[224,1024]{1,0:T(8,128)(2,1)S(1)} %broadcast_select_fusion), channel_id=1, source_target_pairs={{128,130},{129,131},{126,124},{127,125},{130,132},{131,133},{124,1... | collective-permute-start | bytes 1376264 | tf_op jit(solution)/shard_map/ppermute | solution.py:353
  63.6 5.7 %collective-permute-done.7.refs_6_.refs_7_ = bf16[224,1024]{1,0:T(8,128)(2,1)S(1)} collective-permute-done((bf16[224,1024]{1,0:T(8,128)(2,1)S(1)}, bf16[224,1024]{1,0:T(8,128)(2,1)S(1)}, u32[]{:S(2)}, u32[]{:S(2)}) %collective-permute-start.7) | collective-permute-done | bytes 458784 | tf_op jit(solution)/shard_map/ppermute | solution.py:353
  69.3 0.7 collective-permute-start.11
  69.9 1.3 %collective-permute-start.10 = (bf16[224,1024]{1,0:T(8,128)(2,1)S(1)}, bf16[224,1024]{1,0:T(8,128)(2,1)S(1)}, u32[]{:S(2)}, u32[]{:S(2)}) collective-permute-start(bf16[224,1024]{1,0:T(8,128)(2,1)S(1)} %collective-permute-done.6.refs_5_.refs_6_), channel_id=1, source_target_pairs={{0,8},{1,9},{8,16},{9,17},{14,6},{15,7},{16,24},{17,25},{22,14},{2... | collective-permute-start | bytes 1376264 | tf_op jit(solution)/shard_map/ppermute | solution.py:353
  71.3 1.1 block_scores.8
  72.3 1.6 %block_scores.9 = (f32[224,224]{1,0:T(8,128)S(1)}, f32[224,224]{1,0:T(8,128)S(1)}, f32[224,128]{1,0:T(8,128)S(1)}, f32[224,128]{1,0:T(8,128)S(1)}, bf16[224,1024]{1,0:T(8,128)(2,1)S(1)}) custom-call(s32[4]{0:T(128)S(1)} %copy-done.13, bf16[224,1024]{1,0:T(8,128)(2,1)S(1)} %divide_convert_fusion.unit_ref.refs_1_.refs_12_, ...), custom_call_target="tpu_custom_call" | custom-call | flops 205520896 | bytes 2097152 | tf_op jit(solution)/shard_map/block_scores/pallas_call | solution.py:217
  73.9 1.6 %block_scores.10 = (f32[224,224]{1,0:T(8,128)S(1)}, f32[224,224]{1,0:T(8,128)S(1)}, f32[224,128]{1,0:T(8,128)S(1)}, f32[224,128]{1,0:T(8,128)S(1)}, bf16[224,1024]{1,0:T(8,128)(2,1)S(1)}) custom-call(s32[4]{0:T(128)S(1)} %copy-done.13, bf16[224,1024]{1,0:T(8,128)(2,1)S(1)} %divide_convert_fusion.unit_ref.refs_1_.refs_12_, ...), custom_call_target="tpu_custom_call" | custom-call | flops 205520896 | bytes 2097152 | tf_op jit(solution)/shard_map/block_scores/pallas_call | solution.py:217
  75.6 3.0 %collective-permute-done.10.refs_5_ = bf16[224,1024]{1,0:T(8,128)(2,1)S(1)} collective-permute-done((bf16[224,1024]{1,0:T(8,128)(2,1)S(1)}, bf16[224,1024]{1,0:T(8,128)(2,1)S(1)}, u32[]{:S(2)}, u32[]{:S(2)}) %collective-permute-start.10) | collective-permute-done | bytes 458784 | tf_op jit(solution)/shard_map/ppermute | solution.py:353
  78.6 0.6 copy-done.18
  79.2 1.2 block_scores.11
  80.4 15.9 %all_to_all.10.pay_ref = f32[32,8,128]{2,1,0:T(8,128)S(1)} all-to-all(f32[32,8,128]{2,1,0:T(8,128)S(1)} %broadcast_in_dim.2), channel_id=1, replica_groups=mesh['zh'=4,'x'=4,'y'=4,'zl'=4,'core'=2] {'y','zl','core'}, dimensions={0} | all-to-all | bytes 262144 | tf_op jit(solution)/shard_map/all_to_all | solution.py:402
  96.3 0.7 denoms.1
  97.0 24.0 %all_to_all.11.refs_2_ = f32[16,4,2,128]{3,2,1,0:T(2,128)S(1)} all-to-all(f32[16,4,2,128]{3,2,1,0:T(2,128)S(1)} %get-tuple-element.77), channel_id=1, replica_groups=mesh['zh'=4,'x'=4,'y'=4,'zl'=4,'core'=2] {'zh','x'}, dimensions={0} | all-to-all | bytes 131072 | tf_op jit(solution)/shard_map/all_to_all | solution.py:404
  121.1 0.6 copy-done.15
  121.7 2.2 %unit_gradient.2 = (f32[224,1024]{1,0:T(8,128)S(1)}, f32[1,1]{1,0:T(1,128)}) custom-call(s32[4]{0:T(128)S(1)} %copy-done.13, f32[16,2,128]{2,1,0:T(2,128)S(1)} %get-tuple-element.93.refs_1_, f32[16,4,2,128]{3,2,1,0:T(2,128)S(1)} %all_to_all.11.refs_2_, f32[2,128]{1,0:T(2,128)S(1)} %get-tuple-element.78.refs_3_, s32[1,224]{1,0:T(1,128)S(1)} %copy-done.15, ...), custom_call_target="tpu_custom_call" | custom-call | flops 719323136 | bytes 6291456 | tf_op jit(solution)/shard_map/unit_gradient/pallas_call | solution.py:320
  123.9 3.7 %collective-permute-start.12 = (f32[224,1024]{1,0:T(8,128)S(1)}, f32[224,1024]{1,0:T(8,128)S(1)}, u32[]{:S(2)}, u32[]{:S(2)}) collective-permute-start(f32[224,1024]{1,0:T(8,128)S(1)} %get-tuple-element.92), channel_id=1, source_target_pairs={{0,1},{1,0},{2,3},{3,2},{4,5},{5,4},{6,7},{7,6},{8,9},{9,8},{10,11... | collective-permute-start | bytes 2752520 | tf_op jit(solution)/shard_map/ppermute | solution.py:406
  127.6 1.7 %unit_gradient.3.mine_ref = f32[224,1024]{1,0:T(8,128)S(1)} custom-call(s32[4]{0:T(128)S(1)} %copy-done.13, f32[16,2,128]{2,1,0:T(2,128)S(1)} %get-tuple-element.93.refs_1_, f32[16,4,2,128]{3,2,1,0:T(2,128)S(1)} %all_to_all.11.refs_2_, f32[2,128]{1,0:T(2,128)S(1)} %get-tuple-element.94.refs_3_, s32[1,224]{1,0:T(1,128)S(1)} %copy-done.15, ...), custom_call_target="tpu_custom_call" | custom-call | flops 719323136 | bytes 6291456 | tf_op jit(solution)/shard_map/unit_gradient/pallas_call | solution.py:320
  129.3 0.3 collective-permute-done.12.got_ref
  129.7 1.3 %final.1 = f32[224,1024]{1,0:T(8,128)} custom-call(f32[224,1024]{1,0:T(8,128)S(1)} %copy-done, f32[224,1024]{1,0:T(8,128)S(1)} %unit_gradient.3.mine_ref, f32[224,1024]{1,0:T(8,128)S(1)} %collective-permute-done.12.got_ref), custom_call_target="tpu_custom_call" | custom-call | flops 2293760 | bytes 3670016 | tf_op jit(solution)/shard_map/final/pallas_call | solution.py:341
  (39 shorter events, 0.1 us)
Async XLA Ops:
  0.6 1.5 %copy-start = (f32[224,1024]{1,0:T(8,128)S(1)}, f32[224,1024]{1,0:T(8,128)}, u32[]{:S(2)}) copy-start(f32[224,1024]{1,0:T(8,128)} %emb_ref.1) | copy-start | bytes 2752516
  2.1 0.5 copy-start.19
  2.7 39.4 %copy-start.11 = (s32[4]{0:T(128)}, s32[4]{0:T(128)S(1)}, u32[]{:S(2)}) copy-start(s32[4]{0:T(128)S(1)} %pad_add_fusion.ids_ref.refs_0_) | copy-start | bytes 52
  2.7 26.8 %collective-permute-start.2 = (bf16[224,1024]{1,0:T(8,128)(2,1)S(1)}, bf16[224,1024]{1,0:T(8,128)(2,1)S(1)}, u32[]{:S(2)}, u32[]{:S(2)}) collective-permute-start(bf16[224,1024]{1,0:T(8,128)(2,1)S(1)} %divide_convert_fusion.unit_ref.refs_1_.refs_12_), channel_id=1, source_target_pairs={{126,128},{127,129},{128,126},{129,127},{254,256},{255,257},{256,2... | collective-permute-start | bytes 1376264 | tf_op jit(solution)/shard_map/ppermute | solution.py:353
  19.3 13.0 %collective-permute-start.1 = (bf16[224,1024]{1,0:T(8,128)(2,1)S(1)}, bf16[224,1024]{1,0:T(8,128)(2,1)S(1)}, u32[]{:S(2)}, u32[]{:S(2)}) collective-permute-start(bf16[224,1024]{1,0:T(8,128)(2,1)S(1)} %divide_convert_fusion.unit_ref.refs_1_.refs_12_), channel_id=1, source_target_pairs={{0,4},{1,5},{2,0},{3,1},{4,6},{5,7},{6,2},{7,3},{8,12},{9,13},{10,... | collective-permute-start | bytes 1376264 | tf_op jit(solution)/shard_map/ppermute | solution.py:353
  21.2 20.8 %collective-permute-start = (bf16[224,1024]{1,0:T(8,128)(2,1)S(1)}, bf16[224,1024]{1,0:T(8,128)(2,1)S(1)}, u32[]{:S(2)}, u32[]{:S(2)}) collective-permute-start(bf16[224,1024]{1,0:T(8,128)(2,1)S(1)} %divide_convert_fusion.unit_ref.refs_1_.refs_12_), channel_id=1, source_target_pairs={{0,1},{1,0},{2,3},{3,2},{4,5},{5,4},{6,7},{7,6},{8,9},{9,8},{10,11... | collective-permute-start | bytes 1376264 | tf_op jit(solution)/shard_map/ppermute | solution.py:366
  29.5 18.5 %copy-start.1 = (bf16[224,1024]{1,0:T(8,128)(2,1)}, bf16[224,1024]{1,0:T(8,128)(2,1)S(1)}, u32[]{:S(2)}) copy-start(bf16[224,1024]{1,0:T(8,128)(2,1)S(1)} %collective-permute-done.2.refs_7_) | copy-start | bytes 1376260
  32.3 15.8 %collective-permute-start.3 = (bf16[224,1024]{1,0:T(8,128)(2,1)S(1)}, bf16[224,1024]{1,0:T(8,128)(2,1)S(1)}, u32[]{:S(2)}, u32[]{:S(2)}) collective-permute-start(bf16[224,1024]{1,0:T(8,128)(2,1)S(1)} %divide_convert_fusion.unit_ref.refs_1_.refs_12_), channel_id=1, source_target_pairs={{2,6},{3,7},{4,0},{5,1},{0,2},{1,3},{6,4},{7,5},{10,14},{11,15},{1... | collective-permute-start | bytes 1376264 | tf_op jit(solution)/shard_map/ppermute | solution.py:353
  34.2 7.8 %copy-start.16 = (s32[224]{0:T(256)S(1)}, s32[224]{0:T(256)}, u32[]{:S(2)}) copy-start(s32[224]{0:T(256)} %param.3) | copy-start | bytes 2692
  34.2 23.8 %collective-permute-start.5 = (bf16[224,1024]{1,0:T(8,128)(2,1)S(1)}, bf16[224,1024]{1,0:T(8,128)(2,1)}, u32[]{:S(2)}, u32[]{:S(2)}) collective-permute-start(bf16[224,1024]{1,0:T(8,128)(2,1)S(1)} %collective-permute-done.1.refs_5_.refs_13_), channel_id=1, source_target_pairs={{126,128},{127,129},{128,126},{129,127},{254,256},{255,257},{256,2... | collective-permute-start | bytes 1376264 | tf_op jit(solution)/shard_map/ppermute | solution.py:353
  40.0 18.1 %collective-permute-start.4 = (bf16[224,1024]{1,0:T(8,128)(2,1)S(1)}, bf16[224,1024]{1,0:T(8,128)(2,1)}, u32[]{:S(2)}, u32[]{:S(2)}) collective-permute-start(bf16[224,1024]{1,0:T(8,128)(2,1)S(1)} %collective-permute-done.1.refs_5_.refs_13_), channel_id=1, source_target_pairs={{0,8},{1,9},{2,10},{3,11},{8,16},{9,17},{10,18},{11,19},{12,4},{13... | collective-permute-start | bytes 1376264 | tf_op jit(solution)/shard_map/ppermute | solution.py:353
  43.1 0.7 copy-start.5
  43.8 0.5 copy-start.17
  43.8 0.5 copy-start.14
  44.3 0.7 copy-start.12
  46.0 0.7 copy-start.3
  46.7 0.7 copy-start.7
  47.4 0.6 copy-start.9
  48.9 12.3 %collective-permute-start.6 = (bf16[224,1024]{1,0:T(8,128)(2,1)}, bf16[224,1024]{1,0:T(8,128)(2,1)S(1)}, u32[]{:S(2)}, u32[]{:S(2)}) collective-permute-start(bf16[224,1024]{1,0:T(8,128)(2,1)} %broadcast_select_fusion.2), channel_id=1, source_target_pairs={{4,6},{5,7},{2,0},{3,1},{12,14},{13,15},{10,8},{11,9},{20,22},{21,... | collective-permute-start | bytes 1376264 | tf_op jit(solution)/shard_map/ppermute | solution.py:353
  50.8 7.3 %copy-start.10 = (f32[224,128]{1,0:T(8,128)S(1)}, f32[224,128]{1,0:T(8,128)}, u32[]{:S(2)}) copy-start(f32[224,128]{1,0:T(8,128)} %copy-done.9) | copy-start | bytes 344068
  51.7 6.3 %copy-start.13 = (s32[4]{0:T(128)S(1)}, s32[4]{0:T(128)}, u32[]{:S(2)}) copy-start(s32[4]{0:T(128)} %copy-done.11) | copy-start | bytes 52
  51.7 17.5 %collective-permute-start.7 = (bf16[224,1024]{1,0:T(8,128)(2,1)S(1)}, bf16[224,1024]{1,0:T(8,128)(2,1)S(1)}, u32[]{:S(2)}, u32[]{:S(2)}) collective-permute-start(bf16[224,1024]{1,0:T(8,128)(2,1)S(1)} %broadcast_select_fusion.1), channel_id=1, source_target_pairs={{2,4},{3,5},{4,2},{5,3},{10,12},{11,13},{12,10},{13,11},{18,20},{1... | collective-permute-start | bytes 1376264 | tf_op jit(solution)/shard_map/ppermute | solution.py:353
  56.7 12.5 %collective-permute-start.8 = (bf16[224,1024]{1,0:T(8,128)(2,1)S(1)}, bf16[224,1024]{1,0:T(8,128)(2,1)S(1)}, u32[]{:S(2)}, u32[]{:S(2)}) collective-permute-start(bf16[224,1024]{1,0:T(8,128)(2,1)S(1)} %collective-permute-done.3.refs_5_.refs_14_), channel_id=1, source_target_pairs={{0,8},{1,9},{4,12},{5,13},{8,16},{9,17},{12,20},{13,21},{10,2},{11... | collective-permute-start | bytes 1376264 | tf_op jit(solution)/shard_map/ppermute | solution.py:353
  62.2 11.7 %collective-permute-start.9 = (bf16[224,1024]{1,0:T(8,128)(2,1)S(1)}, bf16[224,1024]{1,0:T(8,128)(2,1)S(1)}, u32[]{:S(2)}, u32[]{:S(2)}) collective-permute-start(bf16[224,1024]{1,0:T(8,128)(2,1)S(1)} %broadcast_select_fusion), channel_id=1, source_target_pairs={{128,130},{129,131},{126,124},{127,125},{130,132},{131,133},{124,1... | collective-permute-start | bytes 1376264 | tf_op jit(solution)/shard_map/ppermute | solution.py:353
  69.3 6.3 %collective-permute-start.11 = (bf16[224,1024]{1,0:T(8,128)(2,1)S(1)}, bf16[224,1024]{1,0:T(8,128)(2,1)S(1)}, u32[]{:S(2)}, u32[]{:S(2)}) collective-permute-start(bf16[224,1024]{1,0:T(8,128)(2,1)S(1)} %collective-permute-done.7.refs_6_.refs_7_), channel_id=1, source_target_pairs={{2,10},{3,11},{10,18},{11,19},{12,4},{13,5},{18,26},{19,27},{20,12... | collective-permute-start | bytes 1376264 | tf_op jit(solution)/shard_map/ppermute | solution.py:353
  69.9 8.6 %collective-permute-start.10 = (bf16[224,1024]{1,0:T(8,128)(2,1)S(1)}, bf16[224,1024]{1,0:T(8,128)(2,1)S(1)}, u32[]{:S(2)}, u32[]{:S(2)}) collective-permute-start(bf16[224,1024]{1,0:T(8,128)(2,1)S(1)} %collective-permute-done.6.refs_5_.refs_6_), channel_id=1, source_target_pairs={{0,8},{1,9},{8,16},{9,17},{14,6},{15,7},{16,24},{17,25},{22,14},{2... | collective-permute-start | bytes 1376264 | tf_op jit(solution)/shard_map/ppermute | solution.py:353
  73.9 4.7 %copy-start.2 = (bf16[224,1024]{1,0:T(8,128)(2,1)S(1)}, bf16[224,1024]{1,0:T(8,128)(2,1)}, u32[]{:S(2)}) copy-start(bf16[224,1024]{1,0:T(8,128)(2,1)} %copy-done.1) | copy-start | bytes 1376260
  78.6 0.6 copy-start.18
  80.4 40.7 %copy-start.6 = (f32[224,224]{1,0:T(8,128)S(1)}, f32[224,224]{1,0:T(8,128)}, u32[]{:S(2)}) copy-start(f32[224,224]{1,0:T(8,128)} %copy-done.5) | copy-start | bytes 602116
  80.4 40.7 %copy-start.8 = (f32[224,224]{1,0:T(8,128)S(1)}, f32[224,224]{1,0:T(8,128)}, u32[]{:S(2)}) copy-start(f32[224,224]{1,0:T(8,128)} %copy-done.7) | copy-start | bytes 602116
  121.0 0.6 copy-start.15
  121.7 5.9 %copy-start.4 = (f32[224,224]{1,0:T(8,128)S(1)}, f32[224,224]{1,0:T(8,128)}, u32[]{:S(2)}) copy-start(f32[224,224]{1,0:T(8,128)} %copy-done.3) | copy-start | bytes 602116
  123.9 5.8 %collective-permute-start.12 = (f32[224,1024]{1,0:T(8,128)S(1)}, f32[224,1024]{1,0:T(8,128)S(1)}, u32[]{:S(2)}, u32[]{:S(2)}) collective-permute-start(f32[224,1024]{1,0:T(8,128)S(1)} %get-tuple-element.92), channel_id=1, source_target_pairs={{0,1},{1,0},{2,3},{3,2},{4,5},{5,4},{6,7},{7,6},{8,9},{9,8},{10,11... | collective-permute-start | bytes 2752520 | tf_op jit(solution)/shard_map/ppermute | solution.py:406

commit v6 on v5

--- a/solution.py
+++ b/solution.py
@@ -20,7 +20,7 @@
 
 
 def routes():
-    names = ("P1", "P2", "P3a", "P3b", "Y1", "Y2", "Y3a", "Y3b", "X1", "X2", "X3")
+    names = ("P1", "P2", "P3a", "P3b", "Y1", "Y2", "Y3a", "Y3b", "X1", "X2", "X3", "X4", "X5")
     table = {name: [] for name in names}
 
     def chip(run, k):
@@ -52,11 +52,11 @@
         if crosses(run):
             low = [chip(run, k) for k in range(4)]
             high = [chip(run + 1, k) for k in range(4)]
-            for name in ("X1", "X2", "P3b"):
+            for name in ("X1", "X3", "X4"):
                 add(name, (low[3], high[0]), (high[0], low[3]))
-            for name in ("P3a", "X3"):
+            for name in ("X2", "X5"):
                 add(name, (high[0], high[1]), (low[3], low[2]))
-            add("X3", (high[1], high[2]), (low[2], low[1]))
+            add("X5", (high[1], high[2]), (low[2], low[1]))
     return table
 
 
@@ -75,7 +75,7 @@
     return [pl.BlockSpec(memory_space=pltpu.SMEM)] * count
 
 
-PARAMS = pltpu.CompilerParams(vmem_limit_bytes=8 * 1024 * 1024)
+PARAMS = pltpu.CompilerParams(vmem_limit_bytes=12 * 1024 * 1024)
 
 
 def scores(rows, columns):
@@ -187,12 +187,12 @@
     e_other_ref[...] = expo
     sum_other = sum_other_ref[...] + fold(expo)
     if last:
-        pay_ref[...] = jnp.zeros((8, 128), jnp.float32)
-        for half, total in enumerate((sum_own, sum_other)):
+        positive = jnp.broadcast_to(jnp.sum(pos_ref[...], axis=1, keepdims=True), (1, 256 - ROWS))
+        rows = []
+        for total in (sum_own, sum_other):
             across = jnp.sum(jnp.transpose(total), axis=0, keepdims=True)
-            pay_ref[2 * half : 2 * half + 1, :] = across[:, :128]
-            pay_ref[2 * half + 1 : 2 * half + 2, : ROWS - 128] = across[:, 128:]
-        pay_ref[4:5, :] = pos_ref[...]
+            rows += [across[:, :128], jnp.concatenate([across[:, 128:], positive], axis=1)]
+        pay_ref[...] = jnp.broadcast_to(jnp.concatenate(rows, axis=0)[None], (32, 4, 128))
     else:
         sum_own_out[...] = sum_own
         sum_other_out[...] = sum_other
@@ -204,7 +204,7 @@
     n = len(cands)
     shapes = [jax.ShapeDtypeStruct((ROWS, ROWS), f32)] * 2
     if last:
-        shapes.append(jax.ShapeDtypeStruct((8, 128), f32))
+        shapes.append(jax.ShapeDtypeStruct((32, 4, 128), f32))
     else:
         shapes += [jax.ShapeDtypeStruct((ROWS, 128), f32)] * 2
     if n > 1:
@@ -229,9 +229,32 @@
     return out[:2], out[2:4], block
 
 
+def choose_kernel(ids_ref, outer_ref, inner_ref, out_ref):
+    outer = (ids_ref[1] == 0) | (ids_ref[1] == 3)
+
+    @pl.when(outer)
+    def _():
+        out_ref[...] = outer_ref[...]
+
+    @pl.when(jnp.logical_not(outer))
+    def _():
+        out_ref[...] = inner_ref[...]
+
+
+def choose_call(ids, outer, inner):
+    return pl.pallas_call(
+        choose_kernel,
+        out_shape=jax.ShapeDtypeStruct((ROWS, WIDTH), jnp.bfloat16),
+        in_specs=smem(1) + vmem(2),
+        out_specs=pl.BlockSpec(memory_space=pltpu.VMEM),
+        compiler_params=PARAMS,
+        name="choose",
+    )(ids, outer, inner)
+
+
 def denom_kernel(ids_ref, pay_ref, inv_ref, mine_ref, other_ref, post_ref):
     y, k, core, group = ids_ref[0], ids_ref[1], ids_ref[2], ids_ref[3] // 4
-    pay = pay_ref[...].reshape(16, 2, 8, 128)
+    pay = pay_ref[...].reshape(16, 2, 4, 128)
     lane = lax.broadcasted_iota(jnp.int32, (16, 2, 128), 2)
     part = lax.broadcasted_iota(jnp.int32, (16, 2, 128), 1)
     real = part * 128 + lane < ROWS
@@ -239,8 +262,9 @@
     second = jnp.where(real, pay[:, 1, 0:2] + pay[:, 0, 2:4], 1.0)
     total = jnp.log(first) + jnp.log(second)
     total = jnp.sum(total.reshape(32, 128), axis=0, keepdims=True)
-    total = total - jnp.sum(pay[:, :, 4].reshape(32, 128), axis=0, keepdims=True)
-    total = jnp.sum(total, axis=1, keepdims=True)
+    last = lax.broadcasted_iota(jnp.int32, (1, 128), 1) == 127
+    positive = jnp.sum(pay[:, :, 1].reshape(32, 128), axis=0, keepdims=True)
+    total = jnp.sum(total - jnp.where(last, positive, 0.0), axis=1, keepdims=True)
     first, second = 1.0 / first, 1.0 / second
     inv = jnp.where(core == 0, first, second)
     other_all = jnp.where(core == 0, second, first)
@@ -362,7 +386,7 @@
     partner = partner.reshape(1, ROWS)
 
     r1 = send(unit, "P1")
-    x1 = send(after(unit, ids), "X1")
+    x1 = send(unit, "X1")
     other = lax.ppermute(after(unit, ids), ("core",), [(0, 1), (1, 0)])
     local, e_own, e_other, sum_own, sum_other, pos = own_call(ids, unit, other, partner)
     expos, blocks, sums = [(e_own, e_other)] + [None] * 6, [unit] + [None] * 6, (sum_own, sum_other)
@@ -377,29 +401,28 @@
             return rest
         sums = rest
 
-    outer = (ids[1] == 0) | (ids[1] == 3)
-    end = ((ids[3] % 16 == 15) & (ids[1] == 3)) | ((ids[3] % 16 == 0) & (ids[1] == 0))
-    r1 = after(r1, x1)
     r2 = send(after(unit, r1), "P2")
     y1 = send(r1, "Y1")
-    x2 = send(r1, "X2")
+    x2 = send(after(x1, r1), "X2")
+    x3 = send(r1, "X3")
     add(0, [r1])
     r2 = after(r2, sums[0])
-    y2 = send(r2, "Y2")
-    p3b = send(jnp.where(outer, r2, unit), "P3b")
-    p3a = send(jnp.where(end, x1, after(r1, r2)), "P3a")
-    add(1, [after(r2, y1, x2)])
+    y2 = send(after(r2, y1), "Y2")
+    p3b = send(after(unit, r2), "P3b")
+    p3a = send(after(r1, r2), "P3a")
+    x4 = send(after(r2, x3), "X4")
+    x5 = send(choose_call(ids, x3, after(x2, r2)), "X5")
+    add(1, [r2])
     p3a = after(p3a, sums[0])
     p3b = after(p3b, sums[0])
     y3a = send(after(p3a, y2), "Y3a")
     y3b = send(after(p3b, y2), "Y3b")
-    x3 = send(jnp.where(outer, x2, p3a), "X3")
     add(2, [p3a, p3b])
-    add(3, [y1, p3a, p3b])
-    add(4, [y2, x2, x3])
-    pay = add(5, [y3a, y3b, x1, x3])
-
-    pays = lax.all_to_all(jnp.broadcast_to(pay[None], (32, 8, 128)), DEV_AXES, 0, 0)
+    add(3, [y1, x2, x4])
+    add(4, [y2, x3, x5])
+    pay = add(5, [y3a, y3b, x1, x5])
+
+    pays = lax.all_to_all(pay, DEV_AXES, 0, 0)
     inv, mine_inv, other_inv, post = denom_call(ids, pays)
     posts = lax.all_to_all(post, ("zh", "x"), 0, 0)
     for_other, loss = grad_call(ROWS, ids, inv, posts, other_inv, local, [e[1] for e in expos], blocks)

time: 132 us -> 122 us (0.924)
  starting transfers between devices: 46.3 us -> 54.5 us
  waiting for transfers between devices: 19.2 us -> 11.2 us
  local copies, waits for them, and re-layouts: 5.58 us -> 0.04 us
  other arithmetic: 4.42 us -> 1.62 us
    ppermute x11 -> x13, waiting for transfers between devices: 18.9 us -> 10.8 us  [send(): return lax.ppermute(value, AXES, ROUTES[name])]
    ppermute x11 -> x13, starting transfers between devices: 39.7 us -> 47.5 us  [send(): return lax.ppermute(value, AXES, ROUTES[name])]
    unnamed x40 -> x4, local copies, waits for them, and re-layouts: 5.57 us -> 0.04 us
    select_n x3 -> x0, other arithmetic: 2.8 us -> none  [the longest x1 1.07 us: per_device(): x3 = send(jnp.where(outer, x2, p3a), 'X3')]
  transfers between devices with their start and end apart: 13 -> 15, of which waited for: 6 -> 5; matrix products, arithmetic and copies ran while one was open for 2% -> 0% of each run, Pallas kernels for 7% -> 7%
where the time goes in v6:
time: 122 us; the launch traced here: 121 us
  starting transfers between devices  54.5 us (45%)
  blocking collectives  38.8 us (32%)
  Pallas kernels  14.1 us (12%)
  waiting for transfers between devices  11.2 us (9%)
  other arithmetic  1.62 us (1%)
    ppermute x13, starting transfers between devices, send(): return lax.ppermute(value, AXES, ROUTES[name])  47.5 us
    all_to_all x1, blocking collectives, per_device(): posts = lax.all_to_all(post, ('zh', 'x'), 0, 0)  23.6 us
    all_to_all x1, blocking collectives, per_device(): pays = lax.all_to_all(pay, DEV_AXES, 0, 0)  15.2 us
    ppermute x13, waiting for transfers between devices, send(): return lax.ppermute(value, AXES, ROUTES[name])  10.8 us
    pallas_call x6, Pallas kernels, block_call(): pl.pallas_call(kernel, out_shape=tuple(shapes), in_specs=smem(1) + vmem(l...  6.49 us
    pallas_call x2, Pallas kernels, grad_call(): pl.pallas_call(kernel, out_shape=tuple(shapes), in_specs=smem(1) + vmem(1...  4 us
    ppermute x1, starting transfers between devices, per_device(): got = lax.ppermute(for_other, ('core',), [(0, 1), (1, 0)])  3.76 us
    ppermute x1, starting transfers between devices, per_device(): other = lax.ppermute(after(unit, ids), ('core',), [(0, 1), (1, 0)])  3.27 us
  transfers between devices with their start and end apart: 15, of which 5 were waited for; matrix products, arithmetic and copies ran while one was open for 0% of the time, Pallas kernels for 7%

profile of v6, /device:TPU:1, one launch (start us, length us, event | category | flops | bytes accessed | tf_op | source)
XLA Modules:
  0.0 121.2 jit_solution(3870007541541108125)
XLA Ops:
  0.6 1.4 %multiply_reduce_fusion = f32[224]{0:T(256)S(1)} fusion(f32[224,1024]{1,0:T(8,128)} %emb_ref.1), kind=kLoop, calls=%fused_computation.1 | loop fusion | flops 458528 | bytes 918400 | tf_op jit(solution)/shard_map/reduce_sum | solution.py:381
  2.0 0.0 copy-done
  2.1 0.1 divide_convert_fusion.unit_ref.refs_1_.refs_12_
  2.2 5.7 %collective-permute-start.1 = (bf16[224,1024]{1,0:T(8,128)(2,1)S(1)}, bf16[224,1024]{1,0:T(8,128)(2,1)S(1)}, u32[]{:S(2)}, u32[]{:S(2)}) collective-permute-start(bf16[224,1024]{1,0:T(8,128)(2,1)S(1)} %divide_convert_fusion.unit_ref.refs_1_.refs_12_), channel_id=1, source_target_pairs={{0,4},{1,5},{2,0},{3,1},{4,6},{5,7},{6,2},{7,3},{8,12},{9,13},{10,... | collective-permute-start | bytes 1376264 | tf_op jit(solution)/shard_map/ppermute | solution.py:377
  8.0 13.9 %collective-permute-start.6 = (bf16[224,1024]{1,0:T(8,128)(2,1)S(1)}, bf16[224,1024]{1,0:T(8,128)(2,1)S(1)}, u32[]{:S(2)}, u32[]{:S(2)}) collective-permute-start(bf16[224,1024]{1,0:T(8,128)(2,1)S(1)} %divide_convert_fusion.unit_ref.refs_1_.refs_12_), channel_id=1, source_target_pairs={{126,128},{127,129},{128,126},{129,127},{254,256},{255,257},{256,2... | collective-permute-start | bytes 1376264 | tf_op jit(solution)/shard_map/ppermute | solution.py:377
  21.9 0.1 pad_add_fusion.ids_ref.refs_0_
  22.0 3.3 %collective-permute-start = (bf16[224,1024]{1,0:T(8,128)(2,1)S(1)}, bf16[224,1024]{1,0:T(8,128)(2,1)S(1)}, u32[]{:S(2)}, u32[]{:S(2)}) collective-permute-start(bf16[224,1024]{1,0:T(8,128)(2,1)S(1)} %divide_convert_fusion.unit_ref.refs_1_.refs_12_), channel_id=1, source_target_pairs={{0,1},{1,0},{2,3},{3,2},{4,5},{5,4},{6,7},{7,6},{8,9},{9,8},{10,11... | collective-permute-start | bytes 1376264 | tf_op jit(solution)/shard_map/ppermute | solution.py:390
  25.3 0.0 collective-permute-done.1.refs_5_.refs_13_
  25.3 1.9 %collective-permute-start.2 = (bf16[224,1024]{1,0:T(8,128)(2,1)S(1)}, bf16[224,1024]{1,0:T(8,128)(2,1)S(1)}, u32[]{:S(2)}, u32[]{:S(2)}) collective-permute-start(bf16[224,1024]{1,0:T(8,128)(2,1)S(1)} %divide_convert_fusion.unit_ref.refs_1_.refs_12_), channel_id=1, source_target_pairs={{2,6},{3,7},{4,0},{5,1},{0,2},{1,3},{6,4},{7,5},{10,14},{11,15},{1... | collective-permute-start | bytes 1376264 | tf_op jit(solution)/shard_map/ppermute | solution.py:377
  27.2 1.3 %collective-permute-start.5 = (bf16[224,1024]{1,0:T(8,128)(2,1)S(1)}, bf16[224,1024]{1,0:T(8,128)(2,1)S(1)}, u32[]{:S(2)}, u32[]{:S(2)}) collective-permute-start(bf16[224,1024]{1,0:T(8,128)(2,1)S(1)} %collective-permute-done.1.refs_5_.refs_13_), channel_id=1, source_target_pairs={{0,8},{1,9},{2,10},{3,11},{8,16},{9,17},{10,18},{11,19},{12,4},{13... | collective-permute-start | bytes 1376264 | tf_op jit(solution)/shard_map/ppermute | solution.py:377
  28.5 3.3 %collective-permute-done.6.refs_7_ = bf16[224,1024]{1,0:T(8,128)(2,1)S(1)} collective-permute-done((bf16[224,1024]{1,0:T(8,128)(2,1)S(1)}, bf16[224,1024]{1,0:T(8,128)(2,1)S(1)}, u32[]{:S(2)}, u32[]{:S(2)}) %collective-permute-start.6) | collective-permute-done | bytes 458784 | tf_op jit(solution)/shard_map/ppermute | solution.py:377
  31.8 1.3 %collective-permute-start.7 = (bf16[224,1024]{1,0:T(8,128)(2,1)S(1)}, bf16[224,1024]{1,0:T(8,128)(2,1)S(1)}, u32[]{:S(2)}, u32[]{:S(2)}) collective-permute-start(bf16[224,1024]{1,0:T(8,128)(2,1)S(1)} %collective-permute-done.6.refs_7_), channel_id=1, source_target_pairs={{128,130},{129,131},{126,124},{127,125},{256,258},{257,259},{254,2... | collective-permute-start | bytes 1376264 | tf_op jit(solution)/shard_map/ppermute | solution.py:377
  33.1 8.5 %collective-permute-start.8 = (bf16[224,1024]{1,0:T(8,128)(2,1)S(1)}, bf16[224,1024]{1,0:T(8,128)(2,1)S(1)}, u32[]{:S(2)}, u32[]{:S(2)}) collective-permute-start(bf16[224,1024]{1,0:T(8,128)(2,1)S(1)} %collective-permute-done.1.refs_5_.refs_13_), channel_id=1, source_target_pairs={{126,128},{127,129},{128,126},{129,127},{254,256},{255,257},{256,2... | collective-permute-start | bytes 1376264 | tf_op jit(solution)/shard_map/ppermute | solution.py:377
  41.6 0.0 collective-permute-done.other_ref.refs_2_
  41.6 1.1 own_scores.1
  42.7 1.0 block_scores.6
  43.7 0.0 collective-permute-done.2.refs_5_.refs_14_
  43.8 0.7 collective-permute-start.4
  44.5 1.3 %collective-permute-start.3 = (bf16[224,1024]{1,0:T(8,128)(2,1)S(1)}, bf16[224,1024]{1,0:T(8,128)(2,1)S(1)}, u32[]{:S(2)}, u32[]{:S(2)}) collective-permute-start(bf16[224,1024]{1,0:T(8,128)(2,1)S(1)} %collective-permute-done.1.refs_5_.refs_13_), channel_id=1, source_target_pairs={{4,6},{5,7},{2,0},{3,1},{12,14},{13,15},{10,8},{11,9},{20,22},{21,... | collective-permute-start | bytes 1376264 | tf_op jit(solution)/shard_map/ppermute | solution.py:377
  45.8 0.0 collective-permute-done.5.refs_5_
  45.8 1.3 %collective-permute-start.10 = (bf16[224,1024]{1,0:T(8,128)(2,1)S(1)}, bf16[224,1024]{1,0:T(8,128)(2,1)S(1)}, u32[]{:S(2)}, u32[]{:S(2)}) collective-permute-start(bf16[224,1024]{1,0:T(8,128)(2,1)S(1)} %collective-permute-done.2.refs_5_.refs_14_), channel_id=1, source_target_pairs={{0,8},{1,9},{4,12},{5,13},{8,16},{9,17},{12,20},{13,21},{10,2},{11... | collective-permute-start | bytes 1376264 | tf_op jit(solution)/shard_map/ppermute | solution.py:377
  47.1 3.8 %collective-permute-done.8.outer_ref.refs_6_ = bf16[224,1024]{1,0:T(8,128)(2,1)S(1)} collective-permute-done((bf16[224,1024]{1,0:T(8,128)(2,1)S(1)}, bf16[224,1024]{1,0:T(8,128)(2,1)S(1)}, u32[]{:S(2)}, u32[]{:S(2)}) %collective-permute-start.8) | collective-permute-done | bytes 458784 | tf_op jit(solution)/shard_map/ppermute | solution.py:377
  50.9 8.1 %collective-permute-start.9 = (bf16[224,1024]{1,0:T(8,128)(2,1)S(1)}, bf16[224,1024]{1,0:T(8,128)(2,1)S(1)}, u32[]{:S(2)}, u32[]{:S(2)}) collective-permute-start(bf16[224,1024]{1,0:T(8,128)(2,1)S(1)} %collective-permute-done.2.refs_5_.refs_14_), channel_id=1, source_target_pairs={{126,128},{127,129},{128,126},{129,127},{254,256},{255,257},{256,2... | collective-permute-start | bytes 1376264 | tf_op jit(solution)/shard_map/ppermute | solution.py:377
  59.1 0.0 collective-permute-done.7.refs_6_.inner_ref
  59.1 0.6 choose.1
  59.7 1.3 %collective-permute-start.11 = (bf16[224,1024]{1,0:T(8,128)(2,1)S(1)}, bf16[224,1024]{1,0:T(8,128)(2,1)S(1)}, u32[]{:S(2)}, u32[]{:S(2)}) collective-permute-start(bf16[224,1024]{1,0:T(8,128)(2,1)S(1)} %choose.1), channel_id=1, source_target_pairs={{128,130},{129,131},{126,124},{127,125},{130,132},{131,133},{124,1... | collective-permute-start | bytes 1376264 | tf_op jit(solution)/shard_map/ppermute | solution.py:377
  61.0 1.0 block_scores.7
  62.0 0.0 collective-permute-done.4.refs_6_
  62.0 0.0 collective-permute-done.3.refs_5_
  62.1 0.0 collective-permute-done.10.refs_5_
  62.1 0.7 collective-permute-start.13
  62.8 1.3 %collective-permute-start.12 = (bf16[224,1024]{1,0:T(8,128)(2,1)S(1)}, bf16[224,1024]{1,0:T(8,128)(2,1)S(1)}, u32[]{:S(2)}, u32[]{:S(2)}) collective-permute-start(bf16[224,1024]{1,0:T(8,128)(2,1)S(1)} %collective-permute-done.3.refs_5_), channel_id=1, source_target_pairs={{0,8},{1,9},{8,16},{9,17},{14,6},{15,7},{16,24},{17,25},{22,14},{2... | collective-permute-start | bytes 1376264 | tf_op jit(solution)/shard_map/ppermute | solution.py:377
  64.1 1.1 block_scores.8
  65.2 2.6 %collective-permute-done.9.refs_7_ = bf16[224,1024]{1,0:T(8,128)(2,1)S(1)} collective-permute-done((bf16[224,1024]{1,0:T(8,128)(2,1)S(1)}, bf16[224,1024]{1,0:T(8,128)(2,1)S(1)}, u32[]{:S(2)}, u32[]{:S(2)}) %collective-permute-start.9) | collective-permute-done | bytes 458784 | tf_op jit(solution)/shard_map/ppermute | solution.py:377
  67.8 1.1 block_scores.9
  68.9 0.0 collective-permute-done.11.refs_7_.refs_8_
  68.9 1.1 block_scores.10
  70.0 0.0 collective-permute-done.13.refs_6_
  70.0 1.1 collective-permute-done.12.refs_5_
  71.1 1.2 block_scores.11
  72.3 15.2 %all_to_all.10.pay_ref = f32[32,4,128]{2,1,0:T(4,128)S(1)} all-to-all(f32[32,4,128]{2,1,0:T(4,128)S(1)} %get-tuple-element.81), channel_id=1, replica_groups=mesh['zh'=4,'x'=4,'y'=4,'zl'=4,'core'=2] {'y','zl','core'}, dimensions={0} | all-to-all | bytes 131072 | tf_op jit(solution)/shard_map/all_to_all | solution.py:425
  87.5 0.7 denoms.1
  88.1 23.6 %all_to_all.11.refs_2_ = f32[16,4,2,128]{3,2,1,0:T(2,128)S(1)} all-to-all(f32[16,4,2,128]{3,2,1,0:T(2,128)S(1)} %get-tuple-element.83), channel_id=1, replica_groups=mesh['zh'=4,'x'=4,'y'=4,'zl'=4,'core'=2] {'zh','x'}, dimensions={0} | all-to-all | bytes 131072 | tf_op jit(solution)/shard_map/all_to_all | solution.py:427
  111.7 2.2 %unit_gradient.2 = (f32[224,1024]{1,0:T(8,128)S(1)}, f32[1,1]{1,0:T(1,128)}) custom-call(s32[4]{0:T(128)S(1)} %pad_add_fusion.ids_ref.refs_0_, f32[16,2,128]{2,1,0:T(2,128)S(1)} %get-tuple-element.99.refs_1_, f32[16,4,2,128]{3,2,1,0:T(2,128)S(1)} %all_to_all.11.refs_2_, f32[2,128]{1,0:T(2,128)S(1)} %get-tuple-element.84.refs_3_, ...), custom_call_target="tpu_custom_call" | custom-call | flops 719323136 | bytes 6291456 | tf_op jit(solution)/shard_map/unit_gradient/pallas_call | solution.py:344
  114.0 3.8 %collective-permute-start.14 = (f32[224,1024]{1,0:T(8,128)S(1)}, f32[224,1024]{1,0:T(8,128)S(1)}, u32[]{:S(2)}, u32[]{:S(2)}) collective-permute-start(f32[224,1024]{1,0:T(8,128)S(1)} %get-tuple-element.98), channel_id=1, source_target_pairs={{0,1},{1,0},{2,3},{3,2},{4,5},{5,4},{6,7},{7,6},{8,9},{9,8},{10,11... | collective-permute-start | bytes 2752520 | tf_op jit(solution)/shard_map/ppermute | solution.py:429
  117.7 1.8 %unit_gradient.3.mine_ref = f32[224,1024]{1,0:T(8,128)S(1)} custom-call(s32[4]{0:T(128)S(1)} %pad_add_fusion.ids_ref.refs_0_, f32[16,2,128]{2,1,0:T(2,128)S(1)} %get-tuple-element.99.refs_1_, f32[16,4,2,128]{3,2,1,0:T(2,128)S(1)} %all_to_all.11.refs_2_, f32[2,128]{1,0:T(2,128)S(1)} %get-tuple-element.100.refs_3_, s32[1,224]{1,0:T(1,128)S(1)} %get-tuple-element.85.refs_4_, ...), custom_call_target="tpu_custom_call" | custom-call | flops 719323136 | bytes 6291456 | tf_op jit(solution)/shard_map/unit_gradient/pallas_call | solution.py:344
  119.5 0.3 collective-permute-done.14.got_ref
  119.8 1.3 %final.1 = f32[224,1024]{1,0:T(8,128)} custom-call(f32[224,1024]{1,0:T(8,128)S(1)} %copy-done, f32[224,1024]{1,0:T(8,128)S(1)} %unit_gradient.3.mine_ref, f32[224,1024]{1,0:T(8,128)S(1)} %collective-permute-done.14.got_ref), custom_call_target="tpu_custom_call" | custom-call | flops 2293760 | bytes 3670016 | tf_op jit(solution)/shard_map/final/pallas_call | solution.py:365
  (4 shorter events, 0.0 us)
Async XLA Ops:
  0.6 1.5 %copy-start = (f32[224,1024]{1,0:T(8,128)S(1)}, f32[224,1024]{1,0:T(8,128)}, u32[]{:S(2)}) copy-start(f32[224,1024]{1,0:T(8,128)} %emb_ref.1) | copy-start | bytes 2752516
  2.2 23.1 %collective-permute-start.1 = (bf16[224,1024]{1,0:T(8,128)(2,1)S(1)}, bf16[224,1024]{1,0:T(8,128)(2,1)S(1)}, u32[]{:S(2)}, u32[]{:S(2)}) collective-permute-start(bf16[224,1024]{1,0:T(8,128)(2,1)S(1)} %divide_convert_fusion.unit_ref.refs_1_.refs_12_), channel_id=1, source_target_pairs={{0,4},{1,5},{2,0},{3,1},{4,6},{5,7},{6,2},{7,3},{8,12},{9,13},{10,... | collective-permute-start | bytes 1376264 | tf_op jit(solution)/shard_map/ppermute | solution.py:377
  8.0 23.9 %collective-permute-start.6 = (bf16[224,1024]{1,0:T(8,128)(2,1)S(1)}, bf16[224,1024]{1,0:T(8,128)(2,1)S(1)}, u32[]{:S(2)}, u32[]{:S(2)}) collective-permute-start(bf16[224,1024]{1,0:T(8,128)(2,1)S(1)} %divide_convert_fusion.unit_ref.refs_1_.refs_12_), channel_id=1, source_target_pairs={{126,128},{127,129},{128,126},{129,127},{254,256},{255,257},{256,2... | collective-permute-start | bytes 1376264 | tf_op jit(solution)/shard_map/ppermute | solution.py:377
  22.0 19.6 %copy-start.1 = (s32[224]{0:T(256)S(1)}, s32[224]{0:T(256)}, u32[]{:S(2)}) copy-start(s32[224]{0:T(256)} %param.3) | copy-start | bytes 2692
  22.0 19.6 %collective-permute-start = (bf16[224,1024]{1,0:T(8,128)(2,1)S(1)}, bf16[224,1024]{1,0:T(8,128)(2,1)S(1)}, u32[]{:S(2)}, u32[]{:S(2)}) collective-permute-start(bf16[224,1024]{1,0:T(8,128)(2,1)S(1)} %divide_convert_fusion.unit_ref.refs_1_.refs_12_), channel_id=1, source_target_pairs={{0,1},{1,0},{2,3},{3,2},{4,5},{5,4},{6,7},{7,6},{8,9},{9,8},{10,11... | collective-permute-start | bytes 1376264 | tf_op jit(solution)/shard_map/ppermute | solution.py:390
  25.3 18.5 %collective-permute-start.2 = (bf16[224,1024]{1,0:T(8,128)(2,1)S(1)}, bf16[224,1024]{1,0:T(8,128)(2,1)S(1)}, u32[]{:S(2)}, u32[]{:S(2)}) collective-permute-start(bf16[224,1024]{1,0:T(8,128)(2,1)S(1)} %divide_convert_fusion.unit_ref.refs_1_.refs_12_), channel_id=1, source_target_pairs={{2,6},{3,7},{4,0},{5,1},{0,2},{1,3},{6,4},{7,5},{10,14},{11,15},{1... | collective-permute-start | bytes 1376264 | tf_op jit(solution)/shard_map/ppermute | solution.py:377
  27.2 18.5 %collective-permute-start.5 = (bf16[224,1024]{1,0:T(8,128)(2,1)S(1)}, bf16[224,1024]{1,0:T(8,128)(2,1)S(1)}, u32[]{:S(2)}, u32[]{:S(2)}) collective-permute-start(bf16[224,1024]{1,0:T(8,128)(2,1)S(1)} %collective-permute-done.1.refs_5_.refs_13_), channel_id=1, source_target_pairs={{0,8},{1,9},{2,10},{3,11},{8,16},{9,17},{10,18},{11,19},{12,4},{13... | collective-permute-start | bytes 1376264 | tf_op jit(solution)/shard_map/ppermute | solution.py:377
  31.8 27.3 %collective-permute-start.7 = (bf16[224,1024]{1,0:T(8,128)(2,1)S(1)}, bf16[224,1024]{1,0:T(8,128)(2,1)S(1)}, u32[]{:S(2)}, u32[]{:S(2)}) collective-permute-start(bf16[224,1024]{1,0:T(8,128)(2,1)S(1)} %collective-permute-done.6.refs_7_), channel_id=1, source_target_pairs={{128,130},{129,131},{126,124},{127,125},{256,258},{257,259},{254,2... | collective-permute-start | bytes 1376264 | tf_op jit(solution)/shard_map/ppermute | solution.py:377
  33.1 17.8 %collective-permute-start.8 = (bf16[224,1024]{1,0:T(8,128)(2,1)S(1)}, bf16[224,1024]{1,0:T(8,128)(2,1)S(1)}, u32[]{:S(2)}, u32[]{:S(2)}) collective-permute-start(bf16[224,1024]{1,0:T(8,128)(2,1)S(1)} %collective-permute-done.1.refs_5_.refs_13_), channel_id=1, source_target_pairs={{126,128},{127,129},{128,126},{129,127},{254,256},{255,257},{256,2... | collective-permute-start | bytes 1376264 | tf_op jit(solution)/shard_map/ppermute | solution.py:377
  43.8 18.3 %collective-permute-start.4 = (bf16[224,1024]{1,0:T(8,128)(2,1)S(1)}, bf16[224,1024]{1,0:T(8,128)(2,1)S(1)}, u32[]{:S(2)}, u32[]{:S(2)}) collective-permute-start(bf16[224,1024]{1,0:T(8,128)(2,1)S(1)} %divide_convert_fusion.unit_ref.refs_1_.refs_12_), channel_id=1, source_target_pairs={{2,4},{3,5},{4,2},{5,3},{10,12},{11,13},{12,10},{13,11},{18,20},{1... | collective-permute-start | bytes 1376264 | tf_op jit(solution)/shard_map/ppermute | solution.py:377
  44.5 17.6 %collective-permute-start.3 = (bf16[224,1024]{1,0:T(8,128)(2,1)S(1)}, bf16[224,1024]{1,0:T(8,128)(2,1)S(1)}, u32[]{:S(2)}, u32[]{:S(2)}) collective-permute-start(bf16[224,1024]{1,0:T(8,128)(2,1)S(1)} %collective-permute-done.1.refs_5_.refs_13_), channel_id=1, source_target_pairs={{4,6},{5,7},{2,0},{3,1},{12,14},{13,15},{10,8},{11,9},{20,22},{21,... | collective-permute-start | bytes 1376264 | tf_op jit(solution)/shard_map/ppermute | solution.py:377
  45.8 16.3 %collective-permute-start.10 = (bf16[224,1024]{1,0:T(8,128)(2,1)S(1)}, bf16[224,1024]{1,0:T(8,128)(2,1)S(1)}, u32[]{:S(2)}, u32[]{:S(2)}) collective-permute-start(bf16[224,1024]{1,0:T(8,128)(2,1)S(1)} %collective-permute-done.2.refs_5_.refs_14_), channel_id=1, source_target_pairs={{0,8},{1,9},{4,12},{5,13},{8,16},{9,17},{12,20},{13,21},{10,2},{11... | collective-permute-start | bytes 1376264 | tf_op jit(solution)/shard_map/ppermute | solution.py:377
  50.9 16.9 %collective-permute-start.9 = (bf16[224,1024]{1,0:T(8,128)(2,1)S(1)}, bf16[224,1024]{1,0:T(8,128)(2,1)S(1)}, u32[]{:S(2)}, u32[]{:S(2)}) collective-permute-start(bf16[224,1024]{1,0:T(8,128)(2,1)S(1)} %collective-permute-done.2.refs_5_.refs_14_), channel_id=1, source_target_pairs={{126,128},{127,129},{128,126},{129,127},{254,256},{255,257},{256,2... | collective-permute-start | bytes 1376264 | tf_op jit(solution)/shard_map/ppermute | solution.py:377
  59.7 9.2 %collective-permute-start.11 = (bf16[224,1024]{1,0:T(8,128)(2,1)S(1)}, bf16[224,1024]{1,0:T(8,128)(2,1)S(1)}, u32[]{:S(2)}, u32[]{:S(2)}) collective-permute-start(bf16[224,1024]{1,0:T(8,128)(2,1)S(1)} %choose.1), channel_id=1, source_target_pairs={{128,130},{129,131},{126,124},{127,125},{130,132},{131,133},{124,1... | collective-permute-start | bytes 1376264 | tf_op jit(solution)/shard_map/ppermute | solution.py:377
  62.1 7.9 %collective-permute-start.13 = (bf16[224,1024]{1,0:T(8,128)(2,1)S(1)}, bf16[224,1024]{1,0:T(8,128)(2,1)S(1)}, u32[]{:S(2)}, u32[]{:S(2)}) collective-permute-start(bf16[224,1024]{1,0:T(8,128)(2,1)S(1)} %collective-permute-done.4.refs_6_), channel_id=1, source_target_pairs={{2,10},{3,11},{10,18},{11,19},{12,4},{13,5},{18,26},{19,27},{20,12... | collective-permute-start | bytes 1376264 | tf_op jit(solution)/shard_map/ppermute | solution.py:377
  62.8 8.3 %collective-permute-start.12 = (bf16[224,1024]{1,0:T(8,128)(2,1)S(1)}, bf16[224,1024]{1,0:T(8,128)(2,1)S(1)}, u32[]{:S(2)}, u32[]{:S(2)}) collective-permute-start(bf16[224,1024]{1,0:T(8,128)(2,1)S(1)} %collective-permute-done.3.refs_5_), channel_id=1, source_target_pairs={{0,8},{1,9},{8,16},{9,17},{14,6},{15,7},{16,24},{17,25},{22,14},{2... | collective-permute-start | bytes 1376264 | tf_op jit(solution)/shard_map/ppermute | solution.py:377
  114.0 5.8 %collective-permute-start.14 = (f32[224,1024]{1,0:T(8,128)S(1)}, f32[224,1024]{1,0:T(8,128)S(1)}, u32[]{:S(2)}, u32[]{:S(2)}) collective-permute-start(f32[224,1024]{1,0:T(8,128)S(1)} %get-tuple-element.98), channel_id=1, source_target_pairs={{0,1},{1,0},{2,3},{3,2},{4,5},{5,4},{6,7},{7,6},{8,9},{9,8},{10,11... | collective-permute-start | bytes 2752520 | tf_op jit(solution)/shard_map/ppermute | solution.py:429

commit v7 on v6

--- a/solution.py
+++ b/solution.py
@@ -20,25 +20,26 @@
 
 
 def routes():
-    names = ("P1", "P2", "P3a", "P3b", "Y1", "Y2", "Y3a", "Y3b", "X1", "X2", "X3", "X4", "X5")
+    names = ("P1a", "P1b", "P2", "P3a", "P3b", "Y1", "Y2", "Y3a", "Y3b", "X1", "X2", "X3", "X4", "X5")
     table = {name: [] for name in names}
 
     def chip(run, k):
         return (run % RUNS) * 4 + k
 
-    def add(name, *pairs):
+    def add(name, *pairs, cores=(0, 1)):
         for source, target in pairs:
-            for core in (0, 1):
+            for core in cores:
                 table[name].append((2 * source + core, 2 * target + core))
 
     for run in range(RUNS):
         for name, moves in (
-            ("P1", ((0, 2), (1, 0), (2, 3), (3, 1))),
             ("P2", ((1, 3), (2, 0), (0, 1), (3, 2))),
             ("P3a", ((2, 3), (1, 0))),
             ("P3b", ((1, 2), (2, 1))),
         ):
             add(name, *((chip(run, a), chip(run, b)) for a, b in moves))
+        for name, core in (("P1a", 0), ("P1b", 1)):
+            add(name, *((chip(run, a), chip(run, b)) for a, b in ((0, 2), (1, 0), (2, 3), (3, 1))), cores=(core,))
         for name, ups, downs in (
             ("Y1", (0, 1), (2, 3)),
             ("Y2", (0, 2), (1, 3)),
@@ -229,27 +230,26 @@
     return out[:2], out[2:4], block
 
 
-def choose_kernel(ids_ref, outer_ref, inner_ref, out_ref):
-    outer = (ids_ref[1] == 0) | (ids_ref[1] == 3)
-
-    @pl.when(outer)
-    def _():
-        out_ref[...] = outer_ref[...]
-
-    @pl.when(jnp.logical_not(outer))
-    def _():
-        out_ref[...] = inner_ref[...]
-
-
-def choose_call(ids, outer, inner):
+def choose_call(by_core, ids, first, second):
+    def kernel(ids_ref, first_ref, second_ref, out_ref):
+        is_first = ids_ref[2] == 0 if by_core else (ids_ref[1] == 0) | (ids_ref[1] == 3)
+
+        @pl.when(is_first)
+        def _():
+            out_ref[...] = first_ref[...]
+
+        @pl.when(jnp.logical_not(is_first))
+        def _():
+            out_ref[...] = second_ref[...]
+
     return pl.pallas_call(
-        choose_kernel,
+        kernel,
         out_shape=jax.ShapeDtypeStruct((ROWS, WIDTH), jnp.bfloat16),
         in_specs=smem(1) + vmem(2),
         out_specs=pl.BlockSpec(memory_space=pltpu.VMEM),
         compiler_params=PARAMS,
         name="choose",
-    )(ids, outer, inner)
+    )(ids, first, second)
 
 
 def denom_kernel(ids_ref, pay_ref, inv_ref, mine_ref, other_ref, post_ref):
@@ -303,7 +303,7 @@
     ids_ref, inv_ref, edge_ref, row_ref, partner_ref = refs[:5]
     expos, blocks = refs[5:12], refs[12:19]
     out_ref = refs[19]
-    if shift:
+    if not shift:
         posted = edge_ref[:, 0, 1, :]
         lane = lax.broadcasted_iota(jnp.int32, (16, 128), 1)
         total = jnp.sum(jnp.where(lane == 127, posted, 0.0), axis=0, keepdims=True)
@@ -335,7 +335,7 @@
 
 def grad_call(shift, ids, inv, edge, row, partner, expos, blocks):
     shapes = [jax.ShapeDtypeStruct((ROWS, WIDTH), jnp.float32)]
-    if shift:
+    if not shift:
         shapes.append(jax.ShapeDtypeStruct((1, 1), jnp.float32))
 
     def kernel(*refs):
@@ -385,7 +385,7 @@
     ids = jnp.stack([lax.axis_index(name) for name in DEV_AXES] + [run]).astype(jnp.int32)
     partner = partner.reshape(1, ROWS)
 
-    r1 = send(unit, "P1")
+    p1b = send(unit, "P1b")
     x1 = send(unit, "X1")
     other = lax.ppermute(after(unit, ids), ("core",), [(0, 1), (1, 0)])
     local, e_own, e_other, sum_own, sum_other, pos = own_call(ids, unit, other, partner)
@@ -401,7 +401,9 @@
             return rest
         sums = rest
 
-    r2 = send(after(unit, r1), "P2")
+    p1a = send(after(unit, sums[0]), "P1a")
+    r2 = send(after(unit, p1a, p1b), "P2")
+    r1 = choose_call(True, ids, p1a, p1b)
     y1 = send(r1, "Y1")
     x2 = send(after(x1, r1), "X2")
     x3 = send(r1, "X3")
@@ -411,7 +413,7 @@
     p3b = send(after(unit, r2), "P3b")
     p3a = send(after(r1, r2), "P3a")
     x4 = send(after(r2, x3), "X4")
-    x5 = send(choose_call(ids, x3, after(x2, r2)), "X5")
+    x5 = send(choose_call(False, ids, x3, after(x2, r2)), "X5")
     add(1, [r2])
     p3a = after(p3a, sums[0])
     p3b = after(p3b, sums[0])
@@ -425,9 +427,9 @@
     pays = lax.all_to_all(pay, DEV_AXES, 0, 0)
     inv, mine_inv, other_inv, post = denom_call(ids, pays)
     posts = lax.all_to_all(post, ("zh", "x"), 0, 0)
-    for_other, loss = grad_call(ROWS, ids, inv, posts, other_inv, local, [e[1] for e in expos], blocks)
+    (for_other,) = grad_call(ROWS, ids, inv, posts, other_inv, local, [e[1] for e in expos], blocks)
     got = lax.ppermute(for_other, ("core",), [(0, 1), (1, 0)])
-    (mine,) = grad_call(0, ids, after(inv, for_other), posts, mine_inv, local, [e[0] for e in expos], blocks)
+    mine, loss = grad_call(0, ids, after(inv, for_other), posts, mine_inv, local, [e[0] for e in expos], blocks)
     grad = final_call(embeddings, mine, got)
     loss = loss.reshape(())
     return (loss, grad)

time: 122 us -> 119 us (0.975)
  waiting for transfers between devices: 11.2 us -> 2.24 us
  blocking collectives: 38.8 us -> 43.3 us
    ppermute x13 -> x14, waiting for transfers between devices: 10.8 us -> 2.23 us  [send(): return lax.ppermute(value, AXES, ROUTES[name])]
    ppermute x1, starting transfers between devices: 3.27 us -> 8.91 us  [per_device(): other = lax.ppermute(after(unit, ids), ('core',), [(0, 1), (1, 0)])]
    all_to_all x1, blocking collectives: 15.2 us -> 20.2 us  [per_device(): pays = lax.all_to_all(pay, DEV_AXES, 0, 0)]
    ppermute x13 -> x14, starting transfers between devices: 47.5 us -> 42.7 us  [send(): return lax.ppermute(value, AXES, ROUTES[name])]
  transfers between devices with their start and end apart: 15 -> 16, of which waited for: 5 -> 4; matrix products, arithmetic and copies ran while one was open for 0% -> 0% of each run, Pallas kernels for 7% -> 8%
where the time goes in v7:
time: 119 us; the launch traced here: 118 us
  starting transfers between devices  55.4 us (47%)
  blocking collectives  43.3 us (36%)
  Pallas kernels  14.7 us (12%)
  waiting for transfers between devices  2.24 us (2%)
  other arithmetic  1.62 us (1%)
    ppermute x14, starting transfers between devices, send(): return lax.ppermute(value, AXES, ROUTES[name])  42.7 us
    all_to_all x1, blocking collectives, per_device(): posts = lax.all_to_all(post, ('zh', 'x'), 0, 0)  23.2 us
    all_to_all x1, blocking collectives, per_device(): pays = lax.all_to_all(pay, DEV_AXES, 0, 0)  20.2 us
    ppermute x1, starting transfers between devices, per_device(): other = lax.ppermute(after(unit, ids), ('core',), [(0, 1), (1, 0)])  8.91 us
    pallas_call x6, Pallas kernels, block_call(): pl.pallas_call(kernel, out_shape=tuple(shapes), in_specs=smem(1) + vmem(l...  6.46 us
    pallas_call x2, Pallas kernels, grad_call(): pl.pallas_call(kernel, out_shape=tuple(shapes), in_specs=smem(1) + vmem(1...  3.97 us
    ppermute x1, starting transfers between devices, per_device(): got = lax.ppermute(for_other, ('core',), [(0, 1), (1, 0)])  3.78 us
  transfers between devices with their start and end apart: 16, of which 4 were waited for; matrix products, arithmetic and copies ran while one was open for 0% of the time, Pallas kernels for 8%

profile of v7, /device:TPU:1, one launch (start us, length us, event | category | flops | bytes accessed | tf_op | source)
XLA Modules:
  0.0 118.2 jit_solution(8333354022388575086)
XLA Ops:
  0.6 1.4 %multiply_reduce_fusion = f32[224]{0:T(256)S(1)} fusion(f32[224,1024]{1,0:T(8,128)} %emb_ref.1), kind=kLoop, calls=%fused_computation.1 | loop fusion | flops 458528 | bytes 918400 | tf_op jit(solution)/shard_map/reduce_sum | solution.py:381
  2.1 0.0 copy-done
  2.1 0.1 divide_convert_fusion.unit_ref.refs_1_.refs_12_
  2.2 0.1 pad_add_fusion.ids_ref.refs_0_
  2.3 8.9 %collective-permute-start = (bf16[224,1024]{1,0:T(8,128)(2,1)S(1)}, bf16[224,1024]{1,0:T(8,128)(2,1)S(1)}, u32[]{:S(2)}, u32[]{:S(2)}) collective-permute-start(bf16[224,1024]{1,0:T(8,128)(2,1)S(1)} %divide_convert_fusion.unit_ref.refs_1_.refs_12_), channel_id=1, source_target_pairs={{0,1},{1,0},{2,3},{3,2},{4,5},{5,4},{6,7},{7,6},{8,9},{9,8},{10,11... | collective-permute-start | bytes 1376264 | tf_op jit(solution)/shard_map/ppermute | solution.py:390
  11.2 1.9 %collective-permute-start.2 = (bf16[224,1024]{1,0:T(8,128)(2,1)S(1)}, bf16[224,1024]{1,0:T(8,128)(2,1)S(1)}, u32[]{:S(2)}, u32[]{:S(2)}) collective-permute-start(bf16[224,1024]{1,0:T(8,128)(2,1)S(1)} %divide_convert_fusion.unit_ref.refs_1_.refs_12_), channel_id=1, source_target_pairs={{1,5},{3,1},{5,7},{7,3},{9,13},{11,9},{13,15},{15,11},{17,21},{19,... | collective-permute-start | bytes 1376264 | tf_op jit(solution)/shard_map/ppermute | solution.py:377
  13.2 0.0 collective-permute-done.other_ref.refs_2_
  13.2 1.0 own_scores.1
  14.2 0.7 collective-permute-start.1
  14.9 11.6 %collective-permute-start.7 = (bf16[224,1024]{1,0:T(8,128)(2,1)S(1)}, bf16[224,1024]{1,0:T(8,128)(2,1)S(1)}, u32[]{:S(2)}, u32[]{:S(2)}) collective-permute-start(bf16[224,1024]{1,0:T(8,128)(2,1)S(1)} %divide_convert_fusion.unit_ref.refs_1_.refs_12_), channel_id=1, source_target_pairs={{126,128},{127,129},{128,126},{129,127},{254,256},{255,257},{256,2... | collective-permute-start | bytes 1376264 | tf_op jit(solution)/shard_map/ppermute | solution.py:377
  26.5 0.0 collective-permute-done.2.second_ref
  26.5 0.0 collective-permute-done.1.first_ref
  26.5 1.9 %collective-permute-start.3 = (bf16[224,1024]{1,0:T(8,128)(2,1)S(1)}, bf16[224,1024]{1,0:T(8,128)(2,1)S(1)}, u32[]{:S(2)}, u32[]{:S(2)}) collective-permute-start(bf16[224,1024]{1,0:T(8,128)(2,1)S(1)} %divide_convert_fusion.unit_ref.refs_1_.refs_12_), channel_id=1, source_target_pairs={{2,6},{3,7},{4,0},{5,1},{0,2},{1,3},{6,4},{7,5},{10,14},{11,15},{1... | collective-permute-start | bytes 1376264 | tf_op jit(solution)/shard_map/ppermute | solution.py:377
  28.5 0.6 choose.2.refs_5_.refs_13_
  29.0 1.3 %collective-permute-start.6 = (bf16[224,1024]{1,0:T(8,128)(2,1)S(1)}, bf16[224,1024]{1,0:T(8,128)(2,1)S(1)}, u32[]{:S(2)}, u32[]{:S(2)}) collective-permute-start(bf16[224,1024]{1,0:T(8,128)(2,1)S(1)} %choose.2.refs_5_.refs_13_), channel_id=1, source_target_pairs={{0,8},{1,9},{2,10},{3,11},{8,16},{9,17},{10,18},{11,19},{12,4},{13... | collective-permute-start | bytes 1376264 | tf_op jit(solution)/shard_map/ppermute | solution.py:377
  30.4 8.8 %collective-permute-start.9 = (bf16[224,1024]{1,0:T(8,128)(2,1)S(1)}, bf16[224,1024]{1,0:T(8,128)(2,1)S(1)}, u32[]{:S(2)}, u32[]{:S(2)}) collective-permute-start(bf16[224,1024]{1,0:T(8,128)(2,1)S(1)} %choose.2.refs_5_.refs_13_), channel_id=1, source_target_pairs={{126,128},{127,129},{128,126},{129,127},{254,256},{255,257},{256,2... | collective-permute-start | bytes 1376264 | tf_op jit(solution)/shard_map/ppermute | solution.py:377
  39.2 1.3 %collective-permute-start.8 = (bf16[224,1024]{1,0:T(8,128)(2,1)S(1)}, bf16[224,1024]{1,0:T(8,128)(2,1)S(1)}, u32[]{:S(2)}, u32[]{:S(2)}) collective-permute-start(bf16[224,1024]{1,0:T(8,128)(2,1)S(1)} %collective-permute-done.7.refs_7_), channel_id=1, source_target_pairs={{128,130},{129,131},{126,124},{127,125},{256,258},{257,259},{254,2... | collective-permute-start | bytes 1376264 | tf_op jit(solution)/shard_map/ppermute | solution.py:377
  40.6 1.0 block_scores.6
  41.6 0.0 collective-permute-done.3.refs_5_.refs_14_
  41.6 1.3 %collective-permute-start.4 = (bf16[224,1024]{1,0:T(8,128)(2,1)S(1)}, bf16[224,1024]{1,0:T(8,128)(2,1)S(1)}, u32[]{:S(2)}, u32[]{:S(2)}) collective-permute-start(bf16[224,1024]{1,0:T(8,128)(2,1)S(1)} %choose.2.refs_5_.refs_13_), channel_id=1, source_target_pairs={{4,6},{5,7},{2,0},{3,1},{12,14},{13,15},{10,8},{11,9},{20,22},{21,... | collective-permute-start | bytes 1376264 | tf_op jit(solution)/shard_map/ppermute | solution.py:377
  42.9 0.7 collective-permute-start.5
  43.6 0.0 collective-permute-done.6.refs_5_
  43.6 1.3 %collective-permute-start.11 = (bf16[224,1024]{1,0:T(8,128)(2,1)S(1)}, bf16[224,1024]{1,0:T(8,128)(2,1)S(1)}, u32[]{:S(2)}, u32[]{:S(2)}) collective-permute-start(bf16[224,1024]{1,0:T(8,128)(2,1)S(1)} %collective-permute-done.3.refs_5_.refs_14_), channel_id=1, source_target_pairs={{0,8},{1,9},{4,12},{5,13},{8,16},{9,17},{12,20},{13,21},{10,2},{11... | collective-permute-start | bytes 1376264 | tf_op jit(solution)/shard_map/ppermute | solution.py:377
  44.9 0.8 collective-permute-done.9.first_ref.refs_6_
  45.7 8.5 %collective-permute-start.10 = (bf16[224,1024]{1,0:T(8,128)(2,1)S(1)}, bf16[224,1024]{1,0:T(8,128)(2,1)S(1)}, u32[]{:S(2)}, u32[]{:S(2)}) collective-permute-start(bf16[224,1024]{1,0:T(8,128)(2,1)S(1)} %collective-permute-done.3.refs_5_.refs_14_), channel_id=1, source_target_pairs={{126,128},{127,129},{128,126},{129,127},{254,256},{255,257},{256,2... | collective-permute-start | bytes 1376264 | tf_op jit(solution)/shard_map/ppermute | solution.py:377
  54.2 0.0 collective-permute-done.8.refs_6_.second_ref
  54.2 0.6 choose.3
  54.8 1.3 %collective-permute-start.12 = (bf16[224,1024]{1,0:T(8,128)(2,1)S(1)}, bf16[224,1024]{1,0:T(8,128)(2,1)S(1)}, u32[]{:S(2)}, u32[]{:S(2)}) collective-permute-start(bf16[224,1024]{1,0:T(8,128)(2,1)S(1)} %choose.3), channel_id=1, source_target_pairs={{128,130},{129,131},{126,124},{127,125},{130,132},{131,133},{124,1... | collective-permute-start | bytes 1376264 | tf_op jit(solution)/shard_map/ppermute | solution.py:377
  56.1 1.0 block_scores.7
  57.2 0.0 collective-permute-done.4.refs_5_
  57.2 0.0 collective-permute-done.5.refs_6_
  57.2 1.3 %collective-permute-start.13 = (bf16[224,1024]{1,0:T(8,128)(2,1)S(1)}, bf16[224,1024]{1,0:T(8,128)(2,1)S(1)}, u32[]{:S(2)}, u32[]{:S(2)}) collective-permute-start(bf16[224,1024]{1,0:T(8,128)(2,1)S(1)} %collective-permute-done.4.refs_5_), channel_id=1, source_target_pairs={{0,8},{1,9},{8,16},{9,17},{14,6},{15,7},{16,24},{17,25},{22,14},{2... | collective-permute-start | bytes 1376264 | tf_op jit(solution)/shard_map/ppermute | solution.py:377
  58.5 0.7 collective-permute-start.14
  59.2 1.1 block_scores.8
  60.3 0.1 collective-permute-done.10.refs_7_
  60.3 1.1 block_scores.9
  61.4 0.1 collective-permute-done.12.refs_7_.refs_8_
  61.5 1.1 block_scores.10
  62.6 1.3 %collective-permute-done.13.refs_5_ = bf16[224,1024]{1,0:T(8,128)(2,1)S(1)} collective-permute-done((bf16[224,1024]{1,0:T(8,128)(2,1)S(1)}, bf16[224,1024]{1,0:T(8,128)(2,1)S(1)}, u32[]{:S(2)}, u32[]{:S(2)}) %collective-permute-start.13) | collective-permute-done | bytes 458784 | tf_op jit(solution)/shard_map/ppermute | solution.py:377
  63.9 1.2 %block_scores.11 = (f32[224,224]{1,0:T(8,128)S(1)}, f32[224,224]{1,0:T(8,128)S(1)}, f32[32,4,128]{2,1,0:T(4,128)S(1)}, bf16[224,1024]{1,0:T(8,128)(2,1)S(1)}) custom-call(s32[4]{0:T(128)S(1)} %pad_add_fusion.ids_ref.refs_0_, bf16[224,1024]{1,0:T(8,128)(2,1)S(1)} %divide_convert_fusion.unit_ref.refs_1_.refs_12_, ...), custom_call_target="tpu_custom_call" | custom-call | flops 205520896 | bytes 2097152 | tf_op jit(solution)/shard_map/block_scores/pallas_call | solution.py:218
  65.1 20.2 %all_to_all.10.pay_ref = f32[32,4,128]{2,1,0:T(4,128)S(1)} all-to-all(f32[32,4,128]{2,1,0:T(4,128)S(1)} %get-tuple-element.83), channel_id=1, replica_groups=mesh['zh'=4,'x'=4,'y'=4,'zl'=4,'core'=2] {'y','zl','core'}, dimensions={0} | all-to-all | bytes 131072 | tf_op jit(solution)/shard_map/all_to_all | solution.py:427
  85.3 0.7 denoms.1
  86.0 23.2 %all_to_all.11.refs_2_ = f32[16,4,2,128]{3,2,1,0:T(2,128)S(1)} all-to-all(f32[16,4,2,128]{3,2,1,0:T(2,128)S(1)} %get-tuple-element.85), channel_id=1, replica_groups=mesh['zh'=4,'x'=4,'y'=4,'zl'=4,'core'=2] {'zh','x'}, dimensions={0} | all-to-all | bytes 131072 | tf_op jit(solution)/shard_map/all_to_all | solution.py:429
  109.1 1.7 %unit_gradient.2 = f32[224,1024]{1,0:T(8,128)S(1)} custom-call(s32[4]{0:T(128)S(1)} %pad_add_fusion.ids_ref.refs_0_, f32[16,2,128]{2,1,0:T(2,128)S(1)} %get-tuple-element.99.refs_1_, f32[16,4,2,128]{3,2,1,0:T(2,128)S(1)} %all_to_all.11.refs_2_, f32[2,128]{1,0:T(2,128)S(1)} %get-tuple-element.86.refs_3_, s32[1,224]{1,0:T(1,128)S(1)} %get-tuple-element.87.refs_4_, ...), custom_call_target="tpu_custom_call" | custom-call | flops 719323136 | bytes 6291456 | tf_op jit(solution)/shard_map/unit_gradient/pallas_call | solution.py:344
  110.9 3.8 %collective-permute-start.15 = (f32[224,1024]{1,0:T(8,128)S(1)}, f32[224,1024]{1,0:T(8,128)S(1)}, u32[]{:S(2)}, u32[]{:S(2)}) collective-permute-start(f32[224,1024]{1,0:T(8,128)S(1)} %unit_gradient.2), channel_id=1, source_target_pairs={{0,1},{1,0},{2,3},{3,2},{4,5},{5,4},{6,7},{7,6},{8,9},{9,8},{10,11... | collective-permute-start | bytes 2752520 | tf_op jit(solution)/shard_map/ppermute | solution.py:431
  114.7 2.2 %unit_gradient.3 = (f32[224,1024]{1,0:T(8,128)S(1)}, f32[1,1]{1,0:T(1,128)}) custom-call(s32[4]{0:T(128)S(1)} %pad_add_fusion.ids_ref.refs_0_, f32[16,2,128]{2,1,0:T(2,128)S(1)} %get-tuple-element.99.refs_1_, f32[16,4,2,128]{3,2,1,0:T(2,128)S(1)} %all_to_all.11.refs_2_, f32[2,128]{1,0:T(2,128)S(1)} %get-tuple-element.100.refs_3_, ...), custom_call_target="tpu_custom_call" | custom-call | flops 719323136 | bytes 6291456 | tf_op jit(solution)/shard_map/unit_gradient/pallas_call | solution.py:344
  116.9 0.0 collective-permute-done.15.got_ref
  116.9 1.3 %final.1 = f32[224,1024]{1,0:T(8,128)} custom-call(f32[224,1024]{1,0:T(8,128)S(1)} %copy-done, f32[224,1024]{1,0:T(8,128)S(1)} %get-tuple-element.109.mine_ref, f32[224,1024]{1,0:T(8,128)S(1)} %collective-permute-done.15.got_ref), custom_call_target="tpu_custom_call" | custom-call | flops 2293760 | bytes 3670016 | tf_op jit(solution)/shard_map/final/pallas_call | solution.py:365
  (7 shorter events, 0.0 us)
Async XLA Ops:
  0.6 1.5 %copy-start = (f32[224,1024]{1,0:T(8,128)S(1)}, f32[224,1024]{1,0:T(8,128)}, u32[]{:S(2)}) copy-start(f32[224,1024]{1,0:T(8,128)} %emb_ref.1) | copy-start | bytes 2752516
  2.3 10.9 %copy-start.1 = (s32[224]{0:T(256)S(1)}, s32[224]{0:T(256)}, u32[]{:S(2)}) copy-start(s32[224]{0:T(256)} %param.3) | copy-start | bytes 2692
  2.3 10.8 %collective-permute-start = (bf16[224,1024]{1,0:T(8,128)(2,1)S(1)}, bf16[224,1024]{1,0:T(8,128)(2,1)S(1)}, u32[]{:S(2)}, u32[]{:S(2)}) collective-permute-start(bf16[224,1024]{1,0:T(8,128)(2,1)S(1)} %divide_convert_fusion.unit_ref.refs_1_.refs_12_), channel_id=1, source_target_pairs={{0,1},{1,0},{2,3},{3,2},{4,5},{5,4},{6,7},{7,6},{8,9},{9,8},{10,11... | collective-permute-start | bytes 1376264 | tf_op jit(solution)/shard_map/ppermute | solution.py:390
  11.2 15.3 %collective-permute-start.2 = (bf16[224,1024]{1,0:T(8,128)(2,1)S(1)}, bf16[224,1024]{1,0:T(8,128)(2,1)S(1)}, u32[]{:S(2)}, u32[]{:S(2)}) collective-permute-start(bf16[224,1024]{1,0:T(8,128)(2,1)S(1)} %divide_convert_fusion.unit_ref.refs_1_.refs_12_), channel_id=1, source_target_pairs={{1,5},{3,1},{5,7},{7,3},{9,13},{11,9},{13,15},{15,11},{17,21},{19,... | collective-permute-start | bytes 1376264 | tf_op jit(solution)/shard_map/ppermute | solution.py:377
  14.2 12.3 %collective-permute-start.1 = (bf16[224,1024]{1,0:T(8,128)(2,1)S(1)}, bf16[224,1024]{1,0:T(8,128)(2,1)S(1)}, u32[]{:S(2)}, u32[]{:S(2)}) collective-permute-start(bf16[224,1024]{1,0:T(8,128)(2,1)S(1)} %divide_convert_fusion.unit_ref.refs_1_.refs_12_), channel_id=1, source_target_pairs={{0,4},{2,0},{4,6},{6,2},{8,12},{10,8},{12,14},{14,10},{16,20},{18,... | collective-permute-start | bytes 1376264 | tf_op jit(solution)/shard_map/ppermute | solution.py:377
  14.9 24.3 %collective-permute-start.7 = (bf16[224,1024]{1,0:T(8,128)(2,1)S(1)}, bf16[224,1024]{1,0:T(8,128)(2,1)S(1)}, u32[]{:S(2)}, u32[]{:S(2)}) collective-permute-start(bf16[224,1024]{1,0:T(8,128)(2,1)S(1)} %divide_convert_fusion.unit_ref.refs_1_.refs_12_), channel_id=1, source_target_pairs={{126,128},{127,129},{128,126},{129,127},{254,256},{255,257},{256,2... | collective-permute-start | bytes 1376264 | tf_op jit(solution)/shard_map/ppermute | solution.py:377
  26.5 15.1 %collective-permute-start.3 = (bf16[224,1024]{1,0:T(8,128)(2,1)S(1)}, bf16[224,1024]{1,0:T(8,128)(2,1)S(1)}, u32[]{:S(2)}, u32[]{:S(2)}) collective-permute-start(bf16[224,1024]{1,0:T(8,128)(2,1)S(1)} %divide_convert_fusion.unit_ref.refs_1_.refs_12_), channel_id=1, source_target_pairs={{2,6},{3,7},{4,0},{5,1},{0,2},{1,3},{6,4},{7,5},{10,14},{11,15},{1... | collective-permute-start | bytes 1376264 | tf_op jit(solution)/shard_map/ppermute | solution.py:377
  29.0 14.5 %collective-permute-start.6 = (bf16[224,1024]{1,0:T(8,128)(2,1)S(1)}, bf16[224,1024]{1,0:T(8,128)(2,1)S(1)}, u32[]{:S(2)}, u32[]{:S(2)}) collective-permute-start(bf16[224,1024]{1,0:T(8,128)(2,1)S(1)} %choose.2.refs_5_.refs_13_), channel_id=1, source_target_pairs={{0,8},{1,9},{2,10},{3,11},{8,16},{9,17},{10,18},{11,19},{12,4},{13... | collective-permute-start | bytes 1376264 | tf_op jit(solution)/shard_map/ppermute | solution.py:377
  30.4 15.3 %collective-permute-start.9 = (bf16[224,1024]{1,0:T(8,128)(2,1)S(1)}, bf16[224,1024]{1,0:T(8,128)(2,1)S(1)}, u32[]{:S(2)}, u32[]{:S(2)}) collective-permute-start(bf16[224,1024]{1,0:T(8,128)(2,1)S(1)} %choose.2.refs_5_.refs_13_), channel_id=1, source_target_pairs={{126,128},{127,129},{128,126},{129,127},{254,256},{255,257},{256,2... | collective-permute-start | bytes 1376264 | tf_op jit(solution)/shard_map/ppermute | solution.py:377
  39.2 15.0 %collective-permute-start.8 = (bf16[224,1024]{1,0:T(8,128)(2,1)S(1)}, bf16[224,1024]{1,0:T(8,128)(2,1)S(1)}, u32[]{:S(2)}, u32[]{:S(2)}) collective-permute-start(bf16[224,1024]{1,0:T(8,128)(2,1)S(1)} %collective-permute-done.7.refs_7_), channel_id=1, source_target_pairs={{128,130},{129,131},{126,124},{127,125},{256,258},{257,259},{254,2... | collective-permute-start | bytes 1376264 | tf_op jit(solution)/shard_map/ppermute | solution.py:377
  41.6 15.6 %collective-permute-start.4 = (bf16[224,1024]{1,0:T(8,128)(2,1)S(1)}, bf16[224,1024]{1,0:T(8,128)(2,1)S(1)}, u32[]{:S(2)}, u32[]{:S(2)}) collective-permute-start(bf16[224,1024]{1,0:T(8,128)(2,1)S(1)} %choose.2.refs_5_.refs_13_), channel_id=1, source_target_pairs={{4,6},{5,7},{2,0},{3,1},{12,14},{13,15},{10,8},{11,9},{20,22},{21,... | collective-permute-start | bytes 1376264 | tf_op jit(solution)/shard_map/ppermute | solution.py:377
  42.9 14.3 %collective-permute-start.5 = (bf16[224,1024]{1,0:T(8,128)(2,1)S(1)}, bf16[224,1024]{1,0:T(8,128)(2,1)S(1)}, u32[]{:S(2)}, u32[]{:S(2)}) collective-permute-start(bf16[224,1024]{1,0:T(8,128)(2,1)S(1)} %divide_convert_fusion.unit_ref.refs_1_.refs_12_), channel_id=1, source_target_pairs={{2,4},{3,5},{4,2},{5,3},{10,12},{11,13},{12,10},{13,11},{18,20},{1... | collective-permute-start | bytes 1376264 | tf_op jit(solution)/shard_map/ppermute | solution.py:377
  43.6 13.6 %collective-permute-start.11 = (bf16[224,1024]{1,0:T(8,128)(2,1)S(1)}, bf16[224,1024]{1,0:T(8,128)(2,1)S(1)}, u32[]{:S(2)}, u32[]{:S(2)}) collective-permute-start(bf16[224,1024]{1,0:T(8,128)(2,1)S(1)} %collective-permute-done.3.refs_5_.refs_14_), channel_id=1, source_target_pairs={{0,8},{1,9},{4,12},{5,13},{8,16},{9,17},{12,20},{13,21},{10,2},{11... | collective-permute-start | bytes 1376264 | tf_op jit(solution)/shard_map/ppermute | solution.py:377
  45.7 14.6 %collective-permute-start.10 = (bf16[224,1024]{1,0:T(8,128)(2,1)S(1)}, bf16[224,1024]{1,0:T(8,128)(2,1)S(1)}, u32[]{:S(2)}, u32[]{:S(2)}) collective-permute-start(bf16[224,1024]{1,0:T(8,128)(2,1)S(1)} %collective-permute-done.3.refs_5_.refs_14_), channel_id=1, source_target_pairs={{126,128},{127,129},{128,126},{129,127},{254,256},{255,257},{256,2... | collective-permute-start | bytes 1376264 | tf_op jit(solution)/shard_map/ppermute | solution.py:377
  54.8 6.7 %collective-permute-start.12 = (bf16[224,1024]{1,0:T(8,128)(2,1)S(1)}, bf16[224,1024]{1,0:T(8,128)(2,1)S(1)}, u32[]{:S(2)}, u32[]{:S(2)}) collective-permute-start(bf16[224,1024]{1,0:T(8,128)(2,1)S(1)} %choose.3), channel_id=1, source_target_pairs={{128,130},{129,131},{126,124},{127,125},{130,132},{131,133},{124,1... | collective-permute-start | bytes 1376264 | tf_op jit(solution)/shard_map/ppermute | solution.py:377
  57.2 6.7 %collective-permute-start.13 = (bf16[224,1024]{1,0:T(8,128)(2,1)S(1)}, bf16[224,1024]{1,0:T(8,128)(2,1)S(1)}, u32[]{:S(2)}, u32[]{:S(2)}) collective-permute-start(bf16[224,1024]{1,0:T(8,128)(2,1)S(1)} %collective-permute-done.4.refs_5_), channel_id=1, source_target_pairs={{0,8},{1,9},{8,16},{9,17},{14,6},{15,7},{16,24},{17,25},{22,14},{2... | collective-permute-start | bytes 1376264 | tf_op jit(solution)/shard_map/ppermute | solution.py:377
  58.5 5.4 %collective-permute-start.14 = (bf16[224,1024]{1,0:T(8,128)(2,1)S(1)}, bf16[224,1024]{1,0:T(8,128)(2,1)S(1)}, u32[]{:S(2)}, u32[]{:S(2)}) collective-permute-start(bf16[224,1024]{1,0:T(8,128)(2,1)S(1)} %collective-permute-done.5.refs_6_), channel_id=1, source_target_pairs={{2,10},{3,11},{10,18},{11,19},{12,4},{13,5},{18,26},{19,27},{20,12... | collective-permute-start | bytes 1376264 | tf_op jit(solution)/shard_map/ppermute | solution.py:377
  110.9 6.0 %collective-permute-start.15 = (f32[224,1024]{1,0:T(8,128)S(1)}, f32[224,1024]{1,0:T(8,128)S(1)}, u32[]{:S(2)}, u32[]{:S(2)}) collective-permute-start(f32[224,1024]{1,0:T(8,128)S(1)} %unit_gradient.2), channel_id=1, source_target_pairs={{0,1},{1,0},{2,3},{3,2},{4,5},{5,4},{6,7},{7,6},{8,9},{9,8},{10,11... | collective-permute-start | bytes 2752520 | tf_op jit(solution)/shard_map/ppermute | solution.py:431

commit v8 on v7

--- a/solution.py
+++ b/solution.py
@@ -88,45 +88,63 @@
     return values[:, :128] + tail
 
 
-def own_kernel(ids_ref, unit_ref, other_ref, partner_ref, local_ref, e_own_ref, e_other_ref, sum_own_ref, sum_other_ref, pos_ref):
+def own_kernel(ids_ref, unit_ref, partner_ref, local_ref, expo_ref, sum_ref, pos_ref):
     unit = unit_ref[...]
     row = lax.broadcasted_iota(jnp.int32, (ROWS, ROWS), 0)
     column = lax.broadcasted_iota(jnp.int32, (ROWS, ROWS), 1)
-    shift = ids_ref[2] * ROWS
-    partner = partner_ref[...] - (ids_ref[3] * (8 * ROWS) + ids_ref[1] * (2 * ROWS) + shift)
+    partner = partner_ref[...] - (ids_ref[3] * (8 * ROWS) + ids_ref[1] * (2 * ROWS) + ids_ref[2] * ROWS)
     partner = jnp.where(partner < 0, partner + 2 * ROWS, partner)
     local_ref[...] = partner
     logits = scores(unit, unit) / SOFTMAX_TEMPER
     expo = jnp.where(row == column, 0.0, jnp.exp(logits - 1.0 / SOFTMAX_TEMPER))
-    e_own_ref[...] = expo
-    sum_own_ref[...] = fold(expo)
-    picked = jnp.where(partner == row, logits, 0.0)
-    logits = scores(other_ref[...], unit) / SOFTMAX_TEMPER
-    expo = jnp.exp(logits - 1.0 / SOFTMAX_TEMPER)
-    e_other_ref[...] = expo
-    sum_other_ref[...] = fold(expo)
-    picked = picked + jnp.where(partner == row + ROWS, logits, 0.0)
-    pos_ref[...] = jnp.sum(fold(picked), axis=0, keepdims=True)
-
-
-def own_call(ids, unit, other, partner):
+    expo_ref[...] = expo
+    sum_ref[...] = fold(expo)
+    pos_ref[...] = jnp.sum(fold(jnp.where(partner == row, logits, 0.0)), axis=0, keepdims=True)
+
+
+def own_call(ids, unit, partner):
     f32 = jnp.float32
     return pl.pallas_call(
         own_kernel,
         out_shape=(
             jax.ShapeDtypeStruct((1, ROWS), jnp.int32),
             jax.ShapeDtypeStruct((ROWS, ROWS), f32),
-            jax.ShapeDtypeStruct((ROWS, ROWS), f32),
-            jax.ShapeDtypeStruct((ROWS, 128), f32),
             jax.ShapeDtypeStruct((ROWS, 128), f32),
             jax.ShapeDtypeStruct((1, 128), f32),
         ),
-        in_specs=smem(1) + vmem(3),
-        out_specs=tuple(vmem(6)),
-        compiler_params=PARAMS,
-        cost_estimate=pl.CostEstimate(flops=2 * 448 * ROWS * WIDTH, bytes_accessed=2 << 20, transcendentals=448 * ROWS),
+        in_specs=smem(1) + vmem(2),
+        out_specs=tuple(vmem(4)),
+        compiler_params=PARAMS,
+        cost_estimate=pl.CostEstimate(flops=2 * ROWS * ROWS * WIDTH, bytes_accessed=1 << 20, transcendentals=ROWS * ROWS),
         name="own_scores",
-    )(ids, unit, other, partner)
+    )(ids, unit, partner)
+
+
+def other_kernel(unit_ref, other_ref, local_ref, pos_in_ref, expo_ref, sum_ref, pos_ref):
+    row = lax.broadcasted_iota(jnp.int32, (ROWS, ROWS), 0) + ROWS
+    logits = scores(other_ref[...], unit_ref[...]) / SOFTMAX_TEMPER
+    expo = jnp.exp(logits - 1.0 / SOFTMAX_TEMPER)
+    expo_ref[...] = expo
+    sum_ref[...] = fold(expo)
+    picked = jnp.where(local_ref[...] == row, logits, 0.0)
+    pos_ref[...] = pos_in_ref[...] + jnp.sum(fold(picked), axis=0, keepdims=True)
+
+
+def other_call(unit, other, local, pos):
+    f32 = jnp.float32
+    return pl.pallas_call(
+        other_kernel,
+        out_shape=(
+            jax.ShapeDtypeStruct((ROWS, ROWS), f32),
+            jax.ShapeDtypeStruct((ROWS, 128), f32),
+            jax.ShapeDtypeStruct((1, 128), f32),
+        ),
+        in_specs=vmem(4),
+        out_specs=tuple(vmem(3)),
+        compiler_params=PARAMS,
+        cost_estimate=pl.CostEstimate(flops=2 * ROWS * ROWS * WIDTH, bytes_accessed=1 << 20, transcendentals=ROWS * ROWS),
+        name="other_scores",
+    )(unit, other, local, pos)
 
 
 def received(number, k):
@@ -387,8 +405,10 @@
 
     p1b = send(unit, "P1b")
     x1 = send(unit, "X1")
-    other = lax.ppermute(after(unit, ids), ("core",), [(0, 1), (1, 0)])
-    local, e_own, e_other, sum_own, sum_other, pos = own_call(ids, unit, other, partner)
+    local, e_own, sum_own, pos = own_call(ids, unit, partner)
+    p1a = send(after(unit, sum_own), "P1a")
+    other = lax.ppermute(after(unit, p1b), ("core",), [(0, 1), (1, 0)])
+    e_other, sum_other, pos = other_call(unit, other, local, pos)
     expos, blocks, sums = [(e_own, e_other)] + [None] * 6, [unit] + [None] * 6, (sum_own, sum_other)
 
     def add(number, cands):
@@ -401,7 +421,6 @@
             return rest
         sums = rest
 
-    p1a = send(after(unit, sums[0]), "P1a")
     r2 = send(after(unit, p1a, p1b), "P2")
     r1 = choose_call(True, ids, p1a, p1b)
     y1 = send(r1, "Y1")

time: 119 us -> 119 us (level)
  waiting for transfers between devices: 2.24 us -> 13.6 us
  blocking collectives: 43.3 us -> 37.1 us
  starting transfers between devices: 55.4 us -> 50 us
    ppermute x14, waiting for transfers between devices: 2.23 us -> 13.6 us  [send(): return lax.ppermute(value, AXES, ROUTES[name])]
    all_to_all x1, blocking collectives: 20.2 us -> 14.4 us  [per_device(): pays = lax.all_to_all(pay, DEV_AXES, 0, 0)]
    ppermute x1, starting transfers between devices: 8.91 us -> 3.14 us  [per_device(): other = lax.ppermute(after(unit, p1b), ('core',), [(0, 1), (1, 0)])]
  transfers between devices with their start and end apart: 16 -> 16, of which waited for: 4 -> 3; matrix products, arithmetic and copies ran while one was open for 0% -> 0% of each run, Pallas kernels for 8% -> 8%
where the time goes in v8:
time: 119 us
  starting transfers between devices  50 us (42%)
  blocking collectives  37.1 us (31%)
  Pallas kernels  14.8 us (12%)
  waiting for transfers between devices  13.6 us (11%)
  other arithmetic  1.62 us (1%)
    ppermute x14, starting transfers between devices, send(): return lax.ppermute(value, AXES, ROUTES[name])  43 us
    all_to_all x1, blocking collectives, per_device(): posts = lax.all_to_all(post, ('zh', 'x'), 0, 0)  22.7 us
    all_to_all x1, blocking collectives, per_device(): pays = lax.all_to_all(pay, DEV_AXES, 0, 0)  14.4 us
    ppermute x14, waiting for transfers between devices, send(): return lax.ppermute(value, AXES, ROUTES[name])  13.6 us
    pallas_call x6, Pallas kernels, block_call(): pl.pallas_call(kernel, out_shape=tuple(shapes), in_specs=smem(1) + vmem(l...  6.47 us
    pallas_call x2, Pallas kernels, grad_call(): pl.pallas_call(kernel, out_shape=tuple(shapes), in_specs=smem(1) + vmem(1...  3.98 us
    ppermute x1, starting transfers between devices, per_device(): got = lax.ppermute(for_other, ('core',), [(0, 1), (1, 0)])  3.78 us
    ppermute x1, starting transfers between devices, per_device(): other = lax.ppermute(after(unit, p1b), ('core',), [(0, 1), (1, 0)])  3.14 us
  transfers between devices with their start and end apart: 16, of which 3 were waited for; matrix products, arithmetic and copies ran while one was open for 0% of the time, Pallas kernels for 8%

profile of v8, /device:TPU:1, one launch (start us, length us, event | category | flops | bytes accessed | tf_op | source)
XLA Modules:
  0.0 118.8 jit_solution(2920367351041796515)
XLA Ops:
  0.6 1.4 %multiply_reduce_fusion = f32[224]{0:T(256)S(1)} fusion(f32[224,1024]{1,0:T(8,128)} %emb_ref.1), kind=kLoop, calls=%fused_computation.1 | loop fusion | flops 458528 | bytes 918400 | tf_op jit(solution)/shard_map/reduce_sum | solution.py:399
  2.0 0.0 copy-done
  2.1 0.1 divide_convert_fusion.unit_ref.refs_1_.refs_12_
  2.2 5.7 %collective-permute-start = (bf16[224,1024]{1,0:T(8,128)(2,1)S(1)}, bf16[224,1024]{1,0:T(8,128)(2,1)S(1)}, u32[]{:S(2)}, u32[]{:S(2)}) collective-permute-start(bf16[224,1024]{1,0:T(8,128)(2,1)S(1)} %divide_convert_fusion.unit_ref.refs_1_.refs_12_), channel_id=1, source_target_pairs={{1,5},{3,1},{5,7},{7,3},{9,13},{11,9},{13,15},{15,11},{17,21},{19,... | collective-permute-start | bytes 1376264 | tf_op jit(solution)/shard_map/ppermute | solution.py:395
  8.0 0.1 pad_add_fusion.ids_ref.refs_0_
  8.1 0.7 copy-done.1
  8.7 0.9 own_scores.1
  9.6 0.7 collective-permute-start.2
  10.3 13.9 %collective-permute-start.7 = (bf16[224,1024]{1,0:T(8,128)(2,1)S(1)}, bf16[224,1024]{1,0:T(8,128)(2,1)S(1)}, u32[]{:S(2)}, u32[]{:S(2)}) collective-permute-start(bf16[224,1024]{1,0:T(8,128)(2,1)S(1)} %divide_convert_fusion.unit_ref.refs_1_.refs_12_), channel_id=1, source_target_pairs={{126,128},{127,129},{128,126},{129,127},{254,256},{255,257},{256,2... | collective-permute-start | bytes 1376264 | tf_op jit(solution)/shard_map/ppermute | solution.py:395
  24.3 0.0 collective-permute-done.second_ref
  24.3 3.1 %collective-permute-start.1 = (bf16[224,1024]{1,0:T(8,128)(2,1)S(1)}, bf16[224,1024]{1,0:T(8,128)(2,1)S(1)}, u32[]{:S(2)}, u32[]{:S(2)}) collective-permute-start(bf16[224,1024]{1,0:T(8,128)(2,1)S(1)} %divide_convert_fusion.unit_ref.refs_1_.refs_12_), channel_id=1, source_target_pairs={{0,1},{1,0},{2,3},{3,2},{4,5},{5,4},{6,7},{7,6},{8,9},{9,8},{10,11... | collective-permute-start | bytes 1376264 | tf_op jit(solution)/shard_map/ppermute | solution.py:410
  27.4 0.0 collective-permute-done.2.first_ref
  27.4 1.9 %collective-permute-start.3 = (bf16[224,1024]{1,0:T(8,128)(2,1)S(1)}, bf16[224,1024]{1,0:T(8,128)(2,1)S(1)}, u32[]{:S(2)}, u32[]{:S(2)}) collective-permute-start(bf16[224,1024]{1,0:T(8,128)(2,1)S(1)} %divide_convert_fusion.unit_ref.refs_1_.refs_12_), channel_id=1, source_target_pairs={{2,6},{3,7},{4,0},{5,1},{0,2},{1,3},{6,4},{7,5},{10,14},{11,15},{1... | collective-permute-start | bytes 1376264 | tf_op jit(solution)/shard_map/ppermute | solution.py:395
  29.4 0.6 choose.2.refs_5_.refs_13_
  30.0 1.3 %collective-permute-start.6 = (bf16[224,1024]{1,0:T(8,128)(2,1)S(1)}, bf16[224,1024]{1,0:T(8,128)(2,1)S(1)}, u32[]{:S(2)}, u32[]{:S(2)}) collective-permute-start(bf16[224,1024]{1,0:T(8,128)(2,1)S(1)} %choose.2.refs_5_.refs_13_), channel_id=1, source_target_pairs={{0,8},{1,9},{2,10},{3,11},{8,16},{9,17},{10,18},{11,19},{12,4},{13... | collective-permute-start | bytes 1376264 | tf_op jit(solution)/shard_map/ppermute | solution.py:395
  31.3 6.9 %collective-permute-start.9 = (bf16[224,1024]{1,0:T(8,128)(2,1)S(1)}, bf16[224,1024]{1,0:T(8,128)(2,1)S(1)}, u32[]{:S(2)}, u32[]{:S(2)}) collective-permute-start(bf16[224,1024]{1,0:T(8,128)(2,1)S(1)} %choose.2.refs_5_.refs_13_), channel_id=1, source_target_pairs={{126,128},{127,129},{128,126},{129,127},{254,256},{255,257},{256,2... | collective-permute-start | bytes 1376264 | tf_op jit(solution)/shard_map/ppermute | solution.py:395
  38.2 0.0 collective-permute-done.7.refs_7_
  38.2 1.3 %collective-permute-start.8 = (bf16[224,1024]{1,0:T(8,128)(2,1)S(1)}, bf16[224,1024]{1,0:T(8,128)(2,1)S(1)}, u32[]{:S(2)}, u32[]{:S(2)}) collective-permute-start(bf16[224,1024]{1,0:T(8,128)(2,1)S(1)} %collective-permute-done.7.refs_7_), channel_id=1, source_target_pairs={{128,130},{129,131},{126,124},{127,125},{256,258},{257,259},{254,2... | collective-permute-start | bytes 1376264 | tf_op jit(solution)/shard_map/ppermute | solution.py:395
  39.5 0.0 collective-permute-done.1.other_ref.refs_2_
  39.5 0.3 other_scores.1
  39.9 1.0 block_scores.6
  40.9 1.5 %collective-permute-done.3.refs_5_.refs_14_ = bf16[224,1024]{1,0:T(8,128)(2,1)S(1)} collective-permute-done((bf16[224,1024]{1,0:T(8,128)(2,1)S(1)}, bf16[224,1024]{1,0:T(8,128)(2,1)S(1)}, u32[]{:S(2)}, u32[]{:S(2)}) %collective-permute-start.3) | collective-permute-done | bytes 458784 | tf_op jit(solution)/shard_map/ppermute | solution.py:395
  42.4 1.3 %collective-permute-start.4 = (bf16[224,1024]{1,0:T(8,128)(2,1)S(1)}, bf16[224,1024]{1,0:T(8,128)(2,1)S(1)}, u32[]{:S(2)}, u32[]{:S(2)}) collective-permute-start(bf16[224,1024]{1,0:T(8,128)(2,1)S(1)} %choose.2.refs_5_.refs_13_), channel_id=1, source_target_pairs={{4,6},{5,7},{2,0},{3,1},{12,14},{13,15},{10,8},{11,9},{20,22},{21,... | collective-permute-start | bytes 1376264 | tf_op jit(solution)/shard_map/ppermute | solution.py:395
  43.7 0.7 collective-permute-start.5
  44.4 0.0 collective-permute-done.6.refs_5_
  44.4 1.3 %collective-permute-start.11 = (bf16[224,1024]{1,0:T(8,128)(2,1)S(1)}, bf16[224,1024]{1,0:T(8,128)(2,1)S(1)}, u32[]{:S(2)}, u32[]{:S(2)}) collective-permute-start(bf16[224,1024]{1,0:T(8,128)(2,1)S(1)} %collective-permute-done.3.refs_5_.refs_14_), channel_id=1, source_target_pairs={{0,8},{1,9},{4,12},{5,13},{8,16},{9,17},{12,20},{13,21},{10,2},{11... | collective-permute-start | bytes 1376264 | tf_op jit(solution)/shard_map/ppermute | solution.py:395
  45.7 4.6 %collective-permute-done.9.first_ref.refs_6_ = bf16[224,1024]{1,0:T(8,128)(2,1)S(1)} collective-permute-done((bf16[224,1024]{1,0:T(8,128)(2,1)S(1)}, bf16[224,1024]{1,0:T(8,128)(2,1)S(1)}, u32[]{:S(2)}, u32[]{:S(2)}) %collective-permute-start.9) | collective-permute-done | bytes 458784 | tf_op jit(solution)/shard_map/ppermute | solution.py:395
  50.3 4.6 %collective-permute-start.10 = (bf16[224,1024]{1,0:T(8,128)(2,1)S(1)}, bf16[224,1024]{1,0:T(8,128)(2,1)S(1)}, u32[]{:S(2)}, u32[]{:S(2)}) collective-permute-start(bf16[224,1024]{1,0:T(8,128)(2,1)S(1)} %collective-permute-done.3.refs_5_.refs_14_), channel_id=1, source_target_pairs={{126,128},{127,129},{128,126},{129,127},{254,256},{255,257},{256,2... | collective-permute-start | bytes 1376264 | tf_op jit(solution)/shard_map/ppermute | solution.py:395
  54.9 0.6 choose.3
  55.5 1.3 %collective-permute-start.12 = (bf16[224,1024]{1,0:T(8,128)(2,1)S(1)}, bf16[224,1024]{1,0:T(8,128)(2,1)S(1)}, u32[]{:S(2)}, u32[]{:S(2)}) collective-permute-start(bf16[224,1024]{1,0:T(8,128)(2,1)S(1)} %choose.3), channel_id=1, source_target_pairs={{128,130},{129,131},{126,124},{127,125},{130,132},{131,133},{124,1... | collective-permute-start | bytes 1376264 | tf_op jit(solution)/shard_map/ppermute | solution.py:395
  56.9 1.0 block_scores.7
  57.9 0.0 collective-permute-done.5.refs_6_
  57.9 0.0 collective-permute-done.11.refs_5_
  57.9 1.3 %collective-permute-start.13 = (bf16[224,1024]{1,0:T(8,128)(2,1)S(1)}, bf16[224,1024]{1,0:T(8,128)(2,1)S(1)}, u32[]{:S(2)}, u32[]{:S(2)}) collective-permute-start(bf16[224,1024]{1,0:T(8,128)(2,1)S(1)} %collective-permute-done.4.refs_5_), channel_id=1, source_target_pairs={{0,8},{1,9},{8,16},{9,17},{14,6},{15,7},{16,24},{17,25},{22,14},{2... | collective-permute-start | bytes 1376264 | tf_op jit(solution)/shard_map/ppermute | solution.py:395
  59.2 0.7 collective-permute-start.14
  59.9 1.1 block_scores.8
  61.0 7.4 %collective-permute-done.10.refs_7_ = bf16[224,1024]{1,0:T(8,128)(2,1)S(1)} collective-permute-done((bf16[224,1024]{1,0:T(8,128)(2,1)S(1)}, bf16[224,1024]{1,0:T(8,128)(2,1)S(1)}, u32[]{:S(2)}, u32[]{:S(2)}) %collective-permute-start.10) | collective-permute-done | bytes 458784 | tf_op jit(solution)/shard_map/ppermute | solution.py:395
  68.4 1.1 block_scores.9
  69.5 1.1 block_scores.10
  70.6 0.0 collective-permute-done.13.refs_5_
  70.6 1.2 %block_scores.11 = (f32[224,224]{1,0:T(8,128)S(1)}, f32[224,224]{1,0:T(8,128)S(1)}, f32[32,4,128]{2,1,0:T(4,128)S(1)}, bf16[224,1024]{1,0:T(8,128)(2,1)S(1)}) custom-call(s32[4]{0:T(128)S(1)} %pad_add_fusion.ids_ref.refs_0_, bf16[224,1024]{1,0:T(8,128)(2,1)S(1)} %divide_convert_fusion.unit_ref.refs_1_.refs_12_, ...), custom_call_target="tpu_custom_call" | custom-call | flops 205520896 | bytes 2097152 | tf_op jit(solution)/shard_map/block_scores/pallas_call | solution.py:236
  71.8 14.4 %all_to_all.10.pay_ref = f32[32,4,128]{2,1,0:T(4,128)S(1)} all-to-all(f32[32,4,128]{2,1,0:T(4,128)S(1)} %get-tuple-element.86), channel_id=1, replica_groups=mesh['zh'=4,'x'=4,'y'=4,'zl'=4,'core'=2] {'y','zl','core'}, dimensions={0} | all-to-all | bytes 131072 | tf_op jit(solution)/shard_map/all_to_all | solution.py:446
  86.2 0.7 denoms.1
  86.9 22.7 %all_to_all.11.refs_2_ = f32[16,4,2,128]{3,2,1,0:T(2,128)S(1)} all-to-all(f32[16,4,2,128]{3,2,1,0:T(2,128)S(1)} %get-tuple-element.88), channel_id=1, replica_groups=mesh['zh'=4,'x'=4,'y'=4,'zl'=4,'core'=2] {'zh','x'}, dimensions={0} | all-to-all | bytes 131072 | tf_op jit(solution)/shard_map/all_to_all | solution.py:448
  109.6 1.7 %unit_gradient.2 = f32[224,1024]{1,0:T(8,128)S(1)} custom-call(s32[4]{0:T(128)S(1)} %pad_add_fusion.ids_ref.refs_0_, f32[16,2,128]{2,1,0:T(2,128)S(1)} %get-tuple-element.101.refs_1_, f32[16,4,2,128]{3,2,1,0:T(2,128)S(1)} %all_to_all.11.refs_2_, f32[2,128]{1,0:T(2,128)S(1)} %get-tuple-element.89.refs_3_, s32[1,224]{1,0:T(1,128)S(1)} %get-tuple-element.59.local_ref.refs_4_, ...), custom_call_target="tpu_custom_call" | custom-call | flops 719323136 | bytes 6291456 | tf_op jit(solution)/shard_map/unit_gradient/pallas_call | solution.py:362
  111.4 3.8 %collective-permute-start.15 = (f32[224,1024]{1,0:T(8,128)S(1)}, f32[224,1024]{1,0:T(8,128)S(1)}, u32[]{:S(2)}, u32[]{:S(2)}) collective-permute-start(f32[224,1024]{1,0:T(8,128)S(1)} %unit_gradient.2), channel_id=1, source_target_pairs={{0,1},{1,0},{2,3},{3,2},{4,5},{5,4},{6,7},{7,6},{8,9},{9,8},{10,11... | collective-permute-start | bytes 2752520 | tf_op jit(solution)/shard_map/ppermute | solution.py:450
  115.2 2.2 %unit_gradient.3 = (f32[224,1024]{1,0:T(8,128)S(1)}, f32[1,1]{1,0:T(1,128)}) custom-call(s32[4]{0:T(128)S(1)} %pad_add_fusion.ids_ref.refs_0_, f32[16,2,128]{2,1,0:T(2,128)S(1)} %get-tuple-element.101.refs_1_, f32[16,4,2,128]{3,2,1,0:T(2,128)S(1)} %all_to_all.11.refs_2_, f32[2,128]{1,0:T(2,128)S(1)} %get-tuple-element.102.refs_3_, ...), custom_call_target="tpu_custom_call" | custom-call | flops 719323136 | bytes 6291456 | tf_op jit(solution)/shard_map/unit_gradient/pallas_call | solution.py:362
  117.4 1.3 %final.1 = f32[224,1024]{1,0:T(8,128)} custom-call(f32[224,1024]{1,0:T(8,128)S(1)} %copy-done, f32[224,1024]{1,0:T(8,128)S(1)} %get-tuple-element.111.mine_ref, f32[224,1024]{1,0:T(8,128)S(1)} %collective-permute-done.15.got_ref), custom_call_target="tpu_custom_call" | custom-call | flops 2293760 | bytes 3670016 | tf_op jit(solution)/shard_map/final/pallas_call | solution.py:383
  (8 shorter events, 0.0 us)
Async XLA Ops:
  0.6 1.5 %copy-start = (f32[224,1024]{1,0:T(8,128)S(1)}, f32[224,1024]{1,0:T(8,128)}, u32[]{:S(2)}) copy-start(f32[224,1024]{1,0:T(8,128)} %emb_ref.1) | copy-start | bytes 2752516
  2.2 22.0 %collective-permute-start = (bf16[224,1024]{1,0:T(8,128)(2,1)S(1)}, bf16[224,1024]{1,0:T(8,128)(2,1)S(1)}, u32[]{:S(2)}, u32[]{:S(2)}) collective-permute-start(bf16[224,1024]{1,0:T(8,128)(2,1)S(1)} %divide_convert_fusion.unit_ref.refs_1_.refs_12_), channel_id=1, source_target_pairs={{1,5},{3,1},{5,7},{7,3},{9,13},{11,9},{13,15},{15,11},{17,21},{19,... | collective-permute-start | bytes 1376264 | tf_op jit(solution)/shard_map/ppermute | solution.py:395
  8.1 0.7 copy-start.1
  9.6 17.8 %collective-permute-start.2 = (bf16[224,1024]{1,0:T(8,128)(2,1)S(1)}, bf16[224,1024]{1,0:T(8,128)(2,1)S(1)}, u32[]{:S(2)}, u32[]{:S(2)}) collective-permute-start(bf16[224,1024]{1,0:T(8,128)(2,1)S(1)} %divide_convert_fusion.unit_ref.refs_1_.refs_12_), channel_id=1, source_target_pairs={{0,4},{2,0},{4,6},{6,2},{8,12},{10,8},{12,14},{14,10},{16,20},{18,... | collective-permute-start | bytes 1376264 | tf_op jit(solution)/shard_map/ppermute | solution.py:395
  10.3 27.9 %collective-permute-start.7 = (bf16[224,1024]{1,0:T(8,128)(2,1)S(1)}, bf16[224,1024]{1,0:T(8,128)(2,1)S(1)}, u32[]{:S(2)}, u32[]{:S(2)}) collective-permute-start(bf16[224,1024]{1,0:T(8,128)(2,1)S(1)} %divide_convert_fusion.unit_ref.refs_1_.refs_12_), channel_id=1, source_target_pairs={{126,128},{127,129},{128,126},{129,127},{254,256},{255,257},{256,2... | collective-permute-start | bytes 1376264 | tf_op jit(solution)/shard_map/ppermute | solution.py:395
  24.3 15.2 %collective-permute-start.1 = (bf16[224,1024]{1,0:T(8,128)(2,1)S(1)}, bf16[224,1024]{1,0:T(8,128)(2,1)S(1)}, u32[]{:S(2)}, u32[]{:S(2)}) collective-permute-start(bf16[224,1024]{1,0:T(8,128)(2,1)S(1)} %divide_convert_fusion.unit_ref.refs_1_.refs_12_), channel_id=1, source_target_pairs={{0,1},{1,0},{2,3},{3,2},{4,5},{5,4},{6,7},{7,6},{8,9},{9,8},{10,11... | collective-permute-start | bytes 1376264 | tf_op jit(solution)/shard_map/ppermute | solution.py:410
  27.4 14.9 %collective-permute-start.3 = (bf16[224,1024]{1,0:T(8,128)(2,1)S(1)}, bf16[224,1024]{1,0:T(8,128)(2,1)S(1)}, u32[]{:S(2)}, u32[]{:S(2)}) collective-permute-start(bf16[224,1024]{1,0:T(8,128)(2,1)S(1)} %divide_convert_fusion.unit_ref.refs_1_.refs_12_), channel_id=1, source_target_pairs={{2,6},{3,7},{4,0},{5,1},{0,2},{1,3},{6,4},{7,5},{10,14},{11,15},{1... | collective-permute-start | bytes 1376264 | tf_op jit(solution)/shard_map/ppermute | solution.py:395
  30.0 14.4 %collective-permute-start.6 = (bf16[224,1024]{1,0:T(8,128)(2,1)S(1)}, bf16[224,1024]{1,0:T(8,128)(2,1)S(1)}, u32[]{:S(2)}, u32[]{:S(2)}) collective-permute-start(bf16[224,1024]{1,0:T(8,128)(2,1)S(1)} %choose.2.refs_5_.refs_13_), channel_id=1, source_target_pairs={{0,8},{1,9},{2,10},{3,11},{8,16},{9,17},{10,18},{11,19},{12,4},{13... | collective-permute-start | bytes 1376264 | tf_op jit(solution)/shard_map/ppermute | solution.py:395
  31.3 19.0 %collective-permute-start.9 = (bf16[224,1024]{1,0:T(8,128)(2,1)S(1)}, bf16[224,1024]{1,0:T(8,128)(2,1)S(1)}, u32[]{:S(2)}, u32[]{:S(2)}) collective-permute-start(bf16[224,1024]{1,0:T(8,128)(2,1)S(1)} %choose.2.refs_5_.refs_13_), channel_id=1, source_target_pairs={{126,128},{127,129},{128,126},{129,127},{254,256},{255,257},{256,2... | collective-permute-start | bytes 1376264 | tf_op jit(solution)/shard_map/ppermute | solution.py:395
  38.2 16.8 %collective-permute-start.8 = (bf16[224,1024]{1,0:T(8,128)(2,1)S(1)}, bf16[224,1024]{1,0:T(8,128)(2,1)S(1)}, u32[]{:S(2)}, u32[]{:S(2)}) collective-permute-start(bf16[224,1024]{1,0:T(8,128)(2,1)S(1)} %collective-permute-done.7.refs_7_), channel_id=1, source_target_pairs={{128,130},{129,131},{126,124},{127,125},{256,258},{257,259},{254,2... | collective-permute-start | bytes 1376264 | tf_op jit(solution)/shard_map/ppermute | solution.py:395
  42.4 15.5 %collective-permute-start.4 = (bf16[224,1024]{1,0:T(8,128)(2,1)S(1)}, bf16[224,1024]{1,0:T(8,128)(2,1)S(1)}, u32[]{:S(2)}, u32[]{:S(2)}) collective-permute-start(bf16[224,1024]{1,0:T(8,128)(2,1)S(1)} %choose.2.refs_5_.refs_13_), channel_id=1, source_target_pairs={{4,6},{5,7},{2,0},{3,1},{12,14},{13,15},{10,8},{11,9},{20,22},{21,... | collective-permute-start | bytes 1376264 | tf_op jit(solution)/shard_map/ppermute | solution.py:395
  43.7 14.2 %collective-permute-start.5 = (bf16[224,1024]{1,0:T(8,128)(2,1)S(1)}, bf16[224,1024]{1,0:T(8,128)(2,1)S(1)}, u32[]{:S(2)}, u32[]{:S(2)}) collective-permute-start(bf16[224,1024]{1,0:T(8,128)(2,1)S(1)} %divide_convert_fusion.unit_ref.refs_1_.refs_12_), channel_id=1, source_target_pairs={{2,4},{3,5},{4,2},{5,3},{10,12},{11,13},{12,10},{13,11},{18,20},{1... | collective-permute-start | bytes 1376264 | tf_op jit(solution)/shard_map/ppermute | solution.py:395
  44.4 13.5 %collective-permute-start.11 = (bf16[224,1024]{1,0:T(8,128)(2,1)S(1)}, bf16[224,1024]{1,0:T(8,128)(2,1)S(1)}, u32[]{:S(2)}, u32[]{:S(2)}) collective-permute-start(bf16[224,1024]{1,0:T(8,128)(2,1)S(1)} %collective-permute-done.3.refs_5_.refs_14_), channel_id=1, source_target_pairs={{0,8},{1,9},{4,12},{5,13},{8,16},{9,17},{12,20},{13,21},{10,2},{11... | collective-permute-start | bytes 1376264 | tf_op jit(solution)/shard_map/ppermute | solution.py:395
  50.3 18.1 %collective-permute-start.10 = (bf16[224,1024]{1,0:T(8,128)(2,1)S(1)}, bf16[224,1024]{1,0:T(8,128)(2,1)S(1)}, u32[]{:S(2)}, u32[]{:S(2)}) collective-permute-start(bf16[224,1024]{1,0:T(8,128)(2,1)S(1)} %collective-permute-done.3.refs_5_.refs_14_), channel_id=1, source_target_pairs={{126,128},{127,129},{128,126},{129,127},{254,256},{255,257},{256,2... | collective-permute-start | bytes 1376264 | tf_op jit(solution)/shard_map/ppermute | solution.py:395
  55.5 14.0 %collective-permute-start.12 = (bf16[224,1024]{1,0:T(8,128)(2,1)S(1)}, bf16[224,1024]{1,0:T(8,128)(2,1)S(1)}, u32[]{:S(2)}, u32[]{:S(2)}) collective-permute-start(bf16[224,1024]{1,0:T(8,128)(2,1)S(1)} %choose.3), channel_id=1, source_target_pairs={{128,130},{129,131},{126,124},{127,125},{130,132},{131,133},{124,1... | collective-permute-start | bytes 1376264 | tf_op jit(solution)/shard_map/ppermute | solution.py:395
  57.9 12.7 %collective-permute-start.13 = (bf16[224,1024]{1,0:T(8,128)(2,1)S(1)}, bf16[224,1024]{1,0:T(8,128)(2,1)S(1)}, u32[]{:S(2)}, u32[]{:S(2)}) collective-permute-start(bf16[224,1024]{1,0:T(8,128)(2,1)S(1)} %collective-permute-done.4.refs_5_), channel_id=1, source_target_pairs={{0,8},{1,9},{8,16},{9,17},{14,6},{15,7},{16,24},{17,25},{22,14},{2... | collective-permute-start | bytes 1376264 | tf_op jit(solution)/shard_map/ppermute | solution.py:395
  59.2 11.4 %collective-permute-start.14 = (bf16[224,1024]{1,0:T(8,128)(2,1)S(1)}, bf16[224,1024]{1,0:T(8,128)(2,1)S(1)}, u32[]{:S(2)}, u32[]{:S(2)}) collective-permute-start(bf16[224,1024]{1,0:T(8,128)(2,1)S(1)} %collective-permute-done.5.refs_6_), channel_id=1, source_target_pairs={{2,10},{3,11},{10,18},{11,19},{12,4},{13,5},{18,26},{19,27},{20,12... | collective-permute-start | bytes 1376264 | tf_op jit(solution)/shard_map/ppermute | solution.py:395
  111.4 6.0 %collective-permute-start.15 = (f32[224,1024]{1,0:T(8,128)S(1)}, f32[224,1024]{1,0:T(8,128)S(1)}, u32[]{:S(2)}, u32[]{:S(2)}) collective-permute-start(f32[224,1024]{1,0:T(8,128)S(1)} %unit_gradient.2), channel_id=1, source_target_pairs={{0,1},{1,0},{2,3},{3,2},{4,5},{5,4},{6,7},{7,6},{8,9},{9,8},{10,11... | collective-permute-start | bytes 2752520 | tf_op jit(solution)/shard_map/ppermute | solution.py:450

commit v9 on v8

--- a/solution.py
+++ b/solution.py
@@ -407,7 +407,7 @@
     x1 = send(unit, "X1")
     local, e_own, sum_own, pos = own_call(ids, unit, partner)
     p1a = send(after(unit, sum_own), "P1a")
-    other = lax.ppermute(after(unit, p1b), ("core",), [(0, 1), (1, 0)])
+    other = lax.ppermute(after(unit, ids), ("core",), [(0, 1), (1, 0)])
     e_other, sum_other, pos = other_call(unit, other, local, pos)
     expos, blocks, sums = [(e_own, e_other)] + [None] * 6, [unit] + [None] * 6, (sum_own, sum_other)
 
@@ -421,6 +421,7 @@
             return rest
         sums = rest
 
+    p1b = after(p1b, other)
     r2 = send(after(unit, p1a, p1b), "P2")
     r1 = choose_call(True, ids, p1a, p1b)
     y1 = send(r1, "Y1")

time: 119 us -> 127 us (1.067)
  blocking collectives: 37.1 us -> 54.5 us
  waiting for transfers between devices: 13.6 us -> 6.31 us
  starting transfers between devices: 50 us -> 48.4 us
    all_to_all x1, blocking collectives: 14.4 us -> 28 us  [per_device(): pays = lax.all_to_all(pay, DEV_AXES, 0, 0)]
    ppermute x14, waiting for transfers between devices: 13.6 us -> 6.31 us  [send(): return lax.ppermute(value, AXES, ROUTES[name])]
    all_to_all x1, blocking collectives: 22.7 us -> 26.5 us  [per_device(): posts = lax.all_to_all(post, ('zh', 'x'), 0, 0)]
    ppermute x14, starting transfers between devices: 43 us -> 40.7 us  [send(): return lax.ppermute(value, AXES, ROUTES[name])]
  transfers between devices with their start and end apart: 16 -> 16, of which waited for: 3 -> 4; matrix products, arithmetic and copies ran while one was open for 0% -> 0% of each run, Pallas kernels for 8% -> 8%
where the time goes in v9:
time: 127 us
  blocking collectives  54.5 us (43%)
  starting transfers between devices  48.4 us (38%)
  Pallas kernels  14.9 us (12%)
  waiting for transfers between devices  6.31 us (5%)
  other arithmetic  1.62 us (1%)
    ppermute x14, starting transfers between devices, send(): return lax.ppermute(value, AXES, ROUTES[name])  40.7 us
    all_to_all x1, blocking collectives, per_device(): pays = lax.all_to_all(pay, DEV_AXES, 0, 0)  28 us
    all_to_all x1, blocking collectives, per_device(): posts = lax.all_to_all(post, ('zh', 'x'), 0, 0)  26.5 us
    pallas_call x6, Pallas kernels, block_call(): pl.pallas_call(kernel, out_shape=tuple(shapes), in_specs=smem(1) + vmem(l...  6.47 us
    ppermute x14, waiting for transfers between devices, send(): return lax.ppermute(value, AXES, ROUTES[name])  6.31 us
    pallas_call x2, Pallas kernels, grad_call(): pl.pallas_call(kernel, out_shape=tuple(shapes), in_specs=smem(1) + vmem(1...  3.98 us
    ppermute x1, starting transfers between devices, per_device(): other = lax.ppermute(after(unit, ids), ('core',), [(0, 1), (1, 0)])  3.87 us
    ppermute x1, starting transfers between devices, per_device(): got = lax.ppermute(for_other, ('core',), [(0, 1), (1, 0)])  3.78 us
  transfers between devices with their start and end apart: 16, of which 4 were waited for; matrix products, arithmetic and copies ran while one was open for 0% of the time, Pallas kernels for 8%

profile of v9, /device:TPU:1, one launch (start us, length us, event | category | flops | bytes accessed | tf_op | source)
XLA Modules:
  0.0 126.6 jit_solution(17052523733248004878)
XLA Ops:
  0.6 1.4 %multiply_reduce_fusion = f32[224]{0:T(256)S(1)} fusion(f32[224,1024]{1,0:T(8,128)} %emb_ref.1), kind=kLoop, calls=%fused_computation.1 | loop fusion | flops 458528 | bytes 918400 | tf_op jit(solution)/shard_map/reduce_sum | solution.py:399
  2.0 0.0 copy-done
  2.1 0.1 divide_convert_fusion.unit_ref.refs_1_.refs_12_
  2.2 5.7 %collective-permute-start.2 = (bf16[224,1024]{1,0:T(8,128)(2,1)S(1)}, bf16[224,1024]{1,0:T(8,128)(2,1)S(1)}, u32[]{:S(2)}, u32[]{:S(2)}) collective-permute-start(bf16[224,1024]{1,0:T(8,128)(2,1)S(1)} %divide_convert_fusion.unit_ref.refs_1_.refs_12_), channel_id=1, source_target_pairs={{1,5},{3,1},{5,7},{7,3},{9,13},{11,9},{13,15},{15,11},{17,21},{19,... | collective-permute-start | bytes 1376264 | tf_op jit(solution)/shard_map/ppermute | solution.py:395
  8.0 0.1 pad_add_fusion.ids_ref.refs_0_
  8.1 3.9 %collective-permute-start = (bf16[224,1024]{1,0:T(8,128)(2,1)S(1)}, bf16[224,1024]{1,0:T(8,128)(2,1)S(1)}, u32[]{:S(2)}, u32[]{:S(2)}) collective-permute-start(bf16[224,1024]{1,0:T(8,128)(2,1)S(1)} %divide_convert_fusion.unit_ref.refs_1_.refs_12_), channel_id=1, source_target_pairs={{0,1},{1,0},{2,3},{3,2},{4,5},{5,4},{6,7},{7,6},{8,9},{9,8},{10,11... | collective-permute-start | bytes 1376264 | tf_op jit(solution)/shard_map/ppermute | solution.py:410
  11.9 0.9 own_scores.1
  12.8 0.7 collective-permute-start.1
  13.5 12.1 %collective-permute-start.7 = (bf16[224,1024]{1,0:T(8,128)(2,1)S(1)}, bf16[224,1024]{1,0:T(8,128)(2,1)S(1)}, u32[]{:S(2)}, u32[]{:S(2)}) collective-permute-start(bf16[224,1024]{1,0:T(8,128)(2,1)S(1)} %divide_convert_fusion.unit_ref.refs_1_.refs_12_), channel_id=1, source_target_pairs={{126,128},{127,129},{128,126},{129,127},{254,256},{255,257},{256,2... | collective-permute-start | bytes 1376264 | tf_op jit(solution)/shard_map/ppermute | solution.py:395
  25.7 0.0 collective-permute-done.other_ref.refs_2_
  25.7 0.0 collective-permute-done.2.second_ref
  25.7 0.0 collective-permute-done.1.first_ref
  25.7 1.9 %collective-permute-start.3 = (bf16[224,1024]{1,0:T(8,128)(2,1)S(1)}, bf16[224,1024]{1,0:T(8,128)(2,1)S(1)}, u32[]{:S(2)}, u32[]{:S(2)}) collective-permute-start(bf16[224,1024]{1,0:T(8,128)(2,1)S(1)} %divide_convert_fusion.unit_ref.refs_1_.refs_12_), channel_id=1, source_target_pairs={{2,6},{3,7},{4,0},{5,1},{0,2},{1,3},{6,4},{7,5},{10,14},{11,15},{1... | collective-permute-start | bytes 1376264 | tf_op jit(solution)/shard_map/ppermute | solution.py:395
  27.6 0.6 choose.2.refs_5_.refs_13_
  28.2 1.3 %collective-permute-start.6 = (bf16[224,1024]{1,0:T(8,128)(2,1)S(1)}, bf16[224,1024]{1,0:T(8,128)(2,1)S(1)}, u32[]{:S(2)}, u32[]{:S(2)}) collective-permute-start(bf16[224,1024]{1,0:T(8,128)(2,1)S(1)} %choose.2.refs_5_.refs_13_), channel_id=1, source_target_pairs={{0,8},{1,9},{2,10},{3,11},{8,16},{9,17},{10,18},{11,19},{12,4},{13... | collective-permute-start | bytes 1376264 | tf_op jit(solution)/shard_map/ppermute | solution.py:395
  29.5 5.0 %collective-permute-start.9 = (bf16[224,1024]{1,0:T(8,128)(2,1)S(1)}, bf16[224,1024]{1,0:T(8,128)(2,1)S(1)}, u32[]{:S(2)}, u32[]{:S(2)}) collective-permute-start(bf16[224,1024]{1,0:T(8,128)(2,1)S(1)} %choose.2.refs_5_.refs_13_), channel_id=1, source_target_pairs={{126,128},{127,129},{128,126},{129,127},{254,256},{255,257},{256,2... | collective-permute-start | bytes 1376264 | tf_op jit(solution)/shard_map/ppermute | solution.py:395
  34.6 0.0 collective-permute-done.7.refs_7_
  34.6 1.3 %collective-permute-start.8 = (bf16[224,1024]{1,0:T(8,128)(2,1)S(1)}, bf16[224,1024]{1,0:T(8,128)(2,1)S(1)}, u32[]{:S(2)}, u32[]{:S(2)}) collective-permute-start(bf16[224,1024]{1,0:T(8,128)(2,1)S(1)} %collective-permute-done.7.refs_7_), channel_id=1, source_target_pairs={{128,130},{129,131},{126,124},{127,125},{256,258},{257,259},{254,2... | collective-permute-start | bytes 1376264 | tf_op jit(solution)/shard_map/ppermute | solution.py:395
  35.9 0.3 other_scores.1
  36.3 1.0 block_scores.6
  37.3 0.2 collective-permute-done.3.refs_5_.refs_14_
  37.5 1.3 %collective-permute-start.4 = (bf16[224,1024]{1,0:T(8,128)(2,1)S(1)}, bf16[224,1024]{1,0:T(8,128)(2,1)S(1)}, u32[]{:S(2)}, u32[]{:S(2)}) collective-permute-start(bf16[224,1024]{1,0:T(8,128)(2,1)S(1)} %choose.2.refs_5_.refs_13_), channel_id=1, source_target_pairs={{4,6},{5,7},{2,0},{3,1},{12,14},{13,15},{10,8},{11,9},{20,22},{21,... | collective-permute-start | bytes 1376264 | tf_op jit(solution)/shard_map/ppermute | solution.py:395
  38.8 0.7 collective-permute-start.5
  39.5 0.0 collective-permute-done.6.refs_5_
  39.5 1.3 %collective-permute-start.11 = (bf16[224,1024]{1,0:T(8,128)(2,1)S(1)}, bf16[224,1024]{1,0:T(8,128)(2,1)S(1)}, u32[]{:S(2)}, u32[]{:S(2)}) collective-permute-start(bf16[224,1024]{1,0:T(8,128)(2,1)S(1)} %collective-permute-done.3.refs_5_.refs_14_), channel_id=1, source_target_pairs={{0,8},{1,9},{4,12},{5,13},{8,16},{9,17},{12,20},{13,21},{10,2},{11... | collective-permute-start | bytes 1376264 | tf_op jit(solution)/shard_map/ppermute | solution.py:395
  40.8 3.4 %collective-permute-done.9.first_ref.refs_6_ = bf16[224,1024]{1,0:T(8,128)(2,1)S(1)} collective-permute-done((bf16[224,1024]{1,0:T(8,128)(2,1)S(1)}, bf16[224,1024]{1,0:T(8,128)(2,1)S(1)}, u32[]{:S(2)}, u32[]{:S(2)}) %collective-permute-start.9) | collective-permute-done | bytes 458784 | tf_op jit(solution)/shard_map/ppermute | solution.py:395
  44.2 5.9 %collective-permute-start.10 = (bf16[224,1024]{1,0:T(8,128)(2,1)S(1)}, bf16[224,1024]{1,0:T(8,128)(2,1)S(1)}, u32[]{:S(2)}, u32[]{:S(2)}) collective-permute-start(bf16[224,1024]{1,0:T(8,128)(2,1)S(1)} %collective-permute-done.3.refs_5_.refs_14_), channel_id=1, source_target_pairs={{126,128},{127,129},{128,126},{129,127},{254,256},{255,257},{256,2... | collective-permute-start | bytes 1376264 | tf_op jit(solution)/shard_map/ppermute | solution.py:395
  50.1 0.0 collective-permute-done.8.refs_6_.second_ref
  50.1 0.6 choose.3
  50.7 1.3 %collective-permute-start.12 = (bf16[224,1024]{1,0:T(8,128)(2,1)S(1)}, bf16[224,1024]{1,0:T(8,128)(2,1)S(1)}, u32[]{:S(2)}, u32[]{:S(2)}) collective-permute-start(bf16[224,1024]{1,0:T(8,128)(2,1)S(1)} %choose.3), channel_id=1, source_target_pairs={{128,130},{129,131},{126,124},{127,125},{130,132},{131,133},{124,1... | collective-permute-start | bytes 1376264 | tf_op jit(solution)/shard_map/ppermute | solution.py:395
  52.0 1.0 block_scores.7
  53.1 0.0 collective-permute-done.5.refs_6_
  53.1 1.3 %collective-permute-start.13 = (bf16[224,1024]{1,0:T(8,128)(2,1)S(1)}, bf16[224,1024]{1,0:T(8,128)(2,1)S(1)}, u32[]{:S(2)}, u32[]{:S(2)}) collective-permute-start(bf16[224,1024]{1,0:T(8,128)(2,1)S(1)} %collective-permute-done.4.refs_5_), channel_id=1, source_target_pairs={{0,8},{1,9},{8,16},{9,17},{14,6},{15,7},{16,24},{17,25},{22,14},{2... | collective-permute-start | bytes 1376264 | tf_op jit(solution)/shard_map/ppermute | solution.py:395
  54.4 0.7 collective-permute-start.14
  55.1 1.1 block_scores.8
  56.2 2.6 %collective-permute-done.10.refs_7_ = bf16[224,1024]{1,0:T(8,128)(2,1)S(1)} collective-permute-done((bf16[224,1024]{1,0:T(8,128)(2,1)S(1)}, bf16[224,1024]{1,0:T(8,128)(2,1)S(1)}, u32[]{:S(2)}, u32[]{:S(2)}) %collective-permute-start.10) | collective-permute-done | bytes 458784 | tf_op jit(solution)/shard_map/ppermute | solution.py:395
  58.8 1.1 block_scores.9
  59.9 0.0 collective-permute-done.12.refs_7_.refs_8_
  59.9 1.1 block_scores.10
  61.0 0.1 collective-permute-done.13.refs_5_
  61.1 1.2 block_scores.11
  62.3 28.0 %all_to_all.10.pay_ref = f32[32,4,128]{2,1,0:T(4,128)S(1)} all-to-all(f32[32,4,128]{2,1,0:T(4,128)S(1)} %get-tuple-element.88), channel_id=1, replica_groups=mesh['zh'=4,'x'=4,'y'=4,'zl'=4,'core'=2] {'y','zl','core'}, dimensions={0} | all-to-all | bytes 131072 | tf_op jit(solution)/shard_map/all_to_all | solution.py:447
  90.3 0.7 denoms.1
  91.0 26.5 %all_to_all.11.refs_2_ = f32[16,4,2,128]{3,2,1,0:T(2,128)S(1)} all-to-all(f32[16,4,2,128]{3,2,1,0:T(2,128)S(1)} %get-tuple-element.90), channel_id=1, replica_groups=mesh['zh'=4,'x'=4,'y'=4,'zl'=4,'core'=2] {'zh','x'}, dimensions={0} | all-to-all | bytes 131072 | tf_op jit(solution)/shard_map/all_to_all | solution.py:449
  117.5 1.7 %unit_gradient.2 = f32[224,1024]{1,0:T(8,128)S(1)} custom-call(s32[4]{0:T(128)S(1)} %pad_add_fusion.ids_ref.refs_0_, f32[16,2,128]{2,1,0:T(2,128)S(1)} %get-tuple-element.103.refs_1_, f32[16,4,2,128]{3,2,1,0:T(2,128)S(1)} %all_to_all.11.refs_2_, f32[2,128]{1,0:T(2,128)S(1)} %get-tuple-element.91.refs_3_, s32[1,224]{1,0:T(1,128)S(1)} %get-tuple-element.60.local_ref.refs_4_, ...), custom_call_target="tpu_custom_call" | custom-call | flops 719323136 | bytes 6291456 | tf_op jit(solution)/shard_map/unit_gradient/pallas_call | solution.py:362
  119.3 3.8 %collective-permute-start.15 = (f32[224,1024]{1,0:T(8,128)S(1)}, f32[224,1024]{1,0:T(8,128)S(1)}, u32[]{:S(2)}, u32[]{:S(2)}) collective-permute-start(f32[224,1024]{1,0:T(8,128)S(1)} %unit_gradient.2), channel_id=1, source_target_pairs={{0,1},{1,0},{2,3},{3,2},{4,5},{5,4},{6,7},{7,6},{8,9},{9,8},{10,11... | collective-permute-start | bytes 2752520 | tf_op jit(solution)/shard_map/ppermute | solution.py:451
  123.1 2.2 %unit_gradient.3 = (f32[224,1024]{1,0:T(8,128)S(1)}, f32[1,1]{1,0:T(1,128)}) custom-call(s32[4]{0:T(128)S(1)} %pad_add_fusion.ids_ref.refs_0_, f32[16,2,128]{2,1,0:T(2,128)S(1)} %get-tuple-element.103.refs_1_, f32[16,4,2,128]{3,2,1,0:T(2,128)S(1)} %all_to_all.11.refs_2_, f32[2,128]{1,0:T(2,128)S(1)} %get-tuple-element.104.refs_3_, ...), custom_call_target="tpu_custom_call" | custom-call | flops 719323136 | bytes 6291456 | tf_op jit(solution)/shard_map/unit_gradient/pallas_call | solution.py:362
  125.3 1.3 %final.1 = f32[224,1024]{1,0:T(8,128)} custom-call(f32[224,1024]{1,0:T(8,128)S(1)} %copy-done, f32[224,1024]{1,0:T(8,128)S(1)} %get-tuple-element.113.mine_ref, f32[224,1024]{1,0:T(8,128)S(1)} %collective-permute-done.15.got_ref), custom_call_target="tpu_custom_call" | custom-call | flops 2293760 | bytes 3670016 | tf_op jit(solution)/shard_map/final/pallas_call | solution.py:383
  (8 shorter events, 0.0 us)
Async XLA Ops:
  0.6 1.5 %copy-start = (f32[224,1024]{1,0:T(8,128)S(1)}, f32[224,1024]{1,0:T(8,128)}, u32[]{:S(2)}) copy-start(f32[224,1024]{1,0:T(8,128)} %emb_ref.1) | copy-start | bytes 2752516
  2.2 23.4 %collective-permute-start.2 = (bf16[224,1024]{1,0:T(8,128)(2,1)S(1)}, bf16[224,1024]{1,0:T(8,128)(2,1)S(1)}, u32[]{:S(2)}, u32[]{:S(2)}) collective-permute-start(bf16[224,1024]{1,0:T(8,128)(2,1)S(1)} %divide_convert_fusion.unit_ref.refs_1_.refs_12_), channel_id=1, source_target_pairs={{1,5},{3,1},{5,7},{7,3},{9,13},{11,9},{13,15},{15,11},{17,21},{19,... | collective-permute-start | bytes 1376264 | tf_op jit(solution)/shard_map/ppermute | solution.py:395
  8.1 3.9 %copy-start.1 = (s32[224]{0:T(256)S(1)}, s32[224]{0:T(256)}, u32[]{:S(2)}) copy-start(s32[224]{0:T(256)} %param.3) | copy-start | bytes 2692
  8.1 17.6 %collective-permute-start = (bf16[224,1024]{1,0:T(8,128)(2,1)S(1)}, bf16[224,1024]{1,0:T(8,128)(2,1)S(1)}, u32[]{:S(2)}, u32[]{:S(2)}) collective-permute-start(bf16[224,1024]{1,0:T(8,128)(2,1)S(1)} %divide_convert_fusion.unit_ref.refs_1_.refs_12_), channel_id=1, source_target_pairs={{0,1},{1,0},{2,3},{3,2},{4,5},{5,4},{6,7},{7,6},{8,9},{9,8},{10,11... | collective-permute-start | bytes 1376264 | tf_op jit(solution)/shard_map/ppermute | solution.py:410
  12.8 12.9 %collective-permute-start.1 = (bf16[224,1024]{1,0:T(8,128)(2,1)S(1)}, bf16[224,1024]{1,0:T(8,128)(2,1)S(1)}, u32[]{:S(2)}, u32[]{:S(2)}) collective-permute-start(bf16[224,1024]{1,0:T(8,128)(2,1)S(1)} %divide_convert_fusion.unit_ref.refs_1_.refs_12_), channel_id=1, source_target_pairs={{0,4},{2,0},{4,6},{6,2},{8,12},{10,8},{12,14},{14,10},{16,20},{18,... | collective-permute-start | bytes 1376264 | tf_op jit(solution)/shard_map/ppermute | solution.py:395
  13.5 21.1 %collective-permute-start.7 = (bf16[224,1024]{1,0:T(8,128)(2,1)S(1)}, bf16[224,1024]{1,0:T(8,128)(2,1)S(1)}, u32[]{:S(2)}, u32[]{:S(2)}) collective-permute-start(bf16[224,1024]{1,0:T(8,128)(2,1)S(1)} %divide_convert_fusion.unit_ref.refs_1_.refs_12_), channel_id=1, source_target_pairs={{126,128},{127,129},{128,126},{129,127},{254,256},{255,257},{256,2... | collective-permute-start | bytes 1376264 | tf_op jit(solution)/shard_map/ppermute | solution.py:395
  25.7 11.8 %collective-permute-start.3 = (bf16[224,1024]{1,0:T(8,128)(2,1)S(1)}, bf16[224,1024]{1,0:T(8,128)(2,1)S(1)}, u32[]{:S(2)}, u32[]{:S(2)}) collective-permute-start(bf16[224,1024]{1,0:T(8,128)(2,1)S(1)} %divide_convert_fusion.unit_ref.refs_1_.refs_12_), channel_id=1, source_target_pairs={{2,6},{3,7},{4,0},{5,1},{0,2},{1,3},{6,4},{7,5},{10,14},{11,15},{1... | collective-permute-start | bytes 1376264 | tf_op jit(solution)/shard_map/ppermute | solution.py:395
  28.2 11.3 %collective-permute-start.6 = (bf16[224,1024]{1,0:T(8,128)(2,1)S(1)}, bf16[224,1024]{1,0:T(8,128)(2,1)S(1)}, u32[]{:S(2)}, u32[]{:S(2)}) collective-permute-start(bf16[224,1024]{1,0:T(8,128)(2,1)S(1)} %choose.2.refs_5_.refs_13_), channel_id=1, source_target_pairs={{0,8},{1,9},{2,10},{3,11},{8,16},{9,17},{10,18},{11,19},{12,4},{13... | collective-permute-start | bytes 1376264 | tf_op jit(solution)/shard_map/ppermute | solution.py:395
  29.5 14.7 %collective-permute-start.9 = (bf16[224,1024]{1,0:T(8,128)(2,1)S(1)}, bf16[224,1024]{1,0:T(8,128)(2,1)S(1)}, u32[]{:S(2)}, u32[]{:S(2)}) collective-permute-start(bf16[224,1024]{1,0:T(8,128)(2,1)S(1)} %choose.2.refs_5_.refs_13_), channel_id=1, source_target_pairs={{126,128},{127,129},{128,126},{129,127},{254,256},{255,257},{256,2... | collective-permute-start | bytes 1376264 | tf_op jit(solution)/shard_map/ppermute | solution.py:395
  34.6 15.5 %collective-permute-start.8 = (bf16[224,1024]{1,0:T(8,128)(2,1)S(1)}, bf16[224,1024]{1,0:T(8,128)(2,1)S(1)}, u32[]{:S(2)}, u32[]{:S(2)}) collective-permute-start(bf16[224,1024]{1,0:T(8,128)(2,1)S(1)} %collective-permute-done.7.refs_7_), channel_id=1, source_target_pairs={{128,130},{129,131},{126,124},{127,125},{256,258},{257,259},{254,2... | collective-permute-start | bytes 1376264 | tf_op jit(solution)/shard_map/ppermute | solution.py:395
  37.5 15.6 %collective-permute-start.4 = (bf16[224,1024]{1,0:T(8,128)(2,1)S(1)}, bf16[224,1024]{1,0:T(8,128)(2,1)S(1)}, u32[]{:S(2)}, u32[]{:S(2)}) collective-permute-start(bf16[224,1024]{1,0:T(8,128)(2,1)S(1)} %choose.2.refs_5_.refs_13_), channel_id=1, source_target_pairs={{4,6},{5,7},{2,0},{3,1},{12,14},{13,15},{10,8},{11,9},{20,22},{21,... | collective-permute-start | bytes 1376264 | tf_op jit(solution)/shard_map/ppermute | solution.py:395
  38.8 14.3 %collective-permute-start.5 = (bf16[224,1024]{1,0:T(8,128)(2,1)S(1)}, bf16[224,1024]{1,0:T(8,128)(2,1)S(1)}, u32[]{:S(2)}, u32[]{:S(2)}) collective-permute-start(bf16[224,1024]{1,0:T(8,128)(2,1)S(1)} %divide_convert_fusion.unit_ref.refs_1_.refs_12_), channel_id=1, source_target_pairs={{2,4},{3,5},{4,2},{5,3},{10,12},{11,13},{12,10},{13,11},{18,20},{1... | collective-permute-start | bytes 1376264 | tf_op jit(solution)/shard_map/ppermute | solution.py:395
  39.5 13.6 %collective-permute-start.11 = (bf16[224,1024]{1,0:T(8,128)(2,1)S(1)}, bf16[224,1024]{1,0:T(8,128)(2,1)S(1)}, u32[]{:S(2)}, u32[]{:S(2)}) collective-permute-start(bf16[224,1024]{1,0:T(8,128)(2,1)S(1)} %collective-permute-done.3.refs_5_.refs_14_), channel_id=1, source_target_pairs={{0,8},{1,9},{4,12},{5,13},{8,16},{9,17},{12,20},{13,21},{10,2},{11... | collective-permute-start | bytes 1376264 | tf_op jit(solution)/shard_map/ppermute | solution.py:395
  44.2 14.6 %collective-permute-start.10 = (bf16[224,1024]{1,0:T(8,128)(2,1)S(1)}, bf16[224,1024]{1,0:T(8,128)(2,1)S(1)}, u32[]{:S(2)}, u32[]{:S(2)}) collective-permute-start(bf16[224,1024]{1,0:T(8,128)(2,1)S(1)} %collective-permute-done.3.refs_5_.refs_14_), channel_id=1, source_target_pairs={{126,128},{127,129},{128,126},{129,127},{254,256},{255,257},{256,2... | collective-permute-start | bytes 1376264 | tf_op jit(solution)/shard_map/ppermute | solution.py:395
  50.7 9.2 %collective-permute-start.12 = (bf16[224,1024]{1,0:T(8,128)(2,1)S(1)}, bf16[224,1024]{1,0:T(8,128)(2,1)S(1)}, u32[]{:S(2)}, u32[]{:S(2)}) collective-permute-start(bf16[224,1024]{1,0:T(8,128)(2,1)S(1)} %choose.3), channel_id=1, source_target_pairs={{128,130},{129,131},{126,124},{127,125},{130,132},{131,133},{124,1... | collective-permute-start | bytes 1376264 | tf_op jit(solution)/shard_map/ppermute | solution.py:395
  53.1 8.0 %collective-permute-start.13 = (bf16[224,1024]{1,0:T(8,128)(2,1)S(1)}, bf16[224,1024]{1,0:T(8,128)(2,1)S(1)}, u32[]{:S(2)}, u32[]{:S(2)}) collective-permute-start(bf16[224,1024]{1,0:T(8,128)(2,1)S(1)} %collective-permute-done.4.refs_5_), channel_id=1, source_target_pairs={{0,8},{1,9},{8,16},{9,17},{14,6},{15,7},{16,24},{17,25},{22,14},{2... | collective-permute-start | bytes 1376264 | tf_op jit(solution)/shard_map/ppermute | solution.py:395
  54.4 6.7 %collective-permute-start.14 = (bf16[224,1024]{1,0:T(8,128)(2,1)S(1)}, bf16[224,1024]{1,0:T(8,128)(2,1)S(1)}, u32[]{:S(2)}, u32[]{:S(2)}) collective-permute-start(bf16[224,1024]{1,0:T(8,128)(2,1)S(1)} %collective-permute-done.5.refs_6_), channel_id=1, source_target_pairs={{2,10},{3,11},{10,18},{11,19},{12,4},{13,5},{18,26},{19,27},{20,12... | collective-permute-start | bytes 1376264 | tf_op jit(solution)/shard_map/ppermute | solution.py:395
  119.3 6.0 %collective-permute-start.15 = (f32[224,1024]{1,0:T(8,128)S(1)}, f32[224,1024]{1,0:T(8,128)S(1)}, u32[]{:S(2)}, u32[]{:S(2)}) collective-permute-start(f32[224,1024]{1,0:T(8,128)S(1)} %unit_gradient.2), channel_id=1, source_target_pairs={{0,1},{1,0},{2,3},{3,2},{4,5},{5,4},{6,7},{7,6},{8,9},{9,8},{10,11... | collective-permute-start | bytes 2752520 | tf_op jit(solution)/shard_map/ppermute | solution.py:451

commit v10 on v7

--- a/solution.py
+++ b/solution.py
@@ -373,13 +373,29 @@
     )(emb, mine, got)
 
 
+def unit_kernel(emb_ref, unit_ref):
+    emb = emb_ref[...]
+    norm = jnp.sqrt(jnp.sum(emb * emb, axis=1, keepdims=True) + 1e-06)
+    unit_ref[...] = (emb / norm).astype(jnp.bfloat16)
+
+
+def unit_call(emb):
+    return pl.pallas_call(
+        unit_kernel,
+        out_shape=jax.ShapeDtypeStruct((ROWS, WIDTH), jnp.bfloat16),
+        in_specs=vmem(1),
+        out_specs=pl.BlockSpec(memory_space=pltpu.VMEM),
+        compiler_params=PARAMS,
+        name="unit_rows",
+    )(emb)
+
+
 def send(value, name):
     return lax.ppermute(value, AXES, ROUTES[name])
 
 
 def per_device(embeddings, partner):
-    norm = jnp.sqrt(jnp.sum(embeddings * embeddings, axis=1, keepdims=True) + 1e-06)
-    unit = (embeddings / norm).astype(jnp.bfloat16)
+    unit = unit_call(embeddings)
 
     run = lax.axis_index(("zh", "x", "y"))
     ids = jnp.stack([lax.axis_index(name) for name in DEV_AXES] + [run]).astype(jnp.int32)

time: 119 us -> 119 us (level)
  other arithmetic: 1.62 us -> 0.08 us
    reduce_sum x1 -> x0, other arithmetic: 1.4 us -> none  [per_device(): jnp.sum(embeddings * embeddings, axis=1, keepdims=True) + 1e-06]
where the time goes in v10:
time: 119 us; the launch traced here: 118 us
  starting transfers between devices  55.4 us (47%)
  blocking collectives  43.3 us (36%)
  Pallas kernels  14.9 us (13%)
  waiting for transfers between devices  2.21 us (2%)
    ppermute x14, starting transfers between devices, send(): return lax.ppermute(value, AXES, ROUTES[name])  42.7 us
    all_to_all x1, blocking collectives, per_device(): posts = lax.all_to_all(post, ('zh', 'x'), 0, 0)  23.2 us
    all_to_all x1, blocking collectives, per_device(): pays = lax.all_to_all(pay, DEV_AXES, 0, 0)  20.2 us
    ppermute x1, starting transfers between devices, per_device(): other = lax.ppermute(after(unit, ids), ('core',), [(0, 1), (1, 0)])  8.91 us
    pallas_call x6, Pallas kernels, block_call(): pl.pallas_call(kernel, out_shape=tuple(shapes), in_specs=smem(1) + vmem(l...  6.49 us
    pallas_call x2, Pallas kernels, grad_call(): pl.pallas_call(kernel, out_shape=tuple(shapes), in_specs=smem(1) + vmem(1...  3.97 us
    ppermute x1, starting transfers between devices, per_device(): got = lax.ppermute(for_other, ('core',), [(0, 1), (1, 0)])  3.78 us
  transfers between devices with their start and end apart: 16, of which 4 were waited for; matrix products, arithmetic and copies ran while one was open for 0% of the time, Pallas kernels for 8%

profile of v10, /device:TPU:1, one launch (start us, length us, event | category | flops | bytes accessed | tf_op | source)
XLA Modules:
  0.0 118.0 jit_solution(9240376589199045427)
XLA Ops:
  0.6 0.0 copy-start
  0.6 1.2 copy-done
  1.8 0.2 unit_rows.1.unit_ref.refs_1_.refs_12_
  2.0 0.1 pad_add_fusion.ids_ref.refs_0_
  2.1 8.9 %collective-permute-start = (bf16[224,1024]{1,0:T(8,128)(2,1)S(1)}, bf16[224,1024]{1,0:T(8,128)(2,1)S(1)}, u32[]{:S(2)}, u32[]{:S(2)}) collective-permute-start(bf16[224,1024]{1,0:T(8,128)(2,1)S(1)} %unit_rows.1.unit_ref.refs_1_.refs_12_), channel_id=1, source_target_pairs={{0,1},{1,0},{2,3},{3,2},{4,5},{5,4},{6,7},{7,6},{8,9},{9,8},{10,11... | collective-permute-start | bytes 1376264 | tf_op jit(solution)/shard_map/ppermute | solution.py:406
  11.0 1.9 %collective-permute-start.2 = (bf16[224,1024]{1,0:T(8,128)(2,1)S(1)}, bf16[224,1024]{1,0:T(8,128)(2,1)S(1)}, u32[]{:S(2)}, u32[]{:S(2)}) collective-permute-start(bf16[224,1024]{1,0:T(8,128)(2,1)S(1)} %unit_rows.1.unit_ref.refs_1_.refs_12_), channel_id=1, source_target_pairs={{1,5},{3,1},{5,7},{7,3},{9,13},{11,9},{13,15},{15,11},{17,21},{19,... | collective-permute-start | bytes 1376264 | tf_op jit(solution)/shard_map/ppermute | solution.py:394
  12.9 0.0 collective-permute-done.other_ref.refs_2_
  13.0 1.1 own_scores.1
  14.0 0.7 collective-permute-start.1
  14.7 11.5 %collective-permute-start.7 = (bf16[224,1024]{1,0:T(8,128)(2,1)S(1)}, bf16[224,1024]{1,0:T(8,128)(2,1)S(1)}, u32[]{:S(2)}, u32[]{:S(2)}) collective-permute-start(bf16[224,1024]{1,0:T(8,128)(2,1)S(1)} %unit_rows.1.unit_ref.refs_1_.refs_12_), channel_id=1, source_target_pairs={{126,128},{127,129},{128,126},{129,127},{254,256},{255,257},{256,2... | collective-permute-start | bytes 1376264 | tf_op jit(solution)/shard_map/ppermute | solution.py:394
  26.3 0.0 collective-permute-done.2.second_ref
  26.3 0.0 collective-permute-done.1.first_ref
  26.3 1.9 %collective-permute-start.3 = (bf16[224,1024]{1,0:T(8,128)(2,1)S(1)}, bf16[224,1024]{1,0:T(8,128)(2,1)S(1)}, u32[]{:S(2)}, u32[]{:S(2)}) collective-permute-start(bf16[224,1024]{1,0:T(8,128)(2,1)S(1)} %unit_rows.1.unit_ref.refs_1_.refs_12_), channel_id=1, source_target_pairs={{2,6},{3,7},{4,0},{5,1},{0,2},{1,3},{6,4},{7,5},{10,14},{11,15},{1... | collective-permute-start | bytes 1376264 | tf_op jit(solution)/shard_map/ppermute | solution.py:394
  28.2 0.6 choose.2.refs_5_.refs_13_
  28.8 1.3 %collective-permute-start.6 = (bf16[224,1024]{1,0:T(8,128)(2,1)S(1)}, bf16[224,1024]{1,0:T(8,128)(2,1)S(1)}, u32[]{:S(2)}, u32[]{:S(2)}) collective-permute-start(bf16[224,1024]{1,0:T(8,128)(2,1)S(1)} %choose.2.refs_5_.refs_13_), channel_id=1, source_target_pairs={{0,8},{1,9},{2,10},{3,11},{8,16},{9,17},{10,18},{11,19},{12,4},{13... | collective-permute-start | bytes 1376264 | tf_op jit(solution)/shard_map/ppermute | solution.py:394
  30.1 8.8 %collective-permute-start.9 = (bf16[224,1024]{1,0:T(8,128)(2,1)S(1)}, bf16[224,1024]{1,0:T(8,128)(2,1)S(1)}, u32[]{:S(2)}, u32[]{:S(2)}) collective-permute-start(bf16[224,1024]{1,0:T(8,128)(2,1)S(1)} %choose.2.refs_5_.refs_13_), channel_id=1, source_target_pairs={{126,128},{127,129},{128,126},{129,127},{254,256},{255,257},{256,2... | collective-permute-start | bytes 1376264 | tf_op jit(solution)/shard_map/ppermute | solution.py:394
  39.0 1.3 %collective-permute-start.8 = (bf16[224,1024]{1,0:T(8,128)(2,1)S(1)}, bf16[224,1024]{1,0:T(8,128)(2,1)S(1)}, u32[]{:S(2)}, u32[]{:S(2)}) collective-permute-start(bf16[224,1024]{1,0:T(8,128)(2,1)S(1)} %collective-permute-done.7.refs_7_), channel_id=1, source_target_pairs={{128,130},{129,131},{126,124},{127,125},{256,258},{257,259},{254,2... | collective-permute-start | bytes 1376264 | tf_op jit(solution)/shard_map/ppermute | solution.py:394
  40.3 1.0 block_scores.6
  41.4 1.3 %collective-permute-start.4 = (bf16[224,1024]{1,0:T(8,128)(2,1)S(1)}, bf16[224,1024]{1,0:T(8,128)(2,1)S(1)}, u32[]{:S(2)}, u32[]{:S(2)}) collective-permute-start(bf16[224,1024]{1,0:T(8,128)(2,1)S(1)} %choose.2.refs_5_.refs_13_), channel_id=1, source_target_pairs={{4,6},{5,7},{2,0},{3,1},{12,14},{13,15},{10,8},{11,9},{20,22},{21,... | collective-permute-start | bytes 1376264 | tf_op jit(solution)/shard_map/ppermute | solution.py:394
  42.7 0.7 collective-permute-start.5
  43.4 1.3 %collective-permute-start.11 = (bf16[224,1024]{1,0:T(8,128)(2,1)S(1)}, bf16[224,1024]{1,0:T(8,128)(2,1)S(1)}, u32[]{:S(2)}, u32[]{:S(2)}) collective-permute-start(bf16[224,1024]{1,0:T(8,128)(2,1)S(1)} %collective-permute-done.3.refs_5_.refs_14_), channel_id=1, source_target_pairs={{0,8},{1,9},{4,12},{5,13},{8,16},{9,17},{12,20},{13,21},{10,2},{11... | collective-permute-start | bytes 1376264 | tf_op jit(solution)/shard_map/ppermute | solution.py:394
  44.7 0.8 collective-permute-done.9.first_ref.refs_6_
  45.5 8.5 %collective-permute-start.10 = (bf16[224,1024]{1,0:T(8,128)(2,1)S(1)}, bf16[224,1024]{1,0:T(8,128)(2,1)S(1)}, u32[]{:S(2)}, u32[]{:S(2)}) collective-permute-start(bf16[224,1024]{1,0:T(8,128)(2,1)S(1)} %collective-permute-done.3.refs_5_.refs_14_), channel_id=1, source_target_pairs={{126,128},{127,129},{128,126},{129,127},{254,256},{255,257},{256,2... | collective-permute-start | bytes 1376264 | tf_op jit(solution)/shard_map/ppermute | solution.py:394
  54.0 0.0 collective-permute-done.8.refs_6_.second_ref
  54.0 0.6 choose.3
  54.6 1.3 %collective-permute-start.12 = (bf16[224,1024]{1,0:T(8,128)(2,1)S(1)}, bf16[224,1024]{1,0:T(8,128)(2,1)S(1)}, u32[]{:S(2)}, u32[]{:S(2)}) collective-permute-start(bf16[224,1024]{1,0:T(8,128)(2,1)S(1)} %choose.3), channel_id=1, source_target_pairs={{128,130},{129,131},{126,124},{127,125},{130,132},{131,133},{124,1... | collective-permute-start | bytes 1376264 | tf_op jit(solution)/shard_map/ppermute | solution.py:394
  55.9 1.0 block_scores.7
  56.9 0.0 collective-permute-done.5.refs_6_
  57.0 0.0 collective-permute-done.11.refs_5_
  57.0 1.3 %collective-permute-start.13 = (bf16[224,1024]{1,0:T(8,128)(2,1)S(1)}, bf16[224,1024]{1,0:T(8,128)(2,1)S(1)}, u32[]{:S(2)}, u32[]{:S(2)}) collective-permute-start(bf16[224,1024]{1,0:T(8,128)(2,1)S(1)} %collective-permute-done.4.refs_5_), channel_id=1, source_target_pairs={{0,8},{1,9},{8,16},{9,17},{14,6},{15,7},{16,24},{17,25},{22,14},{2... | collective-permute-start | bytes 1376264 | tf_op jit(solution)/shard_map/ppermute | solution.py:394
  58.3 0.7 collective-permute-start.14
  59.0 1.1 block_scores.8
  60.1 0.1 collective-permute-done.10.refs_7_
  60.1 1.1 block_scores.9
  61.2 0.1 collective-permute-done.12.refs_7_.refs_8_
  61.3 1.1 block_scores.10
  62.4 1.3 %collective-permute-done.13.refs_5_ = bf16[224,1024]{1,0:T(8,128)(2,1)S(1)} collective-permute-done((bf16[224,1024]{1,0:T(8,128)(2,1)S(1)}, bf16[224,1024]{1,0:T(8,128)(2,1)S(1)}, u32[]{:S(2)}, u32[]{:S(2)}) %collective-permute-start.13) | collective-permute-done | bytes 458784 | tf_op jit(solution)/shard_map/ppermute | solution.py:394
  63.7 0.0 collective-permute-done.14.refs_6_
  63.7 1.2 %block_scores.11 = (f32[224,224]{1,0:T(8,128)S(1)}, f32[224,224]{1,0:T(8,128)S(1)}, f32[32,4,128]{2,1,0:T(4,128)S(1)}, bf16[224,1024]{1,0:T(8,128)(2,1)S(1)}) custom-call(s32[4]{0:T(128)S(1)} %pad_add_fusion.ids_ref.refs_0_, bf16[224,1024]{1,0:T(8,128)(2,1)S(1)} %unit_rows.1.unit_ref.refs_1_.refs_12_, ...), custom_call_target="tpu_custom_call" | custom-call | flops 205520896 | bytes 2097152 | tf_op jit(solution)/shard_map/block_scores/pallas_call | solution.py:218
  64.9 20.2 %all_to_all.10.pay_ref = f32[32,4,128]{2,1,0:T(4,128)S(1)} all-to-all(f32[32,4,128]{2,1,0:T(4,128)S(1)} %get-tuple-element.83), channel_id=1, replica_groups=mesh['zh'=4,'x'=4,'y'=4,'zl'=4,'core'=2] {'y','zl','core'}, dimensions={0} | all-to-all | bytes 131072 | tf_op jit(solution)/shard_map/all_to_all | solution.py:443
  85.0 0.7 denoms.1
  85.7 23.2 %all_to_all.11.refs_2_ = f32[16,4,2,128]{3,2,1,0:T(2,128)S(1)} all-to-all(f32[16,4,2,128]{3,2,1,0:T(2,128)S(1)} %get-tuple-element.85), channel_id=1, replica_groups=mesh['zh'=4,'x'=4,'y'=4,'zl'=4,'core'=2] {'zh','x'}, dimensions={0} | all-to-all | bytes 131072 | tf_op jit(solution)/shard_map/all_to_all | solution.py:445
  108.9 1.7 %unit_gradient.2 = f32[224,1024]{1,0:T(8,128)S(1)} custom-call(s32[4]{0:T(128)S(1)} %pad_add_fusion.ids_ref.refs_0_, f32[16,2,128]{2,1,0:T(2,128)S(1)} %get-tuple-element.99.refs_1_, f32[16,4,2,128]{3,2,1,0:T(2,128)S(1)} %all_to_all.11.refs_2_, f32[2,128]{1,0:T(2,128)S(1)} %get-tuple-element.86.refs_3_, s32[1,224]{1,0:T(1,128)S(1)} %get-tuple-element.87.refs_4_, ...), custom_call_target="tpu_custom_call" | custom-call | flops 719323136 | bytes 6291456 | tf_op jit(solution)/shard_map/unit_gradient/pallas_call | solution.py:344
  110.7 3.8 %collective-permute-start.15 = (f32[224,1024]{1,0:T(8,128)S(1)}, f32[224,1024]{1,0:T(8,128)S(1)}, u32[]{:S(2)}, u32[]{:S(2)}) collective-permute-start(f32[224,1024]{1,0:T(8,128)S(1)} %unit_gradient.2), channel_id=1, source_target_pairs={{0,1},{1,0},{2,3},{3,2},{4,5},{5,4},{6,7},{7,6},{8,9},{9,8},{10,11... | collective-permute-start | bytes 2752520 | tf_op jit(solution)/shard_map/ppermute | solution.py:447
  114.4 0.0 copy-start.1
  114.5 2.2 %unit_gradient.3 = (f32[224,1024]{1,0:T(8,128)S(1)}, f32[1,1]{1,0:T(1,128)}) custom-call(s32[4]{0:T(128)S(1)} %pad_add_fusion.ids_ref.refs_0_, f32[16,2,128]{2,1,0:T(2,128)S(1)} %get-tuple-element.99.refs_1_, f32[16,4,2,128]{3,2,1,0:T(2,128)S(1)} %all_to_all.11.refs_2_, f32[2,128]{1,0:T(2,128)S(1)} %get-tuple-element.100.refs_3_, ...), custom_call_target="tpu_custom_call" | custom-call | flops 719323136 | bytes 6291456 | tf_op jit(solution)/shard_map/unit_gradient/pallas_call | solution.py:344
  116.7 0.0 collective-permute-done.15.got_ref
  116.7 1.3 %final.1 = f32[224,1024]{1,0:T(8,128)} custom-call(f32[224,1024]{1,0:T(8,128)S(1)} %copy-done.1, f32[224,1024]{1,0:T(8,128)S(1)} %get-tuple-element.109.mine_ref, f32[224,1024]{1,0:T(8,128)S(1)} %collective-permute-done.15.got_ref), custom_call_target="tpu_custom_call" | custom-call | flops 2293760 | bytes 3670016 | tf_op jit(solution)/shard_map/final/pallas_call | solution.py:365
  (7 shorter events, 0.0 us)
Async XLA Ops:
  0.6 1.2 %copy-start = (f32[224,1024]{1,0:T(8,128)S(1)}, f32[224,1024]{1,0:T(8,128)}, u32[]{:S(2)}) copy-start(f32[224,1024]{1,0:T(8,128)} %emb_ref.3) | copy-start | bytes 2752516
  2.1 10.9 %copy-start.2 = (s32[224]{0:T(256)S(1)}, s32[224]{0:T(256)}, u32[]{:S(2)}) copy-start(s32[224]{0:T(256)} %param.3) | copy-start | bytes 2692
  2.1 10.8 %collective-permute-start = (bf16[224,1024]{1,0:T(8,128)(2,1)S(1)}, bf16[224,1024]{1,0:T(8,128)(2,1)S(1)}, u32[]{:S(2)}, u32[]{:S(2)}) collective-permute-start(bf16[224,1024]{1,0:T(8,128)(2,1)S(1)} %unit_rows.1.unit_ref.refs_1_.refs_12_), channel_id=1, source_target_pairs={{0,1},{1,0},{2,3},{3,2},{4,5},{5,4},{6,7},{7,6},{8,9},{9,8},{10,11... | collective-permute-start | bytes 1376264 | tf_op jit(solution)/shard_map/ppermute | solution.py:406
  11.0 15.3 %collective-permute-start.2 = (bf16[224,1024]{1,0:T(8,128)(2,1)S(1)}, bf16[224,1024]{1,0:T(8,128)(2,1)S(1)}, u32[]{:S(2)}, u32[]{:S(2)}) collective-permute-start(bf16[224,1024]{1,0:T(8,128)(2,1)S(1)} %unit_rows.1.unit_ref.refs_1_.refs_12_), channel_id=1, source_target_pairs={{1,5},{3,1},{5,7},{7,3},{9,13},{11,9},{13,15},{15,11},{17,21},{19,... | collective-permute-start | bytes 1376264 | tf_op jit(solution)/shard_map/ppermute | solution.py:394
  14.0 12.3 %collective-permute-start.1 = (bf16[224,1024]{1,0:T(8,128)(2,1)S(1)}, bf16[224,1024]{1,0:T(8,128)(2,1)S(1)}, u32[]{:S(2)}, u32[]{:S(2)}) collective-permute-start(bf16[224,1024]{1,0:T(8,128)(2,1)S(1)} %unit_rows.1.unit_ref.refs_1_.refs_12_), channel_id=1, source_target_pairs={{0,4},{2,0},{4,6},{6,2},{8,12},{10,8},{12,14},{14,10},{16,20},{18,... | collective-permute-start | bytes 1376264 | tf_op jit(solution)/shard_map/ppermute | solution.py:394
  14.7 24.3 %collective-permute-start.7 = (bf16[224,1024]{1,0:T(8,128)(2,1)S(1)}, bf16[224,1024]{1,0:T(8,128)(2,1)S(1)}, u32[]{:S(2)}, u32[]{:S(2)}) collective-permute-start(bf16[224,1024]{1,0:T(8,128)(2,1)S(1)} %unit_rows.1.unit_ref.refs_1_.refs_12_), channel_id=1, source_target_pairs={{126,128},{127,129},{128,126},{129,127},{254,256},{255,257},{256,2... | collective-permute-start | bytes 1376264 | tf_op jit(solution)/shard_map/ppermute | solution.py:394
  26.3 15.1 %collective-permute-start.3 = (bf16[224,1024]{1,0:T(8,128)(2,1)S(1)}, bf16[224,1024]{1,0:T(8,128)(2,1)S(1)}, u32[]{:S(2)}, u32[]{:S(2)}) collective-permute-start(bf16[224,1024]{1,0:T(8,128)(2,1)S(1)} %unit_rows.1.unit_ref.refs_1_.refs_12_), channel_id=1, source_target_pairs={{2,6},{3,7},{4,0},{5,1},{0,2},{1,3},{6,4},{7,5},{10,14},{11,15},{1... | collective-permute-start | bytes 1376264 | tf_op jit(solution)/shard_map/ppermute | solution.py:394
  28.8 14.6 %collective-permute-start.6 = (bf16[224,1024]{1,0:T(8,128)(2,1)S(1)}, bf16[224,1024]{1,0:T(8,128)(2,1)S(1)}, u32[]{:S(2)}, u32[]{:S(2)}) collective-permute-start(bf16[224,1024]{1,0:T(8,128)(2,1)S(1)} %choose.2.refs_5_.refs_13_), channel_id=1, source_target_pairs={{0,8},{1,9},{2,10},{3,11},{8,16},{9,17},{10,18},{11,19},{12,4},{13... | collective-permute-start | bytes 1376264 | tf_op jit(solution)/shard_map/ppermute | solution.py:394
  30.1 15.3 %collective-permute-start.9 = (bf16[224,1024]{1,0:T(8,128)(2,1)S(1)}, bf16[224,1024]{1,0:T(8,128)(2,1)S(1)}, u32[]{:S(2)}, u32[]{:S(2)}) collective-permute-start(bf16[224,1024]{1,0:T(8,128)(2,1)S(1)} %choose.2.refs_5_.refs_13_), channel_id=1, source_target_pairs={{126,128},{127,129},{128,126},{129,127},{254,256},{255,257},{256,2... | collective-permute-start | bytes 1376264 | tf_op jit(solution)/shard_map/ppermute | solution.py:394
  39.0 15.0 %collective-permute-start.8 = (bf16[224,1024]{1,0:T(8,128)(2,1)S(1)}, bf16[224,1024]{1,0:T(8,128)(2,1)S(1)}, u32[]{:S(2)}, u32[]{:S(2)}) collective-permute-start(bf16[224,1024]{1,0:T(8,128)(2,1)S(1)} %collective-permute-done.7.refs_7_), channel_id=1, source_target_pairs={{128,130},{129,131},{126,124},{127,125},{256,258},{257,259},{254,2... | collective-permute-start | bytes 1376264 | tf_op jit(solution)/shard_map/ppermute | solution.py:394
  41.4 15.6 %collective-permute-start.4 = (bf16[224,1024]{1,0:T(8,128)(2,1)S(1)}, bf16[224,1024]{1,0:T(8,128)(2,1)S(1)}, u32[]{:S(2)}, u32[]{:S(2)}) collective-permute-start(bf16[224,1024]{1,0:T(8,128)(2,1)S(1)} %choose.2.refs_5_.refs_13_), channel_id=1, source_target_pairs={{4,6},{5,7},{2,0},{3,1},{12,14},{13,15},{10,8},{11,9},{20,22},{21,... | collective-permute-start | bytes 1376264 | tf_op jit(solution)/shard_map/ppermute | solution.py:394
  42.7 14.3 %collective-permute-start.5 = (bf16[224,1024]{1,0:T(8,128)(2,1)S(1)}, bf16[224,1024]{1,0:T(8,128)(2,1)S(1)}, u32[]{:S(2)}, u32[]{:S(2)}) collective-permute-start(bf16[224,1024]{1,0:T(8,128)(2,1)S(1)} %unit_rows.1.unit_ref.refs_1_.refs_12_), channel_id=1, source_target_pairs={{2,4},{3,5},{4,2},{5,3},{10,12},{11,13},{12,10},{13,11},{18,20},{1... | collective-permute-start | bytes 1376264 | tf_op jit(solution)/shard_map/ppermute | solution.py:394
  43.4 13.6 %collective-permute-start.11 = (bf16[224,1024]{1,0:T(8,128)(2,1)S(1)}, bf16[224,1024]{1,0:T(8,128)(2,1)S(1)}, u32[]{:S(2)}, u32[]{:S(2)}) collective-permute-start(bf16[224,1024]{1,0:T(8,128)(2,1)S(1)} %collective-permute-done.3.refs_5_.refs_14_), channel_id=1, source_target_pairs={{0,8},{1,9},{4,12},{5,13},{8,16},{9,17},{12,20},{13,21},{10,2},{11... | collective-permute-start | bytes 1376264 | tf_op jit(solution)/shard_map/ppermute | solution.py:394
  45.5 14.6 %collective-permute-start.10 = (bf16[224,1024]{1,0:T(8,128)(2,1)S(1)}, bf16[224,1024]{1,0:T(8,128)(2,1)S(1)}, u32[]{:S(2)}, u32[]{:S(2)}) collective-permute-start(bf16[224,1024]{1,0:T(8,128)(2,1)S(1)} %collective-permute-done.3.refs_5_.refs_14_), channel_id=1, source_target_pairs={{126,128},{127,129},{128,126},{129,127},{254,256},{255,257},{256,2... | collective-permute-start | bytes 1376264 | tf_op jit(solution)/shard_map/ppermute | solution.py:394
  54.6 6.7 %collective-permute-start.12 = (bf16[224,1024]{1,0:T(8,128)(2,1)S(1)}, bf16[224,1024]{1,0:T(8,128)(2,1)S(1)}, u32[]{:S(2)}, u32[]{:S(2)}) collective-permute-start(bf16[224,1024]{1,0:T(8,128)(2,1)S(1)} %choose.3), channel_id=1, source_target_pairs={{128,130},{129,131},{126,124},{127,125},{130,132},{131,133},{124,1... | collective-permute-start | bytes 1376264 | tf_op jit(solution)/shard_map/ppermute | solution.py:394
  57.0 6.7 %collective-permute-start.13 = (bf16[224,1024]{1,0:T(8,128)(2,1)S(1)}, bf16[224,1024]{1,0:T(8,128)(2,1)S(1)}, u32[]{:S(2)}, u32[]{:S(2)}) collective-permute-start(bf16[224,1024]{1,0:T(8,128)(2,1)S(1)} %collective-permute-done.4.refs_5_), channel_id=1, source_target_pairs={{0,8},{1,9},{8,16},{9,17},{14,6},{15,7},{16,24},{17,25},{22,14},{2... | collective-permute-start | bytes 1376264 | tf_op jit(solution)/shard_map/ppermute | solution.py:394
  58.3 5.4 %collective-permute-start.14 = (bf16[224,1024]{1,0:T(8,128)(2,1)S(1)}, bf16[224,1024]{1,0:T(8,128)(2,1)S(1)}, u32[]{:S(2)}, u32[]{:S(2)}) collective-permute-start(bf16[224,1024]{1,0:T(8,128)(2,1)S(1)} %collective-permute-done.5.refs_6_), channel_id=1, source_target_pairs={{2,10},{3,11},{10,18},{11,19},{12,4},{13,5},{18,26},{19,27},{20,12... | collective-permute-start | bytes 1376264 | tf_op jit(solution)/shard_map/ppermute | solution.py:394
  110.7 6.0 %collective-permute-start.15 = (f32[224,1024]{1,0:T(8,128)S(1)}, f32[224,1024]{1,0:T(8,128)S(1)}, u32[]{:S(2)}, u32[]{:S(2)}) collective-permute-start(f32[224,1024]{1,0:T(8,128)S(1)} %unit_gradient.2), channel_id=1, source_target_pairs={{0,1},{1,0},{2,3},{3,2},{4,5},{5,4},{6,7},{7,6},{8,9},{9,8},{10,11... | collective-permute-start | bytes 2752520 | tf_op jit(solution)/shard_map/ppermute | solution.py:447
  114.4 2.2 %copy-start.1 = (f32[224,1024]{1,0:T(8,128)S(1)}, f32[224,1024]{1,0:T(8,128)}, u32[]{:S(2)}) copy-start(f32[224,1024]{1,0:T(8,128)} %emb_ref.3) | copy-start | bytes 2752516

commit v11 on v10

--- a/solution.py
+++ b/solution.py
@@ -373,19 +373,29 @@
     )(emb, mine, got)
 
 
-def unit_kernel(emb_ref, unit_ref):
-    emb = emb_ref[...]
-    norm = jnp.sqrt(jnp.sum(emb * emb, axis=1, keepdims=True) + 1e-06)
-    unit_ref[...] = (emb / norm).astype(jnp.bfloat16)
+def unit_kernel(emb_any, unit_ref, emb_ref, sems):
+    copies = []
+    for part in range(7):
+        rows = pl.ds(part * 32, 32)
+        copies.append(pltpu.make_async_copy(emb_any.at[rows], emb_ref.at[rows], sems.at[part]))
+    for copy in copies:
+        copy.start()
+    for part, copy in enumerate(copies):
+        rows = pl.ds(part * 32, 32)
+        copy.wait()
+        emb = emb_ref[rows, :]
+        norm = jnp.sqrt(jnp.sum(emb * emb, axis=1, keepdims=True) + 1e-06)
+        unit_ref[rows, :] = (emb / norm).astype(jnp.bfloat16)
 
 
 def unit_call(emb):
     return pl.pallas_call(
         unit_kernel,
         out_shape=jax.ShapeDtypeStruct((ROWS, WIDTH), jnp.bfloat16),
-        in_specs=vmem(1),
+        in_specs=[pl.BlockSpec(memory_space=pl.ANY)],
         out_specs=pl.BlockSpec(memory_space=pltpu.VMEM),
-        compiler_params=PARAMS,
+        scratch_shapes=[pltpu.VMEM((ROWS, WIDTH), jnp.float32), pltpu.SemaphoreType.DMA((7,))],
+        compiler_params=pltpu.CompilerParams(vmem_limit_bytes=60 * 1024 * 1024),
         name="unit_rows",
     )(emb)
 

time: 119 us -> 121 us (1.017)
  Pallas kernels: 14.9 us -> 21.7 us
  starting transfers between devices: 55.4 us -> 52.8 us
    pallas_call x6, Pallas kernels: 6.49 us -> 9.4 us  [block_call(): pl.pallas_call(kernel, out_shape=tuple(shapes), in_specs=smem(1) + vmem(l...]
    ppermute x14, starting transfers between devices: 42.7 us -> 40.1 us  [send(): return lax.ppermute(value, AXES, ROUTES[name])]
    pallas_call x1, Pallas kernels: 0.18 us -> 2.49 us  [unit_call(): pl.pallas_call(unit_kernel, out_shape=jax.ShapeDtypeStruct((ROWS, WIDTH),...]
    all_to_all x1, blocking collectives: 23.2 us -> 21.1 us  [per_device(): posts = lax.all_to_all(post, ('zh', 'x'), 0, 0)]
    all_to_all x1, blocking collectives: 20.2 us -> 21.6 us  [per_device(): pays = lax.all_to_all(pay, DEV_AXES, 0, 0)]
  transfers between devices with their start and end apart: 16 -> 16, of which waited for: 4 -> 2; matrix products, arithmetic and copies ran while one was open for 0% -> 0% of each run, Pallas kernels for 8% -> 11%
where the time goes in v11:
time: 121 us; the launch traced here: 120 us
  starting transfers between devices  52.8 us (44%)
  blocking collectives  42.8 us (35%)
  Pallas kernels  21.7 us (18%)
  waiting for transfers between devices  2.17 us (2%)
    ppermute x14, starting transfers between devices, send(): return lax.ppermute(value, AXES, ROUTES[name])  40.1 us
    all_to_all x1, blocking collectives, per_device(): pays = lax.all_to_all(pay, DEV_AXES, 0, 0)  21.6 us
    all_to_all x1, blocking collectives, per_device(): posts = lax.all_to_all(post, ('zh', 'x'), 0, 0)  21.1 us
    pallas_call x6, Pallas kernels, block_call(): pl.pallas_call(kernel, out_shape=tuple(shapes), in_specs=smem(1) + vmem(l...  9.4 us
    ppermute x1, starting transfers between devices, per_device(): other = lax.ppermute(after(unit, ids), ('core',), [(0, 1), (1, 0)])  8.91 us
    pallas_call x2, Pallas kernels, grad_call(): pl.pallas_call(kernel, out_shape=tuple(shapes), in_specs=smem(1) + vmem(1...  5.02 us
    ppermute x1, starting transfers between devices, per_device(): got = lax.ppermute(for_other, ('core',), [(0, 1), (1, 0)])  3.78 us
    pallas_call x1, Pallas kernels, unit_call(): pl.pallas_call(unit_kernel, out_shape=jax.ShapeDtypeStruct((ROWS, WIDTH),...  2.49 us
  transfers between devices with their start and end apart: 16, of which 2 were waited for; matrix products, arithmetic and copies ran while one was open for 0% of the time, Pallas kernels for 11%

profile of v11, /device:TPU:1, one launch (start us, length us, event | category | flops | bytes accessed | tf_op | source)
XLA Modules:
  0.0 120.5 jit_solution(3059140161302526034)
XLA Ops:
  0.6 2.5 %unit_rows.1.unit_ref.refs_1_.refs_12_ = bf16[224,1024]{1,0:T(8,128)(2,1)} custom-call(f32[224,1024]{1,0:T(8,128)} %emb_ref.1), custom_call_target="tpu_custom_call" | custom-call | tf_op jit(solution)/shard_map/unit_rows/pallas_call | solution.py:392
  3.1 0.1 pad_add_fusion.ids_ref.refs_0_
  3.2 8.9 %collective-permute-start = (bf16[224,1024]{1,0:T(8,128)(2,1)}, bf16[224,1024]{1,0:T(8,128)(2,1)S(1)}, u32[]{:S(2)}, u32[]{:S(2)}) collective-permute-start(bf16[224,1024]{1,0:T(8,128)(2,1)} %unit_rows.1.unit_ref.refs_1_.refs_12_), channel_id=1, source_target_pairs={{0,1},{1,0},{2,3},{3,2},{4,5},{5,4},{6,7},{7,6},{8,9},{9,8},{10,11... | collective-permute-start | bytes 1376264 | tf_op jit(solution)/shard_map/ppermute | solution.py:416
  12.1 1.9 %collective-permute-start.2 = (bf16[224,1024]{1,0:T(8,128)(2,1)}, bf16[224,1024]{1,0:T(8,128)(2,1)S(1)}, u32[]{:S(2)}, u32[]{:S(2)}) collective-permute-start(bf16[224,1024]{1,0:T(8,128)(2,1)} %unit_rows.1.unit_ref.refs_1_.refs_12_), channel_id=1, source_target_pairs={{1,5},{3,1},{5,7},{7,3},{9,13},{11,9},{13,15},{15,11},{17,21},{19,... | collective-permute-start | bytes 1376264 | tf_op jit(solution)/shard_map/ppermute | solution.py:404
  14.1 0.0 collective-permute-done.other_ref.refs_2_
  14.1 1.6 %own_scores.1 = (s32[1,224]{1,0:T(1,128)S(1)}, f32[224,224]{1,0:T(8,128)S(1)}, f32[224,224]{1,0:T(8,128)S(1)}, f32[224,128]{1,0:T(8,128)S(1)}, f32[224,128]{1,0:T(8,128)S(1)}, /*index=5*/f32[1,128]{1,0:T(1,128)S(1)}) custom-call(s32[4]{0:T(128)S(1)} %pad_add_fusion.ids_ref.refs_0_, bf16[224,1024]{1,0:T(8,128)(2,1)} %unit_rows.1.unit_ref.refs_1_.refs_12_, ...), custom_call_target="tpu_custom_call" | custom-call | flops 205520896 | bytes 2097152 | tf_op jit(solution)/shard_map/own_scores/pallas_call | solution.py:114
  15.7 0.7 collective-permute-start.1
  16.4 11.6 %collective-permute-start.7 = (bf16[224,1024]{1,0:T(8,128)(2,1)}, bf16[224,1024]{1,0:T(8,128)(2,1)S(1)}, u32[]{:S(2)}, u32[]{:S(2)}) collective-permute-start(bf16[224,1024]{1,0:T(8,128)(2,1)} %unit_rows.1.unit_ref.refs_1_.refs_12_), channel_id=1, source_target_pairs={{126,128},{127,129},{128,126},{129,127},{254,256},{255,257},{256,2... | collective-permute-start | bytes 1376264 | tf_op jit(solution)/shard_map/ppermute | solution.py:404
  27.9 0.0 collective-permute-done.2.second_ref
  27.9 0.0 collective-permute-done.1.first_ref
  27.9 1.9 %collective-permute-start.3 = (bf16[224,1024]{1,0:T(8,128)(2,1)}, bf16[224,1024]{1,0:T(8,128)(2,1)S(1)}, u32[]{:S(2)}, u32[]{:S(2)}) collective-permute-start(bf16[224,1024]{1,0:T(8,128)(2,1)} %unit_rows.1.unit_ref.refs_1_.refs_12_), channel_id=1, source_target_pairs={{2,6},{3,7},{4,0},{5,1},{0,2},{1,3},{6,4},{7,5},{10,14},{11,15},{1... | collective-permute-start | bytes 1376264 | tf_op jit(solution)/shard_map/ppermute | solution.py:404
  29.9 0.6 choose.2.refs_5_.refs_13_
  30.5 1.3 %collective-permute-start.6 = (bf16[224,1024]{1,0:T(8,128)(2,1)S(1)}, bf16[224,1024]{1,0:T(8,128)(2,1)S(1)}, u32[]{:S(2)}, u32[]{:S(2)}) collective-permute-start(bf16[224,1024]{1,0:T(8,128)(2,1)S(1)} %choose.2.refs_5_.refs_13_), channel_id=1, source_target_pairs={{0,8},{1,9},{2,10},{3,11},{8,16},{9,17},{10,18},{11,19},{12,4},{13... | collective-permute-start | bytes 1376264 | tf_op jit(solution)/shard_map/ppermute | solution.py:404
  31.8 7.8 %collective-permute-start.9 = (bf16[224,1024]{1,0:T(8,128)(2,1)S(1)}, bf16[224,1024]{1,0:T(8,128)(2,1)S(1)}, u32[]{:S(2)}, u32[]{:S(2)}) collective-permute-start(bf16[224,1024]{1,0:T(8,128)(2,1)S(1)} %choose.2.refs_5_.refs_13_), channel_id=1, source_target_pairs={{126,128},{127,129},{128,126},{129,127},{254,256},{255,257},{256,2... | collective-permute-start | bytes 1376264 | tf_op jit(solution)/shard_map/ppermute | solution.py:404
  39.6 0.0 collective-permute-done.7.refs_7_
  39.6 1.3 %collective-permute-start.8 = (bf16[224,1024]{1,0:T(8,128)(2,1)S(1)}, bf16[224,1024]{1,0:T(8,128)(2,1)S(1)}, u32[]{:S(2)}, u32[]{:S(2)}) collective-permute-start(bf16[224,1024]{1,0:T(8,128)(2,1)S(1)} %collective-permute-done.7.refs_7_), channel_id=1, source_target_pairs={{128,130},{129,131},{126,124},{127,125},{256,258},{257,259},{254,2... | collective-permute-start | bytes 1376264 | tf_op jit(solution)/shard_map/ppermute | solution.py:404
  41.0 1.5 %block_scores.6 = (f32[224,224]{1,0:T(8,128)S(1)}, f32[224,224]{1,0:T(8,128)S(1)}, f32[224,128]{1,0:T(8,128)S(1)}, f32[224,128]{1,0:T(8,128)S(1)}) custom-call(s32[4]{0:T(128)S(1)} %pad_add_fusion.ids_ref.refs_0_, bf16[224,1024]{1,0:T(8,128)(2,1)} %unit_rows.1.unit_ref.refs_1_.refs_12_, bf16[224,1024]{1,0:T(8,128)(2,1)S(1)} %collective-permute-done.other_ref.refs_2_, ...), custom_call_target="tpu_custom_call" | custom-call | flops 205520896 | bytes 2097152 | tf_op jit(solution)/shard_map/block_scores/pallas_call | solution.py:218
  42.5 0.0 collective-permute-done.3.refs_5_.refs_14_
  42.5 1.3 %collective-permute-start.4 = (bf16[224,1024]{1,0:T(8,128)(2,1)S(1)}, bf16[224,1024]{1,0:T(8,128)(2,1)S(1)}, u32[]{:S(2)}, u32[]{:S(2)}) collective-permute-start(bf16[224,1024]{1,0:T(8,128)(2,1)S(1)} %choose.2.refs_5_.refs_13_), channel_id=1, source_target_pairs={{4,6},{5,7},{2,0},{3,1},{12,14},{13,15},{10,8},{11,9},{20,22},{21,... | collective-permute-start | bytes 1376264 | tf_op jit(solution)/shard_map/ppermute | solution.py:404
  43.8 0.7 collective-permute-start.5
  44.5 0.0 collective-permute-done.6.refs_5_
  44.5 1.3 %collective-permute-start.11 = (bf16[224,1024]{1,0:T(8,128)(2,1)S(1)}, bf16[224,1024]{1,0:T(8,128)(2,1)S(1)}, u32[]{:S(2)}, u32[]{:S(2)}) collective-permute-start(bf16[224,1024]{1,0:T(8,128)(2,1)S(1)} %collective-permute-done.3.refs_5_.refs_14_), channel_id=1, source_target_pairs={{0,8},{1,9},{4,12},{5,13},{8,16},{9,17},{12,20},{13,21},{10,2},{11... | collective-permute-start | bytes 1376264 | tf_op jit(solution)/shard_map/ppermute | solution.py:404
  45.8 1.5 %collective-permute-done.9.first_ref.refs_6_ = bf16[224,1024]{1,0:T(8,128)(2,1)S(1)} collective-permute-done((bf16[224,1024]{1,0:T(8,128)(2,1)S(1)}, bf16[224,1024]{1,0:T(8,128)(2,1)S(1)}, u32[]{:S(2)}, u32[]{:S(2)}) %collective-permute-start.9) | collective-permute-done | bytes 458784 | tf_op jit(solution)/shard_map/ppermute | solution.py:404
  47.3 6.9 %collective-permute-start.10 = (bf16[224,1024]{1,0:T(8,128)(2,1)S(1)}, bf16[224,1024]{1,0:T(8,128)(2,1)S(1)}, u32[]{:S(2)}, u32[]{:S(2)}) collective-permute-start(bf16[224,1024]{1,0:T(8,128)(2,1)S(1)} %collective-permute-done.3.refs_5_.refs_14_), channel_id=1, source_target_pairs={{126,128},{127,129},{128,126},{129,127},{254,256},{255,257},{256,2... | collective-permute-start | bytes 1376264 | tf_op jit(solution)/shard_map/ppermute | solution.py:404
  54.3 0.0 collective-permute-done.8.refs_6_.second_ref
  54.3 0.6 choose.3
  54.9 1.3 %collective-permute-start.12 = (bf16[224,1024]{1,0:T(8,128)(2,1)S(1)}, bf16[224,1024]{1,0:T(8,128)(2,1)S(1)}, u32[]{:S(2)}, u32[]{:S(2)}) collective-permute-start(bf16[224,1024]{1,0:T(8,128)(2,1)S(1)} %choose.3), channel_id=1, source_target_pairs={{128,130},{129,131},{126,124},{127,125},{130,132},{131,133},{124,1... | collective-permute-start | bytes 1376264 | tf_op jit(solution)/shard_map/ppermute | solution.py:404
  56.2 1.5 %block_scores.7 = (f32[224,224]{1,0:T(8,128)S(1)}, f32[224,224]{1,0:T(8,128)S(1)}, f32[224,128]{1,0:T(8,128)S(1)}, f32[224,128]{1,0:T(8,128)S(1)}) custom-call(s32[4]{0:T(128)S(1)} %pad_add_fusion.ids_ref.refs_0_, bf16[224,1024]{1,0:T(8,128)(2,1)} %unit_rows.1.unit_ref.refs_1_.refs_12_, bf16[224,1024]{1,0:T(8,128)(2,1)S(1)} %collective-permute-done.other_ref.refs_2_, ...), custom_call_target="tpu_custom_call" | custom-call | flops 205520896 | bytes 2097152 | tf_op jit(solution)/shard_map/block_scores/pallas_call | solution.py:218
  57.7 0.0 collective-permute-done.4.refs_5_
  57.7 0.0 collective-permute-done.5.refs_6_
  57.7 0.0 collective-permute-done.11.refs_5_
  57.7 1.3 %collective-permute-start.13 = (bf16[224,1024]{1,0:T(8,128)(2,1)S(1)}, bf16[224,1024]{1,0:T(8,128)(2,1)S(1)}, u32[]{:S(2)}, u32[]{:S(2)}) collective-permute-start(bf16[224,1024]{1,0:T(8,128)(2,1)S(1)} %collective-permute-done.4.refs_5_), channel_id=1, source_target_pairs={{0,8},{1,9},{8,16},{9,17},{14,6},{15,7},{16,24},{17,25},{22,14},{2... | collective-permute-start | bytes 1376264 | tf_op jit(solution)/shard_map/ppermute | solution.py:404
  59.1 0.7 collective-permute-start.14
  59.8 1.6 %block_scores.8 = (f32[224,224]{1,0:T(8,128)S(1)}, f32[224,224]{1,0:T(8,128)S(1)}, f32[224,128]{1,0:T(8,128)S(1)}, f32[224,128]{1,0:T(8,128)S(1)}, bf16[224,1024]{1,0:T(8,128)(2,1)S(1)}) custom-call(s32[4]{0:T(128)S(1)} %pad_add_fusion.ids_ref.refs_0_, bf16[224,1024]{1,0:T(8,128)(2,1)} %unit_rows.1.unit_ref.refs_1_.refs_12_, ...), custom_call_target="tpu_custom_call" | custom-call | flops 205520896 | bytes 2097152 | tf_op jit(solution)/shard_map/block_scores/pallas_call | solution.py:218
  61.3 0.6 collective-permute-done.10.refs_7_
  62.0 1.6 %block_scores.9 = (f32[224,224]{1,0:T(8,128)S(1)}, f32[224,224]{1,0:T(8,128)S(1)}, f32[224,128]{1,0:T(8,128)S(1)}, f32[224,128]{1,0:T(8,128)S(1)}, bf16[224,1024]{1,0:T(8,128)(2,1)S(1)}) custom-call(s32[4]{0:T(128)S(1)} %pad_add_fusion.ids_ref.refs_0_, bf16[224,1024]{1,0:T(8,128)(2,1)} %unit_rows.1.unit_ref.refs_1_.refs_12_, ...), custom_call_target="tpu_custom_call" | custom-call | flops 205520896 | bytes 2097152 | tf_op jit(solution)/shard_map/block_scores/pallas_call | solution.py:218
  63.5 0.0 collective-permute-done.12.refs_7_.refs_8_
  63.5 1.6 %block_scores.10 = (f32[224,224]{1,0:T(8,128)S(1)}, f32[224,224]{1,0:T(8,128)S(1)}, f32[224,128]{1,0:T(8,128)S(1)}, f32[224,128]{1,0:T(8,128)S(1)}, bf16[224,1024]{1,0:T(8,128)(2,1)S(1)}) custom-call(s32[4]{0:T(128)S(1)} %pad_add_fusion.ids_ref.refs_0_, bf16[224,1024]{1,0:T(8,128)(2,1)} %unit_rows.1.unit_ref.refs_1_.refs_12_, ...), custom_call_target="tpu_custom_call" | custom-call | flops 205520896 | bytes 2097152 | tf_op jit(solution)/shard_map/block_scores/pallas_call | solution.py:218
  65.1 0.0 collective-permute-done.13.refs_5_
  65.1 1.7 %block_scores.11 = (f32[224,224]{1,0:T(8,128)S(1)}, f32[224,224]{1,0:T(8,128)S(1)}, f32[32,4,128]{2,1,0:T(4,128)S(1)}, bf16[224,1024]{1,0:T(8,128)(2,1)S(1)}) custom-call(s32[4]{0:T(128)S(1)} %pad_add_fusion.ids_ref.refs_0_, bf16[224,1024]{1,0:T(8,128)(2,1)} %unit_rows.1.unit_ref.refs_1_.refs_12_, ...), custom_call_target="tpu_custom_call" | custom-call | flops 205520896 | bytes 2097152 | tf_op jit(solution)/shard_map/block_scores/pallas_call | solution.py:218
  66.8 21.6 %all_to_all.10.pay_ref = f32[32,4,128]{2,1,0:T(4,128)S(1)} all-to-all(f32[32,4,128]{2,1,0:T(4,128)S(1)} %get-tuple-element.83), channel_id=1, replica_groups=mesh['zh'=4,'x'=4,'y'=4,'zl'=4,'core'=2] {'y','zl','core'}, dimensions={0} | all-to-all | bytes 131072 | tf_op jit(solution)/shard_map/all_to_all | solution.py:453
  88.5 0.7 denoms.1
  89.2 21.1 %all_to_all.11.refs_2_ = f32[16,4,2,128]{3,2,1,0:T(2,128)S(1)} all-to-all(f32[16,4,2,128]{3,2,1,0:T(2,128)S(1)} %get-tuple-element.85), channel_id=1, replica_groups=mesh['zh'=4,'x'=4,'y'=4,'zl'=4,'core'=2] {'zh','x'}, dimensions={0} | all-to-all | bytes 131072 | tf_op jit(solution)/shard_map/all_to_all | solution.py:455
  110.3 2.2 %unit_gradient.2 = f32[224,1024]{1,0:T(8,128)S(1)} custom-call(s32[4]{0:T(128)S(1)} %pad_add_fusion.ids_ref.refs_0_, f32[16,2,128]{2,1,0:T(2,128)S(1)} %get-tuple-element.99.refs_1_, f32[16,4,2,128]{3,2,1,0:T(2,128)S(1)} %all_to_all.11.refs_2_, f32[2,128]{1,0:T(2,128)S(1)} %get-tuple-element.86.refs_3_, s32[1,224]{1,0:T(1,128)S(1)} %get-tuple-element.87.refs_4_, ...), custom_call_target="tpu_custom_call" | custom-call | flops 719323136 | bytes 6291456 | tf_op jit(solution)/shard_map/unit_gradient/pallas_call | solution.py:344
  112.6 3.8 %collective-permute-start.15 = (f32[224,1024]{1,0:T(8,128)S(1)}, f32[224,1024]{1,0:T(8,128)S(1)}, u32[]{:S(2)}, u32[]{:S(2)}) collective-permute-start(f32[224,1024]{1,0:T(8,128)S(1)} %unit_gradient.2), channel_id=1, source_target_pairs={{0,1},{1,0},{2,3},{3,2},{4,5},{5,4},{6,7},{7,6},{8,9},{9,8},{10,11... | collective-permute-start | bytes 2752520 | tf_op jit(solution)/shard_map/ppermute | solution.py:457
  116.4 0.0 copy-start
  116.4 2.8 %unit_gradient.3 = (f32[224,1024]{1,0:T(8,128)S(1)}, f32[1,1]{1,0:T(1,128)}) custom-call(s32[4]{0:T(128)S(1)} %pad_add_fusion.ids_ref.refs_0_, f32[16,2,128]{2,1,0:T(2,128)S(1)} %get-tuple-element.99.refs_1_, f32[16,4,2,128]{3,2,1,0:T(2,128)S(1)} %all_to_all.11.refs_2_, f32[2,128]{1,0:T(2,128)S(1)} %get-tuple-element.100.refs_3_, ...), custom_call_target="tpu_custom_call" | custom-call | flops 719323136 | bytes 6291456 | tf_op jit(solution)/shard_map/unit_gradient/pallas_call | solution.py:344
  119.2 1.3 %final.1 = f32[224,1024]{1,0:T(8,128)} custom-call(f32[224,1024]{1,0:T(8,128)S(1)} %copy-done, f32[224,1024]{1,0:T(8,128)S(1)} %get-tuple-element.109.mine_ref, f32[224,1024]{1,0:T(8,128)S(1)} %collective-permute-done.15.got_ref), custom_call_target="tpu_custom_call" | custom-call | flops 2293760 | bytes 3670016 | tf_op jit(solution)/shard_map/final/pallas_call | solution.py:365
  (5 shorter events, 0.0 us)
Async XLA Ops:
  3.2 10.9 %copy-start.1 = (s32[224]{0:T(256)S(1)}, s32[224]{0:T(256)}, u32[]{:S(2)}) copy-start(s32[224]{0:T(256)} %param.3) | copy-start | bytes 2692
  3.2 10.8 %collective-permute-start = (bf16[224,1024]{1,0:T(8,128)(2,1)}, bf16[224,1024]{1,0:T(8,128)(2,1)S(1)}, u32[]{:S(2)}, u32[]{:S(2)}) collective-permute-start(bf16[224,1024]{1,0:T(8,128)(2,1)} %unit_rows.1.unit_ref.refs_1_.refs_12_), channel_id=1, source_target_pairs={{0,1},{1,0},{2,3},{3,2},{4,5},{5,4},{6,7},{7,6},{8,9},{9,8},{10,11... | collective-permute-start | bytes 1376264 | tf_op jit(solution)/shard_map/ppermute | solution.py:416
  12.1 15.8 %collective-permute-start.2 = (bf16[224,1024]{1,0:T(8,128)(2,1)}, bf16[224,1024]{1,0:T(8,128)(2,1)S(1)}, u32[]{:S(2)}, u32[]{:S(2)}) collective-permute-start(bf16[224,1024]{1,0:T(8,128)(2,1)} %unit_rows.1.unit_ref.refs_1_.refs_12_), channel_id=1, source_target_pairs={{1,5},{3,1},{5,7},{7,3},{9,13},{11,9},{13,15},{15,11},{17,21},{19,... | collective-permute-start | bytes 1376264 | tf_op jit(solution)/shard_map/ppermute | solution.py:404
  15.7 12.3 %collective-permute-start.1 = (bf16[224,1024]{1,0:T(8,128)(2,1)}, bf16[224,1024]{1,0:T(8,128)(2,1)S(1)}, u32[]{:S(2)}, u32[]{:S(2)}) collective-permute-start(bf16[224,1024]{1,0:T(8,128)(2,1)} %unit_rows.1.unit_ref.refs_1_.refs_12_), channel_id=1, source_target_pairs={{0,4},{2,0},{4,6},{6,2},{8,12},{10,8},{12,14},{14,10},{16,20},{18,... | collective-permute-start | bytes 1376264 | tf_op jit(solution)/shard_map/ppermute | solution.py:404
  16.4 23.3 %collective-permute-start.7 = (bf16[224,1024]{1,0:T(8,128)(2,1)}, bf16[224,1024]{1,0:T(8,128)(2,1)S(1)}, u32[]{:S(2)}, u32[]{:S(2)}) collective-permute-start(bf16[224,1024]{1,0:T(8,128)(2,1)} %unit_rows.1.unit_ref.refs_1_.refs_12_), channel_id=1, source_target_pairs={{126,128},{127,129},{128,126},{129,127},{254,256},{255,257},{256,2... | collective-permute-start | bytes 1376264 | tf_op jit(solution)/shard_map/ppermute | solution.py:404
  27.9 14.5 %collective-permute-start.3 = (bf16[224,1024]{1,0:T(8,128)(2,1)}, bf16[224,1024]{1,0:T(8,128)(2,1)S(1)}, u32[]{:S(2)}, u32[]{:S(2)}) collective-permute-start(bf16[224,1024]{1,0:T(8,128)(2,1)} %unit_rows.1.unit_ref.refs_1_.refs_12_), channel_id=1, source_target_pairs={{2,6},{3,7},{4,0},{5,1},{0,2},{1,3},{6,4},{7,5},{10,14},{11,15},{1... | collective-permute-start | bytes 1376264 | tf_op jit(solution)/shard_map/ppermute | solution.py:404
  30.5 14.0 %collective-permute-start.6 = (bf16[224,1024]{1,0:T(8,128)(2,1)S(1)}, bf16[224,1024]{1,0:T(8,128)(2,1)S(1)}, u32[]{:S(2)}, u32[]{:S(2)}) collective-permute-start(bf16[224,1024]{1,0:T(8,128)(2,1)S(1)} %choose.2.refs_5_.refs_13_), channel_id=1, source_target_pairs={{0,8},{1,9},{2,10},{3,11},{8,16},{9,17},{10,18},{11,19},{12,4},{13... | collective-permute-start | bytes 1376264 | tf_op jit(solution)/shard_map/ppermute | solution.py:404
  31.8 15.5 %collective-permute-start.9 = (bf16[224,1024]{1,0:T(8,128)(2,1)S(1)}, bf16[224,1024]{1,0:T(8,128)(2,1)S(1)}, u32[]{:S(2)}, u32[]{:S(2)}) collective-permute-start(bf16[224,1024]{1,0:T(8,128)(2,1)S(1)} %choose.2.refs_5_.refs_13_), channel_id=1, source_target_pairs={{126,128},{127,129},{128,126},{129,127},{254,256},{255,257},{256,2... | collective-permute-start | bytes 1376264 | tf_op jit(solution)/shard_map/ppermute | solution.py:404
  39.6 14.6 %collective-permute-start.8 = (bf16[224,1024]{1,0:T(8,128)(2,1)S(1)}, bf16[224,1024]{1,0:T(8,128)(2,1)S(1)}, u32[]{:S(2)}, u32[]{:S(2)}) collective-permute-start(bf16[224,1024]{1,0:T(8,128)(2,1)S(1)} %collective-permute-done.7.refs_7_), channel_id=1, source_target_pairs={{128,130},{129,131},{126,124},{127,125},{256,258},{257,259},{254,2... | collective-permute-start | bytes 1376264 | tf_op jit(solution)/shard_map/ppermute | solution.py:404
  42.5 15.2 %collective-permute-start.4 = (bf16[224,1024]{1,0:T(8,128)(2,1)S(1)}, bf16[224,1024]{1,0:T(8,128)(2,1)S(1)}, u32[]{:S(2)}, u32[]{:S(2)}) collective-permute-start(bf16[224,1024]{1,0:T(8,128)(2,1)S(1)} %choose.2.refs_5_.refs_13_), channel_id=1, source_target_pairs={{4,6},{5,7},{2,0},{3,1},{12,14},{13,15},{10,8},{11,9},{20,22},{21,... | collective-permute-start | bytes 1376264 | tf_op jit(solution)/shard_map/ppermute | solution.py:404
  43.8 13.9 %collective-permute-start.5 = (bf16[224,1024]{1,0:T(8,128)(2,1)}, bf16[224,1024]{1,0:T(8,128)(2,1)S(1)}, u32[]{:S(2)}, u32[]{:S(2)}) collective-permute-start(bf16[224,1024]{1,0:T(8,128)(2,1)} %unit_rows.1.unit_ref.refs_1_.refs_12_), channel_id=1, source_target_pairs={{2,4},{3,5},{4,2},{5,3},{10,12},{11,13},{12,10},{13,11},{18,20},{1... | collective-permute-start | bytes 1376264 | tf_op jit(solution)/shard_map/ppermute | solution.py:404
  44.5 13.2 %collective-permute-start.11 = (bf16[224,1024]{1,0:T(8,128)(2,1)S(1)}, bf16[224,1024]{1,0:T(8,128)(2,1)S(1)}, u32[]{:S(2)}, u32[]{:S(2)}) collective-permute-start(bf16[224,1024]{1,0:T(8,128)(2,1)S(1)} %collective-permute-done.3.refs_5_.refs_14_), channel_id=1, source_target_pairs={{0,8},{1,9},{4,12},{5,13},{8,16},{9,17},{12,20},{13,21},{10,2},{11... | collective-permute-start | bytes 1376264 | tf_op jit(solution)/shard_map/ppermute | solution.py:404
  47.3 14.6 %collective-permute-start.10 = (bf16[224,1024]{1,0:T(8,128)(2,1)S(1)}, bf16[224,1024]{1,0:T(8,128)(2,1)S(1)}, u32[]{:S(2)}, u32[]{:S(2)}) collective-permute-start(bf16[224,1024]{1,0:T(8,128)(2,1)S(1)} %collective-permute-done.3.refs_5_.refs_14_), channel_id=1, source_target_pairs={{126,128},{127,129},{128,126},{129,127},{254,256},{255,257},{256,2... | collective-permute-start | bytes 1376264 | tf_op jit(solution)/shard_map/ppermute | solution.py:404
  54.9 8.7 %collective-permute-start.12 = (bf16[224,1024]{1,0:T(8,128)(2,1)S(1)}, bf16[224,1024]{1,0:T(8,128)(2,1)S(1)}, u32[]{:S(2)}, u32[]{:S(2)}) collective-permute-start(bf16[224,1024]{1,0:T(8,128)(2,1)S(1)} %choose.3), channel_id=1, source_target_pairs={{128,130},{129,131},{126,124},{127,125},{130,132},{131,133},{124,1... | collective-permute-start | bytes 1376264 | tf_op jit(solution)/shard_map/ppermute | solution.py:404
  57.7 7.4 %collective-permute-start.13 = (bf16[224,1024]{1,0:T(8,128)(2,1)S(1)}, bf16[224,1024]{1,0:T(8,128)(2,1)S(1)}, u32[]{:S(2)}, u32[]{:S(2)}) collective-permute-start(bf16[224,1024]{1,0:T(8,128)(2,1)S(1)} %collective-permute-done.4.refs_5_), channel_id=1, source_target_pairs={{0,8},{1,9},{8,16},{9,17},{14,6},{15,7},{16,24},{17,25},{22,14},{2... | collective-permute-start | bytes 1376264 | tf_op jit(solution)/shard_map/ppermute | solution.py:404
  59.1 6.1 %collective-permute-start.14 = (bf16[224,1024]{1,0:T(8,128)(2,1)S(1)}, bf16[224,1024]{1,0:T(8,128)(2,1)S(1)}, u32[]{:S(2)}, u32[]{:S(2)}) collective-permute-start(bf16[224,1024]{1,0:T(8,128)(2,1)S(1)} %collective-permute-done.5.refs_6_), channel_id=1, source_target_pairs={{2,10},{3,11},{10,18},{11,19},{12,4},{13,5},{18,26},{19,27},{20,12... | collective-permute-start | bytes 1376264 | tf_op jit(solution)/shard_map/ppermute | solution.py:404
  112.6 6.6 %collective-permute-start.15 = (f32[224,1024]{1,0:T(8,128)S(1)}, f32[224,1024]{1,0:T(8,128)S(1)}, u32[]{:S(2)}, u32[]{:S(2)}) collective-permute-start(f32[224,1024]{1,0:T(8,128)S(1)} %unit_gradient.2), channel_id=1, source_target_pairs={{0,1},{1,0},{2,3},{3,2},{4,5},{5,4},{6,7},{7,6},{8,9},{9,8},{10,11... | collective-permute-start | bytes 2752520 | tf_op jit(solution)/shard_map/ppermute | solution.py:457
  116.4 2.8 %copy-start = (f32[224,1024]{1,0:T(8,128)S(1)}, f32[224,1024]{1,0:T(8,128)}, u32[]{:S(2)}) copy-start(f32[224,1024]{1,0:T(8,128)} %emb_ref.1) | copy-start | bytes 2752516
